TPU v7x, 32 devices: a whole 2x2x4 slice. The times are simulated.
32 devices in a mesh: seq: 8 (over z, x), head: 4 (over y, core).
Axes of the slice: x: 2, y: 2, z: 4, core: 2. Of those that a mesh axis runs over, the one named last changes fastest.
Arguments:
- layer_input: bfloat16 [4096, 4096], P('seq', 'head'), may hold values from -6 to 6
- query_rows: bfloat16 [4096, 4096], P('seq', 'head'), may hold values from -6 to 6
- key_rows: bfloat16 [4096, 4096], P('seq', 'head'), may hold values from -6 to 6
- value_rows: bfloat16 [4096, 4096], P('seq', 'head'), may hold values from -28 to 28
- out_weight: bfloat16 [4096, 4096], P('head'), may hold values from -0.09375 to 0.09375
- norm_gain: float32 [4096], P('head'), may hold values from 0.1 to 1.9
- cotangent: bfloat16 [4096, 4096], P('seq', 'head'), may hold values from -0.125 to 0.125
Outputs:
- projection_gradient: float32 [4096, 3, 4096], P('seq', None, 'head')
- output_gradient: float32 [4096, 4096], P('head', 'seq')
All inputs are finite; a program needn't handle non-finite values.
Results may differ from a plain program's by a relative error of at most 0.023.
Values may be sent and summed in bfloat16 or wider, within the bound.
No kernel may reach another device: no remote copies, remote signals or barrier semaphores. Data moves between devices by JAX's collectives and lax.ppermute only.
A program may use at most 192 MiB of HBM per device.

v0:
```python
import jax
import jax.numpy as jnp
from jax import lax
from jax.sharding import PartitionSpec as P

HEAD_DIM = 128


def entering(array, axis, combine, identity, reverse):
    size, position = (lax.axis_size(axis), lax.axis_index(axis))
    everything = lax.all_gather(array.astype(jnp.bfloat16), axis)
    start = jnp.broadcast_to(jnp.asarray(identity, array.dtype), array.shape)

    def lap(k, before):
        at = size - 1 - k if reverse else k
        reached = at > position if reverse else at < position
        new = combine(before, everything[at].astype(array.dtype))
        return jnp.where(reached, new, before)

    return lax.fori_loop(0, size, lap, start)


def lower_mask(count):
    rows = lax.broadcasted_iota(jnp.int32, (count, count), 0)
    cols = lax.broadcasted_iota(jnp.int32, (count, count), 1)
    return rows >= cols


def body(layer_input, query_rows, key_rows, value_rows, out_weight, norm_gain, cotangent):
    gathered_input, gathered_cot = (
        lax.all_gather(layer_input, "head", axis=1, tiled=True),
        lax.all_gather(cotangent, "head", axis=1, tiled=True),
    )
    tokens = query_rows.shape[0]
    width = query_rows.shape[1]
    heads = width // HEAD_DIM
    queries = query_rows.reshape(tokens, heads, HEAD_DIM)
    key_heads = key_rows.reshape(tokens, heads, HEAD_DIM)
    value_heads = value_rows.reshape(tokens, heads, HEAD_DIM)
    gain = norm_gain.reshape(heads, HEAD_DIM)
    lower = lower_mask(tokens)[None]
    block_state = jnp.einsum(
        "thd,the->hde", key_heads, value_heads, preferred_element_type=jnp.float32
    )
    state_in = entering(block_state, "seq", jnp.add, jnp.zeros_like(block_state), False)
    state_low = state_in.astype(jnp.bfloat16)
    scores = jnp.einsum("thd,shd->hts", queries, key_heads, preferred_element_type=jnp.float32)
    scores = jnp.where(lower, scores, 0.0).astype(jnp.bfloat16)
    attention = jnp.einsum("hts,she->the", scores, value_heads, preferred_element_type=jnp.float32)
    attention = attention + jnp.einsum(
        "thd,hde->the", queries, state_low, preferred_element_type=jnp.float32
    )
    rms_value = jnp.sqrt(jnp.mean(attention * attention, axis=-1, keepdims=True) + 1e-05)
    normed = attention / rms_value
    gated = (normed * gain).astype(jnp.bfloat16).reshape(tokens, width)
    gated_grad = jnp.einsum(
        "tj,cj->tc", gathered_cot, out_weight, preferred_element_type=jnp.float32
    )
    scaled = gated_grad.reshape(tokens, heads, HEAD_DIM) * gain
    inner = jnp.mean(scaled * normed, axis=-1, keepdims=True)
    pre_grad = ((scaled - normed * inner) / rms_value).astype(jnp.bfloat16)
    mixing = jnp.einsum("the,she->hts", pre_grad, value_heads, preferred_element_type=jnp.float32)
    mixing = jnp.where(lower, mixing, 0.0).astype(jnp.bfloat16)
    query_grad = jnp.einsum("hts,shd->thd", mixing, key_heads, preferred_element_type=jnp.float32)
    query_grad = query_grad + jnp.einsum(
        "the,hde->thd", pre_grad, state_low, preferred_element_type=jnp.float32
    )
    query_grad = query_grad.astype(jnp.bfloat16).reshape(tokens, width)
    grad_block = jnp.einsum("thd,the->hde", queries, pre_grad, preferred_element_type=jnp.float32)
    owned_rows = gathered_input.shape[1] // lax.axis_size("seq")
    grad_state = entering(grad_block, "seq", jnp.add, jnp.zeros_like(grad_block), True)
    grad_low = grad_state.astype(jnp.bfloat16)
    key_grad = jnp.einsum("hts,thd->shd", mixing, queries, preferred_element_type=jnp.float32)
    key_grad = key_grad + jnp.einsum(
        "she,hde->shd", value_heads, grad_low, preferred_element_type=jnp.float32
    )
    value_grad = jnp.einsum("hts,the->she", scores, pre_grad, preferred_element_type=jnp.float32)
    value_grad = value_grad + jnp.einsum(
        "shd,hde->she", key_heads, grad_low, preferred_element_type=jnp.float32
    )
    key_grad, value_grad = (
        key_grad.astype(jnp.bfloat16).reshape(tokens, width),
        value_grad.astype(jnp.bfloat16).reshape(tokens, width),
    )
    stacked = jnp.concatenate([query_grad, key_grad, value_grad], axis=1)
    term = jnp.einsum("tc,tj->cj", gathered_input, stacked, preferred_element_type=jnp.float32)
    projection_gradient = lax.psum_scatter(
        term.reshape(lax.axis_size("seq") * owned_rows, -1, width).astype(jnp.bfloat16),
        "seq",
        scatter_dimension=0,
        tiled=True,
    ).astype(jnp.float32)
    out_term = jnp.einsum("tc,tj->cj", gated, gathered_cot, preferred_element_type=jnp.float32)
    output_gradient = lax.psum_scatter(
        out_term.astype(jnp.bfloat16), "seq", scatter_dimension=1, tiled=True
    ).astype(jnp.float32)
    return (projection_gradient, output_gradient)


def solution(mesh):
    placed = (
        P("seq", "head"),
        P("seq", "head"),
        P("seq", "head"),
        P("seq", "head"),
        P("head", None),
        P("head"),
        P("seq", "head"),
    )
    return jax.shard_map(
        body,
        mesh=mesh,
        in_specs=placed,
        out_specs=(P("seq", None, "head"), P("head", "seq")),
        check_vma=False,
    )
```

profile of v0, /device:TPU:0, one launch (start us, length us, event | category | flops | bytes accessed | tf_op | source)
XLA Modules:
  0.0 771.1 jit_solution(15895079961183148165)
XLA Ops:
  7.2 2.6 copy.55
  9.8 2.4 copy.32
  12.3 2.4 convolution_convert_fusion.3
  15.6 2.5 select_convert_fusion.1
  18.2 2.0 copy-done.3
  20.2 2.8 fusion.8
  23.0 43.8 %all-gather.11.cloned.1.call-done = bf16[64,128,128]{2,1,0:T(8,128)(2,1)} async-done(((bf16[8,128,128]{2,1,0:T(8,128)(2,1)}), bf16[64,128,128]{2,1,0:T(8,128)(2,1)}) %all-gather.11.cloned.1.call-update) | async-done | bytes 2097168 | tf_op jit(solution)/shard_map/all_gather | solution.py:11
  66.8 10.1 %while.30 = (s32[]{:T(128)}, f32[8,128,128]{2,1,0:T(8,128)S(1)}, s32[]{:T(128)}, bf16[8,8,128,128]{3,2,1,0:T(8,128)(2,1)}, s32[]{:T(128)}, /*index=5*/s32[]{:T(128)}) while((s32[]{:T(128)}, f32[8,128,128]{2,1,0:T(8,128)S(1)}, s32[]{:T(128)}, bf16[8,8,128,128]{3,2,1,0:T(8,128)(2,1)}, s32[]{:T(128)}, /*index=5*/s32[]{:T(128)}) %tuple.94), condition=%wide.region_1.2_spmd.clone, body=%wide.region_0.1_spmd.clone.sunk | while | flops 524292 | bytes 1310821 | solution.py:20
  77.0 3.5 multiply_reduce_fusion.1
  80.5 20.9 %all-gather.7.cloned.1.call-done = bf16[512,4096]{1,0:T(8,128)(2,1)} async-done(((bf16[512,1024]{1,0:T(8,128)(2,1)}), bf16[512,4096]{1,0:T(8,128)(2,1)}) %all-gather.7.cloned.1.call-update) | async-done | bytes 4194320 | tf_op jit(solution)/shard_map/all_gather | solution.py:32
  101.4 9.9 %multiply_reduce_fusion = (f32[512,8]{0,1:T(8,128)S(1)}, f32[512,1024]{0,1:T(8,128)S(1)}) fusion(f32[8,128]{1,0:T(8,128)S(1)} %bitcast.127, f32[512,8,128]{0,2,1:T(8,128)} %get-tuple-element.246, f32[512,8]{0,1:T(8,128)S(1)} %add_sqrt_fusion, bf16[512,4096]{1,0:T(8,128)(2,1)} %all-gather.7.cloned.1.call-done, bf16[1024,4096]{1,0:T(8,128)(2,1)} %param.15), kind=kOutput, calls=%fused_computation.19 | convolution fusion | flops 4297060352 | bytes 16814080 | tf_op jit(solution)/shard_map/reshape | solution.py:59
  115.1 10.3 %convolution_convert_fusion.1 = bf16[1024,4096]{1,0:T(8,128)(2,1)} fusion(bf16[512,1024]{0,1:T(8,128)(2,1)} %bitcast.122, bf16[512,4096]{1,0:T(8,128)(2,1)} %all-gather.7.cloned.1.call-done), kind=kOutput, calls=%fused_computation.5 | convolution fusion | flops 4299161600 | bytes 13631488 | tf_op jit(solution)/shard_map/tc,tj->cj/dot_general | solution.py:93
  125.5 2.7 select_convert_fusion
  132.8 2.0 fusion.36
  134.9 28.9 %all-gather.13.cloned.1.call-done = bf16[64,128,128]{2,1,0:T(8,128)(2,1)} async-done(((bf16[8,128,128]{2,1,0:T(8,128)(2,1)}), bf16[64,128,128]{2,1,0:T(8,128)(2,1)}) %all-gather.13.cloned.1.call-update) | async-done | bytes 2097168 | tf_op jit(solution)/shard_map/all_gather | solution.py:11
  163.8 10.3 %while.31 = (s32[]{:T(128)}, f32[8,128,128]{2,1,0:T(8,128)S(1)}, s32[]{:T(128)}, bf16[8,8,128,128]{3,2,1,0:T(8,128)(2,1)}, s32[]{:T(128)}, /*index=5*/s32[]{:T(128)}, s32[]{:T(128)}, s32[]{:T(128)}) while((s32[]{:T(128)}, f32[8,128,128]{2,1,0:T(8,128)S(1)}, s32[]{:T(128)}, bf16[8,8,128,128]{3,2,1,0:T(8,128)(2,1)}, s32[]{:T(128)}, ...), condition=%wide.region_5.6_spmd.clone, body=%wide.region_4.5_spmd.clone.sunk | while | flops 524296 | bytes 1310883 | solution.py:20
  178.5 1.9 fusion.5
  180.3 17.9 %all-gather.9.cloned.1.call-done = bf16[512,4096]{1,0:T(8,128)(2,1)} async-done(((bf16[512,1024]{1,0:T(8,128)(2,1)}), bf16[512,4096]{1,0:T(8,128)(2,1)}) %all-gather.9.cloned.1.call-update) | async-done | bytes 4194320 | tf_op jit(solution)/shard_map/all_gather | solution.py:31
  198.2 21.9 %convolution_convert_fusion = bf16[3072,4096]{1,0:T(8,128)(2,1)} fusion(bf16[512,4096]{1,0:T(8,128)(2,1)} %all-gather.9.cloned.1.call-done, bf16[512,1024]{0,1:T(8,128)(2,1)S(1)} %bitcast.123, bf16[512,1024]{0,1:T(8,128)(2,1)} %bitcast.124, bf16[512,1024]{0,1:T(8,128)(2,1)S(1)} %bitcast.121), kind=kOutput, calls=%fused_computation.2 | convolution fusion | flops 12906921984 | bytes 32505856 | tf_op jit(solution)/shard_map/tc,tj->cj/dot_general | solution.py:86
  220.1 32.8 %copy.46 = bf16[4096,3,1024]{2,0,1:T(8,128)(2,1)} copy(bf16[4096,3,1024]{0,2,1:T(8,128)(2,1)} %bitcast.118) | data formatting | bytes 50331648 | tf_op jit(solution)/shard_map/convert_element_type | solution.py:88
  252.9 98.2 %reduce-scatter.5.cloned.1.call-done = bf16[1024,512]{1,0:T(8,128)(2,1)} async-done(((bf16[1024,4096]{1,0:T(8,128)(2,1)}), bf16[1024,512]{1,0:T(8,128)(2,1)}) %reduce-scatter.5.cloned.1.call-update) | async-done | bytes 1048592 | tf_op jit(solution)/shard_map/reduce_scatter | solution.py:94
  351.1 2.9 convert_element_type.98
  354.0 404.9 %reduce-scatter.3.cloned.1.call-done = bf16[512,3,1024]{2,0,1:T(8,128)(2,1)} async-done(((bf16[4096,3,1024]{2,0,1:T(8,128)(2,1)}), bf16[512,3,1024]{2,0,1:T(8,128)(2,1)}) %reduce-scatter.3.cloned.1.call-update) | async-done | bytes 3145744 | tf_op jit(solution)/shard_map/reduce_scatter | solution.py:87
  758.9 5.3 convert_element_type.95
  (69 shorter events, 33.8 us)
Async XLA Ops:
  7.2 8.4 %copy-start = (bf16[512,1024]{1,0:T(8,128)(2,1)S(1)}, bf16[512,1024]{1,0:T(8,128)(2,1)}, u32[]{:S(2)}) copy-start(bf16[512,1024]{1,0:T(8,128)(2,1)} %param.12) | copy-start | bytes 3145732
  7.2 5.1 copy-start.8
  7.2 59.6 %all-gather.11.cloned.1.call-start = ((), (), s32[]{:S(2)}) async-start(), calls=%async_computation.6 | async-start | bytes 2359296 | tf_op jit(solution)/shard_map/all_gather | solution.py:11
  14.7 86.7 %all-gather.7.cloned.1.call-start = ((), (), s32[]{:S(2)}) async-start(), calls=%async_computation.2 | async-start | bytes 5242880 | tf_op jit(solution)/shard_map/all_gather | solution.py:32
  15.5 148.3 %all-gather.13.cloned.1.call-start = ((), (), s32[]{:S(2)}) async-start(), calls=%async_computation.7 | async-start | bytes 2359296 | tf_op jit(solution)/shard_map/all_gather | solution.py:11
  18.2 2.0 copy-start.3
  77.0 24.4 %copy-start.14 = (f32[1024]{0:T(1024)S(1)}, f32[1024]{0:T(1024)}, u32[]{:S(2)}) copy-start(f32[1024]{0:T(1024)} %param.16) | copy-start | bytes 12292
  101.4 10.0 %copy-start.2 = (f32[512,8,128]{0,2,1:T(8,128)S(1)}, f32[512,8,128]{0,2,1:T(8,128)}, u32[]{:S(2)}) copy-start(f32[512,8,128]{0,2,1:T(8,128)} %get-tuple-element.246) | copy-start | bytes 6291460
  114.3 83.9 %all-gather.9.cloned.1.call-start = ((), (), s32[]{:S(2)}) async-start(), calls=%async_computation.3 | async-start | bytes 5242880 | tf_op jit(solution)/shard_map/all_gather | solution.py:31
  114.9 236.2 %reduce-scatter.5.cloned.1.call-start = ((), (), s32[]{:S(2)}) async-start(), calls=%async_computation.5 | async-start | bytes 9437184 | tf_op jit(solution)/shard_map/reduce_scatter | solution.py:94
  125.4 633.4 %reduce-scatter.3.cloned.1.call-start = ((), (), s32[]{:S(2)}) async-start(), calls=%async_computation.4 | async-start | bytes 28311552 | tf_op jit(solution)/shard_map/reduce_scatter | solution.py:87
  125.5 2.7 copy-start.10
  128.2 2.0 copy-start.5
  130.3 2.6 copy-start.4
  163.8 10.3 %copy-start.9 = (bf16[512,1024]{1,0:T(8,128)(2,1)S(1)}, bf16[512,1024]{1,0:T(8,128)(2,1)}, u32[]{:S(2)}) copy-start(bf16[512,1024]{1,0:T(8,128)(2,1)} %param.14) | copy-start | bytes 3145732
  174.1 1.6 copy-start.7
  174.1 1.8 copy-start.11
  175.9 2.6 copy-start.6
  178.5 19.7 %copy-start.12 = (bf16[512,8,128]{0,2,1:T(8,128)(2,1)S(1)}, bf16[512,8,128]{0,2,1:T(8,128)(2,1)}, u32[]{:S(2)}) copy-start(bf16[512,8,128]{0,2,1:T(8,128)(2,1)} %fusion.6) | copy-start | bytes 3145732
  178.5 19.7 %copy-start.13 = (bf16[8,128,512]{2,1,0:T(8,128)(2,1)S(1)}, bf16[8,128,512]{2,1,0:T(8,128)(2,1)}, u32[]{:S(2)}) copy-start(bf16[8,128,512]{2,1,0:T(8,128)(2,1)} %add_convert_fusion) | copy-start | bytes 3145732
  351.1 413.1 %copy-start.1 = (bf16[512,1024]{1,0:T(8,128)(2,1)S(1)}, bf16[512,1024]{1,0:T(8,128)(2,1)}, u32[]{:S(2)}) copy-start(bf16[512,1024]{1,0:T(8,128)(2,1)} %param.12) | copy-start | bytes 3145732
Sparse Core Ops, SparseCore 0:
  14.8 51.9 all-gather.10
  68.4 32.9 all-gather.6
  114.4 49.2 all-gather.12
  165.2 32.9 all-gather.8
  201.7 149.3 reduce-scatter.4
  355.4 403.4 reduce-scatter.2
where the time goes:
time: 773 us; the launch traced here: 771 us
  waiting for transfers between devices  616 us (80%)
  matrix products  65.2 us (8%)
  local copies, waits for them, and re-layouts  44.9 us (6%)
  other arithmetic  30 us (4%)
  between operations  14.3 us (2%)
    reduce_scatter x1, waiting for transfers between devices, body(): lax.psum_scatter(term.reshape(lax.axis_size('seq') * owned_rows, -1, widt...  405 us
    reduce_scatter x1, waiting for transfers between devices, body(): lax.psum_scatter(out_term.astype(jnp.bfloat16), 'seq', scatter_dimension=...  98.2 us
    all_gather x2, waiting for transfers between devices, entering(): everything = lax.all_gather(array.astype(jnp.bfloat16), axis)  72.7 us
    convert_element_type x1, local copies, waits for them, and re-layouts, body(): term.reshape(lax.axis_size('seq') * owned_rows, -1, width)  32.8 us
    dot_general x1, matrix products, body(): jnp.einsum('tc,tj->cj', gathered_input, stacked, preferred_element_type=j...  21.9 us
    all_gather x1, waiting for transfers between devices, body(): lax.all_gather(cotangent, 'head', axis=1, tiled=True)  20.9 us
    select_n x16, other arithmetic, lap(): return jnp.where(reached, new, before)  20 us
    all_gather x1, waiting for transfers between devices, body(): lax.all_gather(layer_input, 'head', axis=1, tiled=True)  17.9 us
  transfers between devices with their start and end apart: 6, of which 6 were waited for; matrix products, arithmetic and copies ran while one was open for 14% of the time, Pallas kernels for 0%

commit v1 on v0

v1 whole, which is shorter than its diff:
```python
import jax
import jax.numpy as jnp
from jax import lax
from jax.sharding import PartitionSpec as P

HEAD_DIM = 128
F32 = jnp.float32
BF16 = jnp.bfloat16


def flip(array, bit):
    size = lax.axis_size("seq")
    return lax.ppermute(array, "seq", [(i, i ^ (1 << bit)) for i in range(size)])


def entering(block, reverse):
    size, position = lax.axis_size("seq"), lax.axis_index("seq")
    bits = size.bit_length() - 1
    total, before = block, jnp.zeros_like(block)
    for bit in range(bits):
        step = 1 << bit
        if bit < bits - 1:
            new = flip(total.astype(BF16), bit).astype(F32)
            mine = (position >> bit) & 1
            before = before + jnp.where(mine == (0 if reverse else 1), new, 0.0)
            total = total + new
        else:
            pairs = [(i, i ^ step) for i in range(size) if bool(i & step) == reverse]
            before = before + lax.ppermute(total.astype(BF16), "seq", pairs).astype(F32)
    return before


def lower_mask(count):
    rows = lax.broadcasted_iota(jnp.int32, (count, count), 0)
    cols = lax.broadcasted_iota(jnp.int32, (count, count), 1)
    return rows >= cols


def tdot(a, b):
    return lax.dot_general(a, b, (((0,), (0,)), ((), ())), preferred_element_type=F32)


def body(layer_input, query_rows, key_rows, value_rows, out_weight, norm_gain, cotangent):
    size, position = lax.axis_size("seq"), lax.axis_index("seq")
    bits = size.bit_length() - 1
    gather_bit = 1 if bits > 1 else 0
    halving = [bit for bit in range(bits) if bit != gather_bit]
    tokens, width = query_rows.shape
    heads = width // HEAD_DIM
    model = out_weight.shape[1]
    owned = model // size

    gathered_cot = lax.all_gather(cotangent, "head", axis=1, tiled=True)
    gathered_input = lax.all_gather(layer_input, "head", axis=1, tiled=True)

    chunks = 1 << len(halving)
    order = []
    for j in range(chunks):
        toggled = 0
        for i, bit in enumerate(halving):
            if not (j >> (len(halving) - 1 - i)) & 1:
                toggled |= 1 << bit
        order.append(position ^ toggled)

    def pick(array, toggled):
        return jnp.concatenate(
            [lax.dynamic_slice_in_dim(array, (at ^ toggled) * owned, owned, 1) for at in order], axis=1
        )

    def both(array):
        mine = pick(array, 0)
        share = chunks * owned // lax.axis_size("head")
        send = pick(array, 1 << gather_bit)
        send = lax.dynamic_slice_in_dim(send, lax.axis_index("head") * share, share, 1)
        theirs = lax.all_gather(flip(send, gather_bit), "head", axis=1, tiled=True)
        return jnp.concatenate([mine, theirs], axis=0)

    queries = query_rows.reshape(tokens, heads, HEAD_DIM)
    key_heads = key_rows.reshape(tokens, heads, HEAD_DIM)
    value_heads = value_rows.reshape(tokens, heads, HEAD_DIM)
    gain = norm_gain.reshape(heads, HEAD_DIM)
    lower = lower_mask(tokens)[None]
    block_state = jnp.einsum("thd,the->hde", key_heads, value_heads, preferred_element_type=F32)
    state_low = entering(block_state, False).astype(BF16)
    scores = jnp.einsum("thd,shd->hts", queries, key_heads, preferred_element_type=F32)
    scores = jnp.where(lower, scores, 0.0).astype(BF16)
    attention = jnp.einsum("hts,she->the", scores, value_heads, preferred_element_type=F32)
    attention = attention + jnp.einsum("thd,hde->the", queries, state_low, preferred_element_type=F32)
    rms_value = jnp.sqrt(jnp.mean(attention * attention, axis=-1, keepdims=True) + 1e-05)
    normed = attention / rms_value
    gated = (normed * gain).astype(BF16).reshape(tokens, width)
    gated_grad = jnp.einsum("tj,cj->tc", gathered_cot, out_weight, preferred_element_type=F32)
    scaled = gated_grad.reshape(tokens, heads, HEAD_DIM) * gain
    inner = jnp.mean(scaled * normed, axis=-1, keepdims=True)
    pre_grad = ((scaled - normed * inner) / rms_value).astype(BF16)
    grad_block = jnp.einsum("thd,the->hde", queries, pre_grad, preferred_element_type=F32)
    grad_low = entering(grad_block, True).astype(BF16)
    mixing = jnp.einsum("the,she->hts", pre_grad, value_heads, preferred_element_type=F32)
    mixing = jnp.where(lower, mixing, 0.0).astype(BF16)
    query_grad = jnp.einsum("hts,shd->thd", mixing, key_heads, preferred_element_type=F32)
    query_grad = query_grad + jnp.einsum("the,hde->thd", pre_grad, state_low, preferred_element_type=F32)
    query_grad = query_grad.astype(BF16).reshape(tokens, width)
    key_grad = jnp.einsum("hts,thd->shd", mixing, queries, preferred_element_type=F32)
    key_grad = key_grad + jnp.einsum("she,hde->shd", value_heads, grad_low, preferred_element_type=F32)
    value_grad = jnp.einsum("hts,the->she", scores, pre_grad, preferred_element_type=F32)
    value_grad = value_grad + jnp.einsum("shd,hde->she", key_heads, grad_low, preferred_element_type=F32)
    key_grad = key_grad.astype(BF16).reshape(tokens, width)
    value_grad = value_grad.astype(BF16).reshape(tokens, width)

    both_input, both_cot = both(gathered_input), both(gathered_cot)

    def reduced(features, grad, turned):
        grad = jnp.concatenate([grad, flip(grad, gather_bit)], axis=0)

        def term(start, count):
            part = features[:, start * owned : (start + count) * owned]
            return tdot(grad, part) if turned else tdot(part, grad)

        start, count = 0, chunks
        pending = None
        for bit in halving:
            count //= 2
            send = term(start, count)
            if pending is not None:
                send = send + cut(pending, 0, count, turned)
                pending = cut(pending, count, count, turned)
            new = flip(send.astype(BF16), bit).astype(F32)
            pending = new if pending is None else pending + new
            start += count
        return term(start, 1) + pending

    def cut(array, start, count, turned):
        return lax.slice_in_dim(array, start * owned, (start + count) * owned, axis=1 if turned else 0)

    half = width // 2

    def in_halves(features, grad, turned):
        parts = [reduced(features, grad[:, i * half : (i + 1) * half], turned) for i in range(2)]
        return jnp.concatenate(parts, axis=0 if turned else 1)

    output_gradient = in_halves(both_cot, gated, True)
    projected = [in_halves(both_input, grad, False) for grad in (query_grad, key_grad, value_grad)]
    return (jnp.stack(projected, axis=1), output_gradient)


def solution(mesh):
    placed = (
        P("seq", "head"),
        P("seq", "head"),
        P("seq", "head"),
        P("seq", "head"),
        P("head", None),
        P("head"),
        P("seq", "head"),
    )
    return jax.shard_map(
        body,
        mesh=mesh,
        in_specs=placed,
        out_specs=(P("seq", None, "head"), P("head", "seq")),
        check_vma=False,
    )
```

time: 773 us -> 522 us (0.68)
  waiting for transfers between devices: 616 us -> 325 us
  starting transfers between devices: 0.42 us -> 39.4 us
  local copies, waits for them, and re-layouts: 44.9 us -> 21.2 us
  other arithmetic: 30 us -> 47.4 us
    reduce_scatter x2 -> x0, waiting for transfers between devices: 503 us -> none  [the longest x1 405 us: body(): lax.psum_scatter(term.reshape(lax.axis_size('seq') * owned_rows, -1, widt...]
    ppermute x0 -> x32, waiting for transfers between devices: none -> 275 us  [the longest x30 263 us: flip(): return lax.ppermute(array, 'seq', [(i, i ^ 1 << bit) for i in range(size)])]
    all_gather x4, waiting for transfers between devices: 111 us -> 48.2 us  [the longest x1 36.1 us: body(): gathered_input = lax.all_gather(layer_input, 'head', axis=1, tiled=True)]
    ppermute x0 -> x32, starting transfers between devices: none -> 38.7 us  [the longest x30 32.9 us: flip(): return lax.ppermute(array, 'seq', [(i, i ^ 1 << bit) for i in range(size)])]
    convert_element_type x2 -> x0, local copies, waits for them, and re-layouts: 33.6 us -> none  [the longest x1 32.8 us: body(): term.reshape(lax.axis_size('seq') * owned_rows, -1, width)]
    concatenate x0 -> x5, other arithmetic: none -> 26.6 us  [the longest x2 24.2 us: both(): return jnp.concatenate([mine, theirs], axis=0)]
    select_n x16 -> x0, other arithmetic: 20 us -> none  [lap(): return jnp.where(reached, new, before)]
    slice x0 -> x2, other arithmetic: none -> 12.6 us  [term(): part = features[:, start * owned:(start + count) * owned]]
  transfers between devices with their start and end apart: 6 -> 36, of which waited for: 6 -> 22; matrix products, arithmetic and copies ran while one was open for 14% -> 26% of each run, Pallas kernels for 0% -> 0%
where the time goes in v1:
time: 522 us; the launch traced here: 517 us
  waiting for transfers between devices  325 us (62%)
  matrix products  68.7 us (13%)
  other arithmetic  47.4 us (9%)
  starting transfers between devices  39.4 us (8%)
  local copies, waits for them, and re-layouts  21.2 us (4%)
  between operations  15.2 us (3%)
    ppermute x30, waiting for transfers between devices, flip(): return lax.ppermute(array, 'seq', [(i, i ^ 1 << bit) for i in range(size)])  263 us
    dot_general x24, matrix products, tdot(): lax.dot_general(a, b, (((0,), (0,)), ((), ())), preferred_element_type=F32)  43.3 us
    all_gather x1, waiting for transfers between devices, body(): gathered_input = lax.all_gather(layer_input, 'head', axis=1, tiled=True)  36.1 us
    ppermute x30, starting transfers between devices, flip(): return lax.ppermute(array, 'seq', [(i, i ^ 1 << bit) for i in range(size)])  32.9 us
    concatenate x2, other arithmetic, both(): return jnp.concatenate([mine, theirs], axis=0)  24.2 us
    ppermute x2, waiting for transfers between devices, entering(): before = before + lax.ppermute(total.astype(BF16), 'seq', pairs).astype(F32)  12.8 us
    slice x2, other arithmetic, term(): part = features[:, start * owned:(start + count) * owned]  12.6 us
    all_gather x1, waiting for transfers between devices, body(): gathered_cot = lax.all_gather(cotangent, 'head', axis=1, tiled=True)  12.2 us
  transfers between devices with their start and end apart: 36, of which 22 were waited for; matrix products, arithmetic and copies ran while one was open for 26% of the time, Pallas kernels for 0%

profile of v1, /device:TPU:0, one launch (start us, length us, event | category | flops | bytes accessed | tf_op | source)
XLA Modules:
  0.0 517.0 jit_solution(1092946589621821225)
XLA Ops:
  34.7 12.2 %all-gather.9.cloned.1.call-done = bf16[512,4096]{1,0:T(8,128)(2,1)} async-done(((bf16[512,1024]{1,0:T(8,128)(2,1)}), bf16[512,4096]{1,0:T(8,128)(2,1)}) %all-gather.9.cloned.1.call-update) | async-done | bytes 4194320 | tf_op jit(solution)/shard_map/all_gather | solution.py:53
  46.8 36.1 %all-gather.5.cloned.1.call-done = bf16[512,4096]{1,0:T(8,128)(2,1)} async-done(((bf16[512,1024]{1,0:T(8,128)(2,1)}), bf16[512,4096]{1,0:T(8,128)(2,1)}) %all-gather.5.cloned.1.call-update) | async-done | bytes 4194320 | tf_op jit(solution)/shard_map/all_gather | solution.py:54
  82.9 6.1 %constant_dynamic-slice_fusion.7 = (bf16[512,512]{1,0:T(8,128)(2,1)}, bf16[512,512]{1,0:T(8,128)(2,1)}, bf16[512,512]{1,0:T(8,128)(2,1)}, bf16[512,512]{1,0:T(8,...) fusion(bf16[512,4096]{1,0:T(8,128)(2,1)} %all-gather.9.cloned.1, ...), kind=kLoop, calls=%fused_computation.148 | loop fusion | bytes 16777248 | tf_op jit(solution)/shard_map/dynamic_slice | solution.py:67
  91.9 11.8 %collective-permute-done = bf16[512,512]{1,0:T(8,128)(2,1)} collective-permute-done((bf16[512,512]{1,0:T(8,128)(2,1)S(1)}, bf16[512,512]{1,0:T(8,128)(2,1)}, u32[]{:S(2)}, u32[]{:S(2)}) %collective-permute-start) | collective-permute-done | bytes 524320 | tf_op jit(solution)/shard_map/ppermute | solution.py:13
  104.3 8.3 %multiply_reduce_fusion = (f32[512,8]{0,1:T(8,128)S(1)}, f32[512,1024]{0,1:T(8,128)S(1)}) fusion(f32[8,128]{1,0:T(8,128)S(1)} %bitcast.136, f32[512,8,128]{0,2,1:T(8,128)S(1)} %get-tuple-element.37, f32[512,8]{0,1:T(8,128)S(1)} %add_sqrt_fusion, bf16[512,4096]{1,0:T(8,128)(2,1)} %all-gather.9.cloned.1.call-done, bf16[1024,4096]{1,0:T(8,128)(2,1)} %param.11), kind=kOutput, calls=%fused_computation.25 | convolution fusion | flops 4297060352 | bytes 16814080 | tf_op jit(solution)/shard_map/reshape | solution.py:93
  137.4 31.6 %collective-permute-done.11 = bf16[8,128,128]{2,1,0:T(8,128)(2,1)S(1)} collective-permute-done((bf16[8,128,128]{2,1,0:T(8,128)(2,1)S(1)}, bf16[8,128,128]{2,1,0:T(8,128)(2,1)S(1)}, u32[]{:S(2)}, u32[]{:S(2)}) %collective-permute-start.11) | collective-permute-done | bytes 262176 | tf_op jit(solution)/shard_map/ppermute | solution.py:13
  171.4 12.8 %collective-permute-done.12 = bf16[8,128,128]{2,1,0:T(8,128)(2,1)S(1)} collective-permute-done((bf16[8,128,128]{2,1,0:T(8,128)(2,1)S(1)}, bf16[8,128,128]{2,1,0:T(8,128)(2,1)S(1)}, u32[]{:S(2)}, u32[]{:S(2)}) %collective-permute-start.12) | collective-permute-done | bytes 262176 | tf_op jit(solution)/shard_map/ppermute | solution.py:29
  190.0 10.1 %pad_maximum_fusion.1 = bf16[1024,2048]{1,0:T(8,128)(2,1)} fusion(bf16[512,2048]{1,0:T(8,128)(2,1)} %all-gather.7.cloned.1.call-done, bf16[512,512]{1,0:T(8,128)(2,1)} %get-tuple-element.44, bf16[512,512]{1,0:T(8,128)(2,1)S(1)} %copy-done.19, bf16[512,512]{1,0:T(8,128)(2,1)S(1)} %copy-done.18, bf16[512,512]{1,0:T(8,128)(2,1)} %get-tuple-element.49), kind=kLoop, calls=%fused_computation.3 | loop fusion | flops 20971520 | bytes 8388608 | tf_op jit(solution)/shard_map/concatenate | solution.py:76
  200.1 14.2 %pad_maximum_fusion.2 = bf16[1024,2048]{1,0:T(8,128)(2,1)S(1)} fusion(bf16[512,2048]{1,0:T(8,128)(2,1)} %all-gather.11.cloned.1.call-done, bf16[512,512]{1,0:T(8,128)(2,1)S(1)} %copy-done.15, bf16[512,512]{1,0:T(8,128)(2,1)S(1)} %copy-done.16, bf16[512,512]{1,0:T(8,128)(2,1)S(1)} %copy-done.17, bf16[512,512]{1,0:T(8,128)(2,1)S(1)} %copy-done.14), kind=kLoop, calls=%fused_computation.4 | loop fusion | flops 20971520 | bytes 8388608 | tf_op jit(solution)/shard_map/concatenate | solution.py:76
  221.5 7.8 %collective-permute-done.16 = bf16[512,512]{0,1:T(8,128)(2,1)S(1)} collective-permute-done((bf16[512,512]{0,1:T(8,128)(2,1)S(1)}, bf16[512,512]{0,1:T(8,128)(2,1)S(1)}, u32[]{:S(2)}, u32[]{:S(2)}) %collective-permute-start.16) | collective-permute-done | bytes 524320 | tf_op jit(solution)/shard_map/ppermute | solution.py:13
  230.6 9.9 %collective-permute-done.13 = bf16[512,512]{0,1:T(8,128)(2,1)S(1)} collective-permute-done((bf16[512,512]{0,1:T(8,128)(2,1)S(1)}, bf16[512,512]{0,1:T(8,128)(2,1)S(1)}, u32[]{:S(2)}, u32[]{:S(2)}) %collective-permute-start.13) | collective-permute-done | bytes 524320 | tf_op jit(solution)/shard_map/ppermute | solution.py:13
  267.9 6.8 %pad_maximum_fusion.4 = (bf16[1024,512]{1,0:T(8,128)(2,1)S(1)}, bf16[1024,512]{1,0:T(8,128)(2,1)}) fusion(bf16[512,2048]{1,0:T(8,128)(2,1)S(1)} %copy-done.13, bf16[512,512]{1,0:T(8,128)(2,1)S(1)} %copy-done.15, bf16[512,512]{1,0:T(8,128)(2,1)S(1)} %copy-done.16, bf16[512,512]{1,0:T(8,128)(2,1)S(1)} %copy-done.17, bf16[512,512]{1,0:T(8,128)(2,1)S(1)} %copy-done.14), kind=kLoop, calls=%fused_computation.78 | loop fusion | flops 10485760 | bytes 6291456 | tf_op jit(solution)/shard_map/slice | solution.py:116
  274.9 14.2 %collective-permute-done.20 = bf16[1024,512]{0,1:T(8,128)(2,1)S(1)} collective-permute-done((bf16[1024,512]{0,1:T(8,128)(2,1)S(1)}, bf16[1024,512]{0,1:T(8,128)(2,1)S(1)}, u32[]{:S(2)}, u32[]{:S(2)}) %collective-permute-start.20) | collective-permute-done | bytes 1048608 | tf_op jit(solution)/shard_map/ppermute | solution.py:13
  290.6 21.0 %collective-permute-done.17 = bf16[1024,512]{0,1:T(8,128)(2,1)S(1)} collective-permute-done((bf16[1024,512]{0,1:T(8,128)(2,1)S(1)}, bf16[1024,512]{0,1:T(8,128)(2,1)S(1)}, u32[]{:S(2)}, u32[]{:S(2)}) %collective-permute-start.17) | collective-permute-done | bytes 1048608 | tf_op jit(solution)/shard_map/ppermute | solution.py:13
  315.0 19.1 %collective-permute-done.14 = bf16[1024,512]{0,1:T(8,128)(2,1)S(1)} collective-permute-done((bf16[1024,512]{0,1:T(8,128)(2,1)S(1)}, bf16[1024,512]{0,1:T(8,128)(2,1)S(1)}, u32[]{:S(2)}, u32[]{:S(2)}) %collective-permute-start.14) | collective-permute-done | bytes 1048608 | tf_op jit(solution)/shard_map/ppermute | solution.py:13
  336.2 20.3 %collective-permute-done.8 = bf16[1024,512]{0,1:T(8,128)(2,1)S(1)} collective-permute-done((bf16[1024,512]{0,1:T(8,128)(2,1)S(1)}, bf16[1024,512]{0,1:T(8,128)(2,1)S(1)}, u32[]{:S(2)}, u32[]{:S(2)}) %collective-permute-start.8) | collective-permute-done | bytes 1048608 | tf_op jit(solution)/shard_map/ppermute | solution.py:13
  357.5 21.5 %collective-permute-done.5 = bf16[1024,512]{0,1:T(8,128)(2,1)S(1)} collective-permute-done((bf16[1024,512]{0,1:T(8,128)(2,1)S(1)}, bf16[1024,512]{0,1:T(8,128)(2,1)S(1)}, u32[]{:S(2)}, u32[]{:S(2)}) %collective-permute-start.5) | collective-permute-done | bytes 1048608 | tf_op jit(solution)/shard_map/ppermute | solution.py:13
  379.9 21.5 %collective-permute-done.30 = bf16[512,1024]{1,0:T(8,128)(2,1)S(1)} collective-permute-done((bf16[512,1024]{1,0:T(8,128)(2,1)S(1)}, bf16[512,1024]{1,0:T(8,128)(2,1)S(1)}, u32[]{:S(2)}, u32[]{:S(2)}) %collective-permute-start.30) | collective-permute-done | bytes 1048608 | tf_op jit(solution)/shard_map/ppermute | solution.py:13
  405.5 12.3 %collective-permute-done.27 = bf16[512,1024]{1,0:T(8,128)(2,1)S(1)} collective-permute-done((bf16[512,1024]{1,0:T(8,128)(2,1)S(1)}, bf16[512,1024]{1,0:T(8,128)(2,1)S(1)}, u32[]{:S(2)}, u32[]{:S(2)}) %collective-permute-start.27) | collective-permute-done | bytes 1048608 | tf_op jit(solution)/shard_map/ppermute | solution.py:13
  433.8 28.9 %collective-permute-done.15 = bf16[512,512]{0,1:T(8,128)(2,1)S(1)} collective-permute-done((bf16[512,512]{0,1:T(8,128)(2,1)S(1)}, bf16[512,512]{0,1:T(8,128)(2,1)S(1)}, u32[]{:S(2)}, u32[]{:S(2)}) %collective-permute-start.15) | collective-permute-done | bytes 524320 | tf_op jit(solution)/shard_map/ppermute | solution.py:13
  463.6 10.3 %collective-permute-done.9 = bf16[512,512]{0,1:T(8,128)(2,1)S(1)} collective-permute-done((bf16[512,512]{0,1:T(8,128)(2,1)S(1)}, bf16[512,512]{0,1:T(8,128)(2,1)S(1)}, u32[]{:S(2)}, u32[]{:S(2)}) %collective-permute-start.9) | collective-permute-done | bytes 524320 | tf_op jit(solution)/shard_map/ppermute | solution.py:13
  475.9 9.3 %collective-permute-done.6 = bf16[512,512]{0,1:T(8,128)(2,1)S(1)} collective-permute-done((bf16[512,512]{0,1:T(8,128)(2,1)S(1)}, bf16[512,512]{0,1:T(8,128)(2,1)S(1)}, u32[]{:S(2)}, u32[]{:S(2)}) %collective-permute-start.6) | collective-permute-done | bytes 524320 | tf_op jit(solution)/shard_map/ppermute | solution.py:13
  490.9 6.6 %copy.39 = f32[512,3,1024]{2,0,1:T(8,128)} copy(f32[512,3,1024]{0,2,1:T(8,128)} %pad_maximum_fusion) | data formatting | bytes 12582912
  499.8 6.8 %collective-permute-done.28 = bf16[512,512]{1,0:T(8,128)(2,1)} collective-permute-done((bf16[512,512]{1,0:T(8,128)(2,1)}, bf16[512,512]{1,0:T(8,128)(2,1)}, u32[]{:S(2)}, u32[]{:S(2)}) %collective-permute-start.28) | collective-permute-done | bytes 524320 | tf_op jit(solution)/shard_map/ppermute | solution.py:13
  (218 shorter events, 142.2 us)
Async XLA Ops:
  7.2 39.6 %all-gather.9.cloned.1.call-start = ((), (), s32[]{:S(2)}) async-start(), calls=%async_computation.2 | async-start | bytes 5242880 | tf_op jit(solution)/shard_map/all_gather | solution.py:53
  7.9 75.0 %all-gather.5.cloned.1.call-start = ((), (), s32[]{:S(2)}) async-start(), calls=%async_computation | async-start | bytes 5242880 | tf_op jit(solution)/shard_map/all_gather | solution.py:54
  8.7 180.8 %all-gather.7.cloned.1.call-start = ((), (), s32[]{:S(2)}) async-start(), calls=%async_computation.1 | async-start | bytes 2621440 | tf_op jit(solution)/shard_map/all_gather | solution.py:75
  30.2 60.8 %collective-permute-start.3 = (bf16[8,128,128]{2,1,0:T(8,128)(2,1)S(1)}, bf16[8,128,128]{2,1,0:T(8,128)(2,1)S(1)}, u32[]{:S(2)}, u32[]{:S(2)}) collective-permute-start(bf16[8,128,128]{2,1,0:T(8,128)(2,1)S(1)} %fusion.52), channel_id=1, source_target_pairs={{0,16},{4,20},{8,24},{12,28},{1,17},{5,21},{9,25},{13,29},{2,18},{... | collective-permute-start | bytes 786440 | tf_op jit(solution)/shard_map/ppermute | solution.py:29
  103.7 96.4 %all-gather.11.cloned.1.call-start = ((), (), s32[]{:S(2)}) async-start(), calls=%async_computation.3 | async-start | bytes 2621440 | tf_op jit(solution)/shard_map/all_gather | solution.py:75
  123.2 119.8 %collective-permute-start.7 = (bf16[512,512]{0,1:T(8,128)(2,1)}, bf16[512,512]{0,1:T(8,128)(2,1)}, u32[]{:S(2)}, u32[]{:S(2)}) collective-permute-start(bf16[512,512]{0,1:T(8,128)(2,1)} %get-tuple-element.29), channel_id=1, source_target_pairs={{0,8},{4,12},{8,0},{12,4},{16,24},{20,28},{24,16},{28,20},{1,9},{5... | collective-permute-start | bytes 1572872 | tf_op jit(solution)/shard_map/ppermute | solution.py:13
  123.7 122.6 %collective-permute-start.4 = (bf16[512,512]{0,1:T(8,128)(2,1)}, bf16[512,512]{0,1:T(8,128)(2,1)}, u32[]{:S(2)}, u32[]{:S(2)}) collective-permute-start(bf16[512,512]{0,1:T(8,128)(2,1)} %get-tuple-element.28), channel_id=1, source_target_pairs={{0,8},{4,12},{8,0},{12,4},{16,24},{20,28},{24,16},{28,20},{1,9},{5... | collective-permute-start | bytes 1572872 | tf_op jit(solution)/shard_map/ppermute | solution.py:13
  126.3 123.8 %collective-permute-start.29 = (bf16[512,512]{0,1:T(8,128)(2,1)}, bf16[512,512]{0,1:T(8,128)(2,1)}, u32[]{:S(2)}, u32[]{:S(2)}) collective-permute-start(bf16[512,512]{0,1:T(8,128)(2,1)} %get-tuple-element.27), channel_id=1, source_target_pairs={{0,8},{4,12},{8,0},{12,4},{16,24},{20,28},{24,16},{28,20},{1,9},{5... | collective-permute-start | bytes 1572872 | tf_op jit(solution)/shard_map/ppermute | solution.py:13
  132.8 36.2 %collective-permute-start.11 = (bf16[8,128,128]{2,1,0:T(8,128)(2,1)S(1)}, bf16[8,128,128]{2,1,0:T(8,128)(2,1)S(1)}, u32[]{:S(2)}, u32[]{:S(2)}) collective-permute-start(bf16[8,128,128]{2,1,0:T(8,128)(2,1)S(1)} %fusion.64), channel_id=1, source_target_pairs={{0,8},{4,12},{8,0},{12,4},{16,24},{20,28},{24,16},{28,20},{1,9},{5... | collective-permute-start | bytes 786440 | tf_op jit(solution)/shard_map/ppermute | solution.py:13
  243.0 46.1 %collective-permute-start.20 = (bf16[1024,512]{0,1:T(8,128)(2,1)S(1)}, bf16[1024,512]{0,1:T(8,128)(2,1)S(1)}, u32[]{:S(2)}, u32[]{:S(2)}) collective-permute-start(bf16[1024,512]{0,1:T(8,128)(2,1)S(1)} %convolution_convert_fusion.1), channel_id=1, source_target_pairs={{0,4},{4,0},{8,12},{12,8},{16,20},{20,16},{24,28},{28,24},{1,5},{5... | collective-permute-start | bytes 3145736 | tf_op jit(solution)/shard_map/ppermute | solution.py:13
  246.4 65.2 %collective-permute-start.17 = (bf16[1024,512]{0,1:T(8,128)(2,1)S(1)}, bf16[1024,512]{0,1:T(8,128)(2,1)S(1)}, u32[]{:S(2)}, u32[]{:S(2)}) collective-permute-start(bf16[1024,512]{0,1:T(8,128)(2,1)S(1)} %convolution_convert_fusion.2), channel_id=1, source_target_pairs={{0,4},{4,0},{8,12},{12,8},{16,20},{20,16},{24,28},{28,24},{1,5},{5... | collective-permute-start | bytes 3145736 | tf_op jit(solution)/shard_map/ppermute | solution.py:13
  250.1 83.9 %collective-permute-start.14 = (bf16[1024,512]{0,1:T(8,128)(2,1)S(1)}, bf16[1024,512]{0,1:T(8,128)(2,1)S(1)}, u32[]{:S(2)}, u32[]{:S(2)}) collective-permute-start(bf16[1024,512]{0,1:T(8,128)(2,1)S(1)} %convolution_convert_fusion.3), channel_id=1, source_target_pairs={{0,4},{4,0},{8,12},{12,8},{16,20},{20,16},{24,28},{28,24},{1,5},{5... | collective-permute-start | bytes 3145736 | tf_op jit(solution)/shard_map/ppermute | solution.py:13
  253.5 103.0 %collective-permute-start.8 = (bf16[1024,512]{0,1:T(8,128)(2,1)S(1)}, bf16[1024,512]{0,1:T(8,128)(2,1)S(1)}, u32[]{:S(2)}, u32[]{:S(2)}) collective-permute-start(bf16[1024,512]{0,1:T(8,128)(2,1)S(1)} %convolution_convert_fusion.4), channel_id=1, source_target_pairs={{0,4},{4,0},{8,12},{12,8},{16,20},{20,16},{24,28},{28,24},{1,5},{5... | collective-permute-start | bytes 3145736 | tf_op jit(solution)/shard_map/ppermute | solution.py:13
  266.6 112.4 %collective-permute-start.5 = (bf16[1024,512]{0,1:T(8,128)(2,1)S(1)}, bf16[1024,512]{0,1:T(8,128)(2,1)S(1)}, u32[]{:S(2)}, u32[]{:S(2)}) collective-permute-start(bf16[1024,512]{0,1:T(8,128)(2,1)S(1)} %convolution_convert_fusion.5), channel_id=1, source_target_pairs={{0,4},{4,0},{8,12},{12,8},{16,20},{20,16},{24,28},{28,24},{1,5},{5... | collective-permute-start | bytes 3145736 | tf_op jit(solution)/shard_map/ppermute | solution.py:13
  289.1 112.4 %collective-permute-start.30 = (bf16[512,1024]{1,0:T(8,128)(2,1)S(1)}, bf16[512,1024]{1,0:T(8,128)(2,1)S(1)}, u32[]{:S(2)}, u32[]{:S(2)}) collective-permute-start(bf16[512,1024]{1,0:T(8,128)(2,1)S(1)} %fusion.9), channel_id=1, source_target_pairs={{0,4},{4,0},{8,12},{12,8},{16,20},{20,16},{24,28},{28,24},{1,5},{5... | collective-permute-start | bytes 3145736 | tf_op jit(solution)/shard_map/ppermute | solution.py:13
  311.6 106.3 %collective-permute-start.27 = (bf16[512,1024]{1,0:T(8,128)(2,1)S(1)}, bf16[512,1024]{1,0:T(8,128)(2,1)S(1)}, u32[]{:S(2)}, u32[]{:S(2)}) collective-permute-start(bf16[512,1024]{1,0:T(8,128)(2,1)S(1)} %fusion.6), channel_id=1, source_target_pairs={{0,4},{4,0},{8,12},{12,8},{16,20},{20,16},{24,28},{28,24},{1,5},{5... | collective-permute-start | bytes 3145736 | tf_op jit(solution)/shard_map/ppermute | solution.py:13
  334.0 89.2 %collective-permute-start.24 = (bf16[512,512]{0,1:T(8,128)(2,1)S(1)}, bf16[512,512]{0,1:T(8,128)(2,1)S(1)}, u32[]{:S(2)}, u32[]{:S(2)}) collective-permute-start(bf16[512,512]{0,1:T(8,128)(2,1)S(1)} %fusion.19), channel_id=1, source_target_pairs={{0,16},{4,20},{8,24},{12,28},{16,0},{20,4},{24,8},{28,12},{1,17},{... | collective-permute-start | bytes 1572872 | tf_op jit(solution)/shard_map/ppermute | solution.py:13
  356.5 71.5 %collective-permute-start.21 = (bf16[512,512]{0,1:T(8,128)(2,1)S(1)}, bf16[512,512]{0,1:T(8,128)(2,1)S(1)}, u32[]{:S(2)}, u32[]{:S(2)}) collective-permute-start(bf16[512,512]{0,1:T(8,128)(2,1)S(1)} %fusion.18), channel_id=1, source_target_pairs={{0,16},{4,20},{8,24},{12,28},{16,0},{20,4},{24,8},{28,12},{1,17},{... | collective-permute-start | bytes 1572872 | tf_op jit(solution)/shard_map/ppermute | solution.py:13
  379.0 51.1 %collective-permute-start.18 = (bf16[512,512]{0,1:T(8,128)(2,1)S(1)}, bf16[512,512]{0,1:T(8,128)(2,1)S(1)}, u32[]{:S(2)}, u32[]{:S(2)}) collective-permute-start(bf16[512,512]{0,1:T(8,128)(2,1)S(1)} %fusion.17), channel_id=1, source_target_pairs={{0,16},{4,20},{8,24},{12,28},{16,0},{20,4},{24,8},{28,12},{1,17},{... | collective-permute-start | bytes 1572872 | tf_op jit(solution)/shard_map/ppermute | solution.py:13
  401.4 61.3 %collective-permute-start.15 = (bf16[512,512]{0,1:T(8,128)(2,1)S(1)}, bf16[512,512]{0,1:T(8,128)(2,1)S(1)}, u32[]{:S(2)}, u32[]{:S(2)}) collective-permute-start(bf16[512,512]{0,1:T(8,128)(2,1)S(1)} %fusion.16), channel_id=1, source_target_pairs={{0,16},{4,20},{8,24},{12,28},{16,0},{20,4},{24,8},{28,12},{1,17},{... | collective-permute-start | bytes 1572872 | tf_op jit(solution)/shard_map/ppermute | solution.py:13
  417.9 56.1 %collective-permute-start.9 = (bf16[512,512]{0,1:T(8,128)(2,1)S(1)}, bf16[512,512]{0,1:T(8,128)(2,1)S(1)}, u32[]{:S(2)}, u32[]{:S(2)}) collective-permute-start(bf16[512,512]{0,1:T(8,128)(2,1)S(1)} %fusion.15), channel_id=1, source_target_pairs={{0,16},{4,20},{8,24},{12,28},{16,0},{20,4},{24,8},{28,12},{1,17},{... | collective-permute-start | bytes 1572872 | tf_op jit(solution)/shard_map/ppermute | solution.py:13
  423.2 62.0 %collective-permute-start.6 = (bf16[512,512]{0,1:T(8,128)(2,1)S(1)}, bf16[512,512]{0,1:T(8,128)(2,1)S(1)}, u32[]{:S(2)}, u32[]{:S(2)}) collective-permute-start(bf16[512,512]{0,1:T(8,128)(2,1)S(1)} %fusion.14), channel_id=1, source_target_pairs={{0,16},{4,20},{8,24},{12,28},{16,0},{20,4},{24,8},{28,12},{1,17},{... | collective-permute-start | bytes 1572872 | tf_op jit(solution)/shard_map/ppermute | solution.py:13
  428.1 69.5 %collective-permute-start.31 = (bf16[512,512]{1,0:T(8,128)(2,1)}, bf16[512,512]{1,0:T(8,128)(2,1)}, u32[]{:S(2)}, u32[]{:S(2)}) collective-permute-start(bf16[512,512]{1,0:T(8,128)(2,1)} %fusion.13), channel_id=1, source_target_pairs={{0,16},{4,20},{8,24},{12,28},{16,0},{20,4},{24,8},{28,12},{1,17},{... | collective-permute-start | bytes 1572872 | tf_op jit(solution)/shard_map/ppermute | solution.py:13
  430.1 76.5 %collective-permute-start.28 = (bf16[512,512]{1,0:T(8,128)(2,1)}, bf16[512,512]{1,0:T(8,128)(2,1)}, u32[]{:S(2)}, u32[]{:S(2)}) collective-permute-start(bf16[512,512]{1,0:T(8,128)(2,1)} %fusion.12), channel_id=1, source_target_pairs={{0,16},{4,20},{8,24},{12,28},{16,0},{20,4},{24,8},{28,12},{1,17},{... | collective-permute-start | bytes 1572872 | tf_op jit(solution)/shard_map/ppermute | solution.py:13
  (58 other events, 739.8 us)
Sparse Core Ops, SparseCore 0:
  9.6 37.1 all-gather.8
  48.4 34.4 all-gather.4
  103.8 22.5 all-gather.6
  131.8 21.7 all-gather.10

commit v2 on v1

--- a/solution.py
+++ b/solution.py
@@ -51,6 +51,7 @@
     owned = model // size
 
     gathered_cot = lax.all_gather(cotangent, "head", axis=1, tiled=True)
+    layer_input, gathered_cot = lax.optimization_barrier((layer_input, gathered_cot))
     gathered_input = lax.all_gather(layer_input, "head", axis=1, tiled=True)
 
     chunks = 1 << len(halving)
@@ -73,7 +74,7 @@
         send = pick(array, 1 << gather_bit)
         send = lax.dynamic_slice_in_dim(send, lax.axis_index("head") * share, share, 1)
         theirs = lax.all_gather(flip(send, gather_bit), "head", axis=1, tiled=True)
-        return jnp.concatenate([mine, theirs], axis=0)
+        return mine, theirs
 
     queries = query_rows.reshape(tokens, heads, HEAD_DIM)
     key_heads = key_rows.reshape(tokens, heads, HEAD_DIM)
@@ -109,37 +110,58 @@
 
     both_input, both_cot = both(gathered_input), both(gathered_cot)
 
-    def reduced(features, grad, turned):
-        grad = jnp.concatenate([grad, flip(grad, gather_bit)], axis=0)
+    def cut(array, start, count, turned):
+        return lax.slice_in_dim(array, start * owned, (start + count) * owned, axis=1 if turned else 0)
 
-        def term(start, count):
-            part = features[:, start * owned : (start + count) * owned]
-            return tdot(grad, part) if turned else tdot(part, grad)
+    def term(piece, start, count):
+        features, grad, other, turned = piece
+        total = 0.0
+        for part, rows in zip(features, (grad, other)):
+            part = part[:, start * owned : (start + count) * owned]
+            total = total + (tdot(rows, part) if turned else tdot(part, rows))
+        return total
 
+    half = width // 2
+    pieces = []
+    for features, grad, turned in (
+        (both_cot, gated, True),
+        (both_input, query_grad, False),
+        (both_input, key_grad, False),
+        (both_input, value_grad, False),
+    ):
+        for i in range(2):
+            part = grad[:, i * half : (i + 1) * half]
+            pieces.append((features, part, flip(part, gather_bit), turned))
+
+    ready, over, results = [], [], []
+    for i, piece in enumerate(pieces):
+        turned = piece[3]
         start, count = 0, chunks
         pending = None
-        for bit in halving:
+        for place, bit in enumerate(halving):
             count //= 2
-            send = term(start, count)
+            send = term(piece, start, count)
             if pending is not None:
                 send = send + cut(pending, 0, count, turned)
                 pending = cut(pending, count, count, turned)
-            new = flip(send.astype(BF16), bit).astype(F32)
+            send = send.astype(BF16)
+            if place == 0:
+                if i >= 2:
+                    send, ready[i - 2] = lax.optimization_barrier((send, ready[i - 2]))
+                if i >= 3:
+                    send, over[i - 3] = lax.optimization_barrier((send, over[i - 3]))
+            if place == 1:
+                ready.append(send)
+            new = flip(send, bit)
+            if place == 1:
+                over.append(new)
+            new = new.astype(F32)
             pending = new if pending is None else pending + new
             start += count
-        return term(start, 1) + pending
+        results.append(term(piece, start, 1) + pending)
 
-    def cut(array, start, count, turned):
-        return lax.slice_in_dim(array, start * owned, (start + count) * owned, axis=1 if turned else 0)
-
-    half = width // 2
-
-    def in_halves(features, grad, turned):
-        parts = [reduced(features, grad[:, i * half : (i + 1) * half], turned) for i in range(2)]
-        return jnp.concatenate(parts, axis=0 if turned else 1)
-
-    output_gradient = in_halves(both_cot, gated, True)
-    projected = [in_halves(both_input, grad, False) for grad in (query_grad, key_grad, value_grad)]
+    output_gradient = jnp.concatenate(results[:2], axis=0)
+    projected = [jnp.concatenate(results[2 * i + 2 : 2 * i + 4], axis=1) for i in range(3)]
     return (jnp.stack(projected, axis=1), output_gradient)
 
 

time: 522 us -> 461 us (0.88)
  waiting for transfers between devices: 325 us -> 255 us
  matrix products: 68.7 us -> 109 us
  other arithmetic: 47.4 us -> 10.9 us
  local copies, waits for them, and re-layouts: 21.2 us -> 26.9 us
    dot_general x24 -> x48, matrix products: 43.3 us -> 83.8 us  [tdot(): lax.dot_general(a, b, (((0,), (0,)), ((), ())), preferred_element_type=F32)]
    all_gather x1, waiting for transfers between devices: 36.1 us -> 0.01 us  [body(): gathered_input = lax.all_gather(layer_input, 'head', axis=1, tiled=True)]
    ppermute x30, waiting for transfers between devices: 263 us -> 232 us  [flip(): return lax.ppermute(array, 'seq', [(i, i ^ 1 << bit) for i in range(size)])]
    concatenate x3 -> x1, other arithmetic: 25.7 us -> 1.49 us  [body(): output_gradient = jnp.concatenate(results[:2], axis=0)]
    slice x2 -> x0, other arithmetic: 12.6 us -> none  [term(): part = features[:, start * owned:(start + count) * owned]]
    unnamed x94 -> x114, local copies, waits for them, and re-layouts: 9.21 us -> 14.9 us
  transfers between devices with their start and end apart: 36 -> 36, of which waited for: 22 -> 22; matrix products, arithmetic and copies ran while one was open for 26% -> 29% of each run, Pallas kernels for 0% -> 0%
where the time goes in v2:
time: 461 us; the launch traced here: 455 us
  waiting for transfers between devices  255 us (55%)
  matrix products  109 us (24%)
  starting transfers between devices  37.5 us (8%)
  local copies, waits for them, and re-layouts  26.9 us (6%)
  between operations  15.3 us (3%)
  other arithmetic  10.9 us (2%)
    ppermute x30, waiting for transfers between devices, flip(): return lax.ppermute(array, 'seq', [(i, i ^ 1 << bit) for i in range(size)])  232 us
    dot_general x48, matrix products, tdot(): lax.dot_general(a, b, (((0,), (0,)), ((), ())), preferred_element_type=F32)  83.8 us
    ppermute x30, starting transfers between devices, flip(): return lax.ppermute(array, 'seq', [(i, i ^ 1 << bit) for i in range(size)])  31.2 us
    unnamed x114, local copies, waits for them, and re-layouts  14.9 us
    all_gather x1, waiting for transfers between devices, body(): gathered_cot = lax.all_gather(cotangent, 'head', axis=1, tiled=True)  11.6 us
    ppermute x2, waiting for transfers between devices, entering(): before = before + lax.ppermute(total.astype(BF16), 'seq', pairs).astype(F32)  11.2 us
  transfers between devices with their start and end apart: 36, of which 22 were waited for; matrix products, arithmetic and copies ran while one was open for 29% of the time, Pallas kernels for 0%

profile of v2, /device:TPU:0, one launch (start us, length us, event | category | flops | bytes accessed | tf_op | source)
XLA Modules:
  0.0 455.2 jit_solution(3887219008888169715)
XLA Ops:
  19.3 3.7 collective-permute-done
  30.7 4.4 collective-permute-start.2
  35.2 11.6 %all-gather.5.cloned.1.call-done = bf16[512,4096]{1,0:T(8,128)(2,1)} async-done(((bf16[512,1024]{1,0:T(8,128)(2,1)}), bf16[512,4096]{1,0:T(8,128)(2,1)}) %all-gather.5.cloned.1.call-update) | async-done | bytes 4194320 | tf_op jit(solution)/shard_map/all_gather | solution.py:53
  52.6 11.8 %collective-permute-done.6 = bf16[512,512]{1,0:T(8,128)(2,1)} collective-permute-done((bf16[512,512]{1,0:T(8,128)(2,1)S(1)}, bf16[512,512]{1,0:T(8,128)(2,1)}, u32[]{:S(2)}, u32[]{:S(2)}) %collective-permute-start.6) | collective-permute-done | bytes 524320 | tf_op jit(solution)/shard_map/ppermute | solution.py:13
  64.7 8.3 %multiply_reduce_fusion = (f32[512,8]{0,1:T(8,128)S(1)}, f32[512,1024]{0,1:T(8,128)S(1)}) fusion(f32[8,128]{1,0:T(8,128)S(1)} %bitcast.168, f32[512,8,128]{0,2,1:T(8,128)S(1)} %get-tuple-element.55, f32[512,8]{0,1:T(8,128)S(1)} %add_sqrt_fusion, bf16[512,4096]{1,0:T(8,128)(2,1)} %all-gather.5.cloned.1.call-done, bf16[1024,4096]{1,0:T(8,128)(2,1)} %param.11), kind=kOutput, calls=%fused_computation.31 | convolution fusion | flops 4297060352 | bytes 16814080 | tf_op jit(solution)/shard_map/reshape | solution.py:94
  108.4 20.9 %collective-permute-done.17 = bf16[8,128,128]{2,1,0:T(8,128)(2,1)S(1)} collective-permute-done((bf16[8,128,128]{2,1,0:T(8,128)(2,1)S(1)}, bf16[8,128,128]{2,1,0:T(8,128)(2,1)S(1)}, u32[]{:S(2)}, u32[]{:S(2)}) %collective-permute-start.17) | collective-permute-done | bytes 262176 | tf_op jit(solution)/shard_map/ppermute | solution.py:13
  133.4 11.2 %collective-permute-done.18 = bf16[8,128,128]{2,1,0:T(8,128)(2,1)S(1)} collective-permute-done((bf16[8,128,128]{2,1,0:T(8,128)(2,1)S(1)}, bf16[8,128,128]{2,1,0:T(8,128)(2,1)S(1)}, u32[]{:S(2)}, u32[]{:S(2)}) %collective-permute-start.18) | collective-permute-done | bytes 262176 | tf_op jit(solution)/shard_map/ppermute | solution.py:29
  155.6 18.3 %collective-permute-done.7 = bf16[512,1024]{1,0:T(8,128)(2,1)S(1)} collective-permute-done((bf16[512,1024]{1,0:T(8,128)(2,1)S(1)}, bf16[512,1024]{1,0:T(8,128)(2,1)S(1)}, u32[]{:S(2)}, u32[]{:S(2)}) %collective-permute-start.7) | collective-permute-done | bytes 1048608 | tf_op jit(solution)/shard_map/ppermute | solution.py:13
  175.8 18.8 %collective-permute-done.12 = bf16[512,1024]{1,0:T(8,128)(2,1)S(1)} collective-permute-done((bf16[512,1024]{1,0:T(8,128)(2,1)S(1)}, bf16[512,1024]{1,0:T(8,128)(2,1)S(1)}, u32[]{:S(2)}, u32[]{:S(2)}) %collective-permute-start.12) | collective-permute-done | bytes 1048608 | tf_op jit(solution)/shard_map/ppermute | solution.py:13
  197.5 6.2 %collective-permute-done.13 = bf16[512,512]{1,0:T(8,128)(2,1)S(1)} collective-permute-done((bf16[512,512]{1,0:T(8,128)(2,1)S(1)}, bf16[512,512]{1,0:T(8,128)(2,1)S(1)}, u32[]{:S(2)}, u32[]{:S(2)}) %collective-permute-start.13) | collective-permute-done | bytes 524320 | tf_op jit(solution)/shard_map/ppermute | solution.py:13
  205.4 9.7 %collective-permute-done.20 = bf16[512,512]{1,0:T(8,128)(2,1)S(1)} collective-permute-done((bf16[512,512]{1,0:T(8,128)(2,1)S(1)}, bf16[512,512]{1,0:T(8,128)(2,1)S(1)}, u32[]{:S(2)}, u32[]{:S(2)}) %collective-permute-start.20) | collective-permute-done | bytes 524320 | tf_op jit(solution)/shard_map/ppermute | solution.py:13
  218.1 3.2 constant_dynamic-slice_fusion.8
  227.6 9.7 %collective-permute-done.3 = bf16[512,512]{1,0:T(8,128)(2,1)} collective-permute-done((bf16[512,512]{1,0:T(8,128)(2,1)S(1)}, bf16[512,512]{1,0:T(8,128)(2,1)}, u32[]{:S(2)}, u32[]{:S(2)}) %collective-permute-start.3) | collective-permute-done | bytes 524320 | tf_op jit(solution)/shard_map/ppermute | solution.py:13
  273.5 14.6 %collective-permute-done.8 = bf16[1024,512]{0,1:T(8,128)(2,1)S(1)} collective-permute-done((bf16[1024,512]{0,1:T(8,128)(2,1)S(1)}, bf16[1024,512]{0,1:T(8,128)(2,1)S(1)}, u32[]{:S(2)}, u32[]{:S(2)}) %collective-permute-start.8) | collective-permute-done | bytes 1048608 | tf_op jit(solution)/shard_map/ppermute | solution.py:13
  295.8 14.9 %collective-permute-done.14 = bf16[1024,512]{0,1:T(8,128)(2,1)S(1)} collective-permute-done((bf16[1024,512]{0,1:T(8,128)(2,1)S(1)}, bf16[1024,512]{0,1:T(8,128)(2,1)S(1)}, u32[]{:S(2)}, u32[]{:S(2)}) %collective-permute-start.14) | collective-permute-done | bytes 1048608 | tf_op jit(solution)/shard_map/ppermute | solution.py:13
  319.1 14.1 %collective-permute-done.21 = bf16[1024,512]{0,1:T(8,128)(2,1)S(1)} collective-permute-done((bf16[1024,512]{0,1:T(8,128)(2,1)S(1)}, bf16[1024,512]{0,1:T(8,128)(2,1)S(1)}, u32[]{:S(2)}, u32[]{:S(2)}) %collective-permute-start.21) | collective-permute-done | bytes 1048608 | tf_op jit(solution)/shard_map/ppermute | solution.py:13
  338.9 17.7 %collective-permute-done.15 = bf16[512,512]{0,1:T(8,128)(2,1)S(1)} collective-permute-done((bf16[512,512]{0,1:T(8,128)(2,1)S(1)}, bf16[512,512]{0,1:T(8,128)(2,1)S(1)}, u32[]{:S(2)}, u32[]{:S(2)}) %collective-permute-start.15) | collective-permute-done | bytes 524320 | tf_op jit(solution)/shard_map/ppermute | solution.py:13
  359.0 7.0 %collective-permute-done.22 = bf16[512,512]{0,1:T(8,128)(2,1)S(1)} collective-permute-done((bf16[512,512]{0,1:T(8,128)(2,1)S(1)}, bf16[512,512]{0,1:T(8,128)(2,1)S(1)}, u32[]{:S(2)}, u32[]{:S(2)}) %collective-permute-start.22) | collective-permute-done | bytes 524320 | tf_op jit(solution)/shard_map/ppermute | solution.py:13
  371.0 11.7 %collective-permute-done.27 = bf16[1024,512]{0,1:T(8,128)(2,1)S(1)} collective-permute-done((bf16[1024,512]{0,1:T(8,128)(2,1)S(1)}, bf16[1024,512]{0,1:T(8,128)(2,1)S(1)}, u32[]{:S(2)}, u32[]{:S(2)}) %collective-permute-start.27) | collective-permute-done | bytes 1048608 | tf_op jit(solution)/shard_map/ppermute | solution.py:13
  384.6 16.0 %collective-permute-done.30 = bf16[1024,512]{0,1:T(8,128)(2,1)S(1)} collective-permute-done((bf16[1024,512]{0,1:T(8,128)(2,1)S(1)}, bf16[1024,512]{0,1:T(8,128)(2,1)S(1)}, u32[]{:S(2)}, u32[]{:S(2)}) %collective-permute-start.30) | collective-permute-done | bytes 1048608 | tf_op jit(solution)/shard_map/ppermute | solution.py:13
  405.8 20.8 %collective-permute-done.28 = bf16[512,512]{0,1:T(8,128)(2,1)S(1)} collective-permute-done((bf16[512,512]{0,1:T(8,128)(2,1)S(1)}, bf16[512,512]{0,1:T(8,128)(2,1)S(1)}, u32[]{:S(2)}, u32[]{:S(2)}) %collective-permute-start.28) | collective-permute-done | bytes 524320 | tf_op jit(solution)/shard_map/ppermute | solution.py:13
  428.1 9.6 %collective-permute-done.31 = bf16[512,512]{0,1:T(8,128)(2,1)S(1)} collective-permute-done((bf16[512,512]{0,1:T(8,128)(2,1)S(1)}, bf16[512,512]{0,1:T(8,128)(2,1)S(1)}, u32[]{:S(2)}, u32[]{:S(2)}) %collective-permute-start.31) | collective-permute-done | bytes 524320 | tf_op jit(solution)/shard_map/ppermute | solution.py:13
  438.3 3.3 pad_maximum_fusion
  441.6 6.6 %copy.51 = f32[512,3,1024]{2,0,1:T(8,128)} copy(f32[512,3,1024]{0,2,1:T(8,128)} %pad_maximum_fusion) | data formatting | bytes 12582912
  (259 shorter events, 165.8 us)
Async XLA Ops:
  7.2 39.6 %all-gather.5.cloned.1.call-start = ((), (), s32[]{:S(2)}) async-start(), calls=%async_computation | async-start | bytes 5242880 | tf_op jit(solution)/shard_map/all_gather | solution.py:53
  7.9 136.9 %all-gather.11.cloned.1.call-start = ((), (), s32[]{:S(2)}) async-start(), calls=%async_computation.3 | async-start | bytes 2621440 | tf_op jit(solution)/shard_map/all_gather | solution.py:76
  64.5 153.6 %all-gather.7.cloned.1.call-start = ((), (), s32[]{:S(2)}) async-start(), calls=%async_computation.1 | async-start | bytes 5242880 | tf_op jit(solution)/shard_map/all_gather | solution.py:55
  76.4 68.4 %collective-permute-start.5 = (bf16[512,512]{0,1:T(8,128)(2,1)}, bf16[512,512]{0,1:T(8,128)(2,1)}, u32[]{:S(2)}, u32[]{:S(2)}) collective-permute-start(bf16[512,512]{0,1:T(8,128)(2,1)} %get-tuple-element.50), channel_id=1, source_target_pairs={{0,8},{4,12},{8,0},{12,4},{16,24},{20,28},{24,16},{28,20},{1,9},{5... | collective-permute-start | bytes 1572872 | tf_op jit(solution)/shard_map/ppermute | solution.py:13
  77.9 71.9 %collective-permute-start.11 = (bf16[512,512]{0,1:T(8,128)(2,1)}, bf16[512,512]{0,1:T(8,128)(2,1)}, u32[]{:S(2)}, u32[]{:S(2)}) collective-permute-start(bf16[512,512]{0,1:T(8,128)(2,1)} %get-tuple-element.51), channel_id=1, source_target_pairs={{0,8},{4,12},{8,0},{12,4},{16,24},{20,28},{24,16},{28,20},{1,9},{5... | collective-permute-start | bytes 1572872 | tf_op jit(solution)/shard_map/ppermute | solution.py:13
  83.4 175.7 %collective-permute-start.4 = (bf16[512,512]{0,1:T(8,128)(2,1)}, bf16[512,512]{0,1:T(8,128)(2,1)}, u32[]{:S(2)}, u32[]{:S(2)}) collective-permute-start(bf16[512,512]{0,1:T(8,128)(2,1)} %get-tuple-element.48), channel_id=1, source_target_pairs={{0,8},{4,12},{8,0},{12,4},{16,24},{20,28},{24,16},{28,20},{1,9},{5... | collective-permute-start | bytes 1572872 | tf_op jit(solution)/shard_map/ppermute | solution.py:13
  84.9 180.8 %collective-permute-start.10 = (bf16[512,512]{0,1:T(8,128)(2,1)}, bf16[512,512]{0,1:T(8,128)(2,1)}, u32[]{:S(2)}, u32[]{:S(2)}) collective-permute-start(bf16[512,512]{0,1:T(8,128)(2,1)} %get-tuple-element.49), channel_id=1, source_target_pairs={{0,8},{4,12},{8,0},{12,4},{16,24},{20,28},{24,16},{28,20},{1,9},{5... | collective-permute-start | bytes 1572872 | tf_op jit(solution)/shard_map/ppermute | solution.py:13
  90.4 168.7 %all-gather.9.cloned.1.call-start = ((), (), s32[]{:S(2)}) async-start(), calls=%async_computation.2 | async-start | bytes 2621440 | tf_op jit(solution)/shard_map/all_gather | solution.py:76
  147.8 26.2 %collective-permute-start.7 = (bf16[512,1024]{1,0:T(8,128)(2,1)S(1)}, bf16[512,1024]{1,0:T(8,128)(2,1)S(1)}, u32[]{:S(2)}, u32[]{:S(2)}) collective-permute-start(bf16[512,1024]{1,0:T(8,128)(2,1)S(1)} %add_convert_fusion.7), channel_id=1, source_target_pairs={{0,4},{4,0},{8,12},{12,8},{16,20},{20,16},{24,28},{28,24},{1,5},{5... | collective-permute-start | bytes 3145736 | tf_op jit(solution)/shard_map/ppermute | solution.py:13
  152.3 42.3 %collective-permute-start.12 = (bf16[512,1024]{1,0:T(8,128)(2,1)S(1)}, bf16[512,1024]{1,0:T(8,128)(2,1)S(1)}, u32[]{:S(2)}, u32[]{:S(2)}) collective-permute-start(bf16[512,1024]{1,0:T(8,128)(2,1)S(1)} %add_convert_fusion.5), channel_id=1, source_target_pairs={{0,4},{4,0},{8,12},{12,8},{16,20},{20,16},{24,28},{28,24},{1,5},{5... | collective-permute-start | bytes 3145736 | tf_op jit(solution)/shard_map/ppermute | solution.py:13
  154.1 115.5 %collective-permute-start.19 = (bf16[512,512]{0,1:T(8,128)(2,1)}, bf16[512,512]{0,1:T(8,128)(2,1)}, u32[]{:S(2)}, u32[]{:S(2)}) collective-permute-start(bf16[512,512]{0,1:T(8,128)(2,1)} %get-tuple-element.46), channel_id=1, source_target_pairs={{0,8},{4,12},{8,0},{12,4},{16,24},{20,28},{24,16},{28,20},{1,9},{5... | collective-permute-start | bytes 1572872 | tf_op jit(solution)/shard_map/ppermute | solution.py:13
  175.7 28.0 %collective-permute-start.13 = (bf16[512,512]{1,0:T(8,128)(2,1)S(1)}, bf16[512,512]{1,0:T(8,128)(2,1)S(1)}, u32[]{:S(2)}, u32[]{:S(2)}) collective-permute-start(bf16[512,512]{1,0:T(8,128)(2,1)S(1)} %fusion.18), channel_id=1, source_target_pairs={{0,16},{4,20},{8,24},{12,28},{16,0},{20,4},{24,8},{28,12},{1,17},{... | collective-permute-start | bytes 1572872 | tf_op jit(solution)/shard_map/ppermute | solution.py:13
  203.7 88.8 %collective-permute-start.23 = (bf16[512,512]{0,1:T(8,128)(2,1)}, bf16[512,512]{0,1:T(8,128)(2,1)}, u32[]{:S(2)}, u32[]{:S(2)}) collective-permute-start(bf16[512,512]{0,1:T(8,128)(2,1)} %get-tuple-element.47), channel_id=1, source_target_pairs={{0,8},{4,12},{8,0},{12,4},{16,24},{20,28},{24,16},{28,20},{1,9},{5... | collective-permute-start | bytes 1572872 | tf_op jit(solution)/shard_map/ppermute | solution.py:13
  237.3 78.9 %collective-permute-start.26 = (bf16[512,512]{0,1:T(8,128)(2,1)}, bf16[512,512]{0,1:T(8,128)(2,1)}, u32[]{:S(2)}, u32[]{:S(2)}) collective-permute-start(bf16[512,512]{0,1:T(8,128)(2,1)} %get-tuple-element.44), channel_id=1, source_target_pairs={{0,8},{4,12},{8,0},{12,4},{16,24},{20,28},{24,16},{28,20},{1,9},{5... | collective-permute-start | bytes 1572872 | tf_op jit(solution)/shard_map/ppermute | solution.py:13
  267.6 43.1 %collective-permute-start.14 = (bf16[1024,512]{0,1:T(8,128)(2,1)S(1)}, bf16[1024,512]{0,1:T(8,128)(2,1)S(1)}, u32[]{:S(2)}, u32[]{:S(2)}) collective-permute-start(bf16[1024,512]{0,1:T(8,128)(2,1)S(1)} %add_convert_fusion.6), channel_id=1, source_target_pairs={{0,4},{4,0},{8,12},{12,8},{16,20},{20,16},{24,28},{28,24},{1,5},{5... | collective-permute-start | bytes 3145736 | tf_op jit(solution)/shard_map/ppermute | solution.py:13
  269.7 48.3 %collective-permute-start.29 = (bf16[512,512]{0,1:T(8,128)(2,1)S(1)}, bf16[512,512]{0,1:T(8,128)(2,1)S(1)}, u32[]{:S(2)}, u32[]{:S(2)}) collective-permute-start(bf16[512,512]{0,1:T(8,128)(2,1)S(1)} %copy-done.52), channel_id=1, source_target_pairs={{0,8},{4,12},{8,0},{12,4},{16,24},{20,28},{24,16},{28,20},{1,9},{5... | collective-permute-start | bytes 1572872 | tf_op jit(solution)/shard_map/ppermute | solution.py:13
  292.5 40.6 %collective-permute-start.21 = (bf16[1024,512]{0,1:T(8,128)(2,1)S(1)}, bf16[1024,512]{0,1:T(8,128)(2,1)S(1)}, u32[]{:S(2)}, u32[]{:S(2)}) collective-permute-start(bf16[1024,512]{0,1:T(8,128)(2,1)S(1)} %add_convert_fusion.4), channel_id=1, source_target_pairs={{0,4},{4,0},{8,12},{12,8},{16,20},{20,16},{24,28},{28,24},{1,5},{5... | collective-permute-start | bytes 3145736 | tf_op jit(solution)/shard_map/ppermute | solution.py:13
  314.8 42.4 %collective-permute-start.24 = (bf16[1024,512]{0,1:T(8,128)(2,1)S(1)}, bf16[1024,512]{0,1:T(8,128)(2,1)S(1)}, u32[]{:S(2)}, u32[]{:S(2)}) collective-permute-start(bf16[1024,512]{0,1:T(8,128)(2,1)S(1)} %add_convert_fusion.3), channel_id=1, source_target_pairs={{0,4},{4,0},{8,12},{12,8},{16,20},{20,16},{24,28},{28,24},{1,5},{5... | collective-permute-start | bytes 3145736 | tf_op jit(solution)/shard_map/ppermute | solution.py:13
  318.7 37.9 %collective-permute-start.15 = (bf16[512,512]{0,1:T(8,128)(2,1)S(1)}, bf16[512,512]{0,1:T(8,128)(2,1)S(1)}, u32[]{:S(2)}, u32[]{:S(2)}) collective-permute-start(bf16[512,512]{0,1:T(8,128)(2,1)S(1)} %fusion.21), channel_id=1, source_target_pairs={{0,16},{4,20},{8,24},{12,28},{16,0},{20,4},{24,8},{28,12},{1,17},{... | collective-permute-start | bytes 1572872 | tf_op jit(solution)/shard_map/ppermute | solution.py:13
  335.0 31.1 %collective-permute-start.22 = (bf16[512,512]{0,1:T(8,128)(2,1)S(1)}, bf16[512,512]{0,1:T(8,128)(2,1)S(1)}, u32[]{:S(2)}, u32[]{:S(2)}) collective-permute-start(bf16[512,512]{0,1:T(8,128)(2,1)S(1)} %fusion.22), channel_id=1, source_target_pairs={{0,16},{4,20},{8,24},{12,28},{16,0},{20,4},{24,8},{28,12},{1,17},{... | collective-permute-start | bytes 1572872 | tf_op jit(solution)/shard_map/ppermute | solution.py:13
  366.0 34.6 %collective-permute-start.30 = (bf16[1024,512]{0,1:T(8,128)(2,1)S(1)}, bf16[1024,512]{0,1:T(8,128)(2,1)S(1)}, u32[]{:S(2)}, u32[]{:S(2)}) collective-permute-start(bf16[1024,512]{0,1:T(8,128)(2,1)S(1)} %add_convert_fusion), channel_id=1, source_target_pairs={{0,4},{4,0},{8,12},{12,8},{16,20},{20,16},{24,28},{28,24},{1,5},{5... | collective-permute-start | bytes 3145736 | tf_op jit(solution)/shard_map/ppermute | solution.py:13
  368.5 35.6 %collective-permute-start.25 = (bf16[512,512]{0,1:T(8,128)(2,1)S(1)}, bf16[512,512]{0,1:T(8,128)(2,1)S(1)}, u32[]{:S(2)}, u32[]{:S(2)}) collective-permute-start(bf16[512,512]{0,1:T(8,128)(2,1)S(1)} %fusion.23), channel_id=1, source_target_pairs={{0,16},{4,20},{8,24},{12,28},{16,0},{20,4},{24,8},{28,12},{1,17},{... | collective-permute-start | bytes 1572872 | tf_op jit(solution)/shard_map/ppermute | solution.py:13
  384.5 42.1 %collective-permute-start.28 = (bf16[512,512]{0,1:T(8,128)(2,1)S(1)}, bf16[512,512]{0,1:T(8,128)(2,1)S(1)}, u32[]{:S(2)}, u32[]{:S(2)}) collective-permute-start(bf16[512,512]{0,1:T(8,128)(2,1)S(1)} %fusion.24), channel_id=1, source_target_pairs={{0,16},{4,20},{8,24},{12,28},{16,0},{20,4},{24,8},{28,12},{1,17},{... | collective-permute-start | bytes 1572872 | tf_op jit(solution)/shard_map/ppermute | solution.py:13
  401.3 36.3 %collective-permute-start.31 = (bf16[512,512]{0,1:T(8,128)(2,1)S(1)}, bf16[512,512]{0,1:T(8,128)(2,1)S(1)}, u32[]{:S(2)}, u32[]{:S(2)}) collective-permute-start(bf16[512,512]{0,1:T(8,128)(2,1)S(1)} %fusion.25), channel_id=1, source_target_pairs={{0,16},{4,20},{8,24},{12,28},{16,0},{20,4},{24,8},{28,12},{1,17},{... | collective-permute-start | bytes 1572872 | tf_op jit(solution)/shard_map/ppermute | solution.py:13
  (68 other events, 626.4 us)
Sparse Core Ops, SparseCore 0:
  9.6 37.1 all-gather.4
  64.6 22.5 all-gather.10
  90.6 33.8 all-gather.6
  237.5 21.6 all-gather.8

commit v3 on v2

--- a/solution.py
+++ b/solution.py
@@ -1,6 +1,7 @@
 import jax
 import jax.numpy as jnp
 from jax import lax
+from jax.experimental import pallas as pl
 from jax.sharding import PartitionSpec as P
 
 HEAD_DIM = 128
@@ -40,6 +41,32 @@
     return lax.dot_general(a, b, (((0,), (0,)), ((), ())), preferred_element_type=F32)
 
 
+def put_kernel(*refs):
+    kept, new, out = refs[-3:]
+    out[...] = kept[...] + new[...].astype(F32)
+
+
+def put(target, kept, new, shape, place):
+    rows, cols = kept.shape
+    tile = min(rows, 256)
+    block = (None,) * (len(shape) - 2) + (tile, cols)
+
+    def at(r):
+        return (*place[:-2], place[-2] * (rows // tile) + r, place[-1])
+
+    small = pl.BlockSpec((tile, cols), lambda r: (r, 0))
+    old = [] if target is None else [target]
+    return pl.pallas_call(
+        put_kernel,
+        grid=(rows // tile,),
+        in_specs=[pl.BlockSpec(memory_space=pl.ANY)] * len(old) + [small, small],
+        out_specs=pl.BlockSpec(block, at),
+        out_shape=jax.ShapeDtypeStruct(shape, F32),
+        input_output_aliases={0: 0} if old else {},
+        cost_estimate=pl.CostEstimate(flops=rows * cols, bytes_accessed=rows * cols * 10, transcendentals=0),
+    )(*old, kept, new)
+
+
 def body(layer_input, query_rows, key_rows, value_rows, out_weight, norm_gain, cotangent):
     size, position = lax.axis_size("seq"), lax.axis_index("seq")
     bits = size.bit_length() - 1
@@ -50,9 +77,8 @@
     model = out_weight.shape[1]
     owned = model // size
 
+    head_size, head_place = lax.axis_size("head"), lax.axis_index("head")
     gathered_cot = lax.all_gather(cotangent, "head", axis=1, tiled=True)
-    layer_input, gathered_cot = lax.optimization_barrier((layer_input, gathered_cot))
-    gathered_input = lax.all_gather(layer_input, "head", axis=1, tiled=True)
 
     chunks = 1 << len(halving)
     order = []
@@ -68,13 +94,24 @@
             [lax.dynamic_slice_in_dim(array, (at ^ toggled) * owned, owned, 1) for at in order], axis=1
         )
 
-    def both(array):
-        mine = pick(array, 0)
-        share = chunks * owned // lax.axis_size("head")
-        send = pick(array, 1 << gather_bit)
-        send = lax.dynamic_slice_in_dim(send, lax.axis_index("head") * share, share, 1)
+    def both(gathered):
+        share = chunks * owned // head_size
+        send = pick(gathered, 1 << gather_bit)
+        send = lax.dynamic_slice_in_dim(send, head_place * share, share, 1)
         theirs = lax.all_gather(flip(send, gather_bit), "head", axis=1, tiled=True)
-        return mine, theirs
+        return pick(gathered, 0), theirs
+
+    paired = gather_bit == 1 and head_size == 4 and width == 2 * owned
+    aligned = (head_place & 1) == ((position >> 1) & 1)
+
+    def across(array, seq_toggle, head_toggle):
+        pairs = [
+            (s * head_size + h, (s ^ seq_toggle) * head_size + (h ^ head_toggle))
+            for s in range(size)
+            for h in range(head_size)
+            if (h ^ (s >> 1)) & 1
+        ]
+        return lax.ppermute(array, ("seq", "head"), pairs)
 
     queries = query_rows.reshape(tokens, heads, HEAD_DIM)
     key_heads = key_rows.reshape(tokens, heads, HEAD_DIM)
@@ -82,7 +119,29 @@
     gain = norm_gain.reshape(heads, HEAD_DIM)
     lower = lower_mask(tokens)[None]
     block_state = jnp.einsum("thd,the->hde", key_heads, value_heads, preferred_element_type=F32)
-    state_low = entering(block_state, False).astype(BF16)
+    if paired:
+        same_cot = across(cotangent, 2, 1)
+        other_cot = across(same_cot, 0, 2)
+        near_cot, far_cot = across(same_cot, 0, 1), across(other_cot, 0, 1)
+    state_in = entering(block_state, False)
+    if paired:
+        layer_input, state_in = lax.optimization_barrier((layer_input, state_in))
+        swapped = jnp.where(aligned, layer_input, across(layer_input, 2, 1))
+        gathered_input = lax.all_gather(swapped, "head", axis=1, tiled=True)
+        both_input = pick(gathered_input, 0), pick(gathered_input, 2)
+        near_cot = jnp.where(aligned, near_cot, same_cot)
+        far_cot = jnp.where(aligned, far_cot, other_cot)
+
+        def chosen(at):
+            near, far = (lax.dynamic_slice_in_dim(a, (at & 1) * owned, owned, 1) for a in (near_cot, far_cot))
+            return jnp.where((at >> 2) == (head_place >> 1), near, far)
+
+        both_cot = pick(gathered_cot, 0), jnp.concatenate([chosen(at) for at in order], axis=1)
+    else:
+        layer_input, gathered_cot = lax.optimization_barrier((layer_input, gathered_cot))
+        both_input = both(lax.all_gather(layer_input, "head", axis=1, tiled=True))
+        both_cot = both(gathered_cot)
+    state_low = state_in.astype(BF16)
     scores = jnp.einsum("thd,shd->hts", queries, key_heads, preferred_element_type=F32)
     scores = jnp.where(lower, scores, 0.0).astype(BF16)
     attention = jnp.einsum("hts,she->the", scores, value_heads, preferred_element_type=F32)
@@ -108,8 +167,6 @@
     key_grad = key_grad.astype(BF16).reshape(tokens, width)
     value_grad = value_grad.astype(BF16).reshape(tokens, width)
 
-    both_input, both_cot = both(gathered_input), both(gathered_cot)
-
     def cut(array, start, count, turned):
         return lax.slice_in_dim(array, start * owned, (start + count) * owned, axis=1 if turned else 0)
 
@@ -123,6 +180,7 @@
 
     half = width // 2
     pieces = []
+    output_gradient = projected = None
     for features, grad, turned in (
         (both_cot, gated, True),
         (both_input, query_grad, False),
@@ -133,7 +191,7 @@
             part = grad[:, i * half : (i + 1) * half]
             pieces.append((features, part, flip(part, gather_bit), turned))
 
-    ready, over, results = [], [], []
+    ready, over = [], []
     for i, piece in enumerate(pieces):
         turned = piece[3]
         start, count = 0, chunks
@@ -155,14 +213,15 @@
             new = flip(send, bit)
             if place == 1:
                 over.append(new)
-            new = new.astype(F32)
-            pending = new if pending is None else pending + new
             start += count
-        results.append(term(piece, start, 1) + pending)
-
-    output_gradient = jnp.concatenate(results[:2], axis=0)
-    projected = [jnp.concatenate(results[2 * i + 2 : 2 * i + 4], axis=1) for i in range(3)]
-    return (jnp.stack(projected, axis=1), output_gradient)
+            if place < len(halving) - 1:
+                pending = new.astype(F32) if pending is None else pending + new.astype(F32)
+        kept = term(piece, start, 1) + pending
+        if turned:
+            output_gradient = put(output_gradient, kept, new, (width, owned), (i, 0))
+        else:
+            projected = put(projected, kept, new, (3, owned, width), (i // 2 - 1, 0, i % 2))
+    return (projected.transpose(1, 0, 2), output_gradient)
 
 
 def solution(mesh):

time: 461 us -> 414 us (0.90)
  waiting for transfers between devices: 255 us -> 192 us
  Pallas kernels: 0 us -> 18 us
  starting transfers between devices: 37.5 us -> 50.1 us
  matrix products: 109 us -> 99.1 us
  local copies, waits for them, and re-layouts: 26.9 us -> 17.6 us
  other arithmetic: 10.9 us -> 16.2 us
    ppermute x30 -> x28, waiting for transfers between devices: 232 us -> 171 us  [flip(): return lax.ppermute(array, 'seq', [(i, i ^ 1 << bit) for i in range(size)])]
    pallas_call x0 -> x8, Pallas kernels: none -> 18 us  [put(): pl.pallas_call(put_kernel, grid=(rows // tile,), in_specs=[pl.BlockSpec(m...]
    all_gather x1, waiting for transfers between devices: 11.6 us -> 0.01 us  [body(): gathered_cot = lax.all_gather(cotangent, 'head', axis=1, tiled=True)]
    ppermute x0 -> x5, starting transfers between devices: none -> 8.33 us  [across(): return lax.ppermute(array, ('seq', 'head'), pairs)]
    dot_general x48, matrix products: 83.8 us -> 76.5 us  [tdot(): lax.dot_general(a, b, (((0,), (0,)), ((), ())), preferred_element_type=F32)]
    select_n x0 -> x4, other arithmetic: none -> 5.29 us  [the longest x1 1.49 us: chosen(): return jnp.where(at >> 2 == head_place >> 1, near, far)]
    convert_element_type x9 -> x8, other arithmetic: 2.02 us -> 7.12 us  [body(): pending = new.astype(F32) if pending is None else pending + new.astype(F32)]
    ppermute x0 -> x5, waiting for transfers between devices: none -> 4.96 us  [across(): return lax.ppermute(array, ('seq', 'head'), pairs)]
  transfers between devices with their start and end apart: 36 -> 37, of which waited for: 22 -> 19; matrix products, arithmetic and copies ran while one was open for 29% -> 31% of each run, Pallas kernels for 0% -> 4%
where the time goes in v3:
time: 414 us; the launch traced here: 408 us
  waiting for transfers between devices  192 us (46%)
  matrix products  99.1 us (24%)
  starting transfers between devices  50.1 us (12%)
  Pallas kernels  18 us (4%)
  local copies, waits for them, and re-layouts  17.6 us (4%)
  other arithmetic  16.2 us (4%)
  between operations  15.2 us (4%)
    ppermute x28, waiting for transfers between devices, flip(): return lax.ppermute(array, 'seq', [(i, i ^ 1 << bit) for i in range(size)])  171 us
    dot_general x48, matrix products, tdot(): lax.dot_general(a, b, (((0,), (0,)), ((), ())), preferred_element_type=F32)  76.5 us
    ppermute x28, starting transfers between devices, flip(): return lax.ppermute(array, 'seq', [(i, i ^ 1 << bit) for i in range(size)])  34.9 us
    pallas_call x8, Pallas kernels, put(): pl.pallas_call(put_kernel, grid=(rows // tile,), in_specs=[pl.BlockSpec(m...  18 us
    ppermute x2, waiting for transfers between devices, entering(): before = before + lax.ppermute(total.astype(BF16), 'seq', pairs).astype(F32)  15.9 us
    unnamed x99, local copies, waits for them, and re-layouts  10.8 us
    ppermute x5, starting transfers between devices, across(): return lax.ppermute(array, ('seq', 'head'), pairs)  8.33 us
  transfers between devices with their start and end apart: 37, of which 19 were waited for; matrix products, arithmetic and copies ran while one was open for 31% of the time, Pallas kernels for 4%

profile of v3, /device:TPU:0, one launch (start us, length us, event | category | flops | bytes accessed | tf_op | source)
XLA Modules:
  0.0 408.4 jit_solution(15536217146704953675)
XLA Ops:
  12.6 3.0 collective-permute-start
  17.3 4.7 %collective-permute-done = bf16[8,128,128]{2,1,0:T(8,128)(2,1)S(1)} collective-permute-done((bf16[8,128,128]{2,1,0:T(8,128)(2,1)S(1)}, bf16[8,128,128]{2,1,0:T(8,128)(2,1)S(1)}, u32[]{:S(2)}, u32[]{:S(2)}) %collective-permute-start) | collective-permute-done | bytes 262176 | tf_op jit(solution)/shard_map/ppermute | solution.py:14
  23.9 13.8 %collective-permute-done.1 = bf16[8,128,128]{2,1,0:T(8,128)(2,1)S(1)} collective-permute-done((bf16[8,128,128]{2,1,0:T(8,128)(2,1)S(1)}, bf16[8,128,128]{2,1,0:T(8,128)(2,1)S(1)}, u32[]{:S(2)}, u32[]{:S(2)}) %collective-permute-start.1) | collective-permute-done | bytes 262176 | tf_op jit(solution)/shard_map/ppermute | solution.py:14
  38.5 5.2 %collective-permute-start.2 = (bf16[8,128,128]{2,1,0:T(8,128)(2,1)}, bf16[8,128,128]{2,1,0:T(8,128)(2,1)}, u32[]{:S(2)}, u32[]{:S(2)}) collective-permute-start(bf16[8,128,128]{2,1,0:T(8,128)(2,1)} %fusion.53), channel_id=1, source_target_pairs={{0,16},{4,20},{8,24},{12,28},{1,17},{5,21},{9,25},{13,29},{2,18},{... | collective-permute-start | bytes 786440 | tf_op jit(solution)/shard_map/ppermute | solution.py:30
  66.8 3.9 collective-permute-done.9
  74.6 8.3 %multiply_reduce_fusion = (f32[512,8]{0,1:T(8,128)S(1)}, f32[512,1024]{0,1:T(8,128)S(1)}) fusion(f32[8,128]{1,0:T(8,128)S(1)} %bitcast.164, f32[512,8,128]{0,2,1:T(8,128)S(1)} %get-tuple-element.49, f32[512,8]{0,1:T(8,128)S(1)} %add_sqrt_fusion, bf16[512,4096]{1,0:T(8,128)(2,1)} %all-gather.5.cloned.1.call-done, bf16[1024,4096]{1,0:T(8,128)(2,1)} %param.11), kind=kOutput, calls=%fused_computation.18 | convolution fusion | flops 4297060352 | bytes 16814080 | tf_op jit(solution)/shard_map/reshape | solution.py:153
  86.7 7.1 %collective-permute-start.5 = (bf16[512,512]{0,1:T(8,128)(2,1)S(1)}, bf16[512,512]{0,1:T(8,128)(2,1)S(1)}, u32[]{:S(2)}, u32[]{:S(2)}) collective-permute-start(bf16[512,512]{0,1:T(8,128)(2,1)S(1)} %get-tuple-element.43), channel_id=1, source_target_pairs={{0,8},{4,12},{8,0},{12,4},{16,24},{20,28},{24,16},{28,20},{1,9},{5... | collective-permute-start | bytes 1572872 | tf_op jit(solution)/shard_map/ppermute | solution.py:14
  110.3 35.3 %collective-permute-done.20 = bf16[8,128,128]{2,1,0:T(8,128)(2,1)S(1)} collective-permute-done((bf16[8,128,128]{2,1,0:T(8,128)(2,1)S(1)}, bf16[8,128,128]{2,1,0:T(8,128)(2,1)S(1)}, u32[]{:S(2)}, u32[]{:S(2)}) %collective-permute-start.20) | collective-permute-done | bytes 262176 | tf_op jit(solution)/shard_map/ppermute | solution.py:14
  148.2 13.2 %collective-permute-done.21 = bf16[8,128,128]{2,1,0:T(8,128)(2,1)S(1)} collective-permute-done((bf16[8,128,128]{2,1,0:T(8,128)(2,1)S(1)}, bf16[8,128,128]{2,1,0:T(8,128)(2,1)S(1)}, u32[]{:S(2)}, u32[]{:S(2)}) %collective-permute-start.21) | collective-permute-done | bytes 262176 | tf_op jit(solution)/shard_map/ppermute | solution.py:30
  167.1 5.8 %collective-permute-done.15 = bf16[512,1024]{1,0:T(8,128)(2,1)S(1)} collective-permute-done((bf16[512,1024]{1,0:T(8,128)(2,1)S(1)}, bf16[512,1024]{1,0:T(8,128)(2,1)S(1)}, u32[]{:S(2)}, u32[]{:S(2)}) %collective-permute-start.15) | collective-permute-done | bytes 1048608 | tf_op jit(solution)/shard_map/ppermute | solution.py:14
  188.1 3.5 collective-permute-start.16
  203.8 3.0 add_convert_fusion.3
  206.8 13.2 %collective-permute-done.22 = bf16[512,512]{0,1:T(8,128)(2,1)} collective-permute-done((bf16[512,512]{0,1:T(8,128)(2,1)}, bf16[512,512]{0,1:T(8,128)(2,1)}, u32[]{:S(2)}, u32[]{:S(2)}) %collective-permute-start.22) | collective-permute-done | bytes 524320 | tf_op jit(solution)/shard_map/ppermute | solution.py:14
  243.0 16.5 %collective-permute-done.17 = bf16[1024,512]{1,0:T(8,128)(2,1)S(1)} collective-permute-done((bf16[1024,512]{1,0:T(8,128)(2,1)S(1)}, bf16[1024,512]{1,0:T(8,128)(2,1)S(1)}, u32[]{:S(2)}, u32[]{:S(2)}) %collective-permute-start.17) | collective-permute-done | bytes 1048608 | tf_op jit(solution)/shard_map/ppermute | solution.py:14
  269.6 12.5 %collective-permute-done.24 = bf16[1024,512]{1,0:T(8,128)(2,1)} collective-permute-done((bf16[1024,512]{1,0:T(8,128)(2,1)}, bf16[1024,512]{1,0:T(8,128)(2,1)}, u32[]{:S(2)}, u32[]{:S(2)}) %collective-permute-start.24) | collective-permute-done | bytes 1048608 | tf_op jit(solution)/shard_map/ppermute | solution.py:14
  289.0 15.6 %collective-permute-done.18.refs_2_ = bf16[512,512]{1,0:T(8,128)(2,1)S(1)} collective-permute-done((bf16[512,512]{1,0:T(8,128)(2,1)}, bf16[512,512]{1,0:T(8,128)(2,1)S(1)}, u32[]{:S(2)}, u32[]{:S(2)}) %collective-permute-start.18) | collective-permute-done | bytes 524320 | tf_op jit(solution)/shard_map/ppermute | solution.py:14
  310.3 5.5 %collective-permute-done.25.refs_2_ = bf16[512,512]{1,0:T(8,128)(2,1)S(1)} collective-permute-done((bf16[512,512]{1,0:T(8,128)(2,1)S(1)}, bf16[512,512]{1,0:T(8,128)(2,1)S(1)}, u32[]{:S(2)}, u32[]{:S(2)}) %collective-permute-start.25) | collective-permute-done | bytes 524320 | tf_op jit(solution)/shard_map/ppermute | solution.py:14
  326.1 2.9 fusion.11.refs_1_
  331.2 2.9 fusion.9.refs_1_
  340.9 11.5 %collective-permute-done.33 = bf16[1024,512]{1,0:T(8,128)(2,1)} collective-permute-done((bf16[1024,512]{1,0:T(8,128)(2,1)}, bf16[1024,512]{1,0:T(8,128)(2,1)}, u32[]{:S(2)}, u32[]{:S(2)}) %collective-permute-start.33) | collective-permute-done | bytes 1048608 | tf_op jit(solution)/shard_map/ppermute | solution.py:14
  358.9 17.8 %collective-permute-done.28.refs_2_ = bf16[512,512]{1,0:T(8,128)(2,1)} collective-permute-done((bf16[512,512]{1,0:T(8,128)(2,1)}, bf16[512,512]{1,0:T(8,128)(2,1)}, u32[]{:S(2)}, u32[]{:S(2)}) %collective-permute-start.28) | collective-permute-done | bytes 524320 | tf_op jit(solution)/shard_map/ppermute | solution.py:14
  378.8 9.1 %collective-permute-done.31.refs_2_ = bf16[512,512]{1,0:T(8,128)(2,1)} collective-permute-done((bf16[512,512]{1,0:T(8,128)(2,1)}, bf16[512,512]{1,0:T(8,128)(2,1)}, u32[]{:S(2)}, u32[]{:S(2)}) %collective-permute-start.31) | collective-permute-done | bytes 524320 | tf_op jit(solution)/shard_map/ppermute | solution.py:14
  390.1 2.9 fusion.5.refs_1_
  393.0 6.1 %collective-permute-done.34.refs_2_ = bf16[512,512]{1,0:T(8,128)(2,1)} collective-permute-done((bf16[512,512]{1,0:T(8,128)(2,1)}, bf16[512,512]{1,0:T(8,128)(2,1)}, u32[]{:S(2)}, u32[]{:S(2)}) %collective-permute-start.34) | collective-permute-done | bytes 524320 | tf_op jit(solution)/shard_map/ppermute | solution.py:14
  (249 shorter events, 170.1 us)
Async XLA Ops:
  7.2 67.4 %all-gather.5.cloned.1.call-start = ((), (), s32[]{:S(2)}) async-start(), calls=%async_computation.1 | async-start | bytes 5242880 | tf_op jit(solution)/shard_map/all_gather | solution.py:81
  7.9 170.9 %all-gather.3.cloned.1.call-start = ((), (), s32[]{:S(2)}) async-start(), calls=%async_computation | async-start | bytes 5242880 | tf_op jit(solution)/shard_map/all_gather | solution.py:130
  15.7 28.2 %collective-permute-start.6 = (bf16[512,1024]{1,0:T(8,128)(2,1)}, bf16[512,1024]{1,0:T(8,128)(2,1)}, u32[]{:S(2)}, u32[]{:S(2)}) collective-permute-start(bf16[512,1024]{1,0:T(8,128)(2,1)} %param.13), channel_id=1, source_target_pairs={{1,8},{3,10},{5,12},{7,14},{8,1},{10,3},{12,5},{14,7},{17,24},{19,... | collective-permute-start | bytes 3145736 | tf_op jit(solution)/shard_map/ppermute | solution.py:114
  93.8 53.5 %collective-permute-start.14 = (bf16[512,512]{0,1:T(8,128)(2,1)S(1)}, bf16[512,512]{0,1:T(8,128)(2,1)S(1)}, u32[]{:S(2)}, u32[]{:S(2)}) collective-permute-start(bf16[512,512]{0,1:T(8,128)(2,1)S(1)} %get-tuple-element.42), channel_id=1, source_target_pairs={{0,8},{4,12},{8,0},{12,4},{16,24},{20,28},{24,16},{28,20},{1,9},{5... | collective-permute-start | bytes 1572872 | tf_op jit(solution)/shard_map/ppermute | solution.py:14
  97.0 86.2 %collective-permute-start.13 = (bf16[512,512]{0,1:T(8,128)(2,1)}, bf16[512,512]{0,1:T(8,128)(2,1)S(1)}, u32[]{:S(2)}, u32[]{:S(2)}) collective-permute-start(bf16[512,512]{0,1:T(8,128)(2,1)} %get-tuple-element.44), channel_id=1, source_target_pairs={{0,8},{4,12},{8,0},{12,4},{16,24},{20,28},{24,16},{28,20},{1,9},{5... | collective-permute-start | bytes 1572872 | tf_op jit(solution)/shard_map/ppermute | solution.py:14
  99.0 88.9 %collective-permute-start.4 = (bf16[512,512]{0,1:T(8,128)(2,1)}, bf16[512,512]{0,1:T(8,128)(2,1)S(1)}, u32[]{:S(2)}, u32[]{:S(2)}) collective-permute-start(bf16[512,512]{0,1:T(8,128)(2,1)} %get-tuple-element.45), channel_id=1, source_target_pairs={{0,8},{4,12},{8,0},{12,4},{16,24},{20,28},{24,16},{28,20},{1,9},{5... | collective-permute-start | bytes 1572872 | tf_op jit(solution)/shard_map/ppermute | solution.py:14
  105.6 40.0 %collective-permute-start.20 = (bf16[8,128,128]{2,1,0:T(8,128)(2,1)S(1)}, bf16[8,128,128]{2,1,0:T(8,128)(2,1)S(1)}, u32[]{:S(2)}, u32[]{:S(2)}) collective-permute-start(bf16[8,128,128]{2,1,0:T(8,128)(2,1)S(1)} %fusion.67), channel_id=1, source_target_pairs={{0,8},{4,12},{8,0},{12,4},{16,24},{20,28},{24,16},{28,20},{1,9},{5... | collective-permute-start | bytes 786440 | tf_op jit(solution)/shard_map/ppermute | solution.py:14
  108.4 56.5 %collective-permute-start.10 = (bf16[512,1024]{1,0:T(8,128)(2,1)S(1)}, bf16[512,1024]{1,0:T(8,128)(2,1)S(1)}, u32[]{:S(2)}, u32[]{:S(2)}) collective-permute-start(bf16[512,1024]{1,0:T(8,128)(2,1)S(1)} %add_convert_fusion.7), channel_id=1, source_target_pairs={{0,4},{4,0},{8,12},{12,8},{16,20},{20,16},{24,28},{28,24},{1,5},{5... | collective-permute-start | bytes 3145736 | tf_op jit(solution)/shard_map/ppermute | solution.py:14
  163.2 30.9 %collective-permute-start.32 = (bf16[512,512]{0,1:T(8,128)(2,1)}, bf16[512,512]{0,1:T(8,128)(2,1)}, u32[]{:S(2)}, u32[]{:S(2)}) collective-permute-start(bf16[512,512]{0,1:T(8,128)(2,1)} %get-tuple-element.38), channel_id=1, source_target_pairs={{0,8},{4,12},{8,0},{12,4},{16,24},{20,28},{24,16},{28,20},{1,9},{5... | collective-permute-start | bytes 1572872 | tf_op jit(solution)/shard_map/ppermute | solution.py:14
  164.8 36.1 %collective-permute-start.26 = (bf16[512,512]{0,1:T(8,128)(2,1)}, bf16[512,512]{0,1:T(8,128)(2,1)}, u32[]{:S(2)}, u32[]{:S(2)}) collective-permute-start(bf16[512,512]{0,1:T(8,128)(2,1)} %get-tuple-element.40), channel_id=1, source_target_pairs={{0,8},{4,12},{8,0},{12,4},{16,24},{20,28},{24,16},{28,20},{1,9},{5... | collective-permute-start | bytes 1572872 | tf_op jit(solution)/shard_map/ppermute | solution.py:14
  173.0 47.0 %collective-permute-start.22 = (bf16[512,512]{0,1:T(8,128)(2,1)}, bf16[512,512]{0,1:T(8,128)(2,1)}, u32[]{:S(2)}, u32[]{:S(2)}) collective-permute-start(bf16[512,512]{0,1:T(8,128)(2,1)} %get-tuple-element.41), channel_id=1, source_target_pairs={{0,8},{4,12},{8,0},{12,4},{16,24},{20,28},{24,16},{28,20},{1,9},{5... | collective-permute-start | bytes 1572872 | tf_op jit(solution)/shard_map/ppermute | solution.py:14
  183.5 46.7 %collective-permute-start.29 = (bf16[512,512]{0,1:T(8,128)(2,1)S(1)}, bf16[512,512]{0,1:T(8,128)(2,1)S(1)}, u32[]{:S(2)}, u32[]{:S(2)}) collective-permute-start(bf16[512,512]{0,1:T(8,128)(2,1)S(1)} %copy-done.43), channel_id=1, source_target_pairs={{0,8},{4,12},{8,0},{12,4},{16,24},{20,28},{24,16},{28,20},{1,9},{5... | collective-permute-start | bytes 1572872 | tf_op jit(solution)/shard_map/ppermute | solution.py:14
  188.1 45.3 %collective-permute-start.16 = (bf16[512,512]{1,0:T(8,128)(2,1)S(1)}, bf16[512,512]{1,0:T(8,128)(2,1)S(1)}, u32[]{:S(2)}, u32[]{:S(2)}) collective-permute-start(bf16[512,512]{1,0:T(8,128)(2,1)S(1)} %copy-done.42), channel_id=1, source_target_pairs={{0,16},{4,20},{8,24},{12,28},{16,0},{20,4},{24,8},{28,12},{1,17},{... | collective-permute-start | bytes 1572872 | tf_op jit(solution)/shard_map/ppermute | solution.py:14
  194.4 44.2 %collective-permute-start.23 = (bf16[512,512]{1,0:T(8,128)(2,1)S(1)}, bf16[512,512]{1,0:T(8,128)(2,1)S(1)}, u32[]{:S(2)}, u32[]{:S(2)}) collective-permute-start(bf16[512,512]{1,0:T(8,128)(2,1)S(1)} %copy-done.40), channel_id=1, source_target_pairs={{0,16},{4,20},{8,24},{12,28},{16,0},{20,4},{24,8},{28,12},{1,17},{... | collective-permute-start | bytes 1572872 | tf_op jit(solution)/shard_map/ppermute | solution.py:14
  200.9 36.8 %collective-permute-start.11 = (bf16[1024,512]{1,0:T(8,128)(2,1)S(1)}, bf16[1024,512]{1,0:T(8,128)(2,1)S(1)}, u32[]{:S(2)}, u32[]{:S(2)}) collective-permute-start(bf16[1024,512]{1,0:T(8,128)(2,1)S(1)} %add_convert_fusion.8), channel_id=1, source_target_pairs={{0,4},{4,0},{8,12},{12,8},{16,20},{20,16},{24,28},{28,24},{1,5},{5... | collective-permute-start | bytes 3145736 | tf_op jit(solution)/shard_map/ppermute | solution.py:14
  238.7 43.4 %collective-permute-start.24 = (bf16[1024,512]{1,0:T(8,128)(2,1)}, bf16[1024,512]{1,0:T(8,128)(2,1)}, u32[]{:S(2)}, u32[]{:S(2)}) collective-permute-start(bf16[1024,512]{1,0:T(8,128)(2,1)} %add_convert_fusion.4), channel_id=1, source_target_pairs={{0,4},{4,0},{8,12},{12,8},{16,20},{20,16},{24,28},{28,24},{1,5},{5... | collective-permute-start | bytes 3145736 | tf_op jit(solution)/shard_map/ppermute | solution.py:14
  262.5 42.4 %collective-permute-start.27 = (bf16[1024,512]{1,0:T(8,128)(2,1)}, bf16[1024,512]{1,0:T(8,128)(2,1)}, u32[]{:S(2)}, u32[]{:S(2)}) collective-permute-start(bf16[1024,512]{1,0:T(8,128)(2,1)} %add_convert_fusion.3), channel_id=1, source_target_pairs={{0,4},{4,0},{8,12},{12,8},{16,20},{20,16},{24,28},{28,24},{1,5},{5... | collective-permute-start | bytes 3145736 | tf_op jit(solution)/shard_map/ppermute | solution.py:14
  269.6 35.0 %collective-permute-start.18 = (bf16[512,512]{1,0:T(8,128)(2,1)}, bf16[512,512]{1,0:T(8,128)(2,1)S(1)}, u32[]{:S(2)}, u32[]{:S(2)}) collective-permute-start(bf16[512,512]{1,0:T(8,128)(2,1)} %fusion.21), channel_id=1, source_target_pairs={{0,16},{4,20},{8,24},{12,28},{16,0},{20,4},{24,8},{28,12},{1,17},{... | collective-permute-start | bytes 1572872 | tf_op jit(solution)/shard_map/ppermute | solution.py:14
  285.8 30.0 %collective-permute-start.25 = (bf16[512,512]{1,0:T(8,128)(2,1)S(1)}, bf16[512,512]{1,0:T(8,128)(2,1)S(1)}, u32[]{:S(2)}, u32[]{:S(2)}) collective-permute-start(bf16[512,512]{1,0:T(8,128)(2,1)S(1)} %fusion.22), channel_id=1, source_target_pairs={{0,16},{4,20},{8,24},{12,28},{16,0},{20,4},{24,8},{28,12},{1,17},{... | collective-permute-start | bytes 1572872 | tf_op jit(solution)/shard_map/ppermute | solution.py:14
  304.6 29.5 %collective-permute-start.30 = (bf16[1024,512]{1,0:T(8,128)(2,1)}, bf16[1024,512]{1,0:T(8,128)(2,1)}, u32[]{:S(2)}, u32[]{:S(2)}) collective-permute-start(bf16[1024,512]{1,0:T(8,128)(2,1)} %add_convert_fusion.1), channel_id=1, source_target_pairs={{0,4},{4,0},{8,12},{12,8},{16,20},{20,16},{24,28},{28,24},{1,5},{5... | collective-permute-start | bytes 3145736 | tf_op jit(solution)/shard_map/ppermute | solution.py:14
  316.6 35.8 %collective-permute-start.33 = (bf16[1024,512]{1,0:T(8,128)(2,1)}, bf16[1024,512]{1,0:T(8,128)(2,1)}, u32[]{:S(2)}, u32[]{:S(2)}) collective-permute-start(bf16[1024,512]{1,0:T(8,128)(2,1)} %add_convert_fusion), channel_id=1, source_target_pairs={{0,4},{4,0},{8,12},{12,8},{16,20},{20,16},{24,28},{28,24},{1,5},{5... | collective-permute-start | bytes 3145736 | tf_op jit(solution)/shard_map/ppermute | solution.py:14
  328.9 47.7 %collective-permute-start.28 = (bf16[512,512]{1,0:T(8,128)(2,1)}, bf16[512,512]{1,0:T(8,128)(2,1)}, u32[]{:S(2)}, u32[]{:S(2)}) collective-permute-start(bf16[512,512]{1,0:T(8,128)(2,1)} %fusion.23), channel_id=1, source_target_pairs={{0,16},{4,20},{8,24},{12,28},{16,0},{20,4},{24,8},{28,12},{1,17},{... | collective-permute-start | bytes 1572872 | tf_op jit(solution)/shard_map/ppermute | solution.py:14
  338.0 49.9 %collective-permute-start.31 = (bf16[512,512]{1,0:T(8,128)(2,1)}, bf16[512,512]{1,0:T(8,128)(2,1)}, u32[]{:S(2)}, u32[]{:S(2)}) collective-permute-start(bf16[512,512]{1,0:T(8,128)(2,1)} %fusion.24), channel_id=1, source_target_pairs={{0,16},{4,20},{8,24},{12,28},{16,0},{20,4},{24,8},{28,12},{1,17},{... | collective-permute-start | bytes 1572872 | tf_op jit(solution)/shard_map/ppermute | solution.py:14
  356.3 42.7 %collective-permute-start.34 = (bf16[512,512]{1,0:T(8,128)(2,1)}, bf16[512,512]{1,0:T(8,128)(2,1)}, u32[]{:S(2)}, u32[]{:S(2)}) collective-permute-start(bf16[512,512]{1,0:T(8,128)(2,1)} %fusion.25), channel_id=1, source_target_pairs={{0,16},{4,20},{8,24},{12,28},{16,0},{20,4},{24,8},{28,12},{1,17},{... | collective-permute-start | bytes 1572872 | tf_op jit(solution)/shard_map/ppermute | solution.py:14
  (62 other events, 533.1 us)
Sparse Core Ops, SparseCore 0:
  9.6 37.1 all-gather.4
  64.5 45.3 all-gather.2

commit v4 on v1

v4 whole, which is shorter than its diff:
```python
import functools

import jax
import jax.numpy as jnp
from jax import lax
from jax.experimental import pallas as pl
from jax.experimental.pallas import tpu as pltpu
from jax.sharding import PartitionSpec as P

HEAD_DIM = 128
F32 = jnp.float32
BF16 = jnp.bfloat16
PARAMS = pltpu.CompilerParams(vmem_limit_bytes=48 * 1024 * 1024)


def cost(flops, moved):
    return pl.CostEstimate(flops=int(flops), bytes_accessed=int(moved), transcendentals=0)


def after(array, *others):
    return lax.optimization_barrier((array, *others))[0]


def flip(array, bit):
    size = lax.axis_size("seq")
    return lax.ppermute(array, "seq", [(i, i ^ (1 << bit)) for i in range(size)])


def entering(block, low, reverse):
    size, position = lax.axis_size("seq"), lax.axis_index("seq")
    bits = size.bit_length() - 1
    total, before, passed = block, jnp.zeros_like(block), None
    for bit in range(bits):
        step = 1 << bit
        if bit < bits - 1:
            new = flip(low, bit)
            passed = new if bit == 1 or passed is None else passed
            new = new.astype(F32)
            mine = (position >> bit) & 1
            before = before + jnp.where(mine == (0 if reverse else 1), new, 0.0)
            total = total + new
            low = total.astype(BF16)
        else:
            pairs = [(i, i ^ step) for i in range(size) if bool(i & step) == reverse]
            before = before + lax.ppermute(low, "seq", pairs).astype(F32)
    return before.astype(BF16), passed


def mm(a, b):
    return lax.dot_general(a, b, (((1,), (0,)), ((), ())), preferred_element_type=F32)


def mm_t(a, b):
    return lax.dot_general(a, b, (((1,), (1,)), ((), ())), preferred_element_type=F32)


def t_mm(a, b):
    return lax.dot_general(a, b, (((0,), (0,)), ((), ())), preferred_element_type=F32)


def causal(a, b):
    half = a.shape[0] // 2
    rows = lax.broadcasted_iota(jnp.int32, (half, half), 0)
    cols = lax.broadcasted_iota(jnp.int32, (half, half), 1)
    lower = rows >= cols
    a0, a1, b0, b1 = a[:half], a[half:], b[:half], b[half:]
    first = jnp.where(lower, mm_t(a0, b0), 0.0).astype(BF16)
    cross = mm_t(a1, b0).astype(BF16)
    second = jnp.where(lower, mm_t(a1, b1), 0.0).astype(BF16)
    return first, cross, second


def lower_mm(tri, b):
    half = b.shape[0] // 2
    first, cross, second = tri
    return jnp.concatenate([mm(first, b[:half]), mm(cross, b[:half]) + mm(second, b[half:])], axis=0)


def upper_mm(tri, b):
    half = b.shape[0] // 2
    first, cross, second = tri
    return jnp.concatenate([t_mm(first, b[:half]) + t_mm(cross, b[half:]), t_mm(second, b[half:])], axis=0)


def head_slices(ref):
    return [slice(i * HEAD_DIM, (i + 1) * HEAD_DIM) for i in range(ref.shape[1] // HEAD_DIM)]


def state_kernel(k, v, out, low):
    for i, cols in enumerate(head_slices(k)):
        out[i] = t_mm(k[:, cols], v[:, cols])
        low[i] = out[i].astype(BF16)


def local_kernel(q, k, v, out):
    for cols in head_slices(q):
        out[:, cols] = lower_mm(causal(q[:, cols], k[:, cols]), v[:, cols])


def gated_kernel(local, q, state, gain, attention, gated):
    for i, cols in enumerate(head_slices(q)):
        value = local[:, cols] + mm(q[:, cols], state[i])
        attention[:, cols] = value
        rms = jnp.sqrt(jnp.mean(value * value, axis=-1, keepdims=True) + 1e-05)
        gated[:, cols] = (value / rms * gain[:, cols]).astype(BF16)


def pre_kernel(cot, weight, attention, q, gain, pre, out, low):
    gated_grad = mm_t(cot[...], weight[...])
    for i, cols in enumerate(head_slices(q)):
        value = attention[:, cols]
        rms = jnp.sqrt(jnp.mean(value * value, axis=-1, keepdims=True) + 1e-05)
        normed = value / rms
        scaled = gated_grad[:, cols] * gain[:, cols]
        inner = jnp.mean(scaled * normed, axis=-1, keepdims=True)
        grad = ((scaled - normed * inner) / rms).astype(BF16)
        pre[:, cols] = grad
        out[i] = t_mm(q[:, cols], grad)
        low[i] = out[i].astype(BF16)


def query_kernel(pre, q, k, v, state, query_grad, key_local, value_local):
    for i, cols in enumerate(head_slices(q)):
        grad, qh, kh, vh = pre[:, cols], q[:, cols], k[:, cols], v[:, cols]
        mixing = causal(grad, vh)
        query_grad[:, cols] = (lower_mm(mixing, kh) + mm_t(grad, state[i])).astype(BF16)
        key_local[:, cols] = upper_mm(mixing, qh)
        value_local[:, cols] = upper_mm(causal(qh, kh), grad)


def key_value_kernel(key_local, value_local, k, v, state, key_grad, value_grad):
    for i, cols in enumerate(head_slices(k)):
        key_grad[:, cols] = (key_local[:, cols] + mm_t(v[:, cols], state[i])).astype(BF16)
        value_grad[:, cols] = (value_local[:, cols] + mm(k[:, cols], state[i])).astype(BF16)


def by_heads(kernel, args, outs, flops):
    tokens = next(a.shape[0] for kind, a in args if kind == "rows")
    width = next(a.shape[1] for kind, a in args if kind == "rows")
    pair = 2 * HEAD_DIM
    count = width // pair

    def spec(kind, array=None):
        if kind == "rows":
            return pl.BlockSpec((tokens, pair), lambda i: (0, i))
        if kind == "heads":
            return pl.BlockSpec((2, HEAD_DIM, HEAD_DIM), lambda i: (i, 0, 0))
        if kind == "gain":
            return pl.BlockSpec((1, pair), lambda i: (0, i))
        if kind == "weight":
            return pl.BlockSpec((pair, array.shape[1]), lambda i: (i, 0))
        return pl.BlockSpec(array.shape, lambda i: (0, 0))

    shapes = {"rows": (tokens, width), "heads": (2 * count, HEAD_DIM, HEAD_DIM)}
    return pl.pallas_call(
        kernel,
        grid=(count,),
        in_specs=[spec(kind, a) for kind, a in args],
        out_specs=[spec(kind) for kind, _ in outs],
        out_shape=[jax.ShapeDtypeStruct(shapes[kind], dtype) for kind, dtype in outs],
        compiler_params=PARAMS,
        cost_estimate=cost(flops, sum(a.size * a.dtype.itemsize for _, a in args)),
    )(*[a for _, a in args])


def term_kernel(turned, adds, index, mine, theirs, grad, other, *rest):
    out = rest[-1]
    if turned:
        total = t_mm(grad[...], mine[...]) + t_mm(other[...], theirs[...])
    else:
        total = t_mm(mine[...], grad[...]) + t_mm(theirs[...], other[...])
    for ref in rest[:adds]:
        total = total + ref[...].astype(F32)
    out[...] = total.astype(out.dtype)


def term(features, grads, block, cols, turned, owned, start, count, received, target=None):
    mine, theirs, index = features
    grad, other = grads
    tokens, chunks = grad.shape[0], index.shape[0] // 2

    def tile(offset):
        if turned:
            return pl.BlockSpec((cols, owned), lambda r, ix: (0, r + offset))
        return pl.BlockSpec((owned, cols), lambda r, ix: (r + offset, 0))

    rows = pl.BlockSpec((tokens, cols), lambda r, ix: (0, block))
    in_specs = [
        pl.BlockSpec((tokens, owned), lambda r, ix: (0, ix[start + r])),
        pl.BlockSpec((tokens, owned), lambda r, ix: (0, ix[chunks + start + r])),
        rows,
        rows,
    ]
    in_specs += [tile(start - begun) for _, begun in received]
    operands = [index, mine, theirs, grad, other, *[a for a, _ in received]]
    aliases = {}
    if target is None:
        out_spec, dtype = tile(0), BF16
        shape = (cols, count * owned) if turned else (count * owned, cols)
    else:
        old, shape, place = target
        dtype = F32
        out_spec = pl.BlockSpec((None,) * (len(shape) - 2) + ((cols, owned) if turned else (owned, cols)), lambda r, ix: place)
        if old is not None:
            aliases = {len(operands): 0}
            operands.append(old)
            in_specs.append(pl.BlockSpec(memory_space=pl.ANY))
    return pl.pallas_call(
        functools.partial(term_kernel, turned, len(received)),
        grid_spec=pltpu.PrefetchScalarGridSpec(
            num_scalar_prefetch=1, grid=(count,), in_specs=in_specs, out_specs=out_spec
        ),
        out_shape=jax.ShapeDtypeStruct(shape, dtype),
        input_output_aliases=aliases,
        compiler_params=PARAMS,
        cost_estimate=cost(4 * tokens * cols * count * owned, 6 * tokens * count * owned),
    )(*operands)


def body(layer_input, query_rows, key_rows, value_rows, out_weight, norm_gain, cotangent):
    size, position = lax.axis_size("seq"), lax.axis_index("seq")
    head_size, head_place = lax.axis_size("head"), lax.axis_index("head")
    bits = size.bit_length() - 1
    gather_bit = 1
    halving = [bit for bit in range(bits) if bit != gather_bit]
    tokens, width = query_rows.shape
    model = out_weight.shape[1]
    owned = model // size
    work = tokens * width

    chunks = 1 << len(halving)
    order = []
    for j in range(chunks):
        toggled = 0
        for i, bit in enumerate(halving):
            if not (j >> (len(halving) - 1 - i)) & 1:
                toggled |= 1 << bit
        order.append(position ^ toggled)
    there = jnp.stack(order).astype(jnp.int32)
    packed = jnp.arange(chunks, dtype=jnp.int32)

    paired = head_size == 4 and width == 2 * owned
    aligned = (head_place & 1) == ((position >> 1) & 1)

    def across(array, seq_toggle, head_toggle):
        pairs = [
            (s * head_size + h, (s ^ seq_toggle) * head_size + (h ^ head_toggle))
            for s in range(size)
            for h in range(head_size)
            if (h ^ (s >> 1)) & 1
        ]
        return lax.ppermute(array, ("seq", "head"), pairs)

    def both(gathered):
        share = chunks * owned // head_size
        send = jnp.concatenate(
            [lax.dynamic_slice_in_dim(gathered, (at ^ (1 << gather_bit)) * owned, owned, 1) for at in order], axis=1
        )
        send = lax.dynamic_slice_in_dim(send, head_place * share, share, 1)
        theirs = lax.all_gather(flip(send, gather_bit), "head", axis=1, tiled=True)
        return gathered, theirs, jnp.concatenate([there, packed])

    gathered_cot = lax.all_gather(cotangent, "head", axis=1, tiled=True)
    gain = norm_gain.reshape(1, width)
    q, k, v = ("rows", query_rows), ("rows", key_rows), ("rows", value_rows)

    block_state, block_low = by_heads(
        state_kernel, [k, v], [("heads", F32), ("heads", BF16)], 2 * work * HEAD_DIM
    )
    if paired:
        same_cot = across(cotangent, 2, 1)
        other_cot = across(same_cot, 0, 2)
        near_cot, far_cot = across(same_cot, 0, 1), across(other_cot, 0, 1)
    (local,) = by_heads(
        local_kernel, [q, k, ("rows", after(value_rows, block_low))], [("rows", F32)], 3 * work * tokens
    )
    state_low, passed = entering(block_state, block_low, False)
    if paired:
        swapped = jnp.where(aligned, layer_input, across(after(layer_input, passed), 2, 1))
        gathered_input = lax.all_gather(swapped, "head", axis=1, tiled=True)
        both_input = gathered_input, gathered_input, jnp.concatenate([there, there ^ 2])
        near_cot = jnp.where(aligned, near_cot, same_cot)
        far_cot = jnp.where(aligned, far_cot, other_cot)

        def chosen(at):
            near, far = (lax.dynamic_slice_in_dim(a, (at & 1) * owned, owned, 1) for a in (near_cot, far_cot))
            return jnp.where((at >> 2) == (head_place >> 1), near, far)

        partner_cot = jnp.concatenate([chosen(at) for at in order], axis=1)
        both_cot = gathered_cot, partner_cot, jnp.concatenate([there, packed])
    else:
        both_cot = both(gathered_cot)
        both_input = both(lax.all_gather(after(layer_input, gathered_cot), "head", axis=1, tiled=True))

    attention, gated = by_heads(
        gated_kernel,
        [("rows", local), q, ("heads", state_low), ("gain", gain)],
        [("rows", F32), ("rows", BF16)],
        2 * work * HEAD_DIM,
    )
    half = width // 2
    gated_parts = [gated[:, :half], gated[:, half:]]
    gated_parts = [(part, flip(part, gather_bit)) for part in gated_parts]
    pre, grad_block, grad_block_low = by_heads(
        pre_kernel,
        [("whole", gathered_cot), ("weight", out_weight), ("rows", attention), q, ("gain", gain)],
        [("rows", BF16), ("heads", F32), ("heads", BF16)],
        2 * work * (model + HEAD_DIM),
    )
    grad_low, passed = entering(grad_block, grad_block_low, True)
    query_grad, key_local, value_local = by_heads(
        query_kernel,
        [("rows", pre), q, k, v, ("heads", state_low)],
        [("rows", BF16), ("rows", F32), ("rows", F32)],
        8 * work * tokens,
    )
    key_grad, value_grad = by_heads(
        key_value_kernel,
        [("rows", key_local), ("rows", value_local), k, v, ("heads", grad_low)],
        [("rows", BF16), ("rows", BF16)],
        4 * work * HEAD_DIM,
    )

    grads = [(grad, flip(after(grad, passed), gather_bit)) for grad in (query_grad, key_grad, value_grad)]
    pieces = [(both_cot, part, 0, True, (i, 0)) for i, part in enumerate(gated_parts)]
    pieces += [(both_input, pair, i, False, (n, 0, i)) for n, pair in enumerate(grads) for i in range(2)]
    starts = [chunks - (chunks >> i) for i in range(len(halving) + 1)]
    shapes = {True: (width, owned), False: (len(grads), owned, width)}
    targets = {True: None, False: None}
    received = [[] for _ in pieces]
    last = [gated]

    def stage(i, n):
        features, (grad, other), block, turned, place = pieces[i]
        other = after(other, last[0])
        came = received[i]
        if came:
            came[-1] = (after(came[-1][0], last[0]), came[-1][1])
        final = n == len(halving)
        target = (targets[turned], shapes[turned], place) if final else None
        count = 1 if final else chunks >> (n + 1)
        out = term(features, (grad, other), block, half, turned, owned, starts[n], count, came, target)
        last[0] = out
        if final:
            targets[turned] = out
        else:
            came.append((flip(out, halving[n]), starts[n + 1]))

    stages = len(halving) + 1
    for n in range(2):
        stage(n, 0)
    for i in range(len(pieces) + 1):
        for n in range(1, stages - 1):
            if i < len(pieces):
                stage(i, n)
        if i >= 1:
            stage(i - 1, stages - 1)
        if i + 2 < len(pieces):
            stage(i + 2, 0)
    return (targets[False].transpose(1, 0, 2), targets[True])


def solution(mesh):
    placed = (
        P("seq", "head"),
        P("seq", "head"),
        P("seq", "head"),
        P("seq", "head"),
        P("head", None),
        P("head"),
        P("seq", "head"),
    )
    return jax.shard_map(
        body,
        mesh=mesh,
        in_specs=placed,
        out_specs=(P("seq", None, "head"), P("head", "seq")),
        check_vma=False,
    )
```

time: 522 us -> 390 us (0.75)
  waiting for transfers between devices: 325 us -> 165 us
  Pallas kernels: 0 us -> 109 us
  matrix products: 68.7 us -> 0 us
  starting transfers between devices: 39.4 us -> 78.3 us
  other arithmetic: 47.4 us -> 11.6 us
  local copies, waits for them, and re-layouts: 21.2 us -> 9.32 us
    pallas_call x0 -> x30, Pallas kernels: none -> 109 us  [the longest x24 78.5 us: term(): pl.pallas_call(functools.partial(term_kernel, turned, len(received)), gri...]
    ppermute x30 -> x25, waiting for transfers between devices: 263 us -> 165 us  [flip(): return lax.ppermute(array, 'seq', [(i, i ^ 1 << bit) for i in range(size)])]
    dot_general x36 -> x0, matrix products: 60.4 us -> none  [the longest x24 43.3 us: tdot(): lax.dot_general(a, b, (((0,), (0,)), ((), ())), preferred_element_type=F32)]
    all_gather x3 -> x1, waiting for transfers between devices: 36.1 us -> 0.01 us  [body(): gathered_input = lax.all_gather(swapped, 'head', axis=1, tiled=True)]
    ppermute x30 -> x25, starting transfers between devices: 32.9 us -> 64.1 us  [flip(): return lax.ppermute(array, 'seq', [(i, i ^ 1 << bit) for i in range(size)])]
    concatenate x5 -> x1, other arithmetic: 26.6 us -> 0.29 us  [body(): partner_cot = jnp.concatenate([chosen(at) for at in order], axis=1)]
    ppermute x2 -> x7, waiting for transfers between devices: 12.8 us -> 0.02 us  [the longest x5 0.01 us: across(): return lax.ppermute(array, ('seq', 'head'), pairs)]
    slice x2 -> x0, other arithmetic: 12.6 us -> none  [term(): part = features[:, start * owned:(start + count) * owned]]
  transfers between devices with their start and end apart: 36 -> 34, of which waited for: 22 -> 15; matrix products, arithmetic and copies ran while one was open for 26% -> 3% of each run, Pallas kernels for 0% -> 27%
where the time goes in v4:
time: 390 us; the launch traced here: 388 us
  waiting for transfers between devices  165 us (42%)
  Pallas kernels  109 us (28%)
  starting transfers between devices  78.3 us (20%)
  between operations  14.5 us (4%)
  other arithmetic  11.6 us (3%)
  local copies, waits for them, and re-layouts  9.32 us (2%)
    ppermute x25, waiting for transfers between devices, flip(): return lax.ppermute(array, 'seq', [(i, i ^ 1 << bit) for i in range(size)])  165 us
    pallas_call x24, Pallas kernels, term(): pl.pallas_call(functools.partial(term_kernel, turned, len(received)), gri...  78.5 us
    ppermute x25, starting transfers between devices, flip(): return lax.ppermute(array, 'seq', [(i, i ^ 1 << bit) for i in range(size)])  64.1 us
    pallas_call x6, Pallas kernels, by_heads(): pl.pallas_call(kernel, grid=(count,), in_specs=[spec(kind, a) for kind, a...  30.7 us
    unnamed x62, local copies, waits for them, and re-layouts  8.24 us
  transfers between devices with their start and end apart: 34, of which 15 were waited for; matrix products, arithmetic and copies ran while one was open for 3% of the time, Pallas kernels for 27%

profile of v4, /device:TPU:0, one launch (start us, length us, event | category | flops | bytes accessed | tf_op | source)
XLA Modules:
  0.0 388.3 jit_solution(2182564405512160203)
XLA Ops:
  14.9 6.3 %collective-permute-done = bf16[8,128,128]{2,1,0:T(8,128)(2,1)S(1)} collective-permute-done((bf16[8,128,128]{2,1,0:T(8,128)(2,1)S(1)}, bf16[8,128,128]{2,1,0:T(8,128)(2,1)S(1)}, u32[]{:S(2)}, u32[]{:S(2)}) %collective-permute-start) | collective-permute-done | bytes 262176 | tf_op jit(solution)/shard_map/ppermute | solution.py:26
  23.1 5.8 %collective-permute-done.1 = bf16[8,128,128]{2,1,0:T(8,128)(2,1)} collective-permute-done((bf16[8,128,128]{2,1,0:T(8,128)(2,1)S(1)}, bf16[8,128,128]{2,1,0:T(8,128)(2,1)}, u32[]{:S(2)}, u32[]{:S(2)}) %collective-permute-start.1) | collective-permute-done | bytes 262176 | tf_op jit(solution)/shard_map/ppermute | solution.py:26
  38.1 5.1 %collective-permute-start.3 = (bf16[8,128,128]{2,1,0:T(8,128)(2,1)}, bf16[8,128,128]{2,1,0:T(8,128)(2,1)}, u32[]{:S(2)}, u32[]{:S(2)}) collective-permute-start(bf16[8,128,128]{2,1,0:T(8,128)(2,1)} %fusion.3), channel_id=1, source_target_pairs={{0,16},{4,20},{8,24},{12,28},{1,17},{5,21},{9,25},{13,29},{2,18},{... | collective-permute-start | bytes 786440 | tf_op jit(solution)/shard_map/ppermute | solution.py:45
  50.5 3.8 shard_map.88
  56.5 43.3 %collective-permute-start.15 = (bf16[512,512]{1,0:T(8,128)(2,1)S(1)}, bf16[512,512]{1,0:T(8,128)(2,1)S(1)}, u32[]{:S(2)}, u32[]{:S(2)}) collective-permute-start(bf16[512,512]{1,0:T(8,128)(2,1)S(1)} %get-tuple-element.120.grad), channel_id=1, source_target_pairs={{0,8},{4,12},{8,0},{12,4},{16,24},{20,28},{24,16},{28,20},{1,9},{5... | collective-permute-start | bytes 1572872 | tf_op jit(solution)/shard_map/ppermute | solution.py:26
  99.9 12.6 %collective-permute-done.15.other = bf16[512,512]{1,0:T(8,128)(2,1)S(1)} collective-permute-done((bf16[512,512]{1,0:T(8,128)(2,1)S(1)}, bf16[512,512]{1,0:T(8,128)(2,1)S(1)}, u32[]{:S(2)}, u32[]{:S(2)}) %collective-permute-start.15) | collective-permute-done | bytes 524320 | tf_op jit(solution)/shard_map/ppermute | solution.py:26
  116.6 10.2 %shard_map.89 = (bf16[512,1024]{1,0:T(8,128)(2,1)S(1)}, f32[8,128,128]{2,1,0:T(8,128)S(1)}, bf16[8,128,128]{2,1,0:T(8,128)(2,1)S(1)}) custom-call(bf16[512,4096]{1,0:T(8,128)(2,1)} %all-gather.5.cloned.1.call-done.cot.mine, bf16[1024,4096]{1,0:T(8,128)(2,1)} %weight.1, f32[512,1024]{1,0:T(8,128)S(1)} %copy-done.22, bf16[512,1024]{1,0:T(8,128)(2,1)S(1)} %copy-done.16, ...), custom_call_target="tpu_custom_call" | custom-call | flops 4429185024 | bytes 15732736 | tf_op jit(solution)/shard_map/pallas_call | solution.py:155
  128.6 6.7 %collective-permute-done.4 = bf16[8,128,128]{2,1,0:T(8,128)(2,1)S(1)} collective-permute-done((bf16[8,128,128]{2,1,0:T(8,128)(2,1)S(1)}, bf16[8,128,128]{2,1,0:T(8,128)(2,1)S(1)}, u32[]{:S(2)}, u32[]{:S(2)}) %collective-permute-start.4) | collective-permute-done | bytes 262176 | tf_op jit(solution)/shard_map/ppermute | solution.py:26
  138.9 3.9 %shard_map.92 = bf16[512,1024]{1,0:T(8,128)(2,1)} custom-call(s32[8]{0:T(128)S(1)} %concatenate.12.index, bf16[512,4096]{1,0:T(8,128)(2,1)} %all-gather.5.cloned.1.call-done.cot.mine, bf16[512,2048]{1,0:T(8,128)(2,1)S(1)} %pad_maximum_fusion.theirs, bf16[512,512]{1,0:T(8,128)(2,1)S(1)} %get-tuple-element.120.grad, ...), custom_call_target="tpu_custom_call" | custom-call | flops 1073741824 | bytes 3145728 | tf_op jit(solution)/shard_map/pallas_call | solution.py:208
  144.4 8.3 %shard_map.90 = (bf16[512,1024]{1,0:T(8,128)(2,1)S(1)}, f32[512,1024]{1,0:T(8,128)}, f32[512,1024]{1,0:T(8,128)}) custom-call(bf16[512,1024]{1,0:T(8,128)(2,1)S(1)} %get-tuple-element.64.pre, bf16[512,1024]{1,0:T(8,128)(2,1)S(1)} %copy-done.17, bf16[512,1024]{1,0:T(8,128)(2,1)S(1)} %copy-done.2, bf16[512,1024]{1,0:T(8,128)(2,1)S(1)} %copy-done.6, ...), custom_call_target="tpu_custom_call" | custom-call | flops 2147483648 | bytes 4456448 | tf_op jit(solution)/shard_map/pallas_call | solution.py:155
  153.1 4.3 %shard_map.93 = bf16[512,1024]{1,0:T(8,128)(2,1)} custom-call(s32[8]{0:T(128)S(1)} %concatenate.12.index, bf16[512,4096]{1,0:T(8,128)(2,1)} %all-gather.5.cloned.1.call-done.cot.mine, bf16[512,2048]{1,0:T(8,128)(2,1)S(1)} %pad_maximum_fusion.theirs, bf16[512,512]{1,0:T(8,128)(2,1)} %get-tuple-element.121.grad, bf16[512,512]{1,0:T(8,128)(2,1)} %collective-permute-done.14.other), custom_call_target="tpu_custom_call" | custom-call | flops 1073741824 | bytes 3145728 | tf_op jit(solution)/shard_map/pallas_call | solution.py:208
  161.4 7.9 %collective-permute-done.16.rest_0_ = bf16[512,1024]{1,0:T(8,128)(2,1)} collective-permute-done((bf16[512,1024]{1,0:T(8,128)(2,1)}, bf16[512,1024]{1,0:T(8,128)(2,1)}, u32[]{:S(2)}, u32[]{:S(2)}) %collective-permute-start.16) | collective-permute-done | bytes 1048608 | tf_op jit(solution)/shard_map/ppermute | solution.py:26
  177.1 9.2 %collective-permute-done.9.other = bf16[512,1024]{1,0:T(8,128)(2,1)} collective-permute-done((bf16[512,1024]{1,0:T(8,128)(2,1)S(1)}, bf16[512,1024]{1,0:T(8,128)(2,1)}, u32[]{:S(2)}, u32[]{:S(2)}) %collective-permute-start.9) | collective-permute-done | bytes 1048608 | tf_op jit(solution)/shard_map/ppermute | solution.py:26
  191.2 3.7 shard_map.91
  200.9 3.6 shard_map.97.rest_2_
  209.5 6.5 %collective-permute-done.19.rest_0_ = bf16[1024,512]{1,0:T(8,128)(2,1)S(1)} collective-permute-done((bf16[1024,512]{1,0:T(8,128)(2,1)S(1)}, bf16[1024,512]{1,0:T(8,128)(2,1)S(1)}, u32[]{:S(2)}, u32[]{:S(2)}) %collective-permute-start.19) | collective-permute-done | bytes 1048608 | tf_op jit(solution)/shard_map/ppermute | solution.py:26
  219.2 28.4 %collective-permute-done.20.rest_1_ = bf16[512,512]{1,0:T(8,128)(2,1)S(1)} collective-permute-done((bf16[512,512]{1,0:T(8,128)(2,1)S(1)}, bf16[512,512]{1,0:T(8,128)(2,1)S(1)}, u32[]{:S(2)}, u32[]{:S(2)}) %collective-permute-start.20) | collective-permute-done | bytes 524320 | tf_op jit(solution)/shard_map/ppermute | solution.py:26
  247.6 3.8 shard_map.100
  266.5 14.0 %collective-permute-done.23.rest_0_ = bf16[1024,512]{1,0:T(8,128)(2,1)S(1)} collective-permute-done((bf16[1024,512]{1,0:T(8,128)(2,1)S(1)}, bf16[1024,512]{1,0:T(8,128)(2,1)S(1)}, u32[]{:S(2)}, u32[]{:S(2)}) %collective-permute-start.23) | collective-permute-done | bytes 1048608 | tf_op jit(solution)/shard_map/ppermute | solution.py:26
  283.1 16.0 %collective-permute-done.24.rest_1_ = bf16[512,512]{1,0:T(8,128)(2,1)S(1)} collective-permute-done((bf16[512,512]{1,0:T(8,128)(2,1)S(1)}, bf16[512,512]{1,0:T(8,128)(2,1)S(1)}, u32[]{:S(2)}, u32[]{:S(2)}) %collective-permute-start.24) | collective-permute-done | bytes 524320 | tf_op jit(solution)/shard_map/ppermute | solution.py:26
  317.6 13.7 %collective-permute-done.27.rest_0_ = bf16[1024,512]{1,0:T(8,128)(2,1)S(1)} collective-permute-done((bf16[1024,512]{1,0:T(8,128)(2,1)S(1)}, bf16[1024,512]{1,0:T(8,128)(2,1)S(1)}, u32[]{:S(2)}, u32[]{:S(2)}) %collective-permute-start.27) | collective-permute-done | bytes 1048608 | tf_op jit(solution)/shard_map/ppermute | solution.py:26
  333.9 10.5 %collective-permute-done.28.rest_1_ = bf16[512,512]{1,0:T(8,128)(2,1)S(1)} collective-permute-done((bf16[512,512]{1,0:T(8,128)(2,1)S(1)}, bf16[512,512]{1,0:T(8,128)(2,1)S(1)}, u32[]{:S(2)}, u32[]{:S(2)}) %collective-permute-start.28) | collective-permute-done | bytes 524320 | tf_op jit(solution)/shard_map/ppermute | solution.py:26
  350.5 16.4 %collective-permute-done.30.rest_1_ = bf16[512,512]{1,0:T(8,128)(2,1)S(1)} collective-permute-done((bf16[512,512]{1,0:T(8,128)(2,1)S(1)}, bf16[512,512]{1,0:T(8,128)(2,1)S(1)}, u32[]{:S(2)}, u32[]{:S(2)}) %collective-permute-start.30) | collective-permute-done | bytes 524320 | tf_op jit(solution)/shard_map/ppermute | solution.py:26
  370.3 7.7 %collective-permute-done.31.rest_1_ = bf16[512,512]{1,0:T(8,128)(2,1)S(1)} collective-permute-done((bf16[512,512]{1,0:T(8,128)(2,1)S(1)}, bf16[512,512]{1,0:T(8,128)(2,1)S(1)}, u32[]{:S(2)}, u32[]{:S(2)}) %collective-permute-start.31) | collective-permute-done | bytes 524320 | tf_op jit(solution)/shard_map/ppermute | solution.py:26
  (154 shorter events, 122.3 us)
Async XLA Ops:
  7.2 107.8 %all-gather.5.cloned.1.call-start = ((), (), s32[]{:S(2)}) async-start(), calls=%async_computation.1 | async-start | bytes 5242880 | tf_op jit(solution)/shard_map/all_gather | solution.py:263
  7.9 178.4 %all-gather.3.cloned.1.call-start = ((), (), s32[]{:S(2)}) async-start(), calls=%async_computation | async-start | bytes 5242880 | tf_op jit(solution)/shard_map/all_gather | solution.py:280
  47.9 64.5 %collective-permute-start.11 = (bf16[512,1024]{1,0:T(8,128)(2,1)}, bf16[512,1024]{1,0:T(8,128)(2,1)S(1)}, u32[]{:S(2)}, u32[]{:S(2)}) collective-permute-start(bf16[512,1024]{1,0:T(8,128)(2,1)} %collective-permute-done.10), channel_id=1, source_target_pairs={{1,0},{3,2},{5,4},{7,6},{8,9},{10,11},{12,13},{14,15},{17,16},{19,... | collective-permute-start | bytes 3145736 | tf_op jit(solution)/shard_map/ppermute | solution.py:252
  54.3 58.4 %collective-permute-start.13 = (bf16[512,1024]{1,0:T(8,128)(2,1)}, bf16[512,1024]{1,0:T(8,128)(2,1)S(1)}, u32[]{:S(2)}, u32[]{:S(2)}) collective-permute-start(bf16[512,1024]{1,0:T(8,128)(2,1)} %collective-permute-done.12), channel_id=1, source_target_pairs={{1,0},{3,2},{5,4},{7,6},{8,9},{10,11},{12,13},{14,15},{17,16},{19,... | collective-permute-start | bytes 3145736 | tf_op jit(solution)/shard_map/ppermute | solution.py:252
  56.5 56.0 %collective-permute-start.15 = (bf16[512,512]{1,0:T(8,128)(2,1)S(1)}, bf16[512,512]{1,0:T(8,128)(2,1)S(1)}, u32[]{:S(2)}, u32[]{:S(2)}) collective-permute-start(bf16[512,512]{1,0:T(8,128)(2,1)S(1)} %get-tuple-element.120.grad), channel_id=1, source_target_pairs={{0,8},{4,12},{8,0},{12,4},{16,24},{20,28},{24,16},{28,20},{1,9},{5... | collective-permute-start | bytes 1572872 | tf_op jit(solution)/shard_map/ppermute | solution.py:26
  99.8 53.2 %collective-permute-start.14 = (bf16[512,512]{1,0:T(8,128)(2,1)}, bf16[512,512]{1,0:T(8,128)(2,1)}, u32[]{:S(2)}, u32[]{:S(2)}) collective-permute-start(bf16[512,512]{1,0:T(8,128)(2,1)} %get-tuple-element.121.grad), channel_id=1, source_target_pairs={{0,8},{4,12},{8,0},{12,4},{16,24},{20,28},{24,16},{28,20},{1,9},{5... | collective-permute-start | bytes 1572872 | tf_op jit(solution)/shard_map/ppermute | solution.py:26
  142.9 26.4 %collective-permute-start.16 = (bf16[512,1024]{1,0:T(8,128)(2,1)}, bf16[512,1024]{1,0:T(8,128)(2,1)}, u32[]{:S(2)}, u32[]{:S(2)}) collective-permute-start(bf16[512,1024]{1,0:T(8,128)(2,1)} %shard_map.92), channel_id=1, source_target_pairs={{0,4},{4,0},{8,12},{12,8},{16,20},{20,16},{24,28},{28,24},{1,5},{5... | collective-permute-start | bytes 3145736 | tf_op jit(solution)/shard_map/ppermute | solution.py:26
  152.7 33.6 %collective-permute-start.9 = (bf16[512,1024]{1,0:T(8,128)(2,1)S(1)}, bf16[512,1024]{1,0:T(8,128)(2,1)}, u32[]{:S(2)}, u32[]{:S(2)}) collective-permute-start(bf16[512,1024]{1,0:T(8,128)(2,1)S(1)} %get-tuple-element.74.grad), channel_id=1, source_target_pairs={{0,8},{4,12},{8,0},{12,4},{16,24},{20,28},{24,16},{28,20},{1,9},{5... | collective-permute-start | bytes 3145736 | tf_op jit(solution)/shard_map/ppermute | solution.py:26
  157.3 37.6 %collective-permute-start.17 = (bf16[512,1024]{1,0:T(8,128)(2,1)}, bf16[512,1024]{1,0:T(8,128)(2,1)}, u32[]{:S(2)}, u32[]{:S(2)}) collective-permute-start(bf16[512,1024]{1,0:T(8,128)(2,1)} %shard_map.93), channel_id=1, source_target_pairs={{0,4},{4,0},{8,12},{12,8},{16,20},{20,16},{24,28},{28,24},{1,5},{5... | collective-permute-start | bytes 3145736 | tf_op jit(solution)/shard_map/ppermute | solution.py:26
  159.7 30.1 %collective-permute-start.6 = (bf16[8,128,128]{2,1,0:T(8,128)(2,1)}, bf16[8,128,128]{2,1,0:T(8,128)(2,1)}, u32[]{:S(2)}, u32[]{:S(2)}) collective-permute-start(bf16[8,128,128]{2,1,0:T(8,128)(2,1)} %fusion.7), channel_id=1, source_target_pairs={{16,0},{20,4},{24,8},{28,12},{17,1},{21,5},{25,9},{29,13},{18,2},{... | collective-permute-start | bytes 786440 | tf_op jit(solution)/shard_map/ppermute | solution.py:45
  174.7 26.2 %collective-permute-start.18 = (bf16[512,512]{1,0:T(8,128)(2,1)}, bf16[512,512]{1,0:T(8,128)(2,1)}, u32[]{:S(2)}, u32[]{:S(2)}) collective-permute-start(bf16[512,512]{1,0:T(8,128)(2,1)} %shard_map.94), channel_id=1, source_target_pairs={{0,16},{4,20},{8,24},{12,28},{16,0},{20,4},{24,8},{28,12},{1,17},{... | collective-permute-start | bytes 1572872 | tf_op jit(solution)/shard_map/ppermute | solution.py:26
  189.8 26.2 %collective-permute-start.19 = (bf16[1024,512]{1,0:T(8,128)(2,1)S(1)}, bf16[1024,512]{1,0:T(8,128)(2,1)S(1)}, u32[]{:S(2)}, u32[]{:S(2)}) collective-permute-start(bf16[1024,512]{1,0:T(8,128)(2,1)S(1)} %shard_map.95), channel_id=1, source_target_pairs={{0,4},{4,0},{8,12},{12,8},{16,20},{20,16},{24,28},{28,24},{1,5},{5... | collective-permute-start | bytes 3145736 | tf_op jit(solution)/shard_map/ppermute | solution.py:26
  194.9 56.5 %collective-permute-start.8 = (bf16[512,1024]{1,0:T(8,128)(2,1)S(1)}, bf16[512,1024]{1,0:T(8,128)(2,1)S(1)}, u32[]{:S(2)}, u32[]{:S(2)}) collective-permute-start(bf16[512,1024]{1,0:T(8,128)(2,1)S(1)} %get-tuple-element.72.grad), channel_id=1, source_target_pairs={{0,8},{4,12},{8,0},{12,4},{16,24},{20,28},{24,16},{28,20},{1,9},{5... | collective-permute-start | bytes 3145736 | tf_op jit(solution)/shard_map/ppermute | solution.py:26
  208.0 47.4 %collective-permute-start.21 = (bf16[1024,512]{1,0:T(8,128)(2,1)S(1)}, bf16[1024,512]{1,0:T(8,128)(2,1)S(1)}, u32[]{:S(2)}, u32[]{:S(2)}) collective-permute-start(bf16[1024,512]{1,0:T(8,128)(2,1)S(1)} %shard_map.98), channel_id=1, source_target_pairs={{0,4},{4,0},{8,12},{12,8},{16,20},{20,16},{24,28},{28,24},{1,5},{5... | collective-permute-start | bytes 3145736 | tf_op jit(solution)/shard_map/ppermute | solution.py:26
  209.5 38.1 %collective-permute-start.20 = (bf16[512,512]{1,0:T(8,128)(2,1)S(1)}, bf16[512,512]{1,0:T(8,128)(2,1)S(1)}, u32[]{:S(2)}, u32[]{:S(2)}) collective-permute-start(bf16[512,512]{1,0:T(8,128)(2,1)S(1)} %shard_map.96), channel_id=1, source_target_pairs={{0,16},{4,20},{8,24},{12,28},{16,0},{20,4},{24,8},{28,12},{1,17},{... | collective-permute-start | bytes 1572872 | tf_op jit(solution)/shard_map/ppermute | solution.py:26
  218.6 39.4 %collective-permute-start.22 = (bf16[512,512]{1,0:T(8,128)(2,1)S(1)}, bf16[512,512]{1,0:T(8,128)(2,1)S(1)}, u32[]{:S(2)}, u32[]{:S(2)}) collective-permute-start(bf16[512,512]{1,0:T(8,128)(2,1)S(1)} %shard_map.99), channel_id=1, source_target_pairs={{0,16},{4,20},{8,24},{12,28},{16,0},{20,4},{24,8},{28,12},{1,17},{... | collective-permute-start | bytes 1572872 | tf_op jit(solution)/shard_map/ppermute | solution.py:26
  255.4 47.3 %collective-permute-start.7 = (bf16[512,1024]{1,0:T(8,128)(2,1)S(1)}, bf16[512,1024]{1,0:T(8,128)(2,1)S(1)}, u32[]{:S(2)}, u32[]{:S(2)}) collective-permute-start(bf16[512,1024]{1,0:T(8,128)(2,1)S(1)} %get-tuple-element.70.grad), channel_id=1, source_target_pairs={{0,8},{4,12},{8,0},{12,4},{16,24},{20,28},{24,16},{28,20},{1,9},{5... | collective-permute-start | bytes 3145736 | tf_op jit(solution)/shard_map/ppermute | solution.py:26
  265.0 41.9 %collective-permute-start.25 = (bf16[1024,512]{1,0:T(8,128)(2,1)S(1)}, bf16[1024,512]{1,0:T(8,128)(2,1)S(1)}, u32[]{:S(2)}, u32[]{:S(2)}) collective-permute-start(bf16[1024,512]{1,0:T(8,128)(2,1)S(1)} %shard_map.104), channel_id=1, source_target_pairs={{0,4},{4,0},{8,12},{12,8},{16,20},{20,16},{24,28},{28,24},{1,5},{5... | collective-permute-start | bytes 3145736 | tf_op jit(solution)/shard_map/ppermute | solution.py:26
  266.5 32.6 %collective-permute-start.24 = (bf16[512,512]{1,0:T(8,128)(2,1)S(1)}, bf16[512,512]{1,0:T(8,128)(2,1)S(1)}, u32[]{:S(2)}, u32[]{:S(2)}) collective-permute-start(bf16[512,512]{1,0:T(8,128)(2,1)S(1)} %shard_map.102), channel_id=1, source_target_pairs={{0,16},{4,20},{8,24},{12,28},{16,0},{20,4},{24,8},{28,12},{1,17},{... | collective-permute-start | bytes 1572872 | tf_op jit(solution)/shard_map/ppermute | solution.py:26
  283.0 26.4 %collective-permute-start.26 = (bf16[512,512]{1,0:T(8,128)(2,1)S(1)}, bf16[512,512]{1,0:T(8,128)(2,1)S(1)}, u32[]{:S(2)}, u32[]{:S(2)}) collective-permute-start(bf16[512,512]{1,0:T(8,128)(2,1)S(1)} %shard_map.105), channel_id=1, source_target_pairs={{0,16},{4,20},{8,24},{12,28},{16,0},{20,4},{24,8},{28,12},{1,17},{... | collective-permute-start | bytes 1572872 | tf_op jit(solution)/shard_map/ppermute | solution.py:26
  316.4 31.5 %collective-permute-start.29 = (bf16[1024,512]{1,0:T(8,128)(2,1)S(1)}, bf16[1024,512]{1,0:T(8,128)(2,1)S(1)}, u32[]{:S(2)}, u32[]{:S(2)}) collective-permute-start(bf16[1024,512]{1,0:T(8,128)(2,1)S(1)} %shard_map.110), channel_id=1, source_target_pairs={{0,4},{4,0},{8,12},{12,8},{16,20},{20,16},{24,28},{28,24},{1,5},{5... | collective-permute-start | bytes 3145736 | tf_op jit(solution)/shard_map/ppermute | solution.py:26
  317.6 26.8 %collective-permute-start.28 = (bf16[512,512]{1,0:T(8,128)(2,1)S(1)}, bf16[512,512]{1,0:T(8,128)(2,1)S(1)}, u32[]{:S(2)}, u32[]{:S(2)}) collective-permute-start(bf16[512,512]{1,0:T(8,128)(2,1)S(1)} %shard_map.108), channel_id=1, source_target_pairs={{0,16},{4,20},{8,24},{12,28},{16,0},{20,4},{24,8},{28,12},{1,17},{... | collective-permute-start | bytes 1572872 | tf_op jit(solution)/shard_map/ppermute | solution.py:26
  333.8 33.1 %collective-permute-start.30 = (bf16[512,512]{1,0:T(8,128)(2,1)S(1)}, bf16[512,512]{1,0:T(8,128)(2,1)S(1)}, u32[]{:S(2)}, u32[]{:S(2)}) collective-permute-start(bf16[512,512]{1,0:T(8,128)(2,1)S(1)} %shard_map.111), channel_id=1, source_target_pairs={{0,16},{4,20},{8,24},{12,28},{16,0},{20,4},{24,8},{28,12},{1,17},{... | collective-permute-start | bytes 1572872 | tf_op jit(solution)/shard_map/ppermute | solution.py:26
  350.4 27.7 %collective-permute-start.31 = (bf16[512,512]{1,0:T(8,128)(2,1)S(1)}, bf16[512,512]{1,0:T(8,128)(2,1)S(1)}, u32[]{:S(2)}, u32[]{:S(2)}) collective-permute-start(bf16[512,512]{1,0:T(8,128)(2,1)S(1)} %shard_map.113), channel_id=1, source_target_pairs={{0,16},{4,20},{8,24},{12,28},{16,0},{20,4},{24,8},{28,12},{1,17},{... | collective-permute-start | bytes 1572872 | tf_op jit(solution)/shard_map/ppermute | solution.py:26
  (41 other events, 512.1 us)
Sparse Core Ops, SparseCore 0:
  9.6 37.1 all-gather.4
  48.3 45.6 all-gather.2

commit v5 on v4

--- a/solution.py
+++ b/solution.py
@@ -26,14 +26,14 @@
     return lax.ppermute(array, "seq", [(i, i ^ (1 << bit)) for i in range(size)])
 
 
-def entering(block, low, reverse):
+def entering(block, low, reverse, first=()):
     size, position = lax.axis_size("seq"), lax.axis_index("seq")
     bits = size.bit_length() - 1
     total, before, passed = block, jnp.zeros_like(block), None
     for bit in range(bits):
         step = 1 << bit
         if bit < bits - 1:
-            new = flip(low, bit)
+            new = flip(after(low, *first) if bit == 1 and first else low, bit)
             passed = new if bit == 1 or passed is None else passed
             new = new.astype(F32)
             mine = (position >> bit) & 1
@@ -42,8 +42,8 @@
             low = total.astype(BF16)
         else:
             pairs = [(i, i ^ step) for i in range(size) if bool(i & step) == reverse]
-            before = before + lax.ppermute(low, "seq", pairs).astype(F32)
-    return before.astype(BF16), passed
+            new = lax.ppermute(low, "seq", pairs)
+    return (before, new), passed, low
 
 
 def mm(a, b):
@@ -270,15 +270,29 @@
     if paired:
         same_cot = across(cotangent, 2, 1)
         other_cot = across(same_cot, 0, 2)
-        near_cot, far_cot = across(same_cot, 0, 1), across(other_cot, 0, 1)
+        near_cot = across(same_cot, 0, 1)
+    state_parts, passed, last_low = entering(block_state, block_low, False, (same_cot,) if paired else ())
     (local,) = by_heads(
-        local_kernel, [q, k, ("rows", after(value_rows, block_low))], [("rows", F32)], 3 * work * tokens
-    )
-    state_low, passed = entering(block_state, block_low, False)
+        local_kernel, [q, k, ("rows", after(value_rows, last_low))], [("rows", F32)], 3 * work * tokens
+    )
+    state_low = (state_parts[0] + after(state_parts[1], local).astype(F32)).astype(BF16)
     if paired:
-        swapped = jnp.where(aligned, layer_input, across(after(layer_input, passed), 2, 1))
+        swapped = across(after(layer_input, passed), 2, 1)
+        swapped = jnp.where(aligned, layer_input, after(swapped, state_low))
         gathered_input = lax.all_gather(swapped, "head", axis=1, tiled=True)
         both_input = gathered_input, gathered_input, jnp.concatenate([there, there ^ 2])
+        other_cot = after(other_cot, state_low)
+        far_cot = across(other_cot, 0, 1)
+    attention, gated = by_heads(
+        gated_kernel,
+        [("rows", local), q, ("heads", state_low), ("gain", gain)],
+        [("rows", F32), ("rows", BF16)],
+        2 * work * HEAD_DIM,
+    )
+    if paired:
+        near_cot, far_cot, same_cot, other_cot = lax.optimization_barrier(
+            (near_cot, far_cot, same_cot, other_cot, gated)
+        )[:4]
         near_cot = jnp.where(aligned, near_cot, same_cot)
         far_cot = jnp.where(aligned, far_cot, other_cot)
 
@@ -292,69 +306,73 @@
         both_cot = both(gathered_cot)
         both_input = both(lax.all_gather(after(layer_input, gathered_cot), "head", axis=1, tiled=True))
 
-    attention, gated = by_heads(
-        gated_kernel,
-        [("rows", local), q, ("heads", state_low), ("gain", gain)],
-        [("rows", F32), ("rows", BF16)],
-        2 * work * HEAD_DIM,
-    )
     half = width // 2
-    gated_parts = [gated[:, :half], gated[:, half:]]
-    gated_parts = [(part, flip(part, gather_bit)) for part in gated_parts]
+    quarter = half // 2
+    pieces = []
+    for begin, count in ((0, quarter), (quarter, quarter), (half, half)):
+        part = gated[:, begin : begin + count]
+        pieces.append((both_cot, (part, flip(part, gather_bit)), count, 0, True, (begin // count, 0)))
+    starts = [chunks - (chunks >> i) for i in range(len(halving) + 1)]
+    shapes = {True: (width, owned), False: (3, owned, width)}
+    targets = {True: None, False: None}
+    received = {}
+    last = [gated]
+
+    def add_pieces(n, grad, *others):
+        pair = grad, flip(after(grad, *others), gather_bit)
+        pieces.extend((both_input, pair, half, i, False, (n, 0, i)) for i in range(2))
+
+    def stage(i, n):
+        features, (grad, other), cols, block, turned, place = pieces[i]
+        other = after(other, last[0])
+        came = received.setdefault(i, [])
+        if came:
+            came[-1] = (after(came[-1][0], last[0]), came[-1][1])
+        final = n == len(halving)
+        target = (targets[turned], shapes[turned], place) if final else None
+        count = 1 if final else chunks >> (n + 1)
+        out = term(features, (grad, other), block, cols, turned, owned, starts[n], count, came, target)
+        last[0] = out
+        if final:
+            targets[turned] = out
+        else:
+            came.append((flip(out, halving[n]), starts[n + 1]))
+
+    stage(0, 0)
     pre, grad_block, grad_block_low = by_heads(
         pre_kernel,
-        [("whole", gathered_cot), ("weight", out_weight), ("rows", attention), q, ("gain", gain)],
+        [("whole", gathered_cot), ("weight", out_weight), ("rows", after(attention, last[0])), q, ("gain", gain)],
         [("rows", BF16), ("heads", F32), ("heads", BF16)],
         2 * work * (model + HEAD_DIM),
     )
-    grad_low, passed = entering(grad_block, grad_block_low, True)
+    grad_parts, passed, last_low = entering(grad_block, grad_block_low, True)
+    last[0] = pre
+    stage(1, 0)
     query_grad, key_local, value_local = by_heads(
         query_kernel,
-        [("rows", pre), q, k, v, ("heads", state_low)],
+        [("rows", after(pre, last[0])), q, k, v, ("heads", state_low)],
         [("rows", BF16), ("rows", F32), ("rows", F32)],
         8 * work * tokens,
     )
+    add_pieces(0, query_grad, passed)
+    last[0] = query_grad
+    grad_low = (grad_parts[0] + grad_parts[1].astype(F32)).astype(BF16)
     key_grad, value_grad = by_heads(
         key_value_kernel,
         [("rows", key_local), ("rows", value_local), k, v, ("heads", grad_low)],
         [("rows", BF16), ("rows", BF16)],
         4 * work * HEAD_DIM,
     )
-
-    grads = [(grad, flip(after(grad, passed), gather_bit)) for grad in (query_grad, key_grad, value_grad)]
-    pieces = [(both_cot, part, 0, True, (i, 0)) for i, part in enumerate(gated_parts)]
-    pieces += [(both_input, pair, i, False, (n, 0, i)) for n, pair in enumerate(grads) for i in range(2)]
-    starts = [chunks - (chunks >> i) for i in range(len(halving) + 1)]
-    shapes = {True: (width, owned), False: (len(grads), owned, width)}
-    targets = {True: None, False: None}
-    received = [[] for _ in pieces]
-    last = [gated]
-
-    def stage(i, n):
-        features, (grad, other), block, turned, place = pieces[i]
-        other = after(other, last[0])
-        came = received[i]
-        if came:
-            came[-1] = (after(came[-1][0], last[0]), came[-1][1])
-        final = n == len(halving)
-        target = (targets[turned], shapes[turned], place) if final else None
-        count = 1 if final else chunks >> (n + 1)
-        out = term(features, (grad, other), block, half, turned, owned, starts[n], count, came, target)
-        last[0] = out
-        if final:
-            targets[turned] = out
-        else:
-            came.append((flip(out, halving[n]), starts[n + 1]))
+    add_pieces(1, key_grad)
+    add_pieces(2, value_grad)
 
     stages = len(halving) + 1
-    for n in range(2):
-        stage(n, 0)
-    for i in range(len(pieces) + 1):
+    for i in range(len(pieces) + 2):
         for n in range(1, stages - 1):
             if i < len(pieces):
                 stage(i, n)
-        if i >= 1:
-            stage(i - 1, stages - 1)
+        if i >= 2:
+            stage(i - 2, stages - 1)
         if i + 2 < len(pieces):
             stage(i + 2, 0)
     return (targets[False].transpose(1, 0, 2), targets[True])

time: 390 us -> 419 us (1.074)
  starting transfers between devices: 78.3 us -> 101 us
  Pallas kernels: 109 us -> 117 us
    ppermute x25 -> x28, starting transfers between devices: 64.1 us -> 88 us  [flip(): return lax.ppermute(array, 'seq', [(i, i ^ 1 << bit) for i in range(size)])]
    pallas_call x24 -> x27, Pallas kernels: 78.5 us -> 86.1 us  [term(): pl.pallas_call(functools.partial(term_kernel, turned, len(received)), gri...]
    ppermute x25 -> x28, waiting for transfers between devices: 165 us -> 165 us  [flip(): return lax.ppermute(array, 'seq', [(i, i ^ 1 << bit) for i in range(size)])]
  transfers between devices with their start and end apart: 34 -> 37, of which waited for: 15 -> 16; matrix products, arithmetic and copies ran while one was open for 3% -> 2% of each run, Pallas kernels for 27% -> 27%
where the time goes in v5:
time: 419 us; the launch traced here: 418 us
  waiting for transfers between devices  168 us (40%)
  Pallas kernels  117 us (28%)
  starting transfers between devices  101 us (24%)
  between operations  14.7 us (4%)
  other arithmetic  8.39 us (2%)
  local copies, waits for them, and re-layouts  8.3 us (2%)
    ppermute x28, waiting for transfers between devices, flip(): return lax.ppermute(array, 'seq', [(i, i ^ 1 << bit) for i in range(size)])  165 us
    ppermute x28, starting transfers between devices, flip(): return lax.ppermute(array, 'seq', [(i, i ^ 1 << bit) for i in range(size)])  88 us
    pallas_call x27, Pallas kernels, term(): pl.pallas_call(functools.partial(term_kernel, turned, len(received)), gri...  86.1 us
    pallas_call x6, Pallas kernels, by_heads(): pl.pallas_call(kernel, grid=(count,), in_specs=[spec(kind, a) for kind, a...  31.3 us
  transfers between devices with their start and end apart: 37, of which 16 were waited for; matrix products, arithmetic and copies ran while one was open for 2% of the time, Pallas kernels for 27%

profile of v5, /device:TPU:0, one launch (start us, length us, event | category | flops | bytes accessed | tf_op | source)
XLA Modules:
  0.0 417.7 jit_solution(4213104797482423136)
XLA Ops:
  15.6 4.7 %collective-permute-done = bf16[8,128,128]{2,1,0:T(8,128)(2,1)S(1)} collective-permute-done((bf16[8,128,128]{2,1,0:T(8,128)(2,1)S(1)}, bf16[8,128,128]{2,1,0:T(8,128)(2,1)S(1)}, u32[]{:S(2)}, u32[]{:S(2)}) %collective-permute-start) | collective-permute-done | bytes 262176 | tf_op jit(solution)/shard_map/ppermute | solution.py:26
  20.4 6.9 %collective-permute-start.2 = (bf16[8,128,128]{2,1,0:T(8,128)(2,1)S(1)}, bf16[8,128,128]{2,1,0:T(8,128)(2,1)S(1)}, u32[]{:S(2)}, u32[]{:S(2)}) collective-permute-start(bf16[8,128,128]{2,1,0:T(8,128)(2,1)S(1)} %fusion.8), channel_id=1, source_target_pairs={{0,8},{4,12},{8,0},{12,4},{16,24},{20,28},{24,16},{28,20},{1,9},{5... | collective-permute-start | bytes 786440 | tf_op jit(solution)/shard_map/ppermute | solution.py:26
  27.3 7.0 %collective-permute-done.2 = bf16[8,128,128]{2,1,0:T(8,128)(2,1)S(1)} collective-permute-done((bf16[8,128,128]{2,1,0:T(8,128)(2,1)S(1)}, bf16[8,128,128]{2,1,0:T(8,128)(2,1)S(1)}, u32[]{:S(2)}, u32[]{:S(2)}) %collective-permute-start.2) | collective-permute-done | bytes 262176 | tf_op jit(solution)/shard_map/ppermute | solution.py:26
  36.7 5.2 %collective-permute-start.4 = (bf16[8,128,128]{2,1,0:T(8,128)(2,1)}, bf16[8,128,128]{2,1,0:T(8,128)(2,1)}, u32[]{:S(2)}, u32[]{:S(2)}) collective-permute-start(bf16[8,128,128]{2,1,0:T(8,128)(2,1)} %fusion.3), channel_id=1, source_target_pairs={{0,16},{4,20},{8,24},{12,28},{1,17},{5,21},{9,25},{13,29},{2,18},{... | collective-permute-start | bytes 786440 | tf_op jit(solution)/shard_map/ppermute | solution.py:45
  60.9 26.3 %collective-permute-start.8 = (bf16[512,256]{1,0:T(8,128)(2,1)S(1)}, bf16[512,256]{1,0:T(8,128)(2,1)S(1)}, u32[]{:S(2)}, u32[]{:S(2)}) collective-permute-start(bf16[512,256]{1,0:T(8,128)(2,1)S(1)} %get-tuple-element.147.grad), channel_id=1, source_target_pairs={{0,8},{4,12},{8,0},{12,4},{16,24},{20,28},{24,16},{28,20},{1,9},{5... | collective-permute-start | bytes 786440 | tf_op jit(solution)/shard_map/ppermute | solution.py:26
  87.2 4.3 %collective-permute-done.8.other = bf16[512,256]{1,0:T(8,128)(2,1)S(1)} collective-permute-done((bf16[512,256]{1,0:T(8,128)(2,1)S(1)}, bf16[512,256]{1,0:T(8,128)(2,1)S(1)}, u32[]{:S(2)}, u32[]{:S(2)}) %collective-permute-start.8) | collective-permute-done | bytes 262176 | tf_op jit(solution)/shard_map/ppermute | solution.py:26
  99.6 10.1 %shard_map.90 = (bf16[512,1024]{1,0:T(8,128)(2,1)S(1)}, f32[8,128,128]{2,1,0:T(8,128)S(1)}, bf16[8,128,128]{2,1,0:T(8,128)(2,1)S(1)}) custom-call(bf16[512,4096]{1,0:T(8,128)(2,1)} %all-gather.5.cloned.1.call-done.mine.cot, bf16[1024,4096]{1,0:T(8,128)(2,1)} %weight.1, f32[512,1024]{1,0:T(8,128)S(1)} %copy-done.35, bf16[512,1024]{1,0:T(8,128)(2,1)S(1)} %copy-done.13, ...), custom_call_target="tpu_custom_call" | custom-call | flops 4429185024 | bytes 15732736 | tf_op jit(solution)/shard_map/pallas_call | solution.py:155
  121.6 8.1 %shard_map.92 = (bf16[512,1024]{1,0:T(8,128)(2,1)}, f32[512,1024]{1,0:T(8,128)}, f32[512,1024]{1,0:T(8,128)}) custom-call(bf16[512,1024]{1,0:T(8,128)(2,1)S(1)} %get-tuple-element.90.pre, bf16[512,1024]{1,0:T(8,128)(2,1)S(1)} %copy-done.13, bf16[512,1024]{1,0:T(8,128)(2,1)S(1)} %copy-done.1, bf16[512,1024]{1,0:T(8,128)(2,1)S(1)} %copy-done.5, ...), custom_call_target="tpu_custom_call" | custom-call | flops 2147483648 | bytes 4456448 | tf_op jit(solution)/shard_map/pallas_call | solution.py:155
  129.7 4.4 %collective-permute-done.11 = bf16[8,128,128]{2,1,0:T(8,128)(2,1)S(1)} collective-permute-done((bf16[8,128,128]{2,1,0:T(8,128)(2,1)S(1)}, bf16[8,128,128]{2,1,0:T(8,128)(2,1)S(1)}, u32[]{:S(2)}, u32[]{:S(2)}) %collective-permute-start.11) | collective-permute-done | bytes 262176 | tf_op jit(solution)/shard_map/ppermute | solution.py:26
  139.4 3.9 shard_map.95
  148.0 13.3 %collective-permute-start.20 = (bf16[256,512]{1,0:T(8,128)(2,1)}, bf16[256,512]{1,0:T(8,128)(2,1)}, u32[]{:S(2)}, u32[]{:S(2)}) collective-permute-start(bf16[256,512]{1,0:T(8,128)(2,1)} %shard_map.94), channel_id=1, source_target_pairs={{0,16},{4,20},{8,24},{12,28},{16,0},{20,4},{24,8},{28,12},{1,17},{... | collective-permute-start | bytes 786440 | tf_op jit(solution)/shard_map/ppermute | solution.py:26
  161.3 17.8 %collective-permute-done.18.rest_0_ = bf16[256,1024]{1,0:T(8,128)(2,1)S(1)} collective-permute-done((bf16[256,1024]{1,0:T(8,128)(2,1)}, bf16[256,1024]{1,0:T(8,128)(2,1)S(1)}, u32[]{:S(2)}, u32[]{:S(2)}) %collective-permute-start.18) | collective-permute-done | bytes 524320 | tf_op jit(solution)/shard_map/ppermute | solution.py:26
  182.4 4.6 %shard_map.93 = (bf16[512,1024]{1,0:T(8,128)(2,1)}, bf16[512,1024]{1,0:T(8,128)(2,1)S(1)}) custom-call(f32[512,1024]{1,0:T(8,128)} %get-tuple-element.91.key_local, f32[512,1024]{1,0:T(8,128)} %get-tuple-element.92.value_local, bf16[512,1024]{1,0:T(8,128)(2,1)S(1)} %copy-done.2, bf16[512,1024]{1,0:T(8,128)(2,1)S(1)} %copy-done.6, ...), custom_call_target="tpu_custom_call" | custom-call | flops 268435456 | bytes 6553600 | tf_op jit(solution)/shard_map/pallas_call | solution.py:155
  202.3 12.5 %collective-permute-start.24 = (bf16[512,512]{1,0:T(8,128)(2,1)S(1)}, bf16[512,512]{1,0:T(8,128)(2,1)S(1)}, u32[]{:S(2)}, u32[]{:S(2)}) collective-permute-start(bf16[512,512]{1,0:T(8,128)(2,1)S(1)} %shard_map.98), channel_id=1, source_target_pairs={{0,16},{4,20},{8,24},{12,28},{16,0},{20,4},{24,8},{28,12},{1,17},{... | collective-permute-start | bytes 1572872 | tf_op jit(solution)/shard_map/ppermute | solution.py:26
  221.6 23.8 %collective-permute-done.22.rest_1_ = bf16[256,512]{1,0:T(8,128)(2,1)S(1)} collective-permute-done((bf16[256,512]{1,0:T(8,128)(2,1)S(1)}, bf16[256,512]{1,0:T(8,128)(2,1)S(1)}, u32[]{:S(2)}, u32[]{:S(2)}) %collective-permute-start.22) | collective-permute-done | bytes 262176 | tf_op jit(solution)/shard_map/ppermute | solution.py:26
  266.9 11.2 %collective-permute-done.25.rest_0_ = bf16[1024,512]{1,0:T(8,128)(2,1)S(1)} collective-permute-done((bf16[1024,512]{1,0:T(8,128)(2,1)S(1)}, bf16[1024,512]{1,0:T(8,128)(2,1)S(1)}, u32[]{:S(2)}, u32[]{:S(2)}) %collective-permute-start.25) | collective-permute-done | bytes 1048608 | tf_op jit(solution)/shard_map/ppermute | solution.py:26
  280.8 18.5 %collective-permute-done.26.rest_1_ = bf16[512,512]{1,0:T(8,128)(2,1)S(1)} collective-permute-done((bf16[512,512]{1,0:T(8,128)(2,1)S(1)}, bf16[512,512]{1,0:T(8,128)(2,1)S(1)}, u32[]{:S(2)}, u32[]{:S(2)}) %collective-permute-start.26) | collective-permute-done | bytes 524320 | tf_op jit(solution)/shard_map/ppermute | solution.py:26
  299.3 3.8 shard_map.108.rest_2_
  310.2 3.8 shard_map.111.rest_2_
  321.6 11.0 %collective-permute-done.29.rest_0_ = bf16[1024,512]{1,0:T(8,128)(2,1)S(1)} collective-permute-done((bf16[1024,512]{1,0:T(8,128)(2,1)S(1)}, bf16[1024,512]{1,0:T(8,128)(2,1)S(1)}, u32[]{:S(2)}, u32[]{:S(2)}) %collective-permute-start.29) | collective-permute-done | bytes 1048608 | tf_op jit(solution)/shard_map/ppermute | solution.py:26
  335.1 28.2 %collective-permute-done.30.rest_1_ = bf16[512,512]{1,0:T(8,128)(2,1)S(1)} collective-permute-done((bf16[512,512]{1,0:T(8,128)(2,1)S(1)}, bf16[512,512]{1,0:T(8,128)(2,1)S(1)}, u32[]{:S(2)}, u32[]{:S(2)}) %collective-permute-start.30) | collective-permute-done | bytes 524320 | tf_op jit(solution)/shard_map/ppermute | solution.py:26
  369.7 16.1 %collective-permute-done.32.rest_1_ = bf16[512,512]{1,0:T(8,128)(2,1)S(1)} collective-permute-done((bf16[512,512]{1,0:T(8,128)(2,1)S(1)}, bf16[512,512]{1,0:T(8,128)(2,1)S(1)}, u32[]{:S(2)}, u32[]{:S(2)}) %collective-permute-start.32) | collective-permute-done | bytes 524320 | tf_op jit(solution)/shard_map/ppermute | solution.py:26
  389.6 7.5 %collective-permute-done.33.rest_1_ = bf16[512,512]{1,0:T(8,128)(2,1)S(1)} collective-permute-done((bf16[512,512]{1,0:T(8,128)(2,1)S(1)}, bf16[512,512]{1,0:T(8,128)(2,1)S(1)}, u32[]{:S(2)}, u32[]{:S(2)}) %collective-permute-start.33) | collective-permute-done | bytes 524320 | tf_op jit(solution)/shard_map/ppermute | solution.py:26
  400.5 6.8 %collective-permute-done.34.rest_1_ = bf16[512,512]{1,0:T(8,128)(2,1)S(1)} collective-permute-done((bf16[512,512]{1,0:T(8,128)(2,1)S(1)}, bf16[512,512]{1,0:T(8,128)(2,1)S(1)}, u32[]{:S(2)}, u32[]{:S(2)}) %collective-permute-start.34) | collective-permute-done | bytes 524320 | tf_op jit(solution)/shard_map/ppermute | solution.py:26
  (189 shorter events, 143.3 us)
Async XLA Ops:
  7.2 87.6 %all-gather.5.cloned.1.call-start = ((), (), s32[]{:S(2)}) async-start(), calls=%async_computation.1 | async-start | bytes 5242880 | tf_op jit(solution)/shard_map/all_gather | solution.py:263
  7.9 179.1 %all-gather.3.cloned.1.call-start = ((), (), s32[]{:S(2)}) async-start(), calls=%async_computation | async-start | bytes 5242880 | tf_op jit(solution)/shard_map/all_gather | solution.py:282
  52.2 39.3 %collective-permute-start.5 = (bf16[512,1024]{1,0:T(8,128)(2,1)}, bf16[512,1024]{1,0:T(8,128)(2,1)}, u32[]{:S(2)}, u32[]{:S(2)}) collective-permute-start(bf16[512,1024]{1,0:T(8,128)(2,1)} %copy-done.38), channel_id=1, source_target_pairs={{1,0},{3,2},{5,4},{7,6},{8,9},{10,11},{12,13},{14,15},{17,16},{19,... | collective-permute-start | bytes 3145736 | tf_op jit(solution)/shard_map/ppermute | solution.py:252
  53.5 38.0 %collective-permute-start.7 = (bf16[512,1024]{1,0:T(8,128)(2,1)}, bf16[512,1024]{1,0:T(8,128)(2,1)}, u32[]{:S(2)}, u32[]{:S(2)}) collective-permute-start(bf16[512,1024]{1,0:T(8,128)(2,1)} %collective-permute-done.6), channel_id=1, source_target_pairs={{1,0},{3,2},{5,4},{7,6},{8,9},{10,11},{12,13},{14,15},{17,16},{19,... | collective-permute-start | bytes 3145736 | tf_op jit(solution)/shard_map/ppermute | solution.py:252
  60.9 30.6 %collective-permute-start.8 = (bf16[512,256]{1,0:T(8,128)(2,1)S(1)}, bf16[512,256]{1,0:T(8,128)(2,1)S(1)}, u32[]{:S(2)}, u32[]{:S(2)}) collective-permute-start(bf16[512,256]{1,0:T(8,128)(2,1)S(1)} %get-tuple-element.147.grad), channel_id=1, source_target_pairs={{0,8},{4,12},{8,0},{12,4},{16,24},{20,28},{24,16},{28,20},{1,9},{5... | collective-permute-start | bytes 786440 | tf_op jit(solution)/shard_map/ppermute | solution.py:26
  134.1 52.8 %collective-permute-start.15 = (bf16[512,1024]{1,0:T(8,128)(2,1)}, bf16[512,1024]{1,0:T(8,128)(2,1)}, u32[]{:S(2)}, u32[]{:S(2)}) collective-permute-start(bf16[512,1024]{1,0:T(8,128)(2,1)} %get-tuple-element.98.grad), channel_id=1, source_target_pairs={{0,8},{4,12},{8,0},{12,4},{16,24},{20,28},{24,16},{28,20},{1,9},{5... | collective-permute-start | bytes 3145736 | tf_op jit(solution)/shard_map/ppermute | solution.py:26
  143.3 49.8 %collective-permute-start.19 = (bf16[512,1024]{1,0:T(8,128)(2,1)}, bf16[512,1024]{1,0:T(8,128)(2,1)}, u32[]{:S(2)}, u32[]{:S(2)}) collective-permute-start(bf16[512,1024]{1,0:T(8,128)(2,1)} %shard_map.95), channel_id=1, source_target_pairs={{0,4},{4,0},{8,12},{12,8},{16,20},{20,16},{24,28},{28,24},{1,5},{5... | collective-permute-start | bytes 3145736 | tf_op jit(solution)/shard_map/ppermute | solution.py:26
  145.4 33.7 %collective-permute-start.18 = (bf16[256,1024]{1,0:T(8,128)(2,1)}, bf16[256,1024]{1,0:T(8,128)(2,1)S(1)}, u32[]{:S(2)}, u32[]{:S(2)}) collective-permute-start(bf16[256,1024]{1,0:T(8,128)(2,1)} %shard_map.91), channel_id=1, source_target_pairs={{0,4},{4,0},{8,12},{12,8},{16,20},{20,16},{24,28},{28,24},{1,5},{5... | collective-permute-start | bytes 1572872 | tf_op jit(solution)/shard_map/ppermute | solution.py:26
  146.3 34.8 %collective-permute-start.12 = (bf16[8,128,128]{2,1,0:T(8,128)(2,1)}, bf16[8,128,128]{2,1,0:T(8,128)(2,1)}, u32[]{:S(2)}, u32[]{:S(2)}) collective-permute-start(bf16[8,128,128]{2,1,0:T(8,128)(2,1)} %fusion.7), channel_id=1, source_target_pairs={{16,0},{20,4},{24,8},{28,12},{17,1},{21,5},{25,9},{29,13},{18,2},{... | collective-permute-start | bytes 786440 | tf_op jit(solution)/shard_map/ppermute | solution.py:45
  148.0 47.7 %collective-permute-start.20 = (bf16[256,512]{1,0:T(8,128)(2,1)}, bf16[256,512]{1,0:T(8,128)(2,1)}, u32[]{:S(2)}, u32[]{:S(2)}) collective-permute-start(bf16[256,512]{1,0:T(8,128)(2,1)} %shard_map.94), channel_id=1, source_target_pairs={{0,16},{4,20},{8,24},{12,28},{16,0},{20,4},{24,8},{28,12},{1,17},{... | collective-permute-start | bytes 786440 | tf_op jit(solution)/shard_map/ppermute | solution.py:26
  187.0 61.3 %collective-permute-start.14 = (bf16[512,1024]{1,0:T(8,128)(2,1)}, bf16[512,1024]{1,0:T(8,128)(2,1)}, u32[]{:S(2)}, u32[]{:S(2)}) collective-permute-start(bf16[512,1024]{1,0:T(8,128)(2,1)} %get-tuple-element.96.grad), channel_id=1, source_target_pairs={{0,8},{4,12},{8,0},{12,4},{16,24},{20,28},{24,16},{28,20},{1,9},{5... | collective-permute-start | bytes 3145736 | tf_op jit(solution)/shard_map/ppermute | solution.py:26
  202.2 51.3 %collective-permute-start.23 = (bf16[1024,512]{1,0:T(8,128)(2,1)S(1)}, bf16[1024,512]{1,0:T(8,128)(2,1)S(1)}, u32[]{:S(2)}, u32[]{:S(2)}) collective-permute-start(bf16[1024,512]{1,0:T(8,128)(2,1)S(1)} %shard_map.100), channel_id=1, source_target_pairs={{0,4},{4,0},{8,12},{12,8},{16,20},{20,16},{24,28},{28,24},{1,5},{5... | collective-permute-start | bytes 3145736 | tf_op jit(solution)/shard_map/ppermute | solution.py:26
  202.3 54.0 %collective-permute-start.24 = (bf16[512,512]{1,0:T(8,128)(2,1)S(1)}, bf16[512,512]{1,0:T(8,128)(2,1)S(1)}, u32[]{:S(2)}, u32[]{:S(2)}) collective-permute-start(bf16[512,512]{1,0:T(8,128)(2,1)S(1)} %shard_map.98), channel_id=1, source_target_pairs={{0,16},{4,20},{8,24},{12,28},{16,0},{20,4},{24,8},{28,12},{1,17},{... | collective-permute-start | bytes 1572872 | tf_op jit(solution)/shard_map/ppermute | solution.py:26
  214.8 30.6 %collective-permute-start.22 = (bf16[256,512]{1,0:T(8,128)(2,1)S(1)}, bf16[256,512]{1,0:T(8,128)(2,1)S(1)}, u32[]{:S(2)}, u32[]{:S(2)}) collective-permute-start(bf16[256,512]{1,0:T(8,128)(2,1)S(1)} %copy-done.32), channel_id=1, source_target_pairs={{0,16},{4,20},{8,24},{12,28},{16,0},{20,4},{24,8},{28,12},{1,17},{... | collective-permute-start | bytes 786440 | tf_op jit(solution)/shard_map/ppermute | solution.py:26
  216.5 86.6 %collective-permute-start.13 = (bf16[512,1024]{1,0:T(8,128)(2,1)S(1)}, bf16[512,1024]{1,0:T(8,128)(2,1)S(1)}, u32[]{:S(2)}, u32[]{:S(2)}) collective-permute-start(bf16[512,1024]{1,0:T(8,128)(2,1)S(1)} %get-tuple-element.95.grad), channel_id=1, source_target_pairs={{0,8},{4,12},{8,0},{12,4},{16,24},{20,28},{24,16},{28,20},{1,9},{5... | collective-permute-start | bytes 3145736 | tf_op jit(solution)/shard_map/ppermute | solution.py:26
  251.9 26.2 %collective-permute-start.25 = (bf16[1024,512]{1,0:T(8,128)(2,1)S(1)}, bf16[1024,512]{1,0:T(8,128)(2,1)S(1)}, u32[]{:S(2)}, u32[]{:S(2)}) collective-permute-start(bf16[1024,512]{1,0:T(8,128)(2,1)S(1)} %shard_map.103), channel_id=1, source_target_pairs={{0,4},{4,0},{8,12},{12,8},{16,20},{20,16},{24,28},{28,24},{1,5},{5... | collective-permute-start | bytes 3145736 | tf_op jit(solution)/shard_map/ppermute | solution.py:26
  263.5 43.9 %collective-permute-start.27 = (bf16[1024,512]{1,0:T(8,128)(2,1)S(1)}, bf16[1024,512]{1,0:T(8,128)(2,1)S(1)}, u32[]{:S(2)}, u32[]{:S(2)}) collective-permute-start(bf16[1024,512]{1,0:T(8,128)(2,1)S(1)} %shard_map.106), channel_id=1, source_target_pairs={{0,4},{4,0},{8,12},{12,8},{16,20},{20,16},{24,28},{28,24},{1,5},{5... | collective-permute-start | bytes 3145736 | tf_op jit(solution)/shard_map/ppermute | solution.py:26
  263.9 35.4 %collective-permute-start.26 = (bf16[512,512]{1,0:T(8,128)(2,1)S(1)}, bf16[512,512]{1,0:T(8,128)(2,1)S(1)}, u32[]{:S(2)}, u32[]{:S(2)}) collective-permute-start(bf16[512,512]{1,0:T(8,128)(2,1)S(1)} %shard_map.101), channel_id=1, source_target_pairs={{0,16},{4,20},{8,24},{12,28},{16,0},{20,4},{24,8},{28,12},{1,17},{... | collective-permute-start | bytes 1572872 | tf_op jit(solution)/shard_map/ppermute | solution.py:26
  263.9 46.3 %collective-permute-start.28 = (bf16[512,512]{1,0:T(8,128)(2,1)S(1)}, bf16[512,512]{1,0:T(8,128)(2,1)S(1)}, u32[]{:S(2)}, u32[]{:S(2)}) collective-permute-start(bf16[512,512]{1,0:T(8,128)(2,1)S(1)} %shard_map.104), channel_id=1, source_target_pairs={{0,16},{4,20},{8,24},{12,28},{16,0},{20,4},{24,8},{28,12},{1,17},{... | collective-permute-start | bytes 1572872 | tf_op jit(solution)/shard_map/ppermute | solution.py:26
  317.5 49.6 %collective-permute-start.31 = (bf16[1024,512]{1,0:T(8,128)(2,1)S(1)}, bf16[1024,512]{1,0:T(8,128)(2,1)S(1)}, u32[]{:S(2)}, u32[]{:S(2)}) collective-permute-start(bf16[1024,512]{1,0:T(8,128)(2,1)S(1)} %shard_map.112), channel_id=1, source_target_pairs={{0,4},{4,0},{8,12},{12,8},{16,20},{20,16},{24,28},{28,24},{1,5},{5... | collective-permute-start | bytes 3145736 | tf_op jit(solution)/shard_map/ppermute | solution.py:26
  318.7 44.7 %collective-permute-start.30 = (bf16[512,512]{1,0:T(8,128)(2,1)S(1)}, bf16[512,512]{1,0:T(8,128)(2,1)S(1)}, u32[]{:S(2)}, u32[]{:S(2)}) collective-permute-start(bf16[512,512]{1,0:T(8,128)(2,1)S(1)} %shard_map.107), channel_id=1, source_target_pairs={{0,16},{4,20},{8,24},{12,28},{16,0},{20,4},{24,8},{28,12},{1,17},{... | collective-permute-start | bytes 1572872 | tf_op jit(solution)/shard_map/ppermute | solution.py:26
  318.7 67.1 %collective-permute-start.32 = (bf16[512,512]{1,0:T(8,128)(2,1)S(1)}, bf16[512,512]{1,0:T(8,128)(2,1)S(1)}, u32[]{:S(2)}, u32[]{:S(2)}) collective-permute-start(bf16[512,512]{1,0:T(8,128)(2,1)S(1)} %shard_map.110), channel_id=1, source_target_pairs={{0,16},{4,20},{8,24},{12,28},{16,0},{20,4},{24,8},{28,12},{1,17},{... | collective-permute-start | bytes 1572872 | tf_op jit(solution)/shard_map/ppermute | solution.py:26
  335.1 62.0 %collective-permute-start.33 = (bf16[512,512]{1,0:T(8,128)(2,1)S(1)}, bf16[512,512]{1,0:T(8,128)(2,1)S(1)}, u32[]{:S(2)}, u32[]{:S(2)}) collective-permute-start(bf16[512,512]{1,0:T(8,128)(2,1)S(1)} %shard_map.113), channel_id=1, source_target_pairs={{0,16},{4,20},{8,24},{12,28},{16,0},{20,4},{24,8},{28,12},{1,17},{... | collective-permute-start | bytes 1572872 | tf_op jit(solution)/shard_map/ppermute | solution.py:26
  369.6 37.7 %collective-permute-start.34 = (bf16[512,512]{1,0:T(8,128)(2,1)S(1)}, bf16[512,512]{1,0:T(8,128)(2,1)S(1)}, u32[]{:S(2)}, u32[]{:S(2)}) collective-permute-start(bf16[512,512]{1,0:T(8,128)(2,1)S(1)} %shard_map.115), channel_id=1, source_target_pairs={{0,16},{4,20},{8,24},{12,28},{16,0},{20,4},{24,8},{28,12},{1,17},{... | collective-permute-start | bytes 1572872 | tf_op jit(solution)/shard_map/ppermute | solution.py:26
  (57 other events, 800.9 us)
Sparse Core Ops, SparseCore 0:
  9.6 37.1 all-gather.4
  50.7 47.1 all-gather.2

commit v6 on v4

--- a/solution.py
+++ b/solution.py
@@ -26,24 +26,27 @@
     return lax.ppermute(array, "seq", [(i, i ^ (1 << bit)) for i in range(size)])
 
 
-def entering(block, low, reverse):
+def entering(block, low, reverse, waits=None):
     size, position = lax.axis_size("seq"), lax.axis_index("seq")
     bits = size.bit_length() - 1
-    total, before, passed = block, jnp.zeros_like(block), None
+    total, before = block, jnp.zeros_like(block)
+    sent, came = [], []
     for bit in range(bits):
         step = 1 << bit
+        if waits and bit in waits:
+            low = after(low, *waits[bit])
+        sent.append(low)
         if bit < bits - 1:
-            new = flip(low, bit)
-            passed = new if bit == 1 or passed is None else passed
-            new = new.astype(F32)
+            came.append(flip(low, bit))
+            new = came[-1].astype(F32)
             mine = (position >> bit) & 1
             before = before + jnp.where(mine == (0 if reverse else 1), new, 0.0)
             total = total + new
             low = total.astype(BF16)
         else:
             pairs = [(i, i ^ step) for i in range(size) if bool(i & step) == reverse]
-            before = before + lax.ppermute(low, "seq", pairs).astype(F32)
-    return before.astype(BF16), passed
+            came.append(lax.ppermute(low, "seq", pairs))
+    return (before, came[-1]), sent, came
 
 
 def mm(a, b):
@@ -97,16 +100,29 @@
         out[:, cols] = lower_mm(causal(q[:, cols], k[:, cols]), v[:, cols])
 
 
-def gated_kernel(local, q, state, gain, attention, gated):
+def gated_kernel(local, q, state, gain, attention, first, second):
+    step, steps = pl.program_id(0), pl.num_programs(0)
+    parts = []
     for i, cols in enumerate(head_slices(q)):
         value = local[:, cols] + mm(q[:, cols], state[i])
         attention[:, cols] = value
         rms = jnp.sqrt(jnp.mean(value * value, axis=-1, keepdims=True) + 1e-05)
-        gated[:, cols] = (value / rms * gain[:, cols]).astype(BF16)
-
-
-def pre_kernel(cot, weight, attention, q, gain, pre, out, low):
-    gated_grad = mm_t(cot[...], weight[...])
+        parts.append((value / rms * gain[:, cols]).astype(BF16))
+    found = jnp.concatenate(parts, axis=1)
+
+    @pl.when(step < steps // 2)
+    def _():
+        first[...] = found
+
+    @pl.when(step >= steps // 2)
+    def _():
+        second[...] = found
+
+
+def pre_kernel(blocks, index, *refs):
+    cots, weights = refs[:blocks], refs[blocks : 2 * blocks]
+    attention, q, gain, pre, out, low = refs[2 * blocks :]
+    gated_grad = sum(mm_t(c[...], w[...]) for c, w in zip(cots, weights))
     for i, cols in enumerate(head_slices(q)):
         value = attention[:, cols]
         rms = jnp.sqrt(jnp.mean(value * value, axis=-1, keepdims=True) + 1e-05)
@@ -119,13 +135,57 @@
         low[i] = out[i].astype(BF16)
 
 
-def query_kernel(pre, q, k, v, state, query_grad, key_local, value_local):
-    for i, cols in enumerate(head_slices(q)):
-        grad, qh, kh, vh = pre[:, cols], q[:, cols], k[:, cols], v[:, cols]
-        mixing = causal(grad, vh)
-        query_grad[:, cols] = (lower_mm(mixing, kh) + mm_t(grad, state[i])).astype(BF16)
-        key_local[:, cols] = upper_mm(mixing, qh)
-        value_local[:, cols] = upper_mm(causal(qh, kh), grad)
+def pre_grad_of(cots, places, weight, attention, q, gain):
+    tokens, width = q.shape
+    pair = 2 * HEAD_DIM
+    part = cots[0].shape[1]
+    blocks = len(cots)
+    rows = pl.BlockSpec((tokens, pair), lambda i, ix: (0, i))
+    heads = pl.BlockSpec((2, HEAD_DIM, HEAD_DIM), lambda i, ix: (i, 0, 0))
+    whole = pl.BlockSpec((tokens, part), lambda i, ix: (0, 0))
+    shape = (width // HEAD_DIM, HEAD_DIM, HEAD_DIM)
+    return pl.pallas_call(
+        functools.partial(pre_kernel, blocks),
+        grid_spec=pltpu.PrefetchScalarGridSpec(
+            num_scalar_prefetch=1,
+            grid=(width // pair,),
+            in_specs=[whole] * blocks
+            + [pl.BlockSpec((pair, part), lambda i, ix, j=j: (i, ix[j])) for j in range(blocks)]
+            + [rows, rows, pl.BlockSpec((1, pair), lambda i, ix: (0, i))],
+            out_specs=[rows, heads, heads],
+        ),
+        out_shape=[
+            jax.ShapeDtypeStruct((tokens, width), BF16),
+            jax.ShapeDtypeStruct(shape, F32),
+            jax.ShapeDtypeStruct(shape, BF16),
+        ],
+        compiler_params=PARAMS,
+        cost_estimate=cost(2 * tokens * width * part * blocks, 2 * (tokens + width) * part * blocks),
+    )(places, *cots, *[weight] * blocks, attention, q, gain)
+
+
+def query_kernel(pre, k, v, state, first, second):
+    step, steps = pl.program_id(0), pl.num_programs(0)
+    parts = []
+    for i, cols in enumerate(head_slices(k)):
+        grad = pre[:, cols]
+        parts.append((lower_mm(causal(grad, v[:, cols]), k[:, cols]) + mm_t(grad, state[i])).astype(BF16))
+    found = jnp.concatenate(parts, axis=1)
+
+    @pl.when(step < steps // 2)
+    def _():
+        first[...] = found
+
+    @pl.when(step >= steps // 2)
+    def _():
+        second[...] = found
+
+
+def own_kernel(pre, q, k, v, key_local, value_local):
+    for cols in head_slices(q):
+        grad, qh = pre[:, cols], q[:, cols]
+        key_local[:, cols] = upper_mm(causal(grad, v[:, cols]), qh)
+        value_local[:, cols] = upper_mm(causal(qh, k[:, cols]), grad)
 
 
 def key_value_kernel(key_local, value_local, k, v, state, key_grad, value_grad):
@@ -139,24 +199,25 @@
     width = next(a.shape[1] for kind, a in args if kind == "rows")
     pair = 2 * HEAD_DIM
     count = width // pair
-
-    def spec(kind, array=None):
-        if kind == "rows":
-            return pl.BlockSpec((tokens, pair), lambda i: (0, i))
-        if kind == "heads":
-            return pl.BlockSpec((2, HEAD_DIM, HEAD_DIM), lambda i: (i, 0, 0))
-        if kind == "gain":
-            return pl.BlockSpec((1, pair), lambda i: (0, i))
-        if kind == "weight":
-            return pl.BlockSpec((pair, array.shape[1]), lambda i: (i, 0))
-        return pl.BlockSpec(array.shape, lambda i: (0, 0))
-
-    shapes = {"rows": (tokens, width), "heads": (2 * count, HEAD_DIM, HEAD_DIM)}
+    half = count // 2
+    specs = {
+        "rows": pl.BlockSpec((tokens, pair), lambda i: (0, i)),
+        "first": pl.BlockSpec((tokens, pair), lambda i: (0, jnp.minimum(i, half - 1))),
+        "second": pl.BlockSpec((tokens, pair), lambda i: (0, jnp.maximum(i - half, 0))),
+        "heads": pl.BlockSpec((2, HEAD_DIM, HEAD_DIM), lambda i: (i, 0, 0)),
+        "gain": pl.BlockSpec((1, pair), lambda i: (0, i)),
+    }
+    shapes = {
+        "rows": (tokens, width),
+        "first": (tokens, width // 2),
+        "second": (tokens, width // 2),
+        "heads": (2 * count, HEAD_DIM, HEAD_DIM),
+    }
     return pl.pallas_call(
         kernel,
         grid=(count,),
-        in_specs=[spec(kind, a) for kind, a in args],
-        out_specs=[spec(kind) for kind, _ in outs],
+        in_specs=[specs[kind] for kind, _ in args],
+        out_specs=[specs[kind] for kind, _ in outs],
         out_shape=[jax.ShapeDtypeStruct(shapes[kind], dtype) for kind, dtype in outs],
         compiler_params=PARAMS,
         cost_estimate=cost(flops, sum(a.size * a.dtype.itemsize for _, a in args)),
@@ -260,80 +321,92 @@
         theirs = lax.all_gather(flip(send, gather_bit), "head", axis=1, tiled=True)
         return gathered, theirs, jnp.concatenate([there, packed])
 
-    gathered_cot = lax.all_gather(cotangent, "head", axis=1, tiled=True)
     gain = norm_gain.reshape(1, width)
     q, k, v = ("rows", query_rows), ("rows", key_rows), ("rows", value_rows)
 
+    cots, toggles = [cotangent], [0]
+    toggle = head_size // 2
+    while toggle:
+        pairs = [(h, h ^ toggle) for h in range(head_size)]
+        cots += [lax.ppermute(block, "head", pairs) for block in cots]
+        toggles += [t ^ toggle for t in toggles]
+        toggle //= 2
+    places = jnp.stack([head_place ^ t for t in toggles]).astype(jnp.int32)
+
     block_state, block_low = by_heads(
         state_kernel, [k, v], [("heads", F32), ("heads", BF16)], 2 * work * HEAD_DIM
     )
+    waits = {1: [cots[1]]}
     if paired:
-        same_cot = across(cotangent, 2, 1)
-        other_cot = across(same_cot, 0, 2)
-        near_cot, far_cot = across(same_cot, 0, 1), across(other_cot, 0, 1)
+        swapped_input = after(across(layer_input, 2, 1), cots[1])
+        swapped_input = jnp.where(aligned, layer_input, swapped_input)
+    state_parts, sent, came = entering(block_state, block_low, False, waits)
     (local,) = by_heads(
-        local_kernel, [q, k, ("rows", after(value_rows, block_low))], [("rows", F32)], 3 * work * tokens
-    )
-    state_low, passed = entering(block_state, block_low, False)
-    if paired:
-        swapped = jnp.where(aligned, layer_input, across(after(layer_input, passed), 2, 1))
-        gathered_input = lax.all_gather(swapped, "head", axis=1, tiled=True)
-        both_input = gathered_input, gathered_input, jnp.concatenate([there, there ^ 2])
-        near_cot = jnp.where(aligned, near_cot, same_cot)
-        far_cot = jnp.where(aligned, far_cot, other_cot)
-
-        def chosen(at):
-            near, far = (lax.dynamic_slice_in_dim(a, (at & 1) * owned, owned, 1) for a in (near_cot, far_cot))
-            return jnp.where((at >> 2) == (head_place >> 1), near, far)
-
-        partner_cot = jnp.concatenate([chosen(at) for at in order], axis=1)
-        both_cot = gathered_cot, partner_cot, jnp.concatenate([there, packed])
-    else:
-        both_cot = both(gathered_cot)
-        both_input = both(lax.all_gather(after(layer_input, gathered_cot), "head", axis=1, tiled=True))
-
-    attention, gated = by_heads(
+        local_kernel, [q, k, ("rows", after(value_rows, sent[-1]))], [("rows", F32)], 3 * work * tokens
+    )
+    state_low = (state_parts[0] + after(state_parts[1], local).astype(F32)).astype(BF16)
+    attention, *gated = by_heads(
         gated_kernel,
         [("rows", local), q, ("heads", state_low), ("gain", gain)],
-        [("rows", F32), ("rows", BF16)],
+        [("rows", F32), ("first", BF16), ("second", BF16)],
         2 * work * HEAD_DIM,
     )
-    half = width // 2
-    gated_parts = [gated[:, :half], gated[:, half:]]
-    gated_parts = [(part, flip(part, gather_bit)) for part in gated_parts]
-    pre, grad_block, grad_block_low = by_heads(
-        pre_kernel,
-        [("whole", gathered_cot), ("weight", out_weight), ("rows", attention), q, ("gain", gain)],
-        [("rows", BF16), ("heads", F32), ("heads", BF16)],
-        2 * work * (model + HEAD_DIM),
-    )
-    grad_low, passed = entering(grad_block, grad_block_low, True)
-    query_grad, key_local, value_local = by_heads(
+    if paired:
+        swapped_cot = across(after(cotangent, came[1]), 2, 1)
+        swapped_cot = jnp.where(aligned, cotangent, after(swapped_cot, attention))
+        index = jnp.concatenate([there, there ^ 2])
+        both_input, both_cot = (
+            (gathered, gathered, index)
+            for gathered in (lax.all_gather(a, "head", axis=1, tiled=True) for a in (swapped_input, swapped_cot))
+        )
+    else:
+        both_input, both_cot = (
+            both(lax.all_gather(a, "head", axis=1, tiled=True)) for a in (layer_input, cotangent)
+        )
+    gated_first = gated[0], flip(gated[0], gather_bit)
+
+    pre, grad_block, grad_block_low = pre_grad_of(cots, places, out_weight, attention, query_rows, gain)
+    grad_parts, sent, came = entering(grad_block, grad_block_low, True)
+    pre_then = after(pre, gated_first[1])
+    query_grad = by_heads(
         query_kernel,
-        [("rows", pre), q, k, v, ("heads", state_low)],
-        [("rows", BF16), ("rows", F32), ("rows", F32)],
-        8 * work * tokens,
-    )
+        [("rows", pre_then), k, v, ("heads", state_low)],
+        [("first", BF16), ("second", BF16)],
+        4 * work * tokens,
+    )
+    query_grad = [(part, flip(part, gather_bit)) for part in query_grad]
+    key_local, value_local = by_heads(
+        own_kernel,
+        [("rows", after(pre, query_grad[0][0], sent[1])), q, k, v],
+        [("rows", F32), ("rows", F32)],
+        6 * work * tokens,
+    )
+    gated_second = after(gated[1], came[1])
+    gated = [gated_first, (gated_second, flip(gated_second, gather_bit))]
+    grad_low = (grad_parts[0] + grad_parts[1].astype(F32)).astype(BF16)
     key_grad, value_grad = by_heads(
         key_value_kernel,
         [("rows", key_local), ("rows", value_local), k, v, ("heads", grad_low)],
         [("rows", BF16), ("rows", BF16)],
         4 * work * HEAD_DIM,
     )
-
-    grads = [(grad, flip(after(grad, passed), gather_bit)) for grad in (query_grad, key_grad, value_grad)]
-    pieces = [(both_cot, part, 0, True, (i, 0)) for i, part in enumerate(gated_parts)]
-    pieces += [(both_input, pair, i, False, (n, 0, i)) for n, pair in enumerate(grads) for i in range(2)]
+    key_grad, value_grad = ((grad, flip(grad, gather_bit)) for grad in (key_grad, value_grad))
+
+    half = width // 2
+    pieces = [(both_input, query_grad[i], 0, False, (0, 0, i)) for i in range(2)]
+    pieces += [(both_cot, gated[i], 0, True, (i, 0)) for i in range(2)]
+    pieces += [(both_input, key_grad, i, False, (1, 0, i)) for i in range(2)]
+    pieces += [(both_input, value_grad, i, False, (2, 0, i)) for i in range(2)]
     starts = [chunks - (chunks >> i) for i in range(len(halving) + 1)]
-    shapes = {True: (width, owned), False: (len(grads), owned, width)}
+    shapes = {True: (width, owned), False: (3, owned, width)}
     targets = {True: None, False: None}
-    received = [[] for _ in pieces]
-    last = [gated]
+    received = {}
+    last = [key_local]
 
     def stage(i, n):
         features, (grad, other), block, turned, place = pieces[i]
         other = after(other, last[0])
-        came = received[i]
+        came = received.setdefault(i, [])
         if came:
             came[-1] = (after(came[-1][0], last[0]), came[-1][1])
         final = n == len(halving)
@@ -347,8 +420,10 @@
             came.append((flip(out, halving[n]), starts[n + 1]))
 
     stages = len(halving) + 1
-    for n in range(2):
-        stage(n, 0)
+    last[0] = after(last[0], sent[-1])
+    stage(0, 0)
+    stage(1, 0)
+    last[0] = after(last[0], key_grad[0])
     for i in range(len(pieces) + 1):
         for n in range(1, stages - 1):
             if i < len(pieces):

time: 390 us -> 388 us (level)
  starting transfers between devices: 78.3 us -> 50.4 us
  waiting for transfers between devices: 165 us -> 186 us
  Pallas kernels: 109 us -> 116 us
    ppermute x25 -> x26, starting transfers between devices: 64.1 us -> 28.8 us  [flip(): return lax.ppermute(array, 'seq', [(i, i ^ 1 << bit) for i in range(size)])]
    ppermute x2 -> x5, waiting for transfers between devices: 0.01 us -> 27.5 us  [the longest x3 25.8 us: body(): cots += [lax.ppermute(block, 'head', pairs) for block in cots]]
    ppermute x2 -> x5, starting transfers between devices: 6.6 us -> 18.1 us  [the longest x3 11.6 us: body(): cots += [lax.ppermute(block, 'head', pairs) for block in cots]]
    pallas_call x6 -> x7, Pallas kernels: 30.7 us -> 36.8 us  [the longest x6 24.6 us: by_heads(): pl.pallas_call(kernel, grid=(count,), in_specs=[specs[kind] for kind, _ i...]
    ppermute x25 -> x26, waiting for transfers between devices: 165 us -> 159 us  [flip(): return lax.ppermute(array, 'seq', [(i, i ^ 1 << bit) for i in range(size)])]
    ppermute x5 -> x2, starting transfers between devices: 7.53 us -> 3.35 us  [across(): return lax.ppermute(array, ('seq', 'head'), pairs)]
    unnamed x62 -> x56, local copies, waits for them, and re-layouts: 8.24 us -> 9.02 us
  transfers between devices with their start and end apart: 34 -> 35, of which waited for: 15 -> 18; matrix products, arithmetic and copies ran while one was open for 3% -> 2% of each run, Pallas kernels for 27% -> 29%
where the time goes in v6:
time: 388 us; the launch traced here: 387 us
  waiting for transfers between devices  186 us (48%)
  Pallas kernels  116 us (30%)
  starting transfers between devices  50.4 us (13%)
  between operations  14.4 us (4%)
  other arithmetic  10.4 us (3%)
  local copies, waits for them, and re-layouts  9.11 us (2%)
    ppermute x26, waiting for transfers between devices, flip(): return lax.ppermute(array, 'seq', [(i, i ^ 1 << bit) for i in range(size)])  159 us
    pallas_call x24, Pallas kernels, term(): pl.pallas_call(functools.partial(term_kernel, turned, len(received)), gri...  79.4 us
    ppermute x26, starting transfers between devices, flip(): return lax.ppermute(array, 'seq', [(i, i ^ 1 << bit) for i in range(size)])  28.8 us
    ppermute x3, waiting for transfers between devices, body(): cots += [lax.ppermute(block, 'head', pairs) for block in cots]  25.8 us
    pallas_call x6, Pallas kernels, by_heads(): pl.pallas_call(kernel, grid=(count,), in_specs=[specs[kind] for kind, _ i...  24.6 us
    pallas_call x1, Pallas kernels, pre_grad_of(): pl.pallas_call(functools.partial(pre_kernel, blocks), grid_spec=pltpu.Pre...  12.2 us
    ppermute x3, starting transfers between devices, body(): cots += [lax.ppermute(block, 'head', pairs) for block in cots]  11.6 us
    unnamed x56, local copies, waits for them, and re-layouts  9.02 us
  transfers between devices with their start and end apart: 35, of which 18 were waited for; matrix products, arithmetic and copies ran while one was open for 2% of the time, Pallas kernels for 29%

profile of v6, /device:TPU:0, one launch (start us, length us, event | category | flops | bytes accessed | tf_op | source)
XLA Modules:
  0.0 386.8 jit_solution(10158287853565116978)
XLA Ops:
  12.0 21.8 %collective-permute-done.1.refs_1_ = bf16[512,1024]{1,0:T(8,128)(2,1)} collective-permute-done((bf16[512,1024]{1,0:T(8,128)(2,1)}, bf16[512,1024]{1,0:T(8,128)(2,1)}, u32[]{:S(2)}, u32[]{:S(2)}) %collective-permute-start.1) | collective-permute-done | bytes 1048608 | tf_op jit(solution)/shard_map/ppermute | solution.py:331
  39.4 5.8 %collective-permute-done.4 = bf16[8,128,128]{2,1,0:T(8,128)(2,1)S(1)} collective-permute-done((bf16[8,128,128]{2,1,0:T(8,128)(2,1)S(1)}, bf16[8,128,128]{2,1,0:T(8,128)(2,1)S(1)}, u32[]{:S(2)}, u32[]{:S(2)}) %collective-permute-start.4) | collective-permute-done | bytes 262176 | tf_op jit(solution)/shard_map/ppermute | solution.py:26
  46.8 5.1 %collective-permute-done.5 = bf16[8,128,128]{2,1,0:T(8,128)(2,1)S(1)} collective-permute-done((bf16[8,128,128]{2,1,0:T(8,128)(2,1)S(1)}, bf16[8,128,128]{2,1,0:T(8,128)(2,1)S(1)}, u32[]{:S(2)}, u32[]{:S(2)}) %collective-permute-start.5) | collective-permute-done | bytes 262176 | tf_op jit(solution)/shard_map/ppermute | solution.py:26
  54.3 4.9 %collective-permute-start.6 = (bf16[8,128,128]{2,1,0:T(8,128)(2,1)}, bf16[8,128,128]{2,1,0:T(8,128)(2,1)}, u32[]{:S(2)}, u32[]{:S(2)}) collective-permute-start(bf16[8,128,128]{2,1,0:T(8,128)(2,1)} %fusion.3), channel_id=1, source_target_pairs={{0,16},{4,20},{8,24},{12,28},{1,17},{5,21},{9,25},{13,29},{2,18},{... | collective-permute-start | bytes 786440 | tf_op jit(solution)/shard_map/ppermute | solution.py:48
  66.8 3.8 shard_map.88
  74.7 8.5 %collective-permute-start.2 = (bf16[512,1024]{1,0:T(8,128)(2,1)}, bf16[512,1024]{1,0:T(8,128)(2,1)}, u32[]{:S(2)}, u32[]{:S(2)}) collective-permute-start(bf16[512,1024]{1,0:T(8,128)(2,1)} %refs_0_.1), channel_id=1, source_target_pairs={{0,1},{1,0},{2,3},{3,2},{4,5},{5,4},{6,7},{7,6},{8,9},{9,8},{10,11... | collective-permute-start | bytes 3145736 | tf_op jit(solution)/shard_map/ppermute | solution.py:331
  88.6 12.2 %shard_map.89 = (bf16[512,1024]{1,0:T(8,128)(2,1)S(1)}, f32[8,128,128]{2,1,0:T(8,128)S(1)}, bf16[8,128,128]{2,1,0:T(8,128)(2,1)}) custom-call(s32[4]{0:T(128)S(1)} %pad_add_fusion.index, bf16[512,1024]{1,0:T(8,128)(2,1)S(1)} %copy-done.18, bf16[512,1024]{1,0:T(8,128)(2,1)} %collective-permute-done.1.refs_1_, ...), custom_call_target="tpu_custom_call" | custom-call | flops 4294967296 | bytes 12582912 | tf_op jit(solution)/shard_map/pallas_call | solution.py:147
  100.8 4.4 %shard_map.90 = (bf16[512,512]{1,0:T(8,128)(2,1)S(1)}, bf16[512,512]{1,0:T(8,128)(2,1)}) custom-call(bf16[512,1024]{1,0:T(8,128)(2,1)S(1)} %get-tuple-element.78.pre, bf16[512,1024]{1,0:T(8,128)(2,1)S(1)} %copy-done, bf16[512,1024]{1,0:T(8,128)(2,1)S(1)} %copy-done.1, bf16[8,128,128]{2,1,0:T(8,128)(2,1)S(1)} %fusion.2.state), custom_call_target="tpu_custom_call" | custom-call | flops 1073741824 | bytes 3407872 | tf_op jit(solution)/shard_map/pallas_call | solution.py:216
  109.0 5.2 %collective-permute-done.8 = bf16[8,128,128]{2,1,0:T(8,128)(2,1)S(1)} collective-permute-done((bf16[8,128,128]{2,1,0:T(8,128)(2,1)}, bf16[8,128,128]{2,1,0:T(8,128)(2,1)S(1)}, u32[]{:S(2)}, u32[]{:S(2)}) %collective-permute-start.8) | collective-permute-done | bytes 262176 | tf_op jit(solution)/shard_map/ppermute | solution.py:26
  120.1 4.2 %shard_map.93 = bf16[1024,512]{1,0:T(8,128)(2,1)} custom-call(s32[8]{0:T(128)S(1)} %concatenate.4.index, bf16[512,4096]{1,0:T(8,128)(2,1)} %all-gather.3.cloned.1.call-done.mine.theirs, bf16[512,4096]{1,0:T(8,128)(2,1)} %all-gather.3.cloned.1.call-done.mine.theirs, bf16[512,512]{1,0:T(8,128)(2,1)S(1)} %get-tuple-element.75.grad, ...), custom_call_target="tpu_custom_call" | custom-call | flops 1073741824 | bytes 3145728 | tf_op jit(solution)/shard_map/pallas_call | solution.py:269
  126.0 10.6 %collective-permute-done.9 = bf16[8,128,128]{2,1,0:T(8,128)(2,1)} collective-permute-done((bf16[8,128,128]{2,1,0:T(8,128)(2,1)}, bf16[8,128,128]{2,1,0:T(8,128)(2,1)}, u32[]{:S(2)}, u32[]{:S(2)}) %collective-permute-start.9) | collective-permute-done | bytes 262176 | tf_op jit(solution)/shard_map/ppermute | solution.py:26
  139.9 4.5 %shard_map.94 = bf16[1024,512]{1,0:T(8,128)(2,1)} custom-call(s32[8]{0:T(128)S(1)} %concatenate.4.index, bf16[512,4096]{1,0:T(8,128)(2,1)} %all-gather.3.cloned.1.call-done.mine.theirs, bf16[512,4096]{1,0:T(8,128)(2,1)} %all-gather.3.cloned.1.call-done.mine.theirs, bf16[512,512]{1,0:T(8,128)(2,1)} %get-tuple-element.87.grad, ...), custom_call_target="tpu_custom_call" | custom-call | flops 1073741824 | bytes 3145728 | tf_op jit(solution)/shard_map/pallas_call | solution.py:269
  147.0 8.0 %shard_map.91 = (f32[512,1024]{1,0:T(8,128)}, f32[512,1024]{1,0:T(8,128)}) custom-call(bf16[512,1024]{1,0:T(8,128)(2,1)S(1)} %copy-done.24, bf16[512,1024]{1,0:T(8,128)(2,1)S(1)} %copy-done.4, bf16[512,1024]{1,0:T(8,128)(2,1)S(1)} %copy-done, bf16[512,1024]{1,0:T(8,128)(2,1)S(1)} %copy-done.1), custom_call_target="tpu_custom_call" | custom-call | flops 1610612736 | bytes 4194304 | tf_op jit(solution)/shard_map/pallas_call | solution.py:216
  164.7 4.0 %collective-permute-start.19 = (bf16[512,512]{1,0:T(8,128)(2,1)}, bf16[512,512]{1,0:T(8,128)(2,1)}, u32[]{:S(2)}, u32[]{:S(2)}) collective-permute-start(bf16[512,512]{1,0:T(8,128)(2,1)} %shard_map.95), channel_id=1, source_target_pairs={{0,16},{4,20},{8,24},{12,28},{16,0},{20,4},{24,8},{28,12},{1,17},{... | collective-permute-start | bytes 1572872 | tf_op jit(solution)/shard_map/ppermute | solution.py:26
  178.8 12.8 %collective-permute-done.19.rest_1_ = bf16[512,512]{1,0:T(8,128)(2,1)} collective-permute-done((bf16[512,512]{1,0:T(8,128)(2,1)}, bf16[512,512]{1,0:T(8,128)(2,1)}, u32[]{:S(2)}, u32[]{:S(2)}) %collective-permute-start.19) | collective-permute-done | bytes 524320 | tf_op jit(solution)/shard_map/ppermute | solution.py:26
  191.7 3.9 %shard_map.98.rest_2_ = f32[3,512,1024]{2,1,0:T(8,128)} custom-call(s32[8]{0:T(128)S(1)} %concatenate.4.index, bf16[512,4096]{1,0:T(8,128)(2,1)} %all-gather.3.cloned.1.call-done.mine.theirs, bf16[512,4096]{1,0:T(8,128)(2,1)} %all-gather.3.cloned.1.call-done.mine.theirs, bf16[512,512]{1,0:T(8,128)(2,1)S(1)} %copy-done.16, ...), custom_call_target="tpu_custom_call" | custom-call | flops 536870912 | bytes 1572864 | tf_op jit(solution)/shard_map/pallas_call | solution.py:269
  205.2 32.8 %collective-permute-done.21.rest_1_ = bf16[512,512]{1,0:T(8,128)(2,1)S(1)} collective-permute-done((bf16[512,512]{1,0:T(8,128)(2,1)S(1)}, bf16[512,512]{1,0:T(8,128)(2,1)S(1)}, u32[]{:S(2)}, u32[]{:S(2)}) %collective-permute-start.21) | collective-permute-done | bytes 524320 | tf_op jit(solution)/shard_map/ppermute | solution.py:26
  238.0 3.9 %shard_map.101.rest_2_ = f32[3,512,1024]{2,1,0:T(8,128)} custom-call(s32[8]{0:T(128)S(1)} %concatenate.4.index, bf16[512,4096]{1,0:T(8,128)(2,1)} %all-gather.3.cloned.1.call-done.mine.theirs, bf16[512,4096]{1,0:T(8,128)(2,1)} %all-gather.3.cloned.1.call-done.mine.theirs, bf16[512,512]{1,0:T(8,128)(2,1)} %get-tuple-element.87.grad, ...), custom_call_target="tpu_custom_call", output_to_operand_aliasing={{}: (7, {})} | custom-call | flops 536870912 | bytes 1572864 | tf_op jit(solution)/shard_map/pallas_call | solution.py:269
  259.3 4.7 %collective-permute-done.24.rest_0_ = bf16[1024,512]{1,0:T(8,128)(2,1)S(1)} collective-permute-done((bf16[1024,512]{1,0:T(8,128)(2,1)S(1)}, bf16[1024,512]{1,0:T(8,128)(2,1)S(1)}, u32[]{:S(2)}, u32[]{:S(2)}) %collective-permute-start.24) | collective-permute-done | bytes 1048608 | tf_op jit(solution)/shard_map/ppermute | solution.py:26
  266.6 26.0 %collective-permute-done.25.rest_1_ = bf16[512,512]{1,0:T(8,128)(2,1)S(1)} collective-permute-done((bf16[512,512]{1,0:T(8,128)(2,1)S(1)}, bf16[512,512]{1,0:T(8,128)(2,1)S(1)}, u32[]{:S(2)}, u32[]{:S(2)}) %collective-permute-start.25) | collective-permute-done | bytes 524320 | tf_op jit(solution)/shard_map/ppermute | solution.py:26
  311.2 14.7 %collective-permute-done.28.rest_0_ = bf16[1024,512]{1,0:T(8,128)(2,1)S(1)} collective-permute-done((bf16[1024,512]{1,0:T(8,128)(2,1)S(1)}, bf16[1024,512]{1,0:T(8,128)(2,1)S(1)}, u32[]{:S(2)}, u32[]{:S(2)}) %collective-permute-start.28) | collective-permute-done | bytes 1048608 | tf_op jit(solution)/shard_map/ppermute | solution.py:26
  328.5 15.1 %collective-permute-done.29.rest_1_ = bf16[512,512]{1,0:T(8,128)(2,1)S(1)} collective-permute-done((bf16[512,512]{1,0:T(8,128)(2,1)S(1)}, bf16[512,512]{1,0:T(8,128)(2,1)S(1)}, u32[]{:S(2)}, u32[]{:S(2)}) %collective-permute-start.29) | collective-permute-done | bytes 524320 | tf_op jit(solution)/shard_map/ppermute | solution.py:26
  349.6 16.4 %collective-permute-done.31.rest_1_ = bf16[512,512]{1,0:T(8,128)(2,1)S(1)} collective-permute-done((bf16[512,512]{1,0:T(8,128)(2,1)S(1)}, bf16[512,512]{1,0:T(8,128)(2,1)S(1)}, u32[]{:S(2)}, u32[]{:S(2)}) %collective-permute-start.31) | collective-permute-done | bytes 524320 | tf_op jit(solution)/shard_map/ppermute | solution.py:26
  369.5 7.1 %collective-permute-done.32.rest_1_ = bf16[512,512]{1,0:T(8,128)(2,1)S(1)} collective-permute-done((bf16[512,512]{1,0:T(8,128)(2,1)S(1)}, bf16[512,512]{1,0:T(8,128)(2,1)S(1)}, u32[]{:S(2)}, u32[]{:S(2)}) %collective-permute-start.32) | collective-permute-done | bytes 524320 | tf_op jit(solution)/shard_map/ppermute | solution.py:26
  (146 shorter events, 131.9 us)
Async XLA Ops:
  7.2 113.0 %all-gather.3.cloned.1.call-start = ((), (), s32[]{:S(2)}) async-start(), calls=%async_computation | async-start | bytes 5242880 | tf_op jit(solution)/shard_map/all_gather | solution.py:360
  7.2 26.5 %collective-permute-start.1 = (bf16[512,1024]{1,0:T(8,128)(2,1)}, bf16[512,1024]{1,0:T(8,128)(2,1)}, u32[]{:S(2)}, u32[]{:S(2)}) collective-permute-start(bf16[512,1024]{1,0:T(8,128)(2,1)} %refs_0_.1), channel_id=1, source_target_pairs={{0,2},{1,3},{2,0},{3,1},{4,6},{5,7},{6,4},{7,5},{8,10},{9,11},{10,... | collective-permute-start | bytes 3145736 | tf_op jit(solution)/shard_map/ppermute | solution.py:331
  10.3 23.5 %collective-permute-start = (bf16[512,1024]{1,0:T(8,128)(2,1)}, bf16[512,1024]{1,0:T(8,128)(2,1)}, u32[]{:S(2)}, u32[]{:S(2)}) collective-permute-start(bf16[512,1024]{1,0:T(8,128)(2,1)} %param.7), channel_id=1, source_target_pairs={{1,8},{3,10},{5,12},{7,14},{8,1},{10,3},{12,5},{14,7},{17,24},{19,... | collective-permute-start | bytes 3145736 | tf_op jit(solution)/shard_map/ppermute | solution.py:313
  36.1 133.0 %all-gather.5.cloned.1.call-start = ((), (), s32[]{:S(2)}) async-start(), calls=%async_computation.1 | async-start | bytes 5242880 | tf_op jit(solution)/shard_map/all_gather | solution.py:360
  51.9 21.7 %collective-permute-start.13 = (bf16[512,1024]{1,0:T(8,128)(2,1)}, bf16[512,1024]{1,0:T(8,128)(2,1)}, u32[]{:S(2)}, u32[]{:S(2)}) collective-permute-start(bf16[512,1024]{1,0:T(8,128)(2,1)} %refs_0_.1), channel_id=1, source_target_pairs={{1,8},{3,10},{5,12},{7,14},{8,1},{10,3},{12,5},{14,7},{17,24},{19,... | collective-permute-start | bytes 3145736 | tf_op jit(solution)/shard_map/ppermute | solution.py:313
  107.1 32.8 %collective-permute-start.15 = (bf16[512,512]{1,0:T(8,128)(2,1)}, bf16[512,512]{1,0:T(8,128)(2,1)}, u32[]{:S(2)}, u32[]{:S(2)}) collective-permute-start(bf16[512,512]{1,0:T(8,128)(2,1)} %get-tuple-element.87.grad), channel_id=1, source_target_pairs={{0,8},{4,12},{8,0},{12,4},{16,24},{20,28},{24,16},{28,20},{1,9},{5... | collective-permute-start | bytes 1572872 | tf_op jit(solution)/shard_map/ppermute | solution.py:26
  124.4 36.8 %collective-permute-start.17 = (bf16[1024,512]{1,0:T(8,128)(2,1)}, bf16[1024,512]{1,0:T(8,128)(2,1)}, u32[]{:S(2)}, u32[]{:S(2)}) collective-permute-start(bf16[1024,512]{1,0:T(8,128)(2,1)} %shard_map.93), channel_id=1, source_target_pairs={{0,4},{4,0},{8,12},{12,8},{16,20},{20,16},{24,28},{28,24},{1,5},{5... | collective-permute-start | bytes 3145736 | tf_op jit(solution)/shard_map/ppermute | solution.py:26
  144.4 31.5 %collective-permute-start.18 = (bf16[1024,512]{1,0:T(8,128)(2,1)}, bf16[1024,512]{1,0:T(8,128)(2,1)}, u32[]{:S(2)}, u32[]{:S(2)}) collective-permute-start(bf16[1024,512]{1,0:T(8,128)(2,1)} %shard_map.94), channel_id=1, source_target_pairs={{0,4},{4,0},{8,12},{12,8},{16,20},{20,16},{24,28},{28,24},{1,5},{5... | collective-permute-start | bytes 3145736 | tf_op jit(solution)/shard_map/ppermute | solution.py:26
  164.7 26.9 %collective-permute-start.19 = (bf16[512,512]{1,0:T(8,128)(2,1)}, bf16[512,512]{1,0:T(8,128)(2,1)}, u32[]{:S(2)}, u32[]{:S(2)}) collective-permute-start(bf16[512,512]{1,0:T(8,128)(2,1)} %shard_map.95), channel_id=1, source_target_pairs={{0,16},{4,20},{8,24},{12,28},{16,0},{20,4},{24,8},{28,12},{1,17},{... | collective-permute-start | bytes 1572872 | tf_op jit(solution)/shard_map/ppermute | solution.py:26
  168.7 26.8 %collective-permute-start.14 = (bf16[512,512]{1,0:T(8,128)(2,1)S(1)}, bf16[512,512]{1,0:T(8,128)(2,1)}, u32[]{:S(2)}, u32[]{:S(2)}) collective-permute-start(bf16[512,512]{1,0:T(8,128)(2,1)S(1)} %copy-done.7), channel_id=1, source_target_pairs={{0,8},{4,12},{8,0},{12,4},{16,24},{20,28},{24,16},{28,20},{1,9},{5... | collective-permute-start | bytes 1572872 | tf_op jit(solution)/shard_map/ppermute | solution.py:26
  173.5 26.3 %collective-permute-start.20 = (bf16[512,1024]{1,0:T(8,128)(2,1)S(1)}, bf16[512,1024]{1,0:T(8,128)(2,1)S(1)}, u32[]{:S(2)}, u32[]{:S(2)}) collective-permute-start(bf16[512,1024]{1,0:T(8,128)(2,1)S(1)} %shard_map.96), channel_id=1, source_target_pairs={{0,4},{4,0},{8,12},{12,8},{16,20},{20,16},{24,28},{28,24},{1,5},{5... | collective-permute-start | bytes 3145736 | tf_op jit(solution)/shard_map/ppermute | solution.py:26
  174.1 67.8 %collective-permute-start.12 = (bf16[512,1024]{1,0:T(8,128)(2,1)S(1)}, bf16[512,1024]{1,0:T(8,128)(2,1)S(1)}, u32[]{:S(2)}, u32[]{:S(2)}) collective-permute-start(bf16[512,1024]{1,0:T(8,128)(2,1)S(1)} %get-tuple-element.82.grad), channel_id=1, source_target_pairs={{0,8},{4,12},{8,0},{12,4},{16,24},{20,28},{24,16},{28,20},{1,9},{5... | collective-permute-start | bytes 3145736 | tf_op jit(solution)/shard_map/ppermute | solution.py:26
  199.1 47.7 %collective-permute-start.22 = (bf16[512,1024]{1,0:T(8,128)(2,1)S(1)}, bf16[512,1024]{1,0:T(8,128)(2,1)S(1)}, u32[]{:S(2)}, u32[]{:S(2)}) collective-permute-start(bf16[512,1024]{1,0:T(8,128)(2,1)S(1)} %shard_map.99), channel_id=1, source_target_pairs={{0,4},{4,0},{8,12},{12,8},{16,20},{20,16},{24,28},{28,24},{1,5},{5... | collective-permute-start | bytes 3145736 | tf_op jit(solution)/shard_map/ppermute | solution.py:26
  199.7 38.3 %collective-permute-start.21 = (bf16[512,512]{1,0:T(8,128)(2,1)S(1)}, bf16[512,512]{1,0:T(8,128)(2,1)S(1)}, u32[]{:S(2)}, u32[]{:S(2)}) collective-permute-start(bf16[512,512]{1,0:T(8,128)(2,1)S(1)} %shard_map.97), channel_id=1, source_target_pairs={{0,16},{4,20},{8,24},{12,28},{16,0},{20,4},{24,8},{28,12},{1,17},{... | collective-permute-start | bytes 1572872 | tf_op jit(solution)/shard_map/ppermute | solution.py:26
  202.2 47.2 %collective-permute-start.23 = (bf16[512,512]{1,0:T(8,128)(2,1)S(1)}, bf16[512,512]{1,0:T(8,128)(2,1)S(1)}, u32[]{:S(2)}, u32[]{:S(2)}) collective-permute-start(bf16[512,512]{1,0:T(8,128)(2,1)S(1)} %shard_map.100), channel_id=1, source_target_pairs={{0,16},{4,20},{8,24},{12,28},{16,0},{20,4},{24,8},{28,12},{1,17},{... | collective-permute-start | bytes 1572872 | tf_op jit(solution)/shard_map/ppermute | solution.py:26
  246.8 49.4 %collective-permute-start.11 = (bf16[512,1024]{1,0:T(8,128)(2,1)S(1)}, bf16[512,1024]{1,0:T(8,128)(2,1)S(1)}, u32[]{:S(2)}, u32[]{:S(2)}) collective-permute-start(bf16[512,1024]{1,0:T(8,128)(2,1)S(1)} %get-tuple-element.81.grad), channel_id=1, source_target_pairs={{0,8},{4,12},{8,0},{12,4},{16,24},{20,28},{24,16},{28,20},{1,9},{5... | collective-permute-start | bytes 3145736 | tf_op jit(solution)/shard_map/ppermute | solution.py:26
  256.3 44.5 %collective-permute-start.26 = (bf16[1024,512]{1,0:T(8,128)(2,1)S(1)}, bf16[1024,512]{1,0:T(8,128)(2,1)S(1)}, u32[]{:S(2)}, u32[]{:S(2)}) collective-permute-start(bf16[1024,512]{1,0:T(8,128)(2,1)S(1)} %shard_map.105), channel_id=1, source_target_pairs={{0,4},{4,0},{8,12},{12,8},{16,20},{20,16},{24,28},{28,24},{1,5},{5... | collective-permute-start | bytes 3145736 | tf_op jit(solution)/shard_map/ppermute | solution.py:26
  256.9 35.7 %collective-permute-start.25 = (bf16[512,512]{1,0:T(8,128)(2,1)S(1)}, bf16[512,512]{1,0:T(8,128)(2,1)S(1)}, u32[]{:S(2)}, u32[]{:S(2)}) collective-permute-start(bf16[512,512]{1,0:T(8,128)(2,1)S(1)} %shard_map.103), channel_id=1, source_target_pairs={{0,16},{4,20},{8,24},{12,28},{16,0},{20,4},{24,8},{28,12},{1,17},{... | collective-permute-start | bytes 1572872 | tf_op jit(solution)/shard_map/ppermute | solution.py:26
  266.5 36.8 %collective-permute-start.27 = (bf16[512,512]{1,0:T(8,128)(2,1)S(1)}, bf16[512,512]{1,0:T(8,128)(2,1)S(1)}, u32[]{:S(2)}, u32[]{:S(2)}) collective-permute-start(bf16[512,512]{1,0:T(8,128)(2,1)S(1)} %shard_map.106), channel_id=1, source_target_pairs={{0,16},{4,20},{8,24},{12,28},{16,0},{20,4},{24,8},{28,12},{1,17},{... | collective-permute-start | bytes 1572872 | tf_op jit(solution)/shard_map/ppermute | solution.py:26
  299.7 26.2 %collective-permute-start.28 = (bf16[1024,512]{1,0:T(8,128)(2,1)S(1)}, bf16[1024,512]{1,0:T(8,128)(2,1)S(1)}, u32[]{:S(2)}, u32[]{:S(2)}) collective-permute-start(bf16[1024,512]{1,0:T(8,128)(2,1)S(1)} %shard_map.108), channel_id=1, source_target_pairs={{0,4},{4,0},{8,12},{12,8},{16,20},{20,16},{24,28},{28,24},{1,5},{5... | collective-permute-start | bytes 3145736 | tf_op jit(solution)/shard_map/ppermute | solution.py:26
  310.1 36.9 %collective-permute-start.30 = (bf16[1024,512]{1,0:T(8,128)(2,1)S(1)}, bf16[1024,512]{1,0:T(8,128)(2,1)S(1)}, u32[]{:S(2)}, u32[]{:S(2)}) collective-permute-start(bf16[1024,512]{1,0:T(8,128)(2,1)S(1)} %shard_map.111), channel_id=1, source_target_pairs={{0,4},{4,0},{8,12},{12,8},{16,20},{20,16},{24,28},{28,24},{1,5},{5... | collective-permute-start | bytes 3145736 | tf_op jit(solution)/shard_map/ppermute | solution.py:26
  311.2 32.4 %collective-permute-start.29 = (bf16[512,512]{1,0:T(8,128)(2,1)S(1)}, bf16[512,512]{1,0:T(8,128)(2,1)S(1)}, u32[]{:S(2)}, u32[]{:S(2)}) collective-permute-start(bf16[512,512]{1,0:T(8,128)(2,1)S(1)} %shard_map.109), channel_id=1, source_target_pairs={{0,16},{4,20},{8,24},{12,28},{16,0},{20,4},{24,8},{28,12},{1,17},{... | collective-permute-start | bytes 1572872 | tf_op jit(solution)/shard_map/ppermute | solution.py:26
  328.4 37.6 %collective-permute-start.31 = (bf16[512,512]{1,0:T(8,128)(2,1)S(1)}, bf16[512,512]{1,0:T(8,128)(2,1)S(1)}, u32[]{:S(2)}, u32[]{:S(2)}) collective-permute-start(bf16[512,512]{1,0:T(8,128)(2,1)S(1)} %shard_map.112), channel_id=1, source_target_pairs={{0,16},{4,20},{8,24},{12,28},{16,0},{20,4},{24,8},{28,12},{1,17},{... | collective-permute-start | bytes 1572872 | tf_op jit(solution)/shard_map/ppermute | solution.py:26
  349.5 27.0 %collective-permute-start.32 = (bf16[512,512]{1,0:T(8,128)(2,1)S(1)}, bf16[512,512]{1,0:T(8,128)(2,1)S(1)}, u32[]{:S(2)}, u32[]{:S(2)}) collective-permute-start(bf16[512,512]{1,0:T(8,128)(2,1)S(1)} %shard_map.114), channel_id=1, source_target_pairs={{0,16},{4,20},{8,24},{12,28},{16,0},{20,4},{24,8},{28,12},{1,17},{... | collective-permute-start | bytes 1572872 | tf_op jit(solution)/shard_map/ppermute | solution.py:26
  (39 other events, 443.7 us)
Sparse Core Ops, SparseCore 0:
  36.2 35.9 all-gather.2
  74.8 43.3 all-gather.4

commit v7 on v6

--- a/solution.py
+++ b/solution.py
@@ -13,8 +13,7 @@
 PARAMS = pltpu.CompilerParams(vmem_limit_bytes=48 * 1024 * 1024)
 
 
-def cost(flops, moved):
-    return pl.CostEstimate(flops=int(flops), bytes_accessed=int(moved), transcendentals=0)
+COST = pl.CostEstimate(flops=10**10, bytes_accessed=1, transcendentals=0)
 
 
 def after(array, *others):
@@ -34,7 +33,7 @@
     for bit in range(bits):
         step = 1 << bit
         if waits and bit in waits:
-            low = after(low, *waits[bit])
+            low = after(low, *waits[bit](came))
         sent.append(low)
         if bit < bits - 1:
             came.append(flip(low, bit))
@@ -119,10 +118,8 @@
         second[...] = found
 
 
-def pre_kernel(blocks, index, *refs):
-    cots, weights = refs[:blocks], refs[blocks : 2 * blocks]
-    attention, q, gain, pre, out, low = refs[2 * blocks :]
-    gated_grad = sum(mm_t(c[...], w[...]) for c, w in zip(cots, weights))
+def pre_kernel(cot, weight, attention, q, gain, pre, out, low):
+    gated_grad = mm_t(cot[...], weight[...])
     for i, cols in enumerate(head_slices(q)):
         value = attention[:, cols]
         rms = jnp.sqrt(jnp.mean(value * value, axis=-1, keepdims=True) + 1e-05)
@@ -135,35 +132,6 @@
         low[i] = out[i].astype(BF16)
 
 
-def pre_grad_of(cots, places, weight, attention, q, gain):
-    tokens, width = q.shape
-    pair = 2 * HEAD_DIM
-    part = cots[0].shape[1]
-    blocks = len(cots)
-    rows = pl.BlockSpec((tokens, pair), lambda i, ix: (0, i))
-    heads = pl.BlockSpec((2, HEAD_DIM, HEAD_DIM), lambda i, ix: (i, 0, 0))
-    whole = pl.BlockSpec((tokens, part), lambda i, ix: (0, 0))
-    shape = (width // HEAD_DIM, HEAD_DIM, HEAD_DIM)
-    return pl.pallas_call(
-        functools.partial(pre_kernel, blocks),
-        grid_spec=pltpu.PrefetchScalarGridSpec(
-            num_scalar_prefetch=1,
-            grid=(width // pair,),
-            in_specs=[whole] * blocks
-            + [pl.BlockSpec((pair, part), lambda i, ix, j=j: (i, ix[j])) for j in range(blocks)]
-            + [rows, rows, pl.BlockSpec((1, pair), lambda i, ix: (0, i))],
-            out_specs=[rows, heads, heads],
-        ),
-        out_shape=[
-            jax.ShapeDtypeStruct((tokens, width), BF16),
-            jax.ShapeDtypeStruct(shape, F32),
-            jax.ShapeDtypeStruct(shape, BF16),
-        ],
-        compiler_params=PARAMS,
-        cost_estimate=cost(2 * tokens * width * part * blocks, 2 * (tokens + width) * part * blocks),
-    )(places, *cots, *[weight] * blocks, attention, q, gain)
-
-
 def query_kernel(pre, k, v, state, first, second):
     step, steps = pl.program_id(0), pl.num_programs(0)
     parts = []
@@ -194,7 +162,11 @@
         value_grad[:, cols] = (value_local[:, cols] + mm(k[:, cols], state[i])).astype(BF16)
 
 
-def by_heads(kernel, args, outs, flops):
+def without(kernel, first, count):
+    return lambda *refs: kernel(*refs[:first], *refs[first + count :])
+
+
+def by_heads(kernel, args, outs, waits=()):
     tokens = next(a.shape[0] for kind, a in args if kind == "rows")
     width = next(a.shape[1] for kind, a in args if kind == "rows")
     pair = 2 * HEAD_DIM
@@ -207,6 +179,11 @@
         "heads": pl.BlockSpec((2, HEAD_DIM, HEAD_DIM), lambda i: (i, 0, 0)),
         "gain": pl.BlockSpec((1, pair), lambda i: (0, i)),
     }
+    for kind, a in args:
+        if kind == "whole":
+            specs[kind] = pl.BlockSpec(a.shape, lambda i: (0, 0))
+        if kind == "weight":
+            specs[kind] = pl.BlockSpec((pair, a.shape[1]), lambda i: (i, 0))
     shapes = {
         "rows": (tokens, width),
         "first": (tokens, width // 2),
@@ -214,14 +191,14 @@
         "heads": (2 * count, HEAD_DIM, HEAD_DIM),
     }
     return pl.pallas_call(
-        kernel,
+        without(kernel, len(args), len(waits)),
         grid=(count,),
-        in_specs=[specs[kind] for kind, _ in args],
+        in_specs=[specs[kind] for kind, _ in args] + [pl.BlockSpec(memory_space=pl.ANY)] * len(waits),
         out_specs=[specs[kind] for kind, _ in outs],
         out_shape=[jax.ShapeDtypeStruct(shapes[kind], dtype) for kind, dtype in outs],
         compiler_params=PARAMS,
-        cost_estimate=cost(flops, sum(a.size * a.dtype.itemsize for _, a in args)),
-    )(*[a for _, a in args])
+        cost_estimate=COST,
+    )(*[a for _, a in args], *waits)
 
 
 def term_kernel(turned, adds, index, mine, theirs, grad, other, *rest):
@@ -235,7 +212,7 @@
     out[...] = total.astype(out.dtype)
 
 
-def term(features, grads, block, cols, turned, owned, start, count, received, target=None):
+def term(features, grads, block, cols, turned, owned, start, count, received, waits, target=None):
     mine, theirs, index = features
     grad, other = grads
     tokens, chunks = grad.shape[0], index.shape[0] // 2
@@ -253,7 +230,8 @@
         rows,
     ]
     in_specs += [tile(start - begun) for _, begun in received]
-    operands = [index, mine, theirs, grad, other, *[a for a, _ in received]]
+    in_specs += [pl.BlockSpec(memory_space=pl.ANY)] * len(waits)
+    operands = [index, mine, theirs, grad, other, *[a for a, _ in received], *waits]
     aliases = {}
     if target is None:
         out_spec, dtype = tile(0), BF16
@@ -274,7 +252,7 @@
         out_shape=jax.ShapeDtypeStruct(shape, dtype),
         input_output_aliases=aliases,
         compiler_params=PARAMS,
-        cost_estimate=cost(4 * tokens * cols * count * owned, 6 * tokens * count * owned),
+        cost_estimate=COST,
     )(*operands)
 
 
@@ -287,7 +265,6 @@
     tokens, width = query_rows.shape
     model = out_weight.shape[1]
     owned = model // size
-    work = tokens * width
 
     chunks = 1 << len(halving)
     order = []
@@ -324,62 +301,56 @@
     gain = norm_gain.reshape(1, width)
     q, k, v = ("rows", query_rows), ("rows", key_rows), ("rows", value_rows)
 
-    cots, toggles = [cotangent], [0]
-    toggle = head_size // 2
-    while toggle:
-        pairs = [(h, h ^ toggle) for h in range(head_size)]
-        cots += [lax.ppermute(block, "head", pairs) for block in cots]
-        toggles += [t ^ toggle for t in toggles]
-        toggle //= 2
-    places = jnp.stack([head_place ^ t for t in toggles]).astype(jnp.int32)
-
-    block_state, block_low = by_heads(
-        state_kernel, [k, v], [("heads", F32), ("heads", BF16)], 2 * work * HEAD_DIM
-    )
-    waits = {1: [cots[1]]}
-    if paired:
-        swapped_input = after(across(layer_input, 2, 1), cots[1])
-        swapped_input = jnp.where(aligned, layer_input, swapped_input)
+    gathered_cot = lax.all_gather(cotangent, "head", axis=1, tiled=True)
+
+    block_state, block_low = by_heads(state_kernel, [k, v], [("heads", F32), ("heads", BF16)])
+    partner = []
+
+    def partner_shard(came):
+        shard = after(across(cotangent, 2, 1), came[0])
+        partner.append(jnp.where(aligned, across(shard[:, owned:], 0, 1), shard[:, :owned]))
+        return partner
+
+    waits = {2: partner_shard} if paired else {}
     state_parts, sent, came = entering(block_state, block_low, False, waits)
-    (local,) = by_heads(
-        local_kernel, [q, k, ("rows", after(value_rows, sent[-1]))], [("rows", F32)], 3 * work * tokens
-    )
+    (local,) = by_heads(local_kernel, [q, k, v], [("rows", F32)], [sent[-1]])
     state_low = (state_parts[0] + after(state_parts[1], local).astype(F32)).astype(BF16)
     attention, *gated = by_heads(
         gated_kernel,
         [("rows", local), q, ("heads", state_low), ("gain", gain)],
         [("rows", F32), ("first", BF16), ("second", BF16)],
-        2 * work * HEAD_DIM,
     )
     if paired:
-        swapped_cot = across(after(cotangent, came[1]), 2, 1)
-        swapped_cot = jnp.where(aligned, cotangent, after(swapped_cot, attention))
-        index = jnp.concatenate([there, there ^ 2])
-        both_input, both_cot = (
-            (gathered, gathered, index)
-            for gathered in (lax.all_gather(a, "head", axis=1, tiled=True) for a in (swapped_input, swapped_cot))
-        )
+        partner_cot = lax.all_gather(partner[0], "head", axis=1, tiled=True)
+        side = 1 ^ ((position >> 1) & 1) ^ (there & 1)
+        both_cot = gathered_cot, partner_cot, jnp.concatenate([there, (there >> 2) * 2 + side])
+        swapped = across(after(layer_input, came[1]), 2, 1)
+        swapped = jnp.where(aligned, layer_input, after(swapped, attention))
+        gathered_input = lax.all_gather(swapped, "head", axis=1, tiled=True)
+        both_input = gathered_input, gathered_input, jnp.concatenate([there, there ^ 2])
     else:
-        both_input, both_cot = (
-            both(lax.all_gather(a, "head", axis=1, tiled=True)) for a in (layer_input, cotangent)
-        )
+        both_cot = both(gathered_cot)
+        both_input = both(lax.all_gather(layer_input, "head", axis=1, tiled=True))
     gated_first = gated[0], flip(gated[0], gather_bit)
 
-    pre, grad_block, grad_block_low = pre_grad_of(cots, places, out_weight, attention, query_rows, gain)
+    pre, grad_block, grad_block_low = by_heads(
+        pre_kernel,
+        [("whole", gathered_cot), ("weight", out_weight), ("rows", attention), q, ("gain", gain)],
+        [("rows", BF16), ("heads", F32), ("heads", BF16)],
+    )
     grad_parts, sent, came = entering(grad_block, grad_block_low, True)
-    pre_then = after(pre, gated_first[1])
     query_grad = by_heads(
         query_kernel,
-        [("rows", pre_then), k, v, ("heads", state_low)],
+        [("rows", pre), k, v, ("heads", state_low)],
         [("first", BF16), ("second", BF16)],
-        4 * work * tokens,
+        [gated_first[1]],
     )
     query_grad = [(part, flip(part, gather_bit)) for part in query_grad]
     key_local, value_local = by_heads(
         own_kernel,
-        [("rows", after(pre, query_grad[0][0], sent[1])), q, k, v],
+        [("rows", pre), q, k, v],
         [("rows", F32), ("rows", F32)],
-        6 * work * tokens,
+        [query_grad[0][0], sent[1]],
     )
     gated_second = after(gated[1], came[1])
     gated = [gated_first, (gated_second, flip(gated_second, gather_bit))]
@@ -388,50 +359,47 @@
         key_value_kernel,
         [("rows", key_local), ("rows", value_local), k, v, ("heads", grad_low)],
         [("rows", BF16), ("rows", BF16)],
-        4 * work * HEAD_DIM,
-    )
-    key_grad, value_grad = ((grad, flip(grad, gather_bit)) for grad in (key_grad, value_grad))
+    )
+    key_grad = key_grad, flip(key_grad, gather_bit)
+    value_grad = value_grad, flip(after(value_grad, key_grad[1]), gather_bit)
 
     half = width // 2
-    pieces = [(both_input, query_grad[i], 0, False, (0, 0, i)) for i in range(2)]
-    pieces += [(both_cot, gated[i], 0, True, (i, 0)) for i in range(2)]
+    pieces = [(both_cot, gated[i], 0, True, (i, 0)) for i in range(2)]
+    pieces += [(both_input, query_grad[i], 0, False, (0, 0, i)) for i in range(2)]
     pieces += [(both_input, key_grad, i, False, (1, 0, i)) for i in range(2)]
     pieces += [(both_input, value_grad, i, False, (2, 0, i)) for i in range(2)]
     starts = [chunks - (chunks >> i) for i in range(len(halving) + 1)]
     shapes = {True: (width, owned), False: (3, owned, width)}
     targets = {True: None, False: None}
     received = {}
-    last = [key_local]
+    last = [key_local, sent[-1]]
 
     def stage(i, n):
         features, (grad, other), block, turned, place = pieces[i]
-        other = after(other, last[0])
         came = received.setdefault(i, [])
-        if came:
-            came[-1] = (after(came[-1][0], last[0]), came[-1][1])
         final = n == len(halving)
         target = (targets[turned], shapes[turned], place) if final else None
         count = 1 if final else chunks >> (n + 1)
-        out = term(features, (grad, other), block, half, turned, owned, starts[n], count, came, target)
-        last[0] = out
+        out = term(features, (grad, other), block, half, turned, owned, starts[n], count, came, last, target)
+        last[:] = [out]
         if final:
             targets[turned] = out
         else:
             came.append((flip(out, halving[n]), starts[n + 1]))
 
     stages = len(halving) + 1
-    last[0] = after(last[0], sent[-1])
     stage(0, 0)
     stage(1, 0)
-    last[0] = after(last[0], key_grad[0])
-    for i in range(len(pieces) + 1):
+    last.append(key_grad[0])
+    for i in range(len(pieces)):
         for n in range(1, stages - 1):
-            if i < len(pieces):
-                stage(i, n)
+            stage(i, n)
+        if i + 2 < len(pieces):
+            last.extend(([], key_grad[1:], value_grad[1:])[min(i, 2)])
+            stage(i + 2, 0)
         if i >= 1:
             stage(i - 1, stages - 1)
-        if i + 2 < len(pieces):
-            stage(i + 2, 0)
+    stage(len(pieces) - 1, stages - 1)
     return (targets[False].transpose(1, 0, 2), targets[True])
 
 

time: 388 us -> 350 us (0.902)
  waiting for transfers between devices: 186 us -> 155 us
  starting transfers between devices: 50.4 us -> 33.8 us
  local copies, waits for them, and re-layouts: 9.11 us -> 23.4 us
  other arithmetic: 10.4 us -> 3.73 us
    ppermute x3 -> x0, waiting for transfers between devices: 25.8 us -> none  [body(): cots += [lax.ppermute(block, 'head', pairs) for block in cots]]
    ppermute x26, waiting for transfers between devices: 159 us -> 136 us  [flip(): return lax.ppermute(array, 'seq', [(i, i ^ 1 << bit) for i in range(size)])]
    unnamed x56 -> x55, local copies, waits for them, and re-layouts: 9.02 us -> 21.4 us
    ppermute x3 -> x0, starting transfers between devices: 11.6 us -> none  [body(): cots += [lax.ppermute(block, 'head', pairs) for block in cots]]
    ppermute x2, waiting for transfers between devices: 1.76 us -> 12.6 us  [entering(): came.append(lax.ppermute(low, 'seq', pairs))]
    ppermute x2 -> x3, waiting for transfers between devices: 0.01 us -> 5.39 us  [across(): return lax.ppermute(array, ('seq', 'head'), pairs)]
    ppermute x26, starting transfers between devices: 28.8 us -> 24.1 us  [flip(): return lax.ppermute(array, 'seq', [(i, i ^ 1 << bit) for i in range(size)])]
    convert_element_type x4, other arithmetic: 4.44 us -> 0.36 us  [entering(): low = total.astype(BF16)]
  transfers between devices with their start and end apart: 35 -> 34, of which waited for: 18 -> 16; matrix products, arithmetic and copies ran while one was open for 2% -> 4% of each run, Pallas kernels for 29% -> 33%
where the time goes in v7:
time: 350 us; the launch traced here: 348 us
  waiting for transfers between devices  155 us (44%)
  Pallas kernels  118 us (34%)
  starting transfers between devices  33.8 us (10%)
  local copies, waits for them, and re-layouts  23.4 us (7%)
  between operations  14.2 us (4%)
  other arithmetic  3.73 us (1%)
    ppermute x26, waiting for transfers between devices, flip(): return lax.ppermute(array, 'seq', [(i, i ^ 1 << bit) for i in range(size)])  136 us
    pallas_call x24, Pallas kernels, term(): pl.pallas_call(functools.partial(term_kernel, turned, len(received)), gri...  81.4 us
    pallas_call x7, Pallas kernels, by_heads(): pl.pallas_call(without(kernel, len(args), len(waits)), grid=(count,), in_...  36.6 us
    ppermute x26, starting transfers between devices, flip(): return lax.ppermute(array, 'seq', [(i, i ^ 1 << bit) for i in range(size)])  24.1 us
    unnamed x55, local copies, waits for them, and re-layouts  21.4 us
    ppermute x2, waiting for transfers between devices, entering(): came.append(lax.ppermute(low, 'seq', pairs))  12.6 us
  transfers between devices with their start and end apart: 34, of which 16 were waited for; matrix products, arithmetic and copies ran while one was open for 4% of the time, Pallas kernels for 33%

profile of v7, /device:TPU:0, one launch (start us, length us, event | category | flops | bytes accessed | tf_op | source)
XLA Modules:
  0.0 348.2 jit_solution(11320178836151180370)
XLA Ops:
  16.5 5.7 %collective-permute-done = bf16[8,128,128]{2,1,0:T(8,128)(2,1)S(1)} collective-permute-done((bf16[8,128,128]{2,1,0:T(8,128)(2,1)S(1)}, bf16[8,128,128]{2,1,0:T(8,128)(2,1)S(1)}, u32[]{:S(2)}, u32[]{:S(2)}) %collective-permute-start) | collective-permute-done | bytes 262176 | tf_op jit(solution)/shard_map/ppermute | solution.py:25
  25.4 5.4 %collective-permute-done.4 = bf16[512,512]{1,0:T(8,128)(2,1)S(1)} collective-permute-done((bf16[512,512]{1,0:T(8,128)(2,1)}, bf16[512,512]{1,0:T(8,128)(2,1)S(1)}, u32[]{:S(2)}, u32[]{:S(2)}) %collective-permute-start.4) | collective-permute-done | bytes 524320 | tf_op jit(solution)/shard_map/ppermute | solution.py:290
  34.8 6.6 %collective-permute-done.1 = bf16[8,128,128]{2,1,0:T(8,128)(2,1)S(1)} collective-permute-done((bf16[8,128,128]{2,1,0:T(8,128)(2,1)S(1)}, bf16[8,128,128]{2,1,0:T(8,128)(2,1)S(1)}, u32[]{:S(2)}, u32[]{:S(2)}) %collective-permute-start.1) | collective-permute-done | bytes 262176 | tf_op jit(solution)/shard_map/ppermute | solution.py:25
  42.2 4.5 %collective-permute-start.5 = (bf16[8,128,128]{2,1,0:T(8,128)(2,1)S(1)}, bf16[8,128,128]{2,1,0:T(8,128)(2,1)S(1)}, u32[]{:S(2)}, u32[]{:S(2)}) collective-permute-start(bf16[8,128,128]{2,1,0:T(8,128)(2,1)S(1)} %fusion.3.refs_3_), channel_id=1, source_target_pairs={{0,16},{4,20},{8,24},{12,28},{1,17},{5,21},{9,25},{13,29},{2,18},{... | collective-permute-start | bytes 786440 | tf_op jit(solution)/shard_map/ppermute | solution.py:47
  53.6 4.7 %shard_map.88 = (f32[512,1024]{1,0:T(8,128)S(1)}, bf16[512,512]{1,0:T(8,128)(2,1)S(1)}, bf16[512,512]{1,0:T(8,128)(2,1)}) custom-call(f32[512,1024]{1,0:T(8,128)} %copy-done.25, bf16[512,1024]{1,0:T(8,128)(2,1)S(1)} %copy-done.3, bf16[8,128,128]{2,1,0:T(8,128)(2,1)S(1)} %fusion.2.refs_2_.refs_3_, f32[1,1024]{1,0:T(1,128)S(1)} %bitcast.6), custom_call_target="tpu_custom_call" | custom-call | flops 10000000000 | bytes 1 | tf_op jit(solution)/shard_map/pallas_call | solution.py:193
  65.6 10.2 %shard_map.89 = (bf16[512,1024]{1,0:T(8,128)(2,1)S(1)}, f32[8,128,128]{2,1,0:T(8,128)S(1)}, bf16[8,128,128]{2,1,0:T(8,128)(2,1)S(1)}) custom-call(bf16[512,4096]{1,0:T(8,128)(2,1)} %all-gather.6.cloned.1.call-done.refs_0_.mine, bf16[1024,4096]{1,0:T(8,128)(2,1)} %refs_1_.9, f32[512,1024]{1,0:T(8,128)S(1)} %copy-done.24, bf16[512,1024]{1,0:T(8,128)(2,1)S(1)} %copy-done.3, ...), custom_call_target="tpu_custom_call" | custom-call | flops 10000000000 | bytes 1 | tf_op jit(solution)/shard_map/pallas_call | solution.py:193
  77.4 4.4 %shard_map.90 = (bf16[512,512]{1,0:T(8,128)(2,1)}, bf16[512,512]{1,0:T(8,128)(2,1)S(1)}) custom-call(bf16[512,1024]{1,0:T(8,128)(2,1)S(1)} %get-tuple-element.31.refs_0_, bf16[512,1024]{1,0:T(8,128)(2,1)S(1)} %copy-done.5, bf16[512,1024]{1,0:T(8,128)(2,1)S(1)} %copy-done.9, bf16[8,128,128]{2,1,0:T(8,128)(2,1)S(1)} %fusion.2.refs_2_.refs_3_, ...), custom_call_target="tpu_custom_call" | custom-call | flops 10000000000 | bytes 1 | tf_op jit(solution)/shard_map/pallas_call | solution.py:193
  83.9 8.0 %shard_map.91 = (f32[512,1024]{1,0:T(8,128)}, f32[512,1024]{1,0:T(8,128)}) custom-call(bf16[512,1024]{1,0:T(8,128)(2,1)S(1)} %get-tuple-element.31.refs_0_, bf16[512,1024]{1,0:T(8,128)(2,1)S(1)} %copy-done.3, bf16[512,1024]{1,0:T(8,128)(2,1)S(1)} %copy-done.5, bf16[512,1024]{1,0:T(8,128)(2,1)S(1)} %copy-done.9, ...), custom_call_target="tpu_custom_call" | custom-call | flops 10000000000 | bytes 1 | tf_op jit(solution)/shard_map/pallas_call | solution.py:193
  91.9 16.8 %collective-permute-done.8 = bf16[8,128,128]{2,1,0:T(8,128)(2,1)S(1)} collective-permute-done((bf16[8,128,128]{2,1,0:T(8,128)(2,1)S(1)}, bf16[8,128,128]{2,1,0:T(8,128)(2,1)S(1)}, u32[]{:S(2)}, u32[]{:S(2)}) %collective-permute-start.8) | collective-permute-done | bytes 262176 | tf_op jit(solution)/shard_map/ppermute | solution.py:25
  117.1 11.8 %collective-permute-done.9 = bf16[8,128,128]{2,1,0:T(8,128)(2,1)S(1)} collective-permute-done((bf16[8,128,128]{2,1,0:T(8,128)(2,1)S(1)}, bf16[8,128,128]{2,1,0:T(8,128)(2,1)S(1)}, u32[]{:S(2)}, u32[]{:S(2)}) %collective-permute-start.9) | collective-permute-done | bytes 262176 | tf_op jit(solution)/shard_map/ppermute | solution.py:47
  129.0 4.7 %shard_map.92 = (bf16[512,1024]{1,0:T(8,128)(2,1)S(1)}, bf16[512,1024]{1,0:T(8,128)(2,1)}) custom-call(f32[512,1024]{1,0:T(8,128)} %get-tuple-element.36.refs_0_.rest_0_, f32[512,1024]{1,0:T(8,128)} %get-tuple-element.37.refs_1_, bf16[512,1024]{1,0:T(8,128)(2,1)S(1)} %copy-done.6, bf16[512,1024]{1,0:T(8,128)(2,1)S(1)} %copy-done.10, ...), custom_call_target="tpu_custom_call" | custom-call | flops 10000000000 | bytes 1 | tf_op jit(solution)/shard_map/pallas_call | solution.py:193
  133.7 4.3 %shard_map.94.rest_1_ = bf16[512,1024]{1,0:T(8,128)(2,1)} custom-call(s32[8]{0:T(128)S(1)} %concatenate.9.index, bf16[512,4096]{1,0:T(8,128)(2,1)} %all-gather.6.cloned.1.call-done.refs_0_.mine, bf16[512,2048]{1,0:T(8,128)(2,1)S(1)} %copy-done.1, bf16[512,512]{1,0:T(8,128)(2,1)} %get-tuple-element.43.grad, bf16[512,512]{1,0:T(8,128)(2,1)} %collective-permute-done.13.other, ...), custom_call_target="tpu_custom_call" | custom-call | flops 10000000000 | bytes 1 | tf_op jit(solution)/shard_map/pallas_call | solution.py:247
  142.5 7.7 %collective-permute-start.20 = (bf16[512,512]{1,0:T(8,128)(2,1)}, bf16[512,512]{1,0:T(8,128)(2,1)}, u32[]{:S(2)}, u32[]{:S(2)}) collective-permute-start(bf16[512,512]{1,0:T(8,128)(2,1)} %shard_map.95.rest_0_), channel_id=1, source_target_pairs={{0,16},{4,20},{8,24},{12,28},{16,0},{20,4},{24,8},{28,12},{1,17},{... | collective-permute-start | bytes 1572872 | tf_op jit(solution)/shard_map/ppermute | solution.py:25
  150.2 14.8 %collective-permute-done.10.rest_1_.other = bf16[512,1024]{1,0:T(8,128)(2,1)S(1)} collective-permute-done((bf16[512,1024]{1,0:T(8,128)(2,1)S(1)}, bf16[512,1024]{1,0:T(8,128)(2,1)S(1)}, u32[]{:S(2)}, u32[]{:S(2)}) %collective-permute-start.10) | collective-permute-done | bytes 1048608 | tf_op jit(solution)/shard_map/ppermute | solution.py:25
  181.9 14.0 %collective-permute-done.19.rest_0_ = bf16[1024,512]{1,0:T(8,128)(2,1)S(1)} collective-permute-done((bf16[1024,512]{1,0:T(8,128)(2,1)S(1)}, bf16[1024,512]{1,0:T(8,128)(2,1)S(1)}, u32[]{:S(2)}, u32[]{:S(2)}) %collective-permute-start.19) | collective-permute-done | bytes 1048608 | tf_op jit(solution)/shard_map/ppermute | solution.py:25
  201.0 6.8 %collective-permute-done.11.rest_1_.other = bf16[512,1024]{1,0:T(8,128)(2,1)} collective-permute-done((bf16[512,1024]{1,0:T(8,128)(2,1)}, bf16[512,1024]{1,0:T(8,128)(2,1)}, u32[]{:S(2)}, u32[]{:S(2)}) %collective-permute-start.11) | collective-permute-done | bytes 1048608 | tf_op jit(solution)/shard_map/ppermute | solution.py:25
  226.6 11.0 %collective-permute-done.24.rest_1_ = bf16[512,512]{1,0:T(8,128)(2,1)S(1)} collective-permute-done((bf16[512,512]{1,0:T(8,128)(2,1)}, bf16[512,512]{1,0:T(8,128)(2,1)S(1)}, u32[]{:S(2)}, u32[]{:S(2)}) %collective-permute-start.24) | collective-permute-done | bytes 524320 | tf_op jit(solution)/shard_map/ppermute | solution.py:25
  247.7 12.4 %collective-permute-done.22.rest_1_ = bf16[512,512]{1,0:T(8,128)(2,1)S(1)} collective-permute-done((bf16[512,512]{1,0:T(8,128)(2,1)S(1)}, bf16[512,512]{1,0:T(8,128)(2,1)S(1)}, u32[]{:S(2)}, u32[]{:S(2)}) %collective-permute-start.22) | collective-permute-done | bytes 524320 | tf_op jit(solution)/shard_map/ppermute | solution.py:25
  266.3 3.8 %shard_map.110.rest_2_ = bf16[1024,512]{1,0:T(8,128)(2,1)S(1)} custom-call(s32[8]{0:T(128)S(1)} %concatenate.8.index, bf16[512,4096]{1,0:T(8,128)(2,1)} %all-gather.4.cloned.1.call-done.mine.theirs, bf16[512,4096]{1,0:T(8,128)(2,1)} %all-gather.4.cloned.1.call-done.mine.theirs, bf16[512,1024]{1,0:T(8,128)(2,1)} %get-tuple-element.40.grad, ...), custom_call_target="tpu_custom_call" | custom-call | flops 10000000000 | bytes 1 | tf_op jit(solution)/shard_map/pallas_call | solution.py:247
  270.3 12.2 %collective-permute-done.28.rest_1_ = bf16[512,512]{1,0:T(8,128)(2,1)S(1)} collective-permute-done((bf16[512,512]{1,0:T(8,128)(2,1)S(1)}, bf16[512,512]{1,0:T(8,128)(2,1)S(1)}, u32[]{:S(2)}, u32[]{:S(2)}) %collective-permute-start.28) | collective-permute-done | bytes 524320 | tf_op jit(solution)/shard_map/ppermute | solution.py:25
  288.9 16.1 %collective-permute-done.26.rest_1_ = bf16[512,512]{1,0:T(8,128)(2,1)S(1)} collective-permute-done((bf16[512,512]{1,0:T(8,128)(2,1)S(1)}, bf16[512,512]{1,0:T(8,128)(2,1)S(1)}, u32[]{:S(2)}, u32[]{:S(2)}) %collective-permute-start.26) | collective-permute-done | bytes 524320 | tf_op jit(solution)/shard_map/ppermute | solution.py:25
  311.4 16.1 %collective-permute-done.30.rest_1_ = bf16[512,512]{1,0:T(8,128)(2,1)S(1)} collective-permute-done((bf16[512,512]{1,0:T(8,128)(2,1)S(1)}, bf16[512,512]{1,0:T(8,128)(2,1)S(1)}, u32[]{:S(2)}, u32[]{:S(2)}) %collective-permute-start.30) | collective-permute-done | bytes 524320 | tf_op jit(solution)/shard_map/ppermute | solution.py:25
  327.4 3.8 %shard_map.115.rest_2_ = f32[3,512,1024]{2,1,0:T(8,128)} custom-call(s32[8]{0:T(128)S(1)} %concatenate.8.index, bf16[512,4096]{1,0:T(8,128)(2,1)} %all-gather.4.cloned.1.call-done.mine.theirs, bf16[512,4096]{1,0:T(8,128)(2,1)} %all-gather.4.cloned.1.call-done.mine.theirs, bf16[512,1024]{1,0:T(8,128)(2,1)} %get-tuple-element.40.grad, ...), custom_call_target="tpu_custom_call", output_to_operand_aliasing={{}: (8, {})} | custom-call | flops 10000000000 | bytes 1 | tf_op jit(solution)/shard_map/pallas_call | solution.py:247
  331.3 6.6 %copy.20.rest_3_ = f32[3,512,1024]{2,1,0:T(8,128)} copy(f32[3,512,1024]{2,1,0:T(8,128)} %shard_map.115.rest_2_) | data formatting | bytes 12582912
  (146 shorter events, 121.8 us)
Async XLA Ops:
  7.2 56.8 %all-gather.6.cloned.1.call-start = ((), (), s32[]{:S(2)}) async-start(), calls=%async_computation.1 | async-start | bytes 5242880 | tf_op jit(solution)/shard_map/all_gather | solution.py:304
  7.9 102.5 %all-gather.8.cloned.1.call-start = ((), (), s32[]{:S(2)}) async-start(), calls=%async_computation.2 | async-start | bytes 2621440 | tf_op jit(solution)/shard_map/all_gather | solution.py:324
  32.8 133.2 %all-gather.4.cloned.1.call-start = ((), (), s32[]{:S(2)}) async-start(), calls=%async_computation | async-start | bytes 5242880 | tf_op jit(solution)/shard_map/all_gather | solution.py:329
  81.7 91.5 %collective-permute-start.12 = (bf16[512,512]{1,0:T(8,128)(2,1)S(1)}, bf16[512,512]{1,0:T(8,128)(2,1)}, u32[]{:S(2)}, u32[]{:S(2)}) collective-permute-start(bf16[512,512]{1,0:T(8,128)(2,1)S(1)} %get-tuple-element.41.grad), channel_id=1, source_target_pairs={{0,8},{4,12},{8,0},{12,4},{16,24},{20,28},{24,16},{28,20},{1,9},{5... | collective-permute-start | bytes 1572872 | tf_op jit(solution)/shard_map/ppermute | solution.py:25
  81.8 84.2 %collective-permute-start.15 = (bf16[512,512]{1,0:T(8,128)(2,1)}, bf16[512,512]{1,0:T(8,128)(2,1)}, u32[]{:S(2)}, u32[]{:S(2)}) collective-permute-start(bf16[512,512]{1,0:T(8,128)(2,1)} %get-tuple-element.33.refs_4_.grad), channel_id=1, source_target_pairs={{0,8},{4,12},{8,0},{12,4},{16,24},{20,28},{24,16},{28,20},{1,9},{5... | collective-permute-start | bytes 1572872 | tf_op jit(solution)/shard_map/ppermute | solution.py:25
  83.8 24.9 %collective-permute-start.8 = (bf16[8,128,128]{2,1,0:T(8,128)(2,1)S(1)}, bf16[8,128,128]{2,1,0:T(8,128)(2,1)S(1)}, u32[]{:S(2)}, u32[]{:S(2)}) collective-permute-start(bf16[8,128,128]{2,1,0:T(8,128)(2,1)S(1)} %fusion.9.refs_5_), channel_id=1, source_target_pairs={{0,8},{4,12},{8,0},{12,4},{16,24},{20,28},{24,16},{28,20},{1,9},{5... | collective-permute-start | bytes 786440 | tf_op jit(solution)/shard_map/ppermute | solution.py:25
  110.3 23.4 %collective-permute-start.13 = (bf16[512,512]{1,0:T(8,128)(2,1)}, bf16[512,512]{1,0:T(8,128)(2,1)}, u32[]{:S(2)}, u32[]{:S(2)}) collective-permute-start(bf16[512,512]{1,0:T(8,128)(2,1)} %get-tuple-element.43.grad), channel_id=1, source_target_pairs={{0,8},{4,12},{8,0},{12,4},{16,24},{20,28},{24,16},{28,20},{1,9},{5... | collective-permute-start | bytes 1572872 | tf_op jit(solution)/shard_map/ppermute | solution.py:25
  133.7 31.3 %collective-permute-start.10 = (bf16[512,1024]{1,0:T(8,128)(2,1)S(1)}, bf16[512,1024]{1,0:T(8,128)(2,1)S(1)}, u32[]{:S(2)}, u32[]{:S(2)}) collective-permute-start(bf16[512,1024]{1,0:T(8,128)(2,1)S(1)} %get-tuple-element.39.rest_2_.grad), channel_id=1, source_target_pairs={{0,8},{4,12},{8,0},{12,4},{16,24},{20,28},{24,16},{28,20},{1,9},{5... | collective-permute-start | bytes 3145736 | tf_op jit(solution)/shard_map/ppermute | solution.py:25
  138.0 32.3 %collective-permute-start.14 = (bf16[512,1024]{1,0:T(8,128)(2,1)}, bf16[512,1024]{1,0:T(8,128)(2,1)}, u32[]{:S(2)}, u32[]{:S(2)}) collective-permute-start(bf16[512,1024]{1,0:T(8,128)(2,1)} %shard_map.94.rest_1_), channel_id=1, source_target_pairs={{0,4},{4,0},{8,12},{12,8},{16,20},{20,16},{24,28},{28,24},{1,5},{5... | collective-permute-start | bytes 3145736 | tf_op jit(solution)/shard_map/ppermute | solution.py:25
  142.5 35.8 %collective-permute-start.20 = (bf16[512,512]{1,0:T(8,128)(2,1)}, bf16[512,512]{1,0:T(8,128)(2,1)}, u32[]{:S(2)}, u32[]{:S(2)}) collective-permute-start(bf16[512,512]{1,0:T(8,128)(2,1)} %shard_map.95.rest_0_), channel_id=1, source_target_pairs={{0,16},{4,20},{8,24},{12,28},{16,0},{20,4},{24,8},{28,12},{1,17},{... | collective-permute-start | bytes 1572872 | tf_op jit(solution)/shard_map/ppermute | solution.py:25
  166.0 41.8 %collective-permute-start.11 = (bf16[512,1024]{1,0:T(8,128)(2,1)}, bf16[512,1024]{1,0:T(8,128)(2,1)}, u32[]{:S(2)}, u32[]{:S(2)}) collective-permute-start(bf16[512,1024]{1,0:T(8,128)(2,1)} %get-tuple-element.40.grad), channel_id=1, source_target_pairs={{0,8},{4,12},{8,0},{12,4},{16,24},{20,28},{24,16},{28,20},{1,9},{5... | collective-permute-start | bytes 3145736 | tf_op jit(solution)/shard_map/ppermute | solution.py:25
  169.7 26.2 %collective-permute-start.19 = (bf16[1024,512]{1,0:T(8,128)(2,1)S(1)}, bf16[1024,512]{1,0:T(8,128)(2,1)S(1)}, u32[]{:S(2)}, u32[]{:S(2)}) collective-permute-start(bf16[1024,512]{1,0:T(8,128)(2,1)S(1)} %shard_map.96.rest_1_), channel_id=1, source_target_pairs={{0,4},{4,0},{8,12},{12,8},{16,20},{20,16},{24,28},{28,24},{1,5},{5... | collective-permute-start | bytes 3145736 | tf_op jit(solution)/shard_map/ppermute | solution.py:25
  173.2 38.0 %collective-permute-start.18 = (bf16[512,512]{1,0:T(8,128)(2,1)S(1)}, bf16[512,512]{1,0:T(8,128)(2,1)S(1)}, u32[]{:S(2)}, u32[]{:S(2)}) collective-permute-start(bf16[512,512]{1,0:T(8,128)(2,1)S(1)} %shard_map.97.rest_0_), channel_id=1, source_target_pairs={{0,16},{4,20},{8,24},{12,28},{16,0},{20,4},{24,8},{28,12},{1,17},{... | collective-permute-start | bytes 1572872 | tf_op jit(solution)/shard_map/ppermute | solution.py:25
  176.7 41.6 %collective-permute-start.17 = (bf16[1024,512]{1,0:T(8,128)(2,1)S(1)}, bf16[1024,512]{1,0:T(8,128)(2,1)S(1)}, u32[]{:S(2)}, u32[]{:S(2)}) collective-permute-start(bf16[1024,512]{1,0:T(8,128)(2,1)S(1)} %shard_map.98.rest_2_), channel_id=1, source_target_pairs={{0,4},{4,0},{8,12},{12,8},{16,20},{20,16},{24,28},{28,24},{1,5},{5... | collective-permute-start | bytes 3145736 | tf_op jit(solution)/shard_map/ppermute | solution.py:25
  201.0 36.5 %collective-permute-start.24 = (bf16[512,512]{1,0:T(8,128)(2,1)}, bf16[512,512]{1,0:T(8,128)(2,1)S(1)}, u32[]{:S(2)}, u32[]{:S(2)}) collective-permute-start(bf16[512,512]{1,0:T(8,128)(2,1)} %shard_map.100.rest_0_), channel_id=1, source_target_pairs={{0,16},{4,20},{8,24},{12,28},{16,0},{20,4},{24,8},{28,12},{1,17},{... | collective-permute-start | bytes 1572872 | tf_op jit(solution)/shard_map/ppermute | solution.py:25
  211.1 30.3 %collective-permute-start.23 = (bf16[1024,512]{1,0:T(8,128)(2,1)S(1)}, bf16[1024,512]{1,0:T(8,128)(2,1)S(1)}, u32[]{:S(2)}, u32[]{:S(2)}) collective-permute-start(bf16[1024,512]{1,0:T(8,128)(2,1)S(1)} %shard_map.101.rest_2_), channel_id=1, source_target_pairs={{0,4},{4,0},{8,12},{12,8},{16,20},{20,16},{24,28},{28,24},{1,5},{5... | collective-permute-start | bytes 3145736 | tf_op jit(solution)/shard_map/ppermute | solution.py:25
  222.6 37.5 %collective-permute-start.22 = (bf16[512,512]{1,0:T(8,128)(2,1)S(1)}, bf16[512,512]{1,0:T(8,128)(2,1)S(1)}, u32[]{:S(2)}, u32[]{:S(2)}) collective-permute-start(bf16[512,512]{1,0:T(8,128)(2,1)S(1)} %shard_map.103.rest_0_), channel_id=1, source_target_pairs={{0,16},{4,20},{8,24},{12,28},{16,0},{20,4},{24,8},{28,12},{1,17},{... | collective-permute-start | bytes 1572872 | tf_op jit(solution)/shard_map/ppermute | solution.py:25
  225.9 37.8 %collective-permute-start.21 = (bf16[1024,512]{1,0:T(8,128)(2,1)S(1)}, bf16[1024,512]{1,0:T(8,128)(2,1)S(1)}, u32[]{:S(2)}, u32[]{:S(2)}) collective-permute-start(bf16[1024,512]{1,0:T(8,128)(2,1)S(1)} %shard_map.104.rest_2_), channel_id=1, source_target_pairs={{0,4},{4,0},{8,12},{12,8},{16,20},{20,16},{24,28},{28,24},{1,5},{5... | collective-permute-start | bytes 3145736 | tf_op jit(solution)/shard_map/ppermute | solution.py:25
  243.8 38.7 %collective-permute-start.28 = (bf16[512,512]{1,0:T(8,128)(2,1)S(1)}, bf16[512,512]{1,0:T(8,128)(2,1)S(1)}, u32[]{:S(2)}, u32[]{:S(2)}) collective-permute-start(bf16[512,512]{1,0:T(8,128)(2,1)S(1)} %shard_map.106.rest_0_), channel_id=1, source_target_pairs={{0,16},{4,20},{8,24},{12,28},{16,0},{20,4},{24,8},{28,12},{1,17},{... | collective-permute-start | bytes 1572872 | tf_op jit(solution)/shard_map/ppermute | solution.py:25
  247.6 38.5 %collective-permute-start.27 = (bf16[1024,512]{1,0:T(8,128)(2,1)S(1)}, bf16[1024,512]{1,0:T(8,128)(2,1)S(1)}, u32[]{:S(2)}, u32[]{:S(2)}) collective-permute-start(bf16[1024,512]{1,0:T(8,128)(2,1)S(1)} %shard_map.107.rest_2_), channel_id=1, source_target_pairs={{0,4},{4,0},{8,12},{12,8},{16,20},{20,16},{24,28},{28,24},{1,5},{5... | collective-permute-start | bytes 3145736 | tf_op jit(solution)/shard_map/ppermute | solution.py:25
  266.2 38.8 %collective-permute-start.26 = (bf16[512,512]{1,0:T(8,128)(2,1)S(1)}, bf16[512,512]{1,0:T(8,128)(2,1)S(1)}, u32[]{:S(2)}, u32[]{:S(2)}) collective-permute-start(bf16[512,512]{1,0:T(8,128)(2,1)S(1)} %shard_map.109.rest_0_), channel_id=1, source_target_pairs={{0,16},{4,20},{8,24},{12,28},{16,0},{20,4},{24,8},{28,12},{1,17},{... | collective-permute-start | bytes 1572872 | tf_op jit(solution)/shard_map/ppermute | solution.py:25
  270.1 38.3 %collective-permute-start.25 = (bf16[1024,512]{1,0:T(8,128)(2,1)S(1)}, bf16[1024,512]{1,0:T(8,128)(2,1)S(1)}, u32[]{:S(2)}, u32[]{:S(2)}) collective-permute-start(bf16[1024,512]{1,0:T(8,128)(2,1)S(1)} %shard_map.110.rest_2_), channel_id=1, source_target_pairs={{0,4},{4,0},{8,12},{12,8},{16,20},{20,16},{24,28},{28,24},{1,5},{5... | collective-permute-start | bytes 3145736 | tf_op jit(solution)/shard_map/ppermute | solution.py:25
  288.8 38.6 %collective-permute-start.30 = (bf16[512,512]{1,0:T(8,128)(2,1)S(1)}, bf16[512,512]{1,0:T(8,128)(2,1)S(1)}, u32[]{:S(2)}, u32[]{:S(2)}) collective-permute-start(bf16[512,512]{1,0:T(8,128)(2,1)S(1)} %shard_map.112.rest_2_), channel_id=1, source_target_pairs={{0,16},{4,20},{8,24},{12,28},{16,0},{20,4},{24,8},{28,12},{1,17},{... | collective-permute-start | bytes 1572872 | tf_op jit(solution)/shard_map/ppermute | solution.py:25
  311.3 26.6 %collective-permute-start.29 = (bf16[512,512]{1,0:T(8,128)(2,1)S(1)}, bf16[512,512]{1,0:T(8,128)(2,1)S(1)}, u32[]{:S(2)}, u32[]{:S(2)}) collective-permute-start(bf16[512,512]{1,0:T(8,128)(2,1)S(1)} %shard_map.114.rest_2_), channel_id=1, source_target_pairs={{0,16},{4,20},{8,24},{12,28},{16,0},{20,4},{24,8},{28,12},{1,17},{... | collective-permute-start | bytes 1572872 | tf_op jit(solution)/shard_map/ppermute | solution.py:25
  (37 other events, 349.5 us)
Sparse Core Ops, SparseCore 0:
  9.6 37.1 all-gather.5
  48.3 22.5 all-gather.7
  72.5 34.5 all-gather.3

commit v8 on v7

--- a/solution.py
+++ b/solution.py
@@ -10,7 +10,7 @@
 HEAD_DIM = 128
 F32 = jnp.float32
 BF16 = jnp.bfloat16
-PARAMS = pltpu.CompilerParams(vmem_limit_bytes=48 * 1024 * 1024)
+PARAMS = pltpu.CompilerParams(vmem_limit_bytes=60 * 1024 * 1024)
 
 
 COST = pl.CostEstimate(flops=10**10, bytes_accessed=1, transcendentals=0)
@@ -25,15 +25,13 @@
     return lax.ppermute(array, "seq", [(i, i ^ (1 << bit)) for i in range(size)])
 
 
-def entering(block, low, reverse, waits=None):
+def entering(block, low, reverse):
     size, position = lax.axis_size("seq"), lax.axis_index("seq")
     bits = size.bit_length() - 1
     total, before = block, jnp.zeros_like(block)
     sent, came = [], []
     for bit in range(bits):
         step = 1 << bit
-        if waits and bit in waits:
-            low = after(low, *waits[bit](came))
         sent.append(low)
         if bit < bits - 1:
             came.append(flip(low, bit))
@@ -304,16 +302,12 @@
     gathered_cot = lax.all_gather(cotangent, "head", axis=1, tiled=True)
 
     block_state, block_low = by_heads(state_kernel, [k, v], [("heads", F32), ("heads", BF16)])
-    partner = []
-
-    def partner_shard(came):
-        shard = after(across(cotangent, 2, 1), came[0])
-        partner.append(jnp.where(aligned, across(shard[:, owned:], 0, 1), shard[:, :owned]))
-        return partner
-
-    waits = {2: partner_shard} if paired else {}
-    state_parts, sent, came = entering(block_state, block_low, False, waits)
+    state_parts, sent, came = entering(block_state, block_low, False)
     (local,) = by_heads(local_kernel, [q, k, v], [("rows", F32)], [sent[-1]])
+    if paired:
+        partner = after(across(cotangent, 2, 1), came[1])
+        partner_half = after(across(partner[:, owned:], 0, 1), local)
+        partner_half = jnp.where(aligned, partner_half, partner[:, :owned])
     state_low = (state_parts[0] + after(state_parts[1], local).astype(F32)).astype(BF16)
     attention, *gated = by_heads(
         gated_kernel,
@@ -321,7 +315,7 @@
         [("rows", F32), ("first", BF16), ("second", BF16)],
     )
     if paired:
-        partner_cot = lax.all_gather(partner[0], "head", axis=1, tiled=True)
+        partner_cot = lax.all_gather(partner_half, "head", axis=1, tiled=True)
         side = 1 ^ ((position >> 1) & 1) ^ (there & 1)
         both_cot = gathered_cot, partner_cot, jnp.concatenate([there, (there >> 2) * 2 + side])
         swapped = across(after(layer_input, came[1]), 2, 1)
@@ -331,7 +325,7 @@
     else:
         both_cot = both(gathered_cot)
         both_input = both(lax.all_gather(layer_input, "head", axis=1, tiled=True))
-    gated_first = gated[0], flip(gated[0], gather_bit)
+    gated = [(part, flip(part, gather_bit)) for part in gated]
 
     pre, grad_block, grad_block_low = by_heads(
         pre_kernel,
@@ -343,17 +337,15 @@
         query_kernel,
         [("rows", pre), k, v, ("heads", state_low)],
         [("first", BF16), ("second", BF16)],
-        [gated_first[1]],
-    )
-    query_grad = [(part, flip(part, gather_bit)) for part in query_grad]
+        [gated[0][1]],
+    )
+    query_grad = [(part, flip(after(part, came[1]), gather_bit)) for part in query_grad]
     key_local, value_local = by_heads(
         own_kernel,
         [("rows", pre), q, k, v],
         [("rows", F32), ("rows", F32)],
         [query_grad[0][0], sent[1]],
     )
-    gated_second = after(gated[1], came[1])
-    gated = [gated_first, (gated_second, flip(gated_second, gather_bit))]
     grad_low = (grad_parts[0] + grad_parts[1].astype(F32)).astype(BF16)
     key_grad, value_grad = by_heads(
         key_value_kernel,

time: 350 us -> 350 us (level)
  waiting for transfers between devices: 155 us -> 114 us
  Pallas kernels: 118 us -> 147 us
  starting transfers between devices: 33.8 us -> 46.1 us
    ppermute x26, waiting for transfers between devices: 136 us -> 108 us  [flip(): return lax.ppermute(array, 'seq', [(i, i ^ 1 << bit) for i in range(size)])]
    pallas_call x24, Pallas kernels: 81.4 us -> 101 us  [term(): pl.pallas_call(functools.partial(term_kernel, turned, len(received)), gri...]
    ppermute x26, starting transfers between devices: 24.1 us -> 37.8 us  [flip(): return lax.ppermute(array, 'seq', [(i, i ^ 1 << bit) for i in range(size)])]
    pallas_call x7, Pallas kernels: 36.6 us -> 46.2 us  [by_heads(): pl.pallas_call(without(kernel, len(args), len(waits)), grid=(count,), in_...]
    ppermute x2, waiting for transfers between devices: 12.6 us -> 4.96 us  [entering(): came.append(lax.ppermute(low, 'seq', pairs))]
    ppermute x3, waiting for transfers between devices: 5.39 us -> 0.01 us  [across(): return lax.ppermute(array, ('seq', 'head'), pairs)]
    unnamed x55 -> x45, local copies, waits for them, and re-layouts: 21.4 us -> 19.2 us
  transfers between devices with their start and end apart: 34 -> 34, of which waited for: 16 -> 15; matrix products, arithmetic and copies ran while one was open for 4% -> 4% of each run, Pallas kernels for 33% -> 41%
where the time goes in v8:
time: 350 us; the launch traced here: 349 us
  Pallas kernels  147 us (42%)
  waiting for transfers between devices  114 us (33%)
  starting transfers between devices  46.1 us (13%)
  local copies, waits for them, and re-layouts  20.6 us (6%)
  between operations  13.9 us (4%)
  other arithmetic  6.97 us (2%)
    ppermute x26, waiting for transfers between devices, flip(): return lax.ppermute(array, 'seq', [(i, i ^ 1 << bit) for i in range(size)])  108 us
    pallas_call x24, Pallas kernels, term(): pl.pallas_call(functools.partial(term_kernel, turned, len(received)), gri...  101 us
    pallas_call x7, Pallas kernels, by_heads(): pl.pallas_call(without(kernel, len(args), len(waits)), grid=(count,), in_...  46.2 us
    ppermute x26, starting transfers between devices, flip(): return lax.ppermute(array, 'seq', [(i, i ^ 1 << bit) for i in range(size)])  37.8 us
    unnamed x45, local copies, waits for them, and re-layouts  19.2 us
  transfers between devices with their start and end apart: 34, of which 15 were waited for; matrix products, arithmetic and copies ran while one was open for 4% of the time, Pallas kernels for 41%

profile of v8, /device:TPU:0, one launch (start us, length us, event | category | flops | bytes accessed | tf_op | source)
XLA Modules:
  0.0 348.7 jit_solution(10425511053833749538)
XLA Ops:
  15.6 5.0 %collective-permute-done = bf16[8,128,128]{2,1,0:T(8,128)(2,1)S(1)} collective-permute-done((bf16[8,128,128]{2,1,0:T(8,128)(2,1)}, bf16[8,128,128]{2,1,0:T(8,128)(2,1)S(1)}, u32[]{:S(2)}, u32[]{:S(2)}) %collective-permute-start) | collective-permute-done | bytes 262176 | tf_op jit(solution)/shard_map/ppermute | solution.py:25
  25.1 7.1 %collective-permute-done.1 = bf16[8,128,128]{2,1,0:T(8,128)(2,1)S(1)} collective-permute-done((bf16[8,128,128]{2,1,0:T(8,128)(2,1)S(1)}, bf16[8,128,128]{2,1,0:T(8,128)(2,1)S(1)}, u32[]{:S(2)}, u32[]{:S(2)}) %collective-permute-start.1) | collective-permute-done | bytes 262176 | tf_op jit(solution)/shard_map/ppermute | solution.py:25
  35.5 5.4 %shard_map.87.refs_0_ = f32[512,1024]{1,0:T(8,128)} custom-call(bf16[512,1024]{1,0:T(8,128)(2,1)} %refs_1_.11, bf16[512,1024]{1,0:T(8,128)(2,1)} %refs_2_.7, bf16[512,1024]{1,0:T(8,128)(2,1)} %refs_3_.5, bf16[8,128,128]{2,1,0:T(8,128)(2,1)} %fusion.3.refs_3_), custom_call_target="tpu_custom_call" | custom-call | flops 10000000000 | bytes 1 | tf_op jit(solution)/shard_map/pallas_call | solution.py:191
  53.1 5.4 %shard_map.88 = (f32[512,1024]{1,0:T(8,128)}, bf16[512,512]{1,0:T(8,128)(2,1)}, bf16[512,512]{1,0:T(8,128)(2,1)}) custom-call(f32[512,1024]{1,0:T(8,128)} %shard_map.87.refs_0_, bf16[512,1024]{1,0:T(8,128)(2,1)} %refs_1_.11, bf16[8,128,128]{2,1,0:T(8,128)(2,1)} %fusion.2.refs_2_.refs_3_, f32[1,1024]{1,0:T(1,128)} %bitcast.7), custom_call_target="tpu_custom_call" | custom-call | flops 10000000000 | bytes 1 | tf_op jit(solution)/shard_map/pallas_call | solution.py:191
  58.4 5.8 %collective-permute-start.4 = (bf16[512,512]{1,0:T(8,128)(2,1)}, bf16[512,512]{1,0:T(8,128)(2,1)}, u32[]{:S(2)}, u32[]{:S(2)}) collective-permute-start(bf16[512,512]{1,0:T(8,128)(2,1)} %get-tuple-element.31.grad), channel_id=1, source_target_pairs={{0,8},{4,12},{8,0},{12,4},{16,24},{20,28},{24,16},{28,20},{1,9},{5... | collective-permute-start | bytes 1572872 | tf_op jit(solution)/shard_map/ppermute | solution.py:25
  65.5 11.7 %shard_map.89 = (bf16[512,1024]{1,0:T(8,128)(2,1)}, f32[8,128,128]{2,1,0:T(8,128)}, bf16[8,128,128]{2,1,0:T(8,128)(2,1)}) custom-call(bf16[512,4096]{1,0:T(8,128)(2,1)} %all-gather.6.cloned.1.call-done.refs_0_.mine, bf16[1024,4096]{1,0:T(8,128)(2,1)} %refs_1_.9, f32[512,1024]{1,0:T(8,128)} %get-tuple-element.28.refs_2_, bf16[512,1024]{1,0:T(8,128)(2,1)} %refs_1_.11, ...), custom_call_target="tpu_custom_call" | custom-call | flops 10000000000 | bytes 1 | tf_op jit(solution)/shard_map/pallas_call | solution.py:191
  78.7 5.9 %shard_map.90 = (bf16[512,512]{1,0:T(8,128)(2,1)}, bf16[512,512]{1,0:T(8,128)(2,1)}) custom-call(bf16[512,1024]{1,0:T(8,128)(2,1)} %get-tuple-element.30.refs_0_, bf16[512,1024]{1,0:T(8,128)(2,1)} %refs_2_.7, bf16[512,1024]{1,0:T(8,128)(2,1)} %refs_3_.5, bf16[8,128,128]{2,1,0:T(8,128)(2,1)} %fusion.2.refs_2_.refs_3_, ...), custom_call_target="tpu_custom_call" | custom-call | flops 10000000000 | bytes 1 | tf_op jit(solution)/shard_map/pallas_call | solution.py:191
  86.8 8.7 %shard_map.91 = (f32[512,1024]{1,0:T(8,128)}, f32[512,1024]{1,0:T(8,128)}) custom-call(bf16[512,1024]{1,0:T(8,128)(2,1)} %get-tuple-element.30.refs_0_, bf16[512,1024]{1,0:T(8,128)(2,1)} %refs_1_.11, bf16[512,1024]{1,0:T(8,128)(2,1)} %refs_2_.7, bf16[512,1024]{1,0:T(8,128)(2,1)} %refs_3_.5, bf16[512,512]{1,0:T(8,128)(2,1)} %get-tuple-element.45.refs_4_.grad, ...), custom_call_target="tpu_custom_call" | custom-call | flops 10000000000 | bytes 1 | tf_op jit(solution)/shard_map/pallas_call | solution.py:191
  99.1 4.6 %shard_map.93.rest_0_ = bf16[512,1024]{1,0:T(8,128)(2,1)} custom-call(s32[8]{0:T(128)} %concatenate.9.index, bf16[512,4096]{1,0:T(8,128)(2,1)} %all-gather.6.cloned.1.call-done.refs_0_.mine, bf16[512,2048]{1,0:T(8,128)(2,1)} %all-gather.8.cloned.1.call-done.theirs, bf16[512,512]{1,0:T(8,128)(2,1)} %get-tuple-element.31.grad, ...), custom_call_target="tpu_custom_call" | custom-call | flops 10000000000 | bytes 1 | tf_op jit(solution)/shard_map/pallas_call | solution.py:245
  106.0 4.6 %shard_map.94.rest_1_ = bf16[512,1024]{1,0:T(8,128)(2,1)} custom-call(s32[8]{0:T(128)} %concatenate.9.index, bf16[512,4096]{1,0:T(8,128)(2,1)} %all-gather.6.cloned.1.call-done.refs_0_.mine, bf16[512,2048]{1,0:T(8,128)(2,1)} %all-gather.8.cloned.1.call-done.theirs, bf16[512,512]{1,0:T(8,128)(2,1)} %get-tuple-element.44.grad, bf16[512,512]{1,0:T(8,128)(2,1)} %copy-done.15, ...), custom_call_target="tpu_custom_call" | custom-call | flops 10000000000 | bytes 1 | tf_op jit(solution)/shard_map/pallas_call | solution.py:245
  112.6 5.1 %shard_map.92 = (bf16[512,1024]{1,0:T(8,128)(2,1)}, bf16[512,1024]{1,0:T(8,128)(2,1)}) custom-call(f32[512,1024]{1,0:T(8,128)} %get-tuple-element.35.refs_0_.rest_0_, f32[512,1024]{1,0:T(8,128)} %get-tuple-element.36.refs_1_, bf16[512,1024]{1,0:T(8,128)(2,1)} %refs_2_.7, bf16[512,1024]{1,0:T(8,128)(2,1)} %refs_3_.5, bf16[8,128,128]{2,1,0:T(8,128)(2,1)} %fusion.6.refs_4_), custom_call_target="tpu_custom_call" | custom-call | flops 10000000000 | bytes 1 | tf_op jit(solution)/shard_map/pallas_call | solution.py:191
  118.4 11.7 %collective-permute-done.16.rest_0_ = bf16[512,1024]{1,0:T(8,128)(2,1)} collective-permute-done((bf16[512,1024]{1,0:T(8,128)(2,1)}, bf16[512,1024]{1,0:T(8,128)(2,1)}, u32[]{:S(2)}, u32[]{:S(2)}) %collective-permute-start.16) | collective-permute-done | bytes 1048608 | tf_op jit(solution)/shard_map/ppermute | solution.py:25
  137.6 4.5 %shard_map.96.rest_1_ = bf16[1024,512]{1,0:T(8,128)(2,1)} custom-call(s32[8]{0:T(128)} %concatenate.8.index, bf16[512,4096]{1,0:T(8,128)(2,1)} %all-gather.4.cloned.1.call-done.mine.theirs, bf16[512,4096]{1,0:T(8,128)(2,1)} %all-gather.4.cloned.1.call-done.mine.theirs, bf16[512,512]{1,0:T(8,128)(2,1)} %get-tuple-element.45.refs_4_.grad, ...), custom_call_target="tpu_custom_call" | custom-call | flops 10000000000 | bytes 1 | tf_op jit(solution)/shard_map/pallas_call | solution.py:245
  143.5 9.0 %collective-permute-done.14.rest_0_ = bf16[512,1024]{1,0:T(8,128)(2,1)S(1)} collective-permute-done((bf16[512,1024]{1,0:T(8,128)(2,1)}, bf16[512,1024]{1,0:T(8,128)(2,1)S(1)}, u32[]{:S(2)}, u32[]{:S(2)}) %collective-permute-start.14) | collective-permute-done | bytes 1048608 | tf_op jit(solution)/shard_map/ppermute | solution.py:25
  182.5 25.2 %collective-permute-done.9.rest_1_.other = bf16[512,1024]{1,0:T(8,128)(2,1)S(1)} collective-permute-done((bf16[512,1024]{1,0:T(8,128)(2,1)S(1)}, bf16[512,1024]{1,0:T(8,128)(2,1)S(1)}, u32[]{:S(2)}, u32[]{:S(2)}) %collective-permute-start.9) | collective-permute-done | bytes 1048608 | tf_op jit(solution)/shard_map/ppermute | solution.py:25
  208.7 4.5 %shard_map.101.rest_2_ = bf16[1024,512]{1,0:T(8,128)(2,1)} custom-call(s32[8]{0:T(128)} %concatenate.8.index, bf16[512,4096]{1,0:T(8,128)(2,1)} %all-gather.4.cloned.1.call-done.mine.theirs, bf16[512,4096]{1,0:T(8,128)(2,1)} %all-gather.4.cloned.1.call-done.mine.theirs, bf16[512,1024]{1,0:T(8,128)(2,1)} %get-tuple-element.38.rest_2_.grad, ...), custom_call_target="tpu_custom_call" | custom-call | flops 10000000000 | bytes 1 | tf_op jit(solution)/shard_map/pallas_call | solution.py:245
  223.8 4.5 %shard_map.104.rest_2_ = bf16[1024,512]{1,0:T(8,128)(2,1)} custom-call(s32[8]{0:T(128)} %concatenate.8.index, bf16[512,4096]{1,0:T(8,128)(2,1)} %all-gather.4.cloned.1.call-done.mine.theirs, bf16[512,4096]{1,0:T(8,128)(2,1)} %all-gather.4.cloned.1.call-done.mine.theirs, bf16[512,1024]{1,0:T(8,128)(2,1)} %get-tuple-element.38.rest_2_.grad, ...), custom_call_target="tpu_custom_call" | custom-call | flops 10000000000 | bytes 1 | tf_op jit(solution)/shard_map/pallas_call | solution.py:245
  234.0 5.6 %collective-permute-done.23.rest_0_ = bf16[1024,512]{1,0:T(8,128)(2,1)S(1)} collective-permute-done((bf16[1024,512]{1,0:T(8,128)(2,1)}, bf16[1024,512]{1,0:T(8,128)(2,1)S(1)}, u32[]{:S(2)}, u32[]{:S(2)}) %collective-permute-start.23) | collective-permute-done | bytes 1048608 | tf_op jit(solution)/shard_map/ppermute | solution.py:25
  244.4 4.5 %shard_map.107.rest_2_ = bf16[1024,512]{1,0:T(8,128)(2,1)} custom-call(s32[8]{0:T(128)} %concatenate.8.index, bf16[512,4096]{1,0:T(8,128)(2,1)} %all-gather.4.cloned.1.call-done.mine.theirs, bf16[512,4096]{1,0:T(8,128)(2,1)} %all-gather.4.cloned.1.call-done.mine.theirs, bf16[512,1024]{1,0:T(8,128)(2,1)} %get-tuple-element.39.grad, ...), custom_call_target="tpu_custom_call" | custom-call | flops 10000000000 | bytes 1 | tf_op jit(solution)/shard_map/pallas_call | solution.py:245
  250.4 7.7 %collective-permute-done.22.rest_1_ = bf16[512,512]{1,0:T(8,128)(2,1)S(1)} collective-permute-done((bf16[512,512]{1,0:T(8,128)(2,1)}, bf16[512,512]{1,0:T(8,128)(2,1)S(1)}, u32[]{:S(2)}, u32[]{:S(2)}) %collective-permute-start.22) | collective-permute-done | bytes 524320 | tf_op jit(solution)/shard_map/ppermute | solution.py:25
  273.1 7.4 %collective-permute-done.28.rest_1_ = bf16[512,512]{1,0:T(8,128)(2,1)S(1)} collective-permute-done((bf16[512,512]{1,0:T(8,128)(2,1)}, bf16[512,512]{1,0:T(8,128)(2,1)S(1)}, u32[]{:S(2)}, u32[]{:S(2)}) %collective-permute-start.28) | collective-permute-done | bytes 524320 | tf_op jit(solution)/shard_map/ppermute | solution.py:25
  290.5 12.5 %collective-permute-done.26.rest_1_ = bf16[512,512]{1,0:T(8,128)(2,1)S(1)} collective-permute-done((bf16[512,512]{1,0:T(8,128)(2,1)}, bf16[512,512]{1,0:T(8,128)(2,1)S(1)}, u32[]{:S(2)}, u32[]{:S(2)}) %collective-permute-start.26) | collective-permute-done | bytes 524320 | tf_op jit(solution)/shard_map/ppermute | solution.py:25
  313.0 12.5 %collective-permute-done.30.rest_1_ = bf16[512,512]{1,0:T(8,128)(2,1)S(1)} collective-permute-done((bf16[512,512]{1,0:T(8,128)(2,1)}, bf16[512,512]{1,0:T(8,128)(2,1)S(1)}, u32[]{:S(2)}, u32[]{:S(2)}) %collective-permute-start.30) | collective-permute-done | bytes 524320 | tf_op jit(solution)/shard_map/ppermute | solution.py:25
  330.6 6.6 %copy.20.rest_3_ = f32[3,512,1024]{2,1,0:T(8,128)} copy(f32[3,512,1024]{2,1,0:T(8,128)} %shard_map.115.rest_2_) | data formatting | bytes 12582912
  (136 shorter events, 149.2 us)
Async XLA Ops:
  7.2 58.3 %all-gather.6.cloned.1.call-start = ((), (), s32[]{:S(2)}) async-start(), calls=%async_computation.1 | async-start | bytes 5242880 | tf_op jit(solution)/shard_map/all_gather | solution.py:302
  7.9 91.2 %all-gather.8.cloned.1.call-start = ((), (), s32[]{:S(2)}) async-start(), calls=%async_computation.2 | async-start | bytes 2621440 | tf_op jit(solution)/shard_map/all_gather | solution.py:318
  7.9 26.1 %collective-permute-start.11 = (bf16[512,1024]{1,0:T(8,128)(2,1)}, bf16[512,1024]{1,0:T(8,128)(2,1)S(1)}, u32[]{:S(2)}, u32[]{:S(2)}) collective-permute-start(bf16[512,1024]{1,0:T(8,128)(2,1)} %param.13), channel_id=1, source_target_pairs={{1,8},{3,10},{5,12},{7,14},{8,1},{10,3},{12,5},{14,7},{17,24},{19,... | collective-permute-start | bytes 3145736 | tf_op jit(solution)/shard_map/ppermute | solution.py:288
  41.8 95.8 %all-gather.4.cloned.1.call-start = ((), (), s32[]{:S(2)}) async-start(), calls=%async_computation | async-start | bytes 5242880 | tf_op jit(solution)/shard_map/all_gather | solution.py:323
  64.3 40.9 %collective-permute-start.13 = (bf16[512,512]{1,0:T(8,128)(2,1)}, bf16[512,512]{1,0:T(8,128)(2,1)S(1)}, u32[]{:S(2)}, u32[]{:S(2)}) collective-permute-start(bf16[512,512]{1,0:T(8,128)(2,1)} %get-tuple-element.44.grad), channel_id=1, source_target_pairs={{0,8},{4,12},{8,0},{12,4},{16,24},{20,28},{24,16},{28,20},{1,9},{5... | collective-permute-start | bytes 1572872 | tf_op jit(solution)/shard_map/ppermute | solution.py:25
  97.0 40.5 %collective-permute-start.15 = (bf16[512,512]{1,0:T(8,128)(2,1)}, bf16[512,512]{1,0:T(8,128)(2,1)}, u32[]{:S(2)}, u32[]{:S(2)}) collective-permute-start(bf16[512,512]{1,0:T(8,128)(2,1)} %get-tuple-element.45.refs_4_.grad), channel_id=1, source_target_pairs={{0,8},{4,12},{8,0},{12,4},{16,24},{20,28},{24,16},{28,20},{1,9},{5... | collective-permute-start | bytes 1572872 | tf_op jit(solution)/shard_map/ppermute | solution.py:25
  98.4 63.9 %collective-permute-start.10 = (bf16[512,512]{1,0:T(8,128)(2,1)S(1)}, bf16[512,512]{1,0:T(8,128)(2,1)}, u32[]{:S(2)}, u32[]{:S(2)}) collective-permute-start(bf16[512,512]{1,0:T(8,128)(2,1)S(1)} %copy-done.14), channel_id=1, source_target_pairs={{0,8},{4,12},{8,0},{12,4},{16,24},{20,28},{24,16},{28,20},{1,9},{5... | collective-permute-start | bytes 1572872 | tf_op jit(solution)/shard_map/ppermute | solution.py:25
  103.7 26.4 %collective-permute-start.16 = (bf16[512,1024]{1,0:T(8,128)(2,1)}, bf16[512,1024]{1,0:T(8,128)(2,1)}, u32[]{:S(2)}, u32[]{:S(2)}) collective-permute-start(bf16[512,1024]{1,0:T(8,128)(2,1)} %shard_map.93.rest_0_), channel_id=1, source_target_pairs={{0,4},{4,0},{8,12},{12,8},{16,20},{20,16},{24,28},{28,24},{1,5},{5... | collective-permute-start | bytes 3145736 | tf_op jit(solution)/shard_map/ppermute | solution.py:25
  110.5 42.0 %collective-permute-start.14 = (bf16[512,1024]{1,0:T(8,128)(2,1)}, bf16[512,1024]{1,0:T(8,128)(2,1)S(1)}, u32[]{:S(2)}, u32[]{:S(2)}) collective-permute-start(bf16[512,1024]{1,0:T(8,128)(2,1)} %shard_map.94.rest_1_), channel_id=1, source_target_pairs={{0,4},{4,0},{8,12},{12,8},{16,20},{20,16},{24,28},{28,24},{1,5},{5... | collective-permute-start | bytes 3145736 | tf_op jit(solution)/shard_map/ppermute | solution.py:25
  117.7 43.6 %collective-permute-start.8 = (bf16[512,1024]{1,0:T(8,128)(2,1)}, bf16[512,1024]{1,0:T(8,128)(2,1)S(1)}, u32[]{:S(2)}, u32[]{:S(2)}) collective-permute-start(bf16[512,1024]{1,0:T(8,128)(2,1)} %get-tuple-element.38.rest_2_.grad), channel_id=1, source_target_pairs={{0,8},{4,12},{8,0},{12,4},{16,24},{20,28},{24,16},{28,20},{1,9},{5... | collective-permute-start | bytes 3145736 | tf_op jit(solution)/shard_map/ppermute | solution.py:25
  134.0 34.3 %collective-permute-start.20 = (bf16[512,512]{1,0:T(8,128)(2,1)}, bf16[512,512]{1,0:T(8,128)(2,1)}, u32[]{:S(2)}, u32[]{:S(2)}) collective-permute-start(bf16[512,512]{1,0:T(8,128)(2,1)} %shard_map.95.rest_0_), channel_id=1, source_target_pairs={{0,16},{4,20},{8,24},{12,28},{16,0},{20,4},{24,8},{28,12},{1,17},{... | collective-permute-start | bytes 1572872 | tf_op jit(solution)/shard_map/ppermute | solution.py:25
  142.1 33.0 %collective-permute-start.19 = (bf16[1024,512]{1,0:T(8,128)(2,1)}, bf16[1024,512]{1,0:T(8,128)(2,1)}, u32[]{:S(2)}, u32[]{:S(2)}) collective-permute-start(bf16[1024,512]{1,0:T(8,128)(2,1)} %shard_map.96.rest_1_), channel_id=1, source_target_pairs={{0,4},{4,0},{8,12},{12,8},{16,20},{20,16},{24,28},{28,24},{1,5},{5... | collective-permute-start | bytes 3145736 | tf_op jit(solution)/shard_map/ppermute | solution.py:25
  157.3 57.4 %collective-permute-start.18 = (bf16[512,512]{1,0:T(8,128)(2,1)}, bf16[512,512]{1,0:T(8,128)(2,1)}, u32[]{:S(2)}, u32[]{:S(2)}) collective-permute-start(bf16[512,512]{1,0:T(8,128)(2,1)} %shard_map.97.rest_0_), channel_id=1, source_target_pairs={{0,16},{4,20},{8,24},{12,28},{16,0},{20,4},{24,8},{28,12},{1,17},{... | collective-permute-start | bytes 1572872 | tf_op jit(solution)/shard_map/ppermute | solution.py:25
  161.3 46.5 %collective-permute-start.9 = (bf16[512,1024]{1,0:T(8,128)(2,1)S(1)}, bf16[512,1024]{1,0:T(8,128)(2,1)S(1)}, u32[]{:S(2)}, u32[]{:S(2)}) collective-permute-start(bf16[512,1024]{1,0:T(8,128)(2,1)S(1)} %copy-done.5), channel_id=1, source_target_pairs={{0,8},{4,12},{8,0},{12,4},{16,24},{20,28},{24,16},{28,20},{1,9},{5... | collective-permute-start | bytes 3145736 | tf_op jit(solution)/shard_map/ppermute | solution.py:25
  166.9 52.0 %collective-permute-start.17 = (bf16[1024,512]{1,0:T(8,128)(2,1)}, bf16[1024,512]{1,0:T(8,128)(2,1)S(1)}, u32[]{:S(2)}, u32[]{:S(2)}) collective-permute-start(bf16[1024,512]{1,0:T(8,128)(2,1)} %shard_map.98.rest_2_), channel_id=1, source_target_pairs={{0,4},{4,0},{8,12},{12,8},{16,20},{20,16},{24,28},{28,24},{1,5},{5... | collective-permute-start | bytes 3145736 | tf_op jit(solution)/shard_map/ppermute | solution.py:25
  179.0 49.9 %collective-permute-start.24 = (bf16[512,512]{1,0:T(8,128)(2,1)}, bf16[512,512]{1,0:T(8,128)(2,1)S(1)}, u32[]{:S(2)}, u32[]{:S(2)}) collective-permute-start(bf16[512,512]{1,0:T(8,128)(2,1)} %shard_map.100.rest_0_), channel_id=1, source_target_pairs={{0,16},{4,20},{8,24},{12,28},{16,0},{20,4},{24,8},{28,12},{1,17},{... | collective-permute-start | bytes 1572872 | tf_op jit(solution)/shard_map/ppermute | solution.py:25
  213.2 26.3 %collective-permute-start.23 = (bf16[1024,512]{1,0:T(8,128)(2,1)}, bf16[1024,512]{1,0:T(8,128)(2,1)S(1)}, u32[]{:S(2)}, u32[]{:S(2)}) collective-permute-start(bf16[1024,512]{1,0:T(8,128)(2,1)} %shard_map.101.rest_2_), channel_id=1, source_target_pairs={{0,4},{4,0},{8,12},{12,8},{16,20},{20,16},{24,28},{28,24},{1,5},{5... | collective-permute-start | bytes 3145736 | tf_op jit(solution)/shard_map/ppermute | solution.py:25
  223.8 34.3 %collective-permute-start.22 = (bf16[512,512]{1,0:T(8,128)(2,1)}, bf16[512,512]{1,0:T(8,128)(2,1)S(1)}, u32[]{:S(2)}, u32[]{:S(2)}) collective-permute-start(bf16[512,512]{1,0:T(8,128)(2,1)} %shard_map.103.rest_0_), channel_id=1, source_target_pairs={{0,16},{4,20},{8,24},{12,28},{16,0},{20,4},{24,8},{28,12},{1,17},{... | collective-permute-start | bytes 1572872 | tf_op jit(solution)/shard_map/ppermute | solution.py:25
  228.3 34.8 %collective-permute-start.21 = (bf16[1024,512]{1,0:T(8,128)(2,1)}, bf16[1024,512]{1,0:T(8,128)(2,1)S(1)}, u32[]{:S(2)}, u32[]{:S(2)}) collective-permute-start(bf16[1024,512]{1,0:T(8,128)(2,1)} %shard_map.104.rest_2_), channel_id=1, source_target_pairs={{0,4},{4,0},{8,12},{12,8},{16,20},{20,16},{24,28},{28,24},{1,5},{5... | collective-permute-start | bytes 3145736 | tf_op jit(solution)/shard_map/ppermute | solution.py:25
  244.4 36.2 %collective-permute-start.28 = (bf16[512,512]{1,0:T(8,128)(2,1)}, bf16[512,512]{1,0:T(8,128)(2,1)S(1)}, u32[]{:S(2)}, u32[]{:S(2)}) collective-permute-start(bf16[512,512]{1,0:T(8,128)(2,1)} %shard_map.106.rest_0_), channel_id=1, source_target_pairs={{0,16},{4,20},{8,24},{12,28},{16,0},{20,4},{24,8},{28,12},{1,17},{... | collective-permute-start | bytes 1572872 | tf_op jit(solution)/shard_map/ppermute | solution.py:25
  248.9 36.7 %collective-permute-start.27 = (bf16[1024,512]{1,0:T(8,128)(2,1)}, bf16[1024,512]{1,0:T(8,128)(2,1)S(1)}, u32[]{:S(2)}, u32[]{:S(2)}) collective-permute-start(bf16[1024,512]{1,0:T(8,128)(2,1)} %shard_map.107.rest_2_), channel_id=1, source_target_pairs={{0,4},{4,0},{8,12},{12,8},{16,20},{20,16},{24,28},{28,24},{1,5},{5... | collective-permute-start | bytes 3145736 | tf_op jit(solution)/shard_map/ppermute | solution.py:25
  268.0 35.0 %collective-permute-start.26 = (bf16[512,512]{1,0:T(8,128)(2,1)}, bf16[512,512]{1,0:T(8,128)(2,1)S(1)}, u32[]{:S(2)}, u32[]{:S(2)}) collective-permute-start(bf16[512,512]{1,0:T(8,128)(2,1)} %shard_map.109.rest_0_), channel_id=1, source_target_pairs={{0,16},{4,20},{8,24},{12,28},{16,0},{20,4},{24,8},{28,12},{1,17},{... | collective-permute-start | bytes 1572872 | tf_op jit(solution)/shard_map/ppermute | solution.py:25
  272.5 35.6 %collective-permute-start.25 = (bf16[1024,512]{1,0:T(8,128)(2,1)}, bf16[1024,512]{1,0:T(8,128)(2,1)S(1)}, u32[]{:S(2)}, u32[]{:S(2)}) collective-permute-start(bf16[1024,512]{1,0:T(8,128)(2,1)} %shard_map.110.rest_2_), channel_id=1, source_target_pairs={{0,4},{4,0},{8,12},{12,8},{16,20},{20,16},{24,28},{28,24},{1,5},{5... | collective-permute-start | bytes 3145736 | tf_op jit(solution)/shard_map/ppermute | solution.py:25
  290.5 35.0 %collective-permute-start.30 = (bf16[512,512]{1,0:T(8,128)(2,1)}, bf16[512,512]{1,0:T(8,128)(2,1)S(1)}, u32[]{:S(2)}, u32[]{:S(2)}) collective-permute-start(bf16[512,512]{1,0:T(8,128)(2,1)} %shard_map.112.rest_2_), channel_id=1, source_target_pairs={{0,16},{4,20},{8,24},{12,28},{16,0},{20,4},{24,8},{28,12},{1,17},{... | collective-permute-start | bytes 1572872 | tf_op jit(solution)/shard_map/ppermute | solution.py:25
  (32 other events, 208.4 us)
Sparse Core Ops, SparseCore 0:
  9.6 37.1 all-gather.5
  48.3 22.5 all-gather.7
  72.5 34.4 all-gather.3

commit v9 on v8

--- a/solution.py
+++ b/solution.py
@@ -10,7 +10,7 @@
 HEAD_DIM = 128
 F32 = jnp.float32
 BF16 = jnp.bfloat16
-PARAMS = pltpu.CompilerParams(vmem_limit_bytes=60 * 1024 * 1024)
+PARAMS = pltpu.CompilerParams(vmem_limit_bytes=48 * 1024 * 1024)
 
 
 COST = pl.CostEstimate(flops=10**10, bytes_accessed=1, transcendentals=0)
@@ -116,8 +116,11 @@
         second[...] = found
 
 
-def pre_kernel(cot, weight, attention, q, gain, pre, out, low):
-    gated_grad = mm_t(cot[...], weight[...])
+def gated_grad_kernel(cot, weight, out):
+    out[...] = mm_t(cot[...], weight[...])
+
+
+def pre_kernel(gated_grad, attention, q, gain, pre, out, low):
     for i, cols in enumerate(head_slices(q)):
         value = attention[:, cols]
         rms = jnp.sqrt(jnp.mean(value * value, axis=-1, keepdims=True) + 1e-05)
@@ -154,10 +157,23 @@
         value_local[:, cols] = upper_mm(causal(qh, k[:, cols]), grad)
 
 
-def key_value_kernel(key_local, value_local, k, v, state, key_grad, value_grad):
+def key_value_kernel(key_local, value_local, k, v, state, key_first, key_second, value_first, value_second):
+    step, steps = pl.program_id(0), pl.num_programs(0)
+    keys, values = [], []
     for i, cols in enumerate(head_slices(k)):
-        key_grad[:, cols] = (key_local[:, cols] + mm_t(v[:, cols], state[i])).astype(BF16)
-        value_grad[:, cols] = (value_local[:, cols] + mm(k[:, cols], state[i])).astype(BF16)
+        keys.append((key_local[:, cols] + mm_t(v[:, cols], state[i])).astype(BF16))
+        values.append((value_local[:, cols] + mm(k[:, cols], state[i])).astype(BF16))
+    keys, values = jnp.concatenate(keys, axis=1), jnp.concatenate(values, axis=1)
+
+    @pl.when(step < steps // 2)
+    def _():
+        key_first[...] = keys
+        value_first[...] = values
+
+    @pl.when(step >= steps // 2)
+    def _():
+        key_second[...] = keys
+        value_second[...] = values
 
 
 def without(kernel, first, count):
@@ -165,8 +181,8 @@
 
 
 def by_heads(kernel, args, outs, waits=()):
-    tokens = next(a.shape[0] for kind, a in args if kind == "rows")
-    width = next(a.shape[1] for kind, a in args if kind == "rows")
+    tokens = args[0][1].shape[0]
+    width = args[1][1].shape[0 if args[1][0] == "weight" else 1]
     pair = 2 * HEAD_DIM
     count = width // pair
     half = count // 2
@@ -306,9 +322,10 @@
     (local,) = by_heads(local_kernel, [q, k, v], [("rows", F32)], [sent[-1]])
     if paired:
         partner = after(across(cotangent, 2, 1), came[1])
-        partner_half = after(across(partner[:, owned:], 0, 1), local)
-        partner_half = jnp.where(aligned, partner_half, partner[:, :owned])
+        partner_half = across(partner[:, owned:], 0, 1)
     state_low = (state_parts[0] + after(state_parts[1], local).astype(F32)).astype(BF16)
+    if paired:
+        partner_half = jnp.where(aligned, after(partner_half, state_low), partner[:, :owned])
     attention, *gated = by_heads(
         gated_kernel,
         [("rows", local), q, ("heads", state_low), ("gain", gain)],
@@ -327,9 +344,12 @@
         both_input = both(lax.all_gather(layer_input, "head", axis=1, tiled=True))
     gated = [(part, flip(part, gather_bit)) for part in gated]
 
+    (gated_grad,) = by_heads(
+        gated_grad_kernel, [("whole", gathered_cot), ("weight", out_weight)], [("rows", F32)], [attention]
+    )
     pre, grad_block, grad_block_low = by_heads(
         pre_kernel,
-        [("whole", gathered_cot), ("weight", out_weight), ("rows", attention), q, ("gain", gain)],
+        [("rows", gated_grad), ("rows", attention), q, ("gain", gain)],
         [("rows", BF16), ("heads", F32), ("heads", BF16)],
     )
     grad_parts, sent, came = entering(grad_block, grad_block_low, True)
@@ -347,32 +367,36 @@
         [query_grad[0][0], sent[1]],
     )
     grad_low = (grad_parts[0] + grad_parts[1].astype(F32)).astype(BF16)
-    key_grad, value_grad = by_heads(
+    late_grads = by_heads(
         key_value_kernel,
         [("rows", key_local), ("rows", value_local), k, v, ("heads", grad_low)],
-        [("rows", BF16), ("rows", BF16)],
-    )
-    key_grad = key_grad, flip(key_grad, gather_bit)
-    value_grad = value_grad, flip(after(value_grad, key_grad[1]), gather_bit)
+        [("first", BF16), ("second", BF16)] * 2,
+    )
+    chained = []
+    for part in late_grads:
+        chained.append((part, flip(after(part, chained[-1][1]) if chained else part, gather_bit)))
+    late_grads = chained
 
     half = width // 2
-    pieces = [(both_cot, gated[i], 0, True, (i, 0)) for i in range(2)]
-    pieces += [(both_input, query_grad[i], 0, False, (0, 0, i)) for i in range(2)]
-    pieces += [(both_input, key_grad, i, False, (1, 0, i)) for i in range(2)]
-    pieces += [(both_input, value_grad, i, False, (2, 0, i)) for i in range(2)]
+    quarter = half // 2
+    pieces = [(both_cot, gated[0], quarter, i, True, (i, 0)) for i in range(2)]
+    pieces += [(both_cot, gated[1], half, 0, True, (1, 0))]
+    pieces += [(both_input, query_grad[i], half, 0, False, (0, 0, i)) for i in range(2)]
+    pieces += [(both_input, late_grads[i], half, 0, False, (1 + i // 2, 0, i % 2)) for i in range(4)]
     starts = [chunks - (chunks >> i) for i in range(len(halving) + 1)]
     shapes = {True: (width, owned), False: (3, owned, width)}
     targets = {True: None, False: None}
     received = {}
-    last = [key_local, sent[-1]]
+    last = [key_local]
 
     def stage(i, n):
-        features, (grad, other), block, turned, place = pieces[i]
+        features, (grad, other), cols, block, turned, place = pieces[i]
         came = received.setdefault(i, [])
         final = n == len(halving)
         target = (targets[turned], shapes[turned], place) if final else None
         count = 1 if final else chunks >> (n + 1)
-        out = term(features, (grad, other), block, half, turned, owned, starts[n], count, came, last, target)
+        waits = [a for a in last if not final or a is not targets[turned]]
+        out = term(features, (grad, other), block, cols, turned, owned, starts[n], count, came, waits, target)
         last[:] = [out]
         if final:
             targets[turned] = out
@@ -382,12 +406,14 @@
     stages = len(halving) + 1
     stage(0, 0)
     stage(1, 0)
-    last.append(key_grad[0])
     for i in range(len(pieces)):
         for n in range(1, stages - 1):
             stage(i, n)
         if i + 2 < len(pieces):
-            last.extend(([], key_grad[1:], value_grad[1:])[min(i, 2)])
+            if i == 0:
+                last.append(late_grads[0][0])
+            if 2 <= i < 6:
+                last.append(late_grads[i - 2][1])
             stage(i + 2, 0)
         if i >= 1:
             stage(i - 1, stages - 1)

time: 350 us -> 355 us (1.014)
  waiting for transfers between devices: 114 us -> 140 us
  Pallas kernels: 147 us -> 125 us
    ppermute x26 -> x30, waiting for transfers between devices: 108 us -> 130 us  [flip(): return lax.ppermute(array, 'seq', [(i, i ^ 1 << bit) for i in range(size)])]
    pallas_call x24 -> x27, Pallas kernels: 101 us -> 86.9 us  [term(): pl.pallas_call(functools.partial(term_kernel, turned, len(received)), gri...]
    pallas_call x7 -> x8, Pallas kernels: 46.2 us -> 38.5 us  [by_heads(): pl.pallas_call(without(kernel, len(args), len(waits)), grid=(count,), in_...]
    ppermute x26 -> x30, starting transfers between devices: 37.8 us -> 32.5 us  [flip(): return lax.ppermute(array, 'seq', [(i, i ^ 1 << bit) for i in range(size)])]
    ppermute x2, waiting for transfers between devices: 4.96 us -> 10 us  [entering(): came.append(lax.ppermute(low, 'seq', pairs))]
    unnamed x45 -> x92, local copies, waits for them, and re-layouts: 19.2 us -> 22.4 us
  transfers between devices with their start and end apart: 34 -> 38, of which waited for: 15 -> 12; matrix products, arithmetic and copies ran while one was open for 4% -> 2% of each run, Pallas kernels for 41% -> 34%
where the time goes in v9:
time: 355 us; the launch traced here: 354 us
  waiting for transfers between devices  140 us (39%)
  Pallas kernels  125 us (35%)
  starting transfers between devices  44.1 us (12%)
  local copies, waits for them, and re-layouts  23.6 us (7%)
  between operations  14.3 us (4%)
  other arithmetic  5.68 us (2%)
    ppermute x30, waiting for transfers between devices, flip(): return lax.ppermute(array, 'seq', [(i, i ^ 1 << bit) for i in range(size)])  130 us
    pallas_call x27, Pallas kernels, term(): pl.pallas_call(functools.partial(term_kernel, turned, len(received)), gri...  86.9 us
    pallas_call x8, Pallas kernels, by_heads(): pl.pallas_call(without(kernel, len(args), len(waits)), grid=(count,), in_...  38.5 us
    ppermute x30, starting transfers between devices, flip(): return lax.ppermute(array, 'seq', [(i, i ^ 1 << bit) for i in range(size)])  32.5 us
    unnamed x92, local copies, waits for them, and re-layouts  22.4 us
    ppermute x2, waiting for transfers between devices, entering(): came.append(lax.ppermute(low, 'seq', pairs))  10 us
  transfers between devices with their start and end apart: 38, of which 12 were waited for; matrix products, arithmetic and copies ran while one was open for 2% of the time, Pallas kernels for 34%

profile of v9, /device:TPU:0, one launch (start us, length us, event | category | flops | bytes accessed | tf_op | source)
XLA Modules:
  0.0 353.6 jit_solution(16181309071867468456)
XLA Ops:
  16.6 5.7 %collective-permute-done = bf16[8,128,128]{2,1,0:T(8,128)(2,1)S(1)} collective-permute-done((bf16[8,128,128]{2,1,0:T(8,128)(2,1)S(1)}, bf16[8,128,128]{2,1,0:T(8,128)(2,1)S(1)}, u32[]{:S(2)}, u32[]{:S(2)}) %collective-permute-start) | collective-permute-done | bytes 262176 | tf_op jit(solution)/shard_map/ppermute | solution.py:25
  24.9 6.9 %collective-permute-done.1 = bf16[8,128,128]{2,1,0:T(8,128)(2,1)S(1)} collective-permute-done((bf16[8,128,128]{2,1,0:T(8,128)(2,1)S(1)}, bf16[8,128,128]{2,1,0:T(8,128)(2,1)S(1)}, u32[]{:S(2)}, u32[]{:S(2)}) %collective-permute-start.1) | collective-permute-done | bytes 262176 | tf_op jit(solution)/shard_map/ppermute | solution.py:25
  31.9 5.2 %collective-permute-start.3 = (bf16[8,128,128]{2,1,0:T(8,128)(2,1)S(1)}, bf16[8,128,128]{2,1,0:T(8,128)(2,1)S(1)}, u32[]{:S(2)}, u32[]{:S(2)}) collective-permute-start(bf16[8,128,128]{2,1,0:T(8,128)(2,1)S(1)} %fusion.3.refs_3_), channel_id=1, source_target_pairs={{0,16},{4,20},{8,24},{12,28},{1,17},{5,21},{9,25},{13,29},{2,18},{... | collective-permute-start | bytes 786440 | tf_op jit(solution)/shard_map/ppermute | solution.py:45
  49.4 4.7 %shard_map.88 = (f32[512,1024]{1,0:T(8,128)S(1)}, bf16[512,512]{1,0:T(8,128)(2,1)S(1)}, bf16[512,512]{1,0:T(8,128)(2,1)}) custom-call(f32[512,1024]{1,0:T(8,128)} %copy-done.42, bf16[512,1024]{1,0:T(8,128)(2,1)S(1)} %copy-done.2, bf16[8,128,128]{2,1,0:T(8,128)(2,1)S(1)} %fusion.2.refs_2_.refs_3_, f32[1,1024]{1,0:T(1,128)S(1)} %bitcast.6), custom_call_target="tpu_custom_call" | custom-call | flops 10000000000 | bytes 1 | tf_op jit(solution)/shard_map/pallas_call | solution.py:207
  61.6 8.5 %shard_map.89.refs_0_ = f32[512,1024]{1,0:T(8,128)S(1)} custom-call(bf16[512,4096]{1,0:T(8,128)(2,1)} %all-gather.6.cloned.1.call-done.refs_0_.mine, bf16[1024,4096]{1,0:T(8,128)(2,1)} %refs_1_.9, f32[512,1024]{1,0:T(8,128)S(1)} %copy-done.40), custom_call_target="tpu_custom_call" | custom-call | flops 10000000000 | bytes 1 | tf_op jit(solution)/shard_map/pallas_call | solution.py:207
  70.1 4.4 %shard_map.90 = (bf16[512,1024]{1,0:T(8,128)(2,1)S(1)}, f32[8,128,128]{2,1,0:T(8,128)S(1)}, bf16[8,128,128]{2,1,0:T(8,128)(2,1)S(1)}) custom-call(f32[512,1024]{1,0:T(8,128)S(1)} %shard_map.89.refs_0_, f32[512,1024]{1,0:T(8,128)} %copy-done.39, bf16[512,1024]{1,0:T(8,128)(2,1)S(1)} %copy-done.2, f32[1,1024]{1,0:T(1,128)S(1)} %bitcast.7), custom_call_target="tpu_custom_call" | custom-call | flops 10000000000 | bytes 1 | tf_op jit(solution)/shard_map/pallas_call | solution.py:207
  76.1 12.0 %collective-permute-done.4.refs_4_.other = bf16[512,512]{1,0:T(8,128)(2,1)} collective-permute-done((bf16[512,512]{1,0:T(8,128)(2,1)S(1)}, bf16[512,512]{1,0:T(8,128)(2,1)}, u32[]{:S(2)}, u32[]{:S(2)}) %collective-permute-start.4) | collective-permute-done | bytes 524320 | tf_op jit(solution)/shard_map/ppermute | solution.py:25
  88.2 3.7 %shard_map.91 = (bf16[512,512]{1,0:T(8,128)(2,1)S(1)}, bf16[512,512]{1,0:T(8,128)(2,1)S(1)}) custom-call(bf16[512,1024]{1,0:T(8,128)(2,1)S(1)} %get-tuple-element.34.refs_0_, bf16[512,1024]{1,0:T(8,128)(2,1)S(1)} %copy-done.4, bf16[512,1024]{1,0:T(8,128)(2,1)S(1)} %copy-done.8, bf16[8,128,128]{2,1,0:T(8,128)(2,1)S(1)} %fusion.2.refs_2_.refs_3_, ...), custom_call_target="tpu_custom_call" | custom-call | flops 10000000000 | bytes 1 | tf_op jit(solution)/shard_map/pallas_call | solution.py:207
  95.8 8.0 %shard_map.92 = (f32[512,1024]{1,0:T(8,128)}, f32[512,1024]{1,0:T(8,128)}) custom-call(bf16[512,1024]{1,0:T(8,128)(2,1)S(1)} %get-tuple-element.34.refs_0_, bf16[512,1024]{1,0:T(8,128)(2,1)S(1)} %copy-done.2, bf16[512,1024]{1,0:T(8,128)(2,1)S(1)} %copy-done.4, bf16[512,1024]{1,0:T(8,128)(2,1)S(1)} %copy-done.8, ...), custom_call_target="tpu_custom_call" | custom-call | flops 10000000000 | bytes 1 | tf_op jit(solution)/shard_map/pallas_call | solution.py:207
  118.5 10.0 %collective-permute-done.7 = bf16[8,128,128]{2,1,0:T(8,128)(2,1)S(1)} collective-permute-done((bf16[8,128,128]{2,1,0:T(8,128)(2,1)S(1)}, bf16[8,128,128]{2,1,0:T(8,128)(2,1)S(1)}, u32[]{:S(2)}, u32[]{:S(2)}) %collective-permute-start.7) | collective-permute-done | bytes 262176 | tf_op jit(solution)/shard_map/ppermute | solution.py:45
  129.6 4.5 %shard_map.93 = (bf16[512,512]{1,0:T(8,128)(2,1)S(1)}, bf16[512,512]{1,0:T(8,128)(2,1)}, bf16[512,512]{1,0:T(8,128)(2,1)S(1)}, bf16[512,512]{1,0:T(8,128)(2,1)S(1)}) custom-call(f32[512,1024]{1,0:T(8,128)} %get-tuple-element.39.refs_0_.rest_0_, f32[512,1024]{1,0:T(8,128)} %get-tuple-element.40.refs_1_, bf16[512,1024]{1,0:T(8,128)(2,1)S(1)} %copy-done.5, ...), custom_call_target="tpu_custom_call" | custom-call | flops 10000000000 | bytes 1 | tf_op jit(solution)/shard_map/pallas_call | solution.py:207
  139.9 4.2 %shard_map.97.rest_1_ = bf16[512,1024]{1,0:T(8,128)(2,1)} custom-call(s32[8]{0:T(128)S(1)} %concatenate.9.index, bf16[512,4096]{1,0:T(8,128)(2,1)} %all-gather.6.cloned.1.call-done.refs_0_.mine, bf16[512,2048]{1,0:T(8,128)(2,1)S(1)} %copy-done.1, bf16[512,512]{1,0:T(8,128)(2,1)} %get-tuple-element.52.grad, bf16[512,512]{1,0:T(8,128)(2,1)} %collective-permute-done.15.other, ...), custom_call_target="tpu_custom_call" | custom-call | flops 10000000000 | bytes 1 | tf_op jit(solution)/shard_map/pallas_call | solution.py:261
  147.6 15.8 %collective-permute-done.8.rest_1_.other = bf16[512,512]{1,0:T(8,128)(2,1)S(1)} collective-permute-done((bf16[512,512]{1,0:T(8,128)(2,1)S(1)}, bf16[512,512]{1,0:T(8,128)(2,1)S(1)}, u32[]{:S(2)}, u32[]{:S(2)}) %collective-permute-start.8) | collective-permute-done | bytes 524320 | tf_op jit(solution)/shard_map/ppermute | solution.py:25
  190.7 17.1 %collective-permute-done.10.rest_1_.other = bf16[512,512]{1,0:T(8,128)(2,1)S(1)} collective-permute-done((bf16[512,512]{1,0:T(8,128)(2,1)S(1)}, bf16[512,512]{1,0:T(8,128)(2,1)S(1)}, u32[]{:S(2)}, u32[]{:S(2)}) %collective-permute-start.10) | collective-permute-done | bytes 524320 | tf_op jit(solution)/shard_map/ppermute | solution.py:25
  220.3 3.8 %shard_map.106.rest_1_ = f32[1024,512]{1,0:T(8,128)} custom-call(s32[8]{0:T(128)S(1)} %concatenate.9.index, bf16[512,4096]{1,0:T(8,128)(2,1)} %all-gather.6.cloned.1.call-done.refs_0_.mine, bf16[512,2048]{1,0:T(8,128)(2,1)S(1)} %copy-done.1, bf16[512,512]{1,0:T(8,128)(2,1)} %get-tuple-element.52.grad, ...), custom_call_target="tpu_custom_call", output_to_operand_aliasing={{}: (8, {})} | custom-call | flops 10000000000 | bytes 1 | tf_op jit(solution)/shard_map/pallas_call | solution.py:261
  228.5 3.6 %shard_map.108.rest_2_ = bf16[1024,512]{1,0:T(8,128)(2,1)S(1)} custom-call(s32[8]{0:T(128)S(1)} %concatenate.8.index, bf16[512,4096]{1,0:T(8,128)(2,1)} %all-gather.4.cloned.1.call-done.mine.theirs, bf16[512,4096]{1,0:T(8,128)(2,1)} %all-gather.4.cloned.1.call-done.mine.theirs, bf16[512,512]{1,0:T(8,128)(2,1)} %get-tuple-element.45.grad, ...), custom_call_target="tpu_custom_call" | custom-call | flops 10000000000 | bytes 1 | tf_op jit(solution)/shard_map/pallas_call | solution.py:261
  233.7 12.7 %collective-permute-done.28.rest_1_ = bf16[512,512]{1,0:T(8,128)(2,1)} collective-permute-done((bf16[512,512]{1,0:T(8,128)(2,1)}, bf16[512,512]{1,0:T(8,128)(2,1)}, u32[]{:S(2)}, u32[]{:S(2)}) %collective-permute-start.28) | collective-permute-done | bytes 524320 | tf_op jit(solution)/shard_map/ppermute | solution.py:25
  246.5 3.6 %shard_map.109.rest_1_.rest_3_ = f32[3,512,1024]{2,1,0:T(8,128)} custom-call(s32[8]{0:T(128)S(1)} %concatenate.8.index, bf16[512,4096]{1,0:T(8,128)(2,1)} %all-gather.4.cloned.1.call-done.mine.theirs, bf16[512,4096]{1,0:T(8,128)(2,1)} %all-gather.4.cloned.1.call-done.mine.theirs, bf16[512,512]{1,0:T(8,128)(2,1)S(1)} %copy-done.15, ...), custom_call_target="tpu_custom_call" | custom-call | flops 10000000000 | bytes 1 | tf_op jit(solution)/shard_map/pallas_call | solution.py:261
  258.3 16.2 %collective-permute-done.26.rest_1_ = bf16[512,512]{1,0:T(8,128)(2,1)S(1)} collective-permute-done((bf16[512,512]{1,0:T(8,128)(2,1)S(1)}, bf16[512,512]{1,0:T(8,128)(2,1)S(1)}, u32[]{:S(2)}, u32[]{:S(2)}) %collective-permute-start.26) | collective-permute-done | bytes 524320 | tf_op jit(solution)/shard_map/ppermute | solution.py:25
  284.6 12.4 %collective-permute-done.32.rest_1_ = bf16[512,512]{1,0:T(8,128)(2,1)S(1)} collective-permute-done((bf16[512,512]{1,0:T(8,128)(2,1)S(1)}, bf16[512,512]{1,0:T(8,128)(2,1)S(1)}, u32[]{:S(2)}, u32[]{:S(2)}) %collective-permute-start.32) | collective-permute-done | bytes 524320 | tf_op jit(solution)/shard_map/ppermute | solution.py:25
  303.0 16.4 %collective-permute-done.30.rest_1_ = bf16[512,512]{1,0:T(8,128)(2,1)S(1)} collective-permute-done((bf16[512,512]{1,0:T(8,128)(2,1)S(1)}, bf16[512,512]{1,0:T(8,128)(2,1)S(1)}, u32[]{:S(2)}, u32[]{:S(2)}) %collective-permute-start.30) | collective-permute-done | bytes 524320 | tf_op jit(solution)/shard_map/ppermute | solution.py:25
  319.4 3.8 %shard_map.117.rest_1_.rest_3_ = f32[3,512,1024]{2,1,0:T(8,128)} custom-call(s32[8]{0:T(128)S(1)} %concatenate.8.index, bf16[512,4096]{1,0:T(8,128)(2,1)} %all-gather.4.cloned.1.call-done.mine.theirs, bf16[512,4096]{1,0:T(8,128)(2,1)} %all-gather.4.cloned.1.call-done.mine.theirs, ...), custom_call_target="tpu_custom_call", output_to_operand_aliasing={{}: (8, {})} | custom-call | flops 10000000000 | bytes 1 | tf_op jit(solution)/shard_map/pallas_call | solution.py:261
  325.7 10.5 %collective-permute-done.34.rest_1_ = bf16[512,512]{1,0:T(8,128)(2,1)S(1)} collective-permute-done((bf16[512,512]{1,0:T(8,128)(2,1)S(1)}, bf16[512,512]{1,0:T(8,128)(2,1)S(1)}, u32[]{:S(2)}, u32[]{:S(2)}) %collective-permute-start.34) | collective-permute-done | bytes 524320 | tf_op jit(solution)/shard_map/ppermute | solution.py:25
  339.7 3.9 %collective-permute-done.33.rest_1_ = bf16[512,512]{1,0:T(8,128)(2,1)S(1)} collective-permute-done((bf16[512,512]{1,0:T(8,128)(2,1)S(1)}, bf16[512,512]{1,0:T(8,128)(2,1)S(1)}, u32[]{:S(2)}, u32[]{:S(2)}) %collective-permute-start.33) | collective-permute-done | bytes 524320 | tf_op jit(solution)/shard_map/ppermute | solution.py:25
  (195 shorter events, 141.6 us)
Async XLA Ops:
  7.2 52.9 %all-gather.6.cloned.1.call-start = ((), (), s32[]{:S(2)}) async-start(), calls=%async_computation.1 | async-start | bytes 5242880 | tf_op jit(solution)/shard_map/all_gather | solution.py:318
  7.9 95.9 %all-gather.8.cloned.1.call-start = ((), (), s32[]{:S(2)}) async-start(), calls=%async_computation.2 | async-start | bytes 2621440 | tf_op jit(solution)/shard_map/all_gather | solution.py:335
  8.0 29.1 %collective-permute-start.13 = (bf16[512,1024]{1,0:T(8,128)(2,1)}, bf16[512,1024]{1,0:T(8,128)(2,1)}, u32[]{:S(2)}, u32[]{:S(2)}) collective-permute-start(bf16[512,1024]{1,0:T(8,128)(2,1)} %param.13), channel_id=1, source_target_pairs={{1,8},{3,10},{5,12},{7,14},{8,1},{10,3},{12,5},{14,7},{17,24},{19,... | collective-permute-start | bytes 3145736 | tf_op jit(solution)/shard_map/ppermute | solution.py:304
  47.5 117.6 %all-gather.4.cloned.1.call-start = ((), (), s32[]{:S(2)}) async-start(), calls=%async_computation | async-start | bytes 5242880 | tf_op jit(solution)/shard_map/all_gather | solution.py:340
  55.4 84.4 %collective-permute-start.15 = (bf16[512,512]{1,0:T(8,128)(2,1)}, bf16[512,512]{1,0:T(8,128)(2,1)}, u32[]{:S(2)}, u32[]{:S(2)}) collective-permute-start(bf16[512,512]{1,0:T(8,128)(2,1)} %get-tuple-element.52.grad), channel_id=1, source_target_pairs={{0,8},{4,12},{8,0},{12,4},{16,24},{20,28},{24,16},{28,20},{1,9},{5... | collective-permute-start | bytes 1572872 | tf_op jit(solution)/shard_map/ppermute | solution.py:25
  58.8 29.3 %collective-permute-start.4 = (bf16[512,512]{1,0:T(8,128)(2,1)S(1)}, bf16[512,512]{1,0:T(8,128)(2,1)}, u32[]{:S(2)}, u32[]{:S(2)}) collective-permute-start(bf16[512,512]{1,0:T(8,128)(2,1)S(1)} %get-tuple-element.35.grad), channel_id=1, source_target_pairs={{0,8},{4,12},{8,0},{12,4},{16,24},{20,28},{24,16},{28,20},{1,9},{5... | collective-permute-start | bytes 1572872 | tf_op jit(solution)/shard_map/ppermute | solution.py:25
  118.5 45.8 %collective-permute-start.19 = (bf16[512,512]{1,0:T(8,128)(2,1)S(1)}, bf16[512,512]{1,0:T(8,128)(2,1)S(1)}, u32[]{:S(2)}, u32[]{:S(2)}) collective-permute-start(bf16[512,512]{1,0:T(8,128)(2,1)S(1)} %copy-done.13), channel_id=1, source_target_pairs={{0,8},{4,12},{8,0},{12,4},{16,24},{20,28},{24,16},{28,20},{1,9},{5... | collective-permute-start | bytes 1572872 | tf_op jit(solution)/shard_map/ppermute | solution.py:25
  128.5 53.1 %collective-permute-start.12 = (bf16[512,512]{1,0:T(8,128)(2,1)S(1)}, bf16[512,512]{1,0:T(8,128)(2,1)}, u32[]{:S(2)}, u32[]{:S(2)}) collective-permute-start(bf16[512,512]{1,0:T(8,128)(2,1)S(1)} %get-tuple-element.49.grad), channel_id=1, source_target_pairs={{0,8},{4,12},{8,0},{12,4},{16,24},{20,28},{24,16},{28,20},{1,9},{5... | collective-permute-start | bytes 1572872 | tf_op jit(solution)/shard_map/ppermute | solution.py:25
  135.0 28.5 %collective-permute-start.8 = (bf16[512,512]{1,0:T(8,128)(2,1)S(1)}, bf16[512,512]{1,0:T(8,128)(2,1)S(1)}, u32[]{:S(2)}, u32[]{:S(2)}) collective-permute-start(bf16[512,512]{1,0:T(8,128)(2,1)S(1)} %get-tuple-element.44.rest_1_.grad), channel_id=1, source_target_pairs={{0,8},{4,12},{8,0},{12,4},{16,24},{20,28},{24,16},{28,20},{1,9},{5... | collective-permute-start | bytes 1572872 | tf_op jit(solution)/shard_map/ppermute | solution.py:25
  139.8 30.6 %collective-permute-start.18 = (bf16[256,512]{1,0:T(8,128)(2,1)}, bf16[256,512]{1,0:T(8,128)(2,1)}, u32[]{:S(2)}, u32[]{:S(2)}) collective-permute-start(bf16[256,512]{1,0:T(8,128)(2,1)} %shard_map.96.rest_0_), channel_id=1, source_target_pairs={{0,16},{4,20},{8,24},{12,28},{16,0},{20,4},{24,8},{28,12},{1,17},{... | collective-permute-start | bytes 786440 | tf_op jit(solution)/shard_map/ppermute | solution.py:25
  144.1 31.0 %collective-permute-start.17 = (bf16[512,1024]{1,0:T(8,128)(2,1)}, bf16[512,1024]{1,0:T(8,128)(2,1)}, u32[]{:S(2)}, u32[]{:S(2)}) collective-permute-start(bf16[512,1024]{1,0:T(8,128)(2,1)} %shard_map.97.rest_1_), channel_id=1, source_target_pairs={{0,4},{4,0},{8,12},{12,8},{16,20},{20,16},{24,28},{28,24},{1,5},{5... | collective-permute-start | bytes 3145736 | tf_op jit(solution)/shard_map/ppermute | solution.py:25
  170.4 38.2 %collective-permute-start.23 = (bf16[1024,512]{1,0:T(8,128)(2,1)S(1)}, bf16[1024,512]{1,0:T(8,128)(2,1)S(1)}, u32[]{:S(2)}, u32[]{:S(2)}) collective-permute-start(bf16[1024,512]{1,0:T(8,128)(2,1)S(1)} %shard_map.99.rest_2_), channel_id=1, source_target_pairs={{0,4},{4,0},{8,12},{12,8},{16,20},{20,16},{24,28},{28,24},{1,5},{5... | collective-permute-start | bytes 3145736 | tf_op jit(solution)/shard_map/ppermute | solution.py:25
  178.7 41.7 %collective-permute-start.22 = (bf16[512,512]{1,0:T(8,128)(2,1)}, bf16[512,512]{1,0:T(8,128)(2,1)S(1)}, u32[]{:S(2)}, u32[]{:S(2)}) collective-permute-start(bf16[512,512]{1,0:T(8,128)(2,1)} %shard_map.101.rest_0_), channel_id=1, source_target_pairs={{0,16},{4,20},{8,24},{12,28},{16,0},{20,4},{24,8},{28,12},{1,17},{... | collective-permute-start | bytes 1572872 | tf_op jit(solution)/shard_map/ppermute | solution.py:25
  185.1 39.1 %collective-permute-start.21 = (bf16[1024,512]{1,0:T(8,128)(2,1)S(1)}, bf16[1024,512]{1,0:T(8,128)(2,1)S(1)}, u32[]{:S(2)}, u32[]{:S(2)}) collective-permute-start(bf16[1024,512]{1,0:T(8,128)(2,1)S(1)} %shard_map.102.rest_2_), channel_id=1, source_target_pairs={{0,4},{4,0},{8,12},{12,8},{16,20},{20,16},{24,28},{28,24},{1,5},{5... | collective-permute-start | bytes 3145736 | tf_op jit(solution)/shard_map/ppermute | solution.py:25
  208.6 44.1 %collective-permute-start.11 = (bf16[512,512]{1,0:T(8,128)(2,1)S(1)}, bf16[512,512]{1,0:T(8,128)(2,1)S(1)}, u32[]{:S(2)}, u32[]{:S(2)}) collective-permute-start(bf16[512,512]{1,0:T(8,128)(2,1)S(1)} %get-tuple-element.47.grad), channel_id=1, source_target_pairs={{0,8},{4,12},{8,0},{12,4},{16,24},{20,28},{24,16},{28,20},{1,9},{5... | collective-permute-start | bytes 1572872 | tf_op jit(solution)/shard_map/ppermute | solution.py:25
  213.5 32.9 %collective-permute-start.28 = (bf16[512,512]{1,0:T(8,128)(2,1)}, bf16[512,512]{1,0:T(8,128)(2,1)}, u32[]{:S(2)}, u32[]{:S(2)}) collective-permute-start(bf16[512,512]{1,0:T(8,128)(2,1)} %shard_map.104.rest_0_), channel_id=1, source_target_pairs={{0,16},{4,20},{8,24},{12,28},{16,0},{20,4},{24,8},{28,12},{1,17},{... | collective-permute-start | bytes 1572872 | tf_op jit(solution)/shard_map/ppermute | solution.py:25
  219.8 30.3 %collective-permute-start.27 = (bf16[1024,512]{1,0:T(8,128)(2,1)S(1)}, bf16[1024,512]{1,0:T(8,128)(2,1)S(1)}, u32[]{:S(2)}, u32[]{:S(2)}) collective-permute-start(bf16[1024,512]{1,0:T(8,128)(2,1)S(1)} %shard_map.105.rest_2_), channel_id=1, source_target_pairs={{0,4},{4,0},{8,12},{12,8},{16,20},{20,16},{24,28},{28,24},{1,5},{5... | collective-permute-start | bytes 3145736 | tf_op jit(solution)/shard_map/ppermute | solution.py:25
  228.4 46.0 %collective-permute-start.26 = (bf16[512,512]{1,0:T(8,128)(2,1)S(1)}, bf16[512,512]{1,0:T(8,128)(2,1)S(1)}, u32[]{:S(2)}, u32[]{:S(2)}) collective-permute-start(bf16[512,512]{1,0:T(8,128)(2,1)S(1)} %shard_map.107.rest_0_), channel_id=1, source_target_pairs={{0,16},{4,20},{8,24},{12,28},{16,0},{20,4},{24,8},{28,12},{1,17},{... | collective-permute-start | bytes 1572872 | tf_op jit(solution)/shard_map/ppermute | solution.py:25
  232.1 45.9 %collective-permute-start.25 = (bf16[1024,512]{1,0:T(8,128)(2,1)S(1)}, bf16[1024,512]{1,0:T(8,128)(2,1)S(1)}, u32[]{:S(2)}, u32[]{:S(2)}) collective-permute-start(bf16[1024,512]{1,0:T(8,128)(2,1)S(1)} %shard_map.108.rest_2_), channel_id=1, source_target_pairs={{0,4},{4,0},{8,12},{12,8},{16,20},{20,16},{24,28},{28,24},{1,5},{5... | collective-permute-start | bytes 3145736 | tf_op jit(solution)/shard_map/ppermute | solution.py:25
  252.6 44.3 %collective-permute-start.32 = (bf16[512,512]{1,0:T(8,128)(2,1)S(1)}, bf16[512,512]{1,0:T(8,128)(2,1)S(1)}, u32[]{:S(2)}, u32[]{:S(2)}) collective-permute-start(bf16[512,512]{1,0:T(8,128)(2,1)S(1)} %shard_map.110.rest_0_), channel_id=1, source_target_pairs={{0,16},{4,20},{8,24},{12,28},{16,0},{20,4},{24,8},{28,12},{1,17},{... | collective-permute-start | bytes 1572872 | tf_op jit(solution)/shard_map/ppermute | solution.py:25
  256.8 43.6 %collective-permute-start.31 = (bf16[1024,512]{1,0:T(8,128)(2,1)S(1)}, bf16[1024,512]{1,0:T(8,128)(2,1)S(1)}, u32[]{:S(2)}, u32[]{:S(2)}) collective-permute-start(bf16[1024,512]{1,0:T(8,128)(2,1)S(1)} %shard_map.111.rest_2_), channel_id=1, source_target_pairs={{0,4},{4,0},{8,12},{12,8},{16,20},{20,16},{24,28},{28,24},{1,5},{5... | collective-permute-start | bytes 3145736 | tf_op jit(solution)/shard_map/ppermute | solution.py:25
  280.9 38.5 %collective-permute-start.30 = (bf16[512,512]{1,0:T(8,128)(2,1)S(1)}, bf16[512,512]{1,0:T(8,128)(2,1)S(1)}, u32[]{:S(2)}, u32[]{:S(2)}) collective-permute-start(bf16[512,512]{1,0:T(8,128)(2,1)S(1)} %shard_map.113.rest_0_), channel_id=1, source_target_pairs={{0,16},{4,20},{8,24},{12,28},{16,0},{20,4},{24,8},{28,12},{1,17},{... | collective-permute-start | bytes 1572872 | tf_op jit(solution)/shard_map/ppermute | solution.py:25
  284.5 38.7 %collective-permute-start.29 = (bf16[1024,512]{1,0:T(8,128)(2,1)S(1)}, bf16[1024,512]{1,0:T(8,128)(2,1)S(1)}, u32[]{:S(2)}, u32[]{:S(2)}) collective-permute-start(bf16[1024,512]{1,0:T(8,128)(2,1)S(1)} %shard_map.114.rest_2_), channel_id=1, source_target_pairs={{0,4},{4,0},{8,12},{12,8},{16,20},{20,16},{24,28},{28,24},{1,5},{5... | collective-permute-start | bytes 3145736 | tf_op jit(solution)/shard_map/ppermute | solution.py:25
  302.9 33.4 %collective-permute-start.34 = (bf16[512,512]{1,0:T(8,128)(2,1)S(1)}, bf16[512,512]{1,0:T(8,128)(2,1)S(1)}, u32[]{:S(2)}, u32[]{:S(2)}) collective-permute-start(bf16[512,512]{1,0:T(8,128)(2,1)S(1)} %shard_map.116.rest_2_), channel_id=1, source_target_pairs={{0,16},{4,20},{8,24},{12,28},{16,0},{20,4},{24,8},{28,12},{1,17},{... | collective-permute-start | bytes 1572872 | tf_op jit(solution)/shard_map/ppermute | solution.py:25
  (60 other events, 558.3 us)
Sparse Core Ops, SparseCore 0:
  9.6 37.1 all-gather.5
  48.3 25.3 all-gather.7
  75.3 34.4 all-gather.3

commit v10 on v9

--- a/solution.py
+++ b/solution.py
@@ -13,7 +13,7 @@
 PARAMS = pltpu.CompilerParams(vmem_limit_bytes=48 * 1024 * 1024)
 
 
-COST = pl.CostEstimate(flops=10**10, bytes_accessed=1, transcendentals=0)
+COST = pl.CostEstimate(flops=5*10**9, bytes_accessed=1, transcendentals=0)
 
 
 def after(array, *others):
@@ -25,13 +25,15 @@
     return lax.ppermute(array, "seq", [(i, i ^ (1 << bit)) for i in range(size)])
 
 
-def entering(block, low, reverse):
+def entering(block, low, reverse, last=None):
     size, position = lax.axis_size("seq"), lax.axis_index("seq")
     bits = size.bit_length() - 1
     total, before = block, jnp.zeros_like(block)
     sent, came = [], []
     for bit in range(bits):
         step = 1 << bit
+        if bit == bits - 1 and last is not None:
+            low = after(low, last(came))
         sent.append(low)
         if bit < bits - 1:
             came.append(flip(low, bit))
@@ -157,23 +159,10 @@
         value_local[:, cols] = upper_mm(causal(qh, k[:, cols]), grad)
 
 
-def key_value_kernel(key_local, value_local, k, v, state, key_first, key_second, value_first, value_second):
-    step, steps = pl.program_id(0), pl.num_programs(0)
-    keys, values = [], []
+def key_value_kernel(key_local, value_local, k, v, state, key_grad, value_grad):
     for i, cols in enumerate(head_slices(k)):
-        keys.append((key_local[:, cols] + mm_t(v[:, cols], state[i])).astype(BF16))
-        values.append((value_local[:, cols] + mm(k[:, cols], state[i])).astype(BF16))
-    keys, values = jnp.concatenate(keys, axis=1), jnp.concatenate(values, axis=1)
-
-    @pl.when(step < steps // 2)
-    def _():
-        key_first[...] = keys
-        value_first[...] = values
-
-    @pl.when(step >= steps // 2)
-    def _():
-        key_second[...] = keys
-        value_second[...] = values
+        key_grad[:, cols] = (key_local[:, cols] + mm_t(v[:, cols], state[i])).astype(BF16)
+        value_grad[:, cols] = (value_local[:, cols] + mm(k[:, cols], state[i])).astype(BF16)
 
 
 def without(kernel, first, count):
@@ -357,37 +346,15 @@
         query_kernel,
         [("rows", pre), k, v, ("heads", state_low)],
         [("first", BF16), ("second", BF16)],
-        [gated[0][1]],
-    )
-    query_grad = [(part, flip(after(part, came[1]), gather_bit)) for part in query_grad]
-    key_local, value_local = by_heads(
-        own_kernel,
-        [("rows", pre), q, k, v],
-        [("rows", F32), ("rows", F32)],
-        [query_grad[0][0], sent[1]],
-    )
-    grad_low = (grad_parts[0] + grad_parts[1].astype(F32)).astype(BF16)
-    late_grads = by_heads(
-        key_value_kernel,
-        [("rows", key_local), ("rows", value_local), k, v, ("heads", grad_low)],
-        [("first", BF16), ("second", BF16)] * 2,
-    )
-    chained = []
-    for part in late_grads:
-        chained.append((part, flip(after(part, chained[-1][1]) if chained else part, gather_bit)))
-    late_grads = chained
-
+    )
     half = width // 2
     quarter = half // 2
-    pieces = [(both_cot, gated[0], quarter, i, True, (i, 0)) for i in range(2)]
-    pieces += [(both_cot, gated[1], half, 0, True, (1, 0))]
-    pieces += [(both_input, query_grad[i], half, 0, False, (0, 0, i)) for i in range(2)]
-    pieces += [(both_input, late_grads[i], half, 0, False, (1 + i // 2, 0, i % 2)) for i in range(4)]
+    pieces = [(both_cot, gated[i], half, 0, True, (i, 0)) for i in range(2)]
     starts = [chunks - (chunks >> i) for i in range(len(halving) + 1)]
     shapes = {True: (width, owned), False: (3, owned, width)}
     targets = {True: None, False: None}
     received = {}
-    last = [key_local]
+    last = [query_grad[0]]
 
     def stage(i, n):
         features, (grad, other), cols, block, turned, place = pieces[i]
@@ -406,14 +373,31 @@
     stages = len(halving) + 1
     stage(0, 0)
     stage(1, 0)
+    key_local, value_local = by_heads(
+        own_kernel,
+        [("rows", pre), q, k, v],
+        [("rows", F32), ("rows", F32)],
+        [*last, sent[1]],
+    )
+    last.append(key_local)
+    grad_low = (grad_parts[0] + grad_parts[1].astype(F32)).astype(BF16)
+    late_grads = by_heads(
+        key_value_kernel,
+        [("rows", key_local), ("rows", value_local), k, v, ("heads", grad_low)],
+        [("rows", BF16)] * 2,
+    )
+    first = [(part, flip(after(part, came[1]), gather_bit)) for part in query_grad]
+    key_grad = late_grads[0], flip(late_grads[0], gather_bit)
+    value_grad = late_grads[1], flip(after(late_grads[1], key_grad[1]), gather_bit)
+    pieces += [(both_input, first[i], half, 0, False, (0, 0, i)) for i in range(2)]
+    pieces += [(both_input, key_grad, half, i, False, (1, 0, i)) for i in range(2)]
+    pieces += [(both_input, value_grad, half, i, False, (2, 0, i)) for i in range(2)]
     for i in range(len(pieces)):
         for n in range(1, stages - 1):
             stage(i, n)
         if i + 2 < len(pieces):
-            if i == 0:
-                last.append(late_grads[0][0])
-            if 2 <= i < 6:
-                last.append(late_grads[i - 2][1])
+            if i == 1:
+                last.append(late_grads[0])
             stage(i + 2, 0)
         if i >= 1:
             stage(i - 1, stages - 1)

time: 355 us -> 348 us (0.980)
  the two profiles are of different devices: /device:TPU:0 before, /device:TPU:28 now
where the time goes in v10:
time: 348 us; the launch traced here: 347 us
  waiting for transfers between devices  152 us (44%)
  Pallas kernels  119 us (34%)
  starting transfers between devices  37.1 us (11%)
  local copies, waits for them, and re-layouts  20.6 us (6%)
  between operations  14.2 us (4%)
  other arithmetic  3.7 us (1%)
    ppermute x26, waiting for transfers between devices, flip(): return lax.ppermute(array, 'seq', [(i, i ^ 1 << bit) for i in range(size)])  136 us
    pallas_call x24, Pallas kernels, term(): pl.pallas_call(functools.partial(term_kernel, turned, len(received)), gri...  80.9 us
    pallas_call x8, Pallas kernels, by_heads(): pl.pallas_call(without(kernel, len(args), len(waits)), grid=(count,), in_...  38.5 us
    ppermute x26, starting transfers between devices, flip(): return lax.ppermute(array, 'seq', [(i, i ^ 1 << bit) for i in range(size)])  28.7 us
    unnamed x68, local copies, waits for them, and re-layouts  19.4 us
    ppermute x3, waiting for transfers between devices, across(): return lax.ppermute(array, ('seq', 'head'), pairs)  8.29 us
  transfers between devices with their start and end apart: 34, of which 18 were waited for; matrix products, arithmetic and copies ran while one was open for 1% of the time, Pallas kernels for 33%

profile of v10, /device:TPU:28, one launch (start us, length us, event | category | flops | bytes accessed | tf_op | source)
XLA Modules:
  0.0 346.6 jit_solution(16048409554721934888)
XLA Ops:
  15.5 6.3 %collective-permute-done = bf16[8,128,128]{2,1,0:T(8,128)(2,1)S(1)} collective-permute-done((bf16[8,128,128]{2,1,0:T(8,128)(2,1)S(1)}, bf16[8,128,128]{2,1,0:T(8,128)(2,1)S(1)}, u32[]{:S(2)}, u32[]{:S(2)}) %collective-permute-start) | collective-permute-done | bytes 262176 | tf_op jit(solution)/shard_map/ppermute | solution.py:25
  22.5 7.7 %collective-permute-done.1 = bf16[8,128,128]{2,1,0:T(8,128)(2,1)S(1)} collective-permute-done((bf16[8,128,128]{2,1,0:T(8,128)(2,1)S(1)}, bf16[8,128,128]{2,1,0:T(8,128)(2,1)S(1)}, u32[]{:S(2)}, u32[]{:S(2)}) %collective-permute-start.1) | collective-permute-done | bytes 262176 | tf_op jit(solution)/shard_map/ppermute | solution.py:25
  39.8 6.4 %collective-permute-done.3 = bf16[8,128,128]{2,1,0:T(8,128)(2,1)S(1)} collective-permute-done((bf16[8,128,128]{2,1,0:T(8,128)(2,1)S(1)}, bf16[8,128,128]{2,1,0:T(8,128)(2,1)S(1)}, u32[]{:S(2)}, u32[]{:S(2)}) %collective-permute-start.3) | collective-permute-done | bytes 262176 | tf_op jit(solution)/shard_map/ppermute | solution.py:47
  50.3 4.8 %shard_map.88 = (f32[512,1024]{1,0:T(8,128)S(1)}, bf16[512,512]{1,0:T(8,128)(2,1)}, bf16[512,512]{1,0:T(8,128)(2,1)}) custom-call(f32[512,1024]{1,0:T(8,128)} %copy-done.30, bf16[512,1024]{1,0:T(8,128)(2,1)S(1)} %copy-done.3, bf16[8,128,128]{2,1,0:T(8,128)(2,1)S(1)} %fusion.2.refs_2_.refs_3_, f32[1,1024]{1,0:T(1,128)S(1)} %bitcast.6), custom_call_target="tpu_custom_call" | custom-call | flops 5000000000 | bytes 1 | tf_op jit(solution)/shard_map/pallas_call | solution.py:196
  56.4 8.3 %collective-permute-done.2 = bf16[512,1024]{1,0:T(8,128)(2,1)S(1)} collective-permute-done((bf16[512,1024]{1,0:T(8,128)(2,1)}, bf16[512,1024]{1,0:T(8,128)(2,1)S(1)}, u32[]{:S(2)}, u32[]{:S(2)}) %collective-permute-start.2) | collective-permute-done | bytes 1048608 | tf_op jit(solution)/shard_map/ppermute | solution.py:293
  69.7 8.4 %shard_map.89.refs_0_ = f32[512,1024]{1,0:T(8,128)S(1)} custom-call(bf16[512,4096]{1,0:T(8,128)(2,1)} %all-gather.6.cloned.1.call-done.refs_0_.mine, bf16[1024,4096]{1,0:T(8,128)(2,1)} %refs_1_.9, f32[512,1024]{1,0:T(8,128)S(1)} %copy-done.29), custom_call_target="tpu_custom_call" | custom-call | flops 5000000000 | bytes 1 | tf_op jit(solution)/shard_map/pallas_call | solution.py:196
  78.2 4.5 %shard_map.90 = (bf16[512,1024]{1,0:T(8,128)(2,1)S(1)}, f32[8,128,128]{2,1,0:T(8,128)S(1)}, bf16[8,128,128]{2,1,0:T(8,128)(2,1)S(1)}) custom-call(f32[512,1024]{1,0:T(8,128)S(1)} %shard_map.89.refs_0_, f32[512,1024]{1,0:T(8,128)} %copy-done.28, bf16[512,1024]{1,0:T(8,128)(2,1)S(1)} %copy-done.3, f32[1,1024]{1,0:T(1,128)S(1)} %bitcast.7), custom_call_target="tpu_custom_call" | custom-call | flops 5000000000 | bytes 1 | tf_op jit(solution)/shard_map/pallas_call | solution.py:196
  84.3 4.4 %shard_map.91 = (bf16[512,512]{1,0:T(8,128)(2,1)S(1)}, bf16[512,512]{1,0:T(8,128)(2,1)}) custom-call(bf16[512,1024]{1,0:T(8,128)(2,1)S(1)} %get-tuple-element.30.refs_0_, bf16[512,1024]{1,0:T(8,128)(2,1)S(1)} %copy-done.5, bf16[512,1024]{1,0:T(8,128)(2,1)S(1)} %copy-done.9, bf16[8,128,128]{2,1,0:T(8,128)(2,1)S(1)} %fusion.2.refs_2_.refs_3_), custom_call_target="tpu_custom_call" | custom-call | flops 5000000000 | bytes 1 | tf_op jit(solution)/shard_map/pallas_call | solution.py:196
  100.3 4.3 %shard_map.93.refs_4_.rest_1_ = bf16[512,1024]{1,0:T(8,128)(2,1)} custom-call(s32[8]{0:T(128)S(1)} %concatenate.9.index, bf16[512,4096]{1,0:T(8,128)(2,1)} %all-gather.6.cloned.1.call-done.refs_0_.mine, bf16[512,2048]{1,0:T(8,128)(2,1)S(1)} %copy-done.1, bf16[512,512]{1,0:T(8,128)(2,1)} %get-tuple-element.33.grad, ...), custom_call_target="tpu_custom_call" | custom-call | flops 5000000000 | bytes 1 | tf_op jit(solution)/shard_map/pallas_call | solution.py:250
  108.3 8.0 %shard_map.94 = (f32[512,1024]{1,0:T(8,128)}, f32[512,1024]{1,0:T(8,128)}) custom-call(bf16[512,1024]{1,0:T(8,128)(2,1)S(1)} %copy-done.32, bf16[512,1024]{1,0:T(8,128)(2,1)S(1)} %copy-done.3, bf16[512,1024]{1,0:T(8,128)(2,1)S(1)} %copy-done.5, bf16[512,1024]{1,0:T(8,128)(2,1)S(1)} %copy-done.10, bf16[512,1024]{1,0:T(8,128)(2,1)} %shard_map.93.refs_4_.rest_1_, ...), custom_call_target="tpu_custom_call" | custom-call | flops 5000000000 | bytes 1 | tf_op jit(solution)/shard_map/pallas_call | solution.py:196
  138.0 7.5 %collective-permute-done.14.rest_0_ = bf16[512,1024]{1,0:T(8,128)(2,1)} collective-permute-done((bf16[512,1024]{1,0:T(8,128)(2,1)}, bf16[512,1024]{1,0:T(8,128)(2,1)}, u32[]{:S(2)}, u32[]{:S(2)}) %collective-permute-start.14) | collective-permute-done | bytes 1048608 | tf_op jit(solution)/shard_map/ppermute | solution.py:25
  149.1 15.8 %collective-permute-done.13.other = bf16[512,512]{1,0:T(8,128)(2,1)} collective-permute-done((bf16[512,512]{1,0:T(8,128)(2,1)}, bf16[512,512]{1,0:T(8,128)(2,1)}, u32[]{:S(2)}, u32[]{:S(2)}) %collective-permute-start.13) | collective-permute-done | bytes 524320 | tf_op jit(solution)/shard_map/ppermute | solution.py:25
  169.2 6.2 %collective-permute-done.20.rest_1_ = bf16[512,512]{1,0:T(8,128)(2,1)} collective-permute-done((bf16[512,512]{1,0:T(8,128)(2,1)}, bf16[512,512]{1,0:T(8,128)(2,1)}, u32[]{:S(2)}, u32[]{:S(2)}) %collective-permute-start.20) | collective-permute-done | bytes 524320 | tf_op jit(solution)/shard_map/ppermute | solution.py:25
  175.5 3.8 %shard_map.100.rest_1_.rest_3_ = f32[1024,512]{1,0:T(8,128)} custom-call(s32[8]{0:T(128)S(1)} %concatenate.9.index, bf16[512,4096]{1,0:T(8,128)(2,1)} %all-gather.6.cloned.1.call-done.refs_0_.mine, bf16[512,2048]{1,0:T(8,128)(2,1)S(1)} %copy-done.2, bf16[512,512]{1,0:T(8,128)(2,1)} %get-tuple-element.34.grad, bf16[512,512]{1,0:T(8,128)(2,1)} %collective-permute-done.7.other, ...), custom_call_target="tpu_custom_call" | custom-call | flops 5000000000 | bytes 1 | tf_op jit(solution)/shard_map/pallas_call | solution.py:250
  179.3 5.9 %collective-permute-done.11.other = bf16[512,1024]{1,0:T(8,128)(2,1)S(1)} collective-permute-done((bf16[512,1024]{1,0:T(8,128)(2,1)S(1)}, bf16[512,1024]{1,0:T(8,128)(2,1)S(1)}, u32[]{:S(2)}, u32[]{:S(2)}) %collective-permute-start.11) | collective-permute-done | bytes 1048608 | tf_op jit(solution)/shard_map/ppermute | solution.py:25
  190.0 5.6 %collective-permute-start.24 = (bf16[512,512]{1,0:T(8,128)(2,1)}, bf16[512,512]{1,0:T(8,128)(2,1)}, u32[]{:S(2)}, u32[]{:S(2)}) collective-permute-start(bf16[512,512]{1,0:T(8,128)(2,1)} %shard_map.101.rest_0_), channel_id=1, source_target_pairs={{0,16},{4,20},{8,24},{12,28},{16,0},{20,4},{24,8},{28,12},{1,17},{... | collective-permute-start | bytes 1572872 | tf_op jit(solution)/shard_map/ppermute | solution.py:25
  195.7 4.1 %shard_map.102.rest_2_ = bf16[1024,512]{1,0:T(8,128)(2,1)} custom-call(s32[8]{0:T(128)S(1)} %concatenate.8.index, bf16[512,4096]{1,0:T(8,128)(2,1)} %all-gather.4.cloned.1.call-done.mine.theirs, bf16[512,4096]{1,0:T(8,128)(2,1)} %all-gather.4.cloned.1.call-done.mine.theirs, bf16[512,1024]{1,0:T(8,128)(2,1)S(1)} %get-tuple-element.41.rest_1_.grad, ...), custom_call_target="tpu_custom_call" | custom-call | flops 5000000000 | bytes 1 | tf_op jit(solution)/shard_map/pallas_call | solution.py:250
  202.1 3.8 %shard_map.103.rest_1_ = f32[1024,512]{1,0:T(8,128)} custom-call(s32[8]{0:T(128)S(1)} %concatenate.9.index, bf16[512,4096]{1,0:T(8,128)(2,1)} %all-gather.6.cloned.1.call-done.refs_0_.mine, bf16[512,2048]{1,0:T(8,128)(2,1)S(1)} %copy-done.2, bf16[512,512]{1,0:T(8,128)(2,1)} %get-tuple-element.33.grad, ...), custom_call_target="tpu_custom_call", output_to_operand_aliasing={{}: (8, {})} | custom-call | flops 5000000000 | bytes 1 | tf_op jit(solution)/shard_map/pallas_call | solution.py:250
  215.3 4.8 %collective-permute-done.24.rest_1_ = bf16[512,512]{1,0:T(8,128)(2,1)} collective-permute-done((bf16[512,512]{1,0:T(8,128)(2,1)}, bf16[512,512]{1,0:T(8,128)(2,1)}, u32[]{:S(2)}, u32[]{:S(2)}) %collective-permute-start.24) | collective-permute-done | bytes 524320 | tf_op jit(solution)/shard_map/ppermute | solution.py:25
  233.6 25.0 %collective-permute-done.22.rest_1_ = bf16[512,512]{1,0:T(8,128)(2,1)S(1)} collective-permute-done((bf16[512,512]{1,0:T(8,128)(2,1)S(1)}, bf16[512,512]{1,0:T(8,128)(2,1)S(1)}, u32[]{:S(2)}, u32[]{:S(2)}) %collective-permute-start.22) | collective-permute-done | bytes 524320 | tf_op jit(solution)/shard_map/ppermute | solution.py:25
  269.1 23.3 %collective-permute-done.28.rest_1_ = bf16[512,512]{1,0:T(8,128)(2,1)S(1)} collective-permute-done((bf16[512,512]{1,0:T(8,128)(2,1)S(1)}, bf16[512,512]{1,0:T(8,128)(2,1)S(1)}, u32[]{:S(2)}, u32[]{:S(2)}) %collective-permute-start.28) | collective-permute-done | bytes 524320 | tf_op jit(solution)/shard_map/ppermute | solution.py:25
  298.4 16.4 %collective-permute-done.26.rest_1_ = bf16[512,512]{1,0:T(8,128)(2,1)S(1)} collective-permute-done((bf16[512,512]{1,0:T(8,128)(2,1)S(1)}, bf16[512,512]{1,0:T(8,128)(2,1)S(1)}, u32[]{:S(2)}, u32[]{:S(2)}) %collective-permute-start.26) | collective-permute-done | bytes 524320 | tf_op jit(solution)/shard_map/ppermute | solution.py:25
  320.9 5.2 %collective-permute-done.30.rest_1_ = bf16[512,512]{1,0:T(8,128)(2,1)S(1)} collective-permute-done((bf16[512,512]{1,0:T(8,128)(2,1)S(1)}, bf16[512,512]{1,0:T(8,128)(2,1)S(1)}, u32[]{:S(2)}, u32[]{:S(2)}) %collective-permute-start.30) | collective-permute-done | bytes 524320 | tf_op jit(solution)/shard_map/ppermute | solution.py:25
  329.5 7.1 %collective-permute-done.29.rest_1_ = bf16[512,512]{1,0:T(8,128)(2,1)S(1)} collective-permute-done((bf16[512,512]{1,0:T(8,128)(2,1)S(1)}, bf16[512,512]{1,0:T(8,128)(2,1)S(1)}, u32[]{:S(2)}, u32[]{:S(2)}) %collective-permute-start.29) | collective-permute-done | bytes 524320 | tf_op jit(solution)/shard_map/ppermute | solution.py:25
  (160 shorter events, 134.8 us)
Async XLA Ops:
  7.2 61.0 %all-gather.6.cloned.1.call-start = ((), (), s32[]{:S(2)}) async-start(), calls=%async_computation.1 | async-start | bytes 5242880 | tf_op jit(solution)/shard_map/all_gather | solution.py:307
  7.9 82.6 %all-gather.8.cloned.1.call-start = ((), (), s32[]{:S(2)}) async-start(), calls=%async_computation.2 | async-start | bytes 2621440 | tf_op jit(solution)/shard_map/all_gather | solution.py:324
  8.0 23.6 %collective-permute-start.4 = (bf16[512,1024]{1,0:T(8,128)(2,1)}, bf16[512,1024]{1,0:T(8,128)(2,1)}, u32[]{:S(2)}, u32[]{:S(2)}) collective-permute-start(bf16[512,1024]{1,0:T(8,128)(2,1)} %param.13), channel_id=1, source_target_pairs={{1,8},{3,10},{5,12},{7,14},{8,1},{10,3},{12,5},{14,7},{17,24},{19,... | collective-permute-start | bytes 3145736 | tf_op jit(solution)/shard_map/ppermute | solution.py:293
  48.3 83.7 %all-gather.4.cloned.1.call-start = ((), (), s32[]{:S(2)}) async-start(), calls=%async_computation | async-start | bytes 5242880 | tf_op jit(solution)/shard_map/all_gather | solution.py:329
  66.1 34.2 %collective-permute-start.6 = (bf16[512,512]{1,0:T(8,128)(2,1)}, bf16[512,512]{1,0:T(8,128)(2,1)}, u32[]{:S(2)}, u32[]{:S(2)}) collective-permute-start(bf16[512,512]{1,0:T(8,128)(2,1)} %get-tuple-element.33.grad), channel_id=1, source_target_pairs={{0,8},{4,12},{8,0},{12,4},{16,24},{20,28},{24,16},{28,20},{1,9},{5... | collective-permute-start | bytes 1572872 | tf_op jit(solution)/shard_map/ppermute | solution.py:25
  66.1 24.4 %collective-permute-start.7 = (bf16[512,512]{1,0:T(8,128)(2,1)}, bf16[512,512]{1,0:T(8,128)(2,1)}, u32[]{:S(2)}, u32[]{:S(2)}) collective-permute-start(bf16[512,512]{1,0:T(8,128)(2,1)} %get-tuple-element.34.grad), channel_id=1, source_target_pairs={{0,8},{4,12},{8,0},{12,4},{16,24},{20,28},{24,16},{28,20},{1,9},{5... | collective-permute-start | bytes 1572872 | tf_op jit(solution)/shard_map/ppermute | solution.py:25
  96.8 27.2 %collective-permute-start.16 = (bf16[512,1024]{1,0:T(8,128)(2,1)S(1)}, bf16[512,1024]{1,0:T(8,128)(2,1)S(1)}, u32[]{:S(2)}, u32[]{:S(2)}) collective-permute-start(bf16[512,1024]{1,0:T(8,128)(2,1)S(1)} %shard_map.92.rest_0_), channel_id=1, source_target_pairs={{0,4},{4,0},{8,12},{12,8},{16,20},{20,16},{24,28},{28,24},{1,5},{5... | collective-permute-start | bytes 3145736 | tf_op jit(solution)/shard_map/ppermute | solution.py:25
  104.6 40.9 %collective-permute-start.14 = (bf16[512,1024]{1,0:T(8,128)(2,1)}, bf16[512,1024]{1,0:T(8,128)(2,1)}, u32[]{:S(2)}, u32[]{:S(2)}) collective-permute-start(bf16[512,1024]{1,0:T(8,128)(2,1)} %shard_map.93.refs_4_.rest_1_), channel_id=1, source_target_pairs={{0,4},{4,0},{8,12},{12,8},{16,20},{20,16},{24,28},{28,24},{1,5},{5... | collective-permute-start | bytes 3145736 | tf_op jit(solution)/shard_map/ppermute | solution.py:25
  118.0 46.9 %collective-permute-start.13 = (bf16[512,512]{1,0:T(8,128)(2,1)}, bf16[512,512]{1,0:T(8,128)(2,1)}, u32[]{:S(2)}, u32[]{:S(2)}) collective-permute-start(bf16[512,512]{1,0:T(8,128)(2,1)} %get-tuple-element.44.grad), channel_id=1, source_target_pairs={{0,8},{4,12},{8,0},{12,4},{16,24},{20,28},{24,16},{28,20},{1,9},{5... | collective-permute-start | bytes 1572872 | tf_op jit(solution)/shard_map/ppermute | solution.py:25
  122.1 63.0 %collective-permute-start.11 = (bf16[512,1024]{1,0:T(8,128)(2,1)S(1)}, bf16[512,1024]{1,0:T(8,128)(2,1)S(1)}, u32[]{:S(2)}, u32[]{:S(2)}) collective-permute-start(bf16[512,1024]{1,0:T(8,128)(2,1)S(1)} %get-tuple-element.41.rest_1_.grad), channel_id=1, source_target_pairs={{0,8},{4,12},{8,0},{12,4},{16,24},{20,28},{24,16},{28,20},{1,9},{5... | collective-permute-start | bytes 3145736 | tf_op jit(solution)/shard_map/ppermute | solution.py:25
  127.4 48.1 %collective-permute-start.20 = (bf16[512,512]{1,0:T(8,128)(2,1)}, bf16[512,512]{1,0:T(8,128)(2,1)}, u32[]{:S(2)}, u32[]{:S(2)}) collective-permute-start(bf16[512,512]{1,0:T(8,128)(2,1)} %shard_map.96.rest_0_), channel_id=1, source_target_pairs={{0,16},{4,20},{8,24},{12,28},{16,0},{20,4},{24,8},{28,12},{1,17},{... | collective-permute-start | bytes 1572872 | tf_op jit(solution)/shard_map/ppermute | solution.py:25
  137.4 47.7 %collective-permute-start.19 = (bf16[1024,512]{1,0:T(8,128)(2,1)S(1)}, bf16[1024,512]{1,0:T(8,128)(2,1)S(1)}, u32[]{:S(2)}, u32[]{:S(2)}) collective-permute-start(bf16[1024,512]{1,0:T(8,128)(2,1)S(1)} %shard_map.97.rest_1_), channel_id=1, source_target_pairs={{0,4},{4,0},{8,12},{12,8},{16,20},{20,16},{24,28},{28,24},{1,5},{5... | collective-permute-start | bytes 3145736 | tf_op jit(solution)/shard_map/ppermute | solution.py:25
  149.1 51.2 %collective-permute-start.18 = (bf16[512,512]{1,0:T(8,128)(2,1)}, bf16[512,512]{1,0:T(8,128)(2,1)S(1)}, u32[]{:S(2)}, u32[]{:S(2)}) collective-permute-start(bf16[512,512]{1,0:T(8,128)(2,1)} %shard_map.98.rest_0_), channel_id=1, source_target_pairs={{0,16},{4,20},{8,24},{12,28},{16,0},{20,4},{24,8},{28,12},{1,17},{... | collective-permute-start | bytes 1572872 | tf_op jit(solution)/shard_map/ppermute | solution.py:25
  168.6 37.4 %collective-permute-start.17 = (bf16[1024,512]{1,0:T(8,128)(2,1)S(1)}, bf16[1024,512]{1,0:T(8,128)(2,1)S(1)}, u32[]{:S(2)}, u32[]{:S(2)}) collective-permute-start(bf16[1024,512]{1,0:T(8,128)(2,1)S(1)} %shard_map.99.rest_2_), channel_id=1, source_target_pairs={{0,4},{4,0},{8,12},{12,8},{16,20},{20,16},{24,28},{28,24},{1,5},{5... | collective-permute-start | bytes 3145736 | tf_op jit(solution)/shard_map/ppermute | solution.py:25
  185.1 44.6 %collective-permute-start.12 = (bf16[512,1024]{1,0:T(8,128)(2,1)S(1)}, bf16[512,1024]{1,0:T(8,128)(2,1)S(1)}, u32[]{:S(2)}, u32[]{:S(2)}) collective-permute-start(bf16[512,1024]{1,0:T(8,128)(2,1)S(1)} %get-tuple-element.42.grad), channel_id=1, source_target_pairs={{0,8},{4,12},{8,0},{12,4},{16,24},{20,28},{24,16},{28,20},{1,9},{5... | collective-permute-start | bytes 3145736 | tf_op jit(solution)/shard_map/ppermute | solution.py:25
  190.0 30.1 %collective-permute-start.24 = (bf16[512,512]{1,0:T(8,128)(2,1)}, bf16[512,512]{1,0:T(8,128)(2,1)}, u32[]{:S(2)}, u32[]{:S(2)}) collective-permute-start(bf16[512,512]{1,0:T(8,128)(2,1)} %shard_map.101.rest_0_), channel_id=1, source_target_pairs={{0,16},{4,20},{8,24},{12,28},{16,0},{20,4},{24,8},{28,12},{1,17},{... | collective-permute-start | bytes 1572872 | tf_op jit(solution)/shard_map/ppermute | solution.py:25
  199.8 26.3 %collective-permute-start.23 = (bf16[1024,512]{1,0:T(8,128)(2,1)}, bf16[1024,512]{1,0:T(8,128)(2,1)S(1)}, u32[]{:S(2)}, u32[]{:S(2)}) collective-permute-start(bf16[1024,512]{1,0:T(8,128)(2,1)} %shard_map.102.rest_2_), channel_id=1, source_target_pairs={{0,4},{4,0},{8,12},{12,8},{16,20},{20,16},{24,28},{28,24},{1,5},{5... | collective-permute-start | bytes 3145736 | tf_op jit(solution)/shard_map/ppermute | solution.py:25
  210.4 48.3 %collective-permute-start.22 = (bf16[512,512]{1,0:T(8,128)(2,1)S(1)}, bf16[512,512]{1,0:T(8,128)(2,1)S(1)}, u32[]{:S(2)}, u32[]{:S(2)}) collective-permute-start(bf16[512,512]{1,0:T(8,128)(2,1)S(1)} %shard_map.104.rest_0_), channel_id=1, source_target_pairs={{0,16},{4,20},{8,24},{12,28},{16,0},{20,4},{24,8},{28,12},{1,17},{... | collective-permute-start | bytes 1572872 | tf_op jit(solution)/shard_map/ppermute | solution.py:25
  213.7 48.7 %collective-permute-start.21 = (bf16[1024,512]{1,0:T(8,128)(2,1)S(1)}, bf16[1024,512]{1,0:T(8,128)(2,1)S(1)}, u32[]{:S(2)}, u32[]{:S(2)}) collective-permute-start(bf16[1024,512]{1,0:T(8,128)(2,1)S(1)} %shard_map.105.rest_2_), channel_id=1, source_target_pairs={{0,4},{4,0},{8,12},{12,8},{16,20},{20,16},{24,28},{28,24},{1,5},{5... | collective-permute-start | bytes 3145736 | tf_op jit(solution)/shard_map/ppermute | solution.py:25
  228.6 63.8 %collective-permute-start.28 = (bf16[512,512]{1,0:T(8,128)(2,1)S(1)}, bf16[512,512]{1,0:T(8,128)(2,1)S(1)}, u32[]{:S(2)}, u32[]{:S(2)}) collective-permute-start(bf16[512,512]{1,0:T(8,128)(2,1)S(1)} %shard_map.107.rest_0_), channel_id=1, source_target_pairs={{0,16},{4,20},{8,24},{12,28},{16,0},{20,4},{24,8},{28,12},{1,17},{... | collective-permute-start | bytes 1572872 | tf_op jit(solution)/shard_map/ppermute | solution.py:25
  233.1 62.8 %collective-permute-start.27 = (bf16[1024,512]{1,0:T(8,128)(2,1)S(1)}, bf16[1024,512]{1,0:T(8,128)(2,1)S(1)}, u32[]{:S(2)}, u32[]{:S(2)}) collective-permute-start(bf16[1024,512]{1,0:T(8,128)(2,1)S(1)} %shard_map.108.rest_2_), channel_id=1, source_target_pairs={{0,4},{4,0},{8,12},{12,8},{16,20},{20,16},{24,28},{28,24},{1,5},{5... | collective-permute-start | bytes 3145736 | tf_op jit(solution)/shard_map/ppermute | solution.py:25
  264.9 49.9 %collective-permute-start.26 = (bf16[512,512]{1,0:T(8,128)(2,1)S(1)}, bf16[512,512]{1,0:T(8,128)(2,1)S(1)}, u32[]{:S(2)}, u32[]{:S(2)}) collective-permute-start(bf16[512,512]{1,0:T(8,128)(2,1)S(1)} %shard_map.110.rest_0_), channel_id=1, source_target_pairs={{0,16},{4,20},{8,24},{12,28},{16,0},{20,4},{24,8},{28,12},{1,17},{... | collective-permute-start | bytes 1572872 | tf_op jit(solution)/shard_map/ppermute | solution.py:25
  268.5 49.8 %collective-permute-start.25 = (bf16[1024,512]{1,0:T(8,128)(2,1)S(1)}, bf16[1024,512]{1,0:T(8,128)(2,1)S(1)}, u32[]{:S(2)}, u32[]{:S(2)}) collective-permute-start(bf16[1024,512]{1,0:T(8,128)(2,1)S(1)} %shard_map.111.rest_2_), channel_id=1, source_target_pairs={{0,4},{4,0},{8,12},{12,8},{16,20},{20,16},{24,28},{28,24},{1,5},{5... | collective-permute-start | bytes 3145736 | tf_op jit(solution)/shard_map/ppermute | solution.py:25
  298.3 27.7 %collective-permute-start.30 = (bf16[512,512]{1,0:T(8,128)(2,1)S(1)}, bf16[512,512]{1,0:T(8,128)(2,1)S(1)}, u32[]{:S(2)}, u32[]{:S(2)}) collective-permute-start(bf16[512,512]{1,0:T(8,128)(2,1)S(1)} %shard_map.113.rest_2_), channel_id=1, source_target_pairs={{0,16},{4,20},{8,24},{12,28},{16,0},{20,4},{24,8},{28,12},{1,17},{... | collective-permute-start | bytes 1572872 | tf_op jit(solution)/shard_map/ppermute | solution.py:25
  (44 other events, 384.3 us)
Sparse Core Ops, SparseCore 0:
  9.6 34.4 all-gather.5
  48.4 22.5 all-gather.7
  72.6 34.4 all-gather.3

commit v11 on v10

--- a/solution.py
+++ b/solution.py
@@ -307,10 +307,10 @@
     gathered_cot = lax.all_gather(cotangent, "head", axis=1, tiled=True)
 
     block_state, block_low = by_heads(state_kernel, [k, v], [("heads", F32), ("heads", BF16)])
-    state_parts, sent, came = entering(block_state, block_low, False)
+    state_parts, sent, came_in = entering(block_state, block_low, False)
     (local,) = by_heads(local_kernel, [q, k, v], [("rows", F32)], [sent[-1]])
     if paired:
-        partner = after(across(cotangent, 2, 1), came[1])
+        partner = after(across(cotangent, 2, 1), came_in[1])
         partner_half = across(partner[:, owned:], 0, 1)
     state_low = (state_parts[0] + after(state_parts[1], local).astype(F32)).astype(BF16)
     if paired:
@@ -324,18 +324,20 @@
         partner_cot = lax.all_gather(partner_half, "head", axis=1, tiled=True)
         side = 1 ^ ((position >> 1) & 1) ^ (there & 1)
         both_cot = gathered_cot, partner_cot, jnp.concatenate([there, (there >> 2) * 2 + side])
-        swapped = across(after(layer_input, came[1]), 2, 1)
-        swapped = jnp.where(aligned, layer_input, after(swapped, attention))
+    else:
+        both_cot = both(gathered_cot)
+    gated = [(part, flip(part, gather_bit)) for part in gated]
+
+    (gated_grad,) = by_heads(
+        gated_grad_kernel, [("whole", gathered_cot), ("weight", out_weight)], [("rows", F32)], [attention]
+    )
+    if paired:
+        swapped = across(after(layer_input, came_in[1]), 2, 1)
+        swapped = jnp.where(aligned, layer_input, after(swapped, gated_grad))
         gathered_input = lax.all_gather(swapped, "head", axis=1, tiled=True)
         both_input = gathered_input, gathered_input, jnp.concatenate([there, there ^ 2])
     else:
-        both_cot = both(gathered_cot)
         both_input = both(lax.all_gather(layer_input, "head", axis=1, tiled=True))
-    gated = [(part, flip(part, gather_bit)) for part in gated]
-
-    (gated_grad,) = by_heads(
-        gated_grad_kernel, [("whole", gathered_cot), ("weight", out_weight)], [("rows", F32)], [attention]
-    )
     pre, grad_block, grad_block_low = by_heads(
         pre_kernel,
         [("rows", gated_grad), ("rows", attention), q, ("gain", gain)],
@@ -354,7 +356,7 @@
     shapes = {True: (width, owned), False: (3, owned, width)}
     targets = {True: None, False: None}
     received = {}
-    last = [query_grad[0]]
+    last = [query_grad[0], sent[1]]
 
     def stage(i, n):
         features, (grad, other), cols, block, turned, place = pieces[i]
@@ -372,7 +374,6 @@
 
     stages = len(halving) + 1
     stage(0, 0)
-    stage(1, 0)
     key_local, value_local = by_heads(
         own_kernel,
         [("rows", pre), q, k, v],
@@ -380,25 +381,28 @@
         [*last, sent[1]],
     )
     last.append(key_local)
+    stage(1, 0)
     grad_low = (grad_parts[0] + grad_parts[1].astype(F32)).astype(BF16)
     late_grads = by_heads(
         key_value_kernel,
         [("rows", key_local), ("rows", value_local), k, v, ("heads", grad_low)],
         [("rows", BF16)] * 2,
     )
-    first = [(part, flip(after(part, came[1]), gather_bit)) for part in query_grad]
+    first = [(part, flip(after(part, sent[1]), gather_bit)) for part in query_grad]
     key_grad = late_grads[0], flip(late_grads[0], gather_bit)
-    value_grad = late_grads[1], flip(after(late_grads[1], key_grad[1]), gather_bit)
     pieces += [(both_input, first[i], half, 0, False, (0, 0, i)) for i in range(2)]
     pieces += [(both_input, key_grad, half, i, False, (1, 0, i)) for i in range(2)]
-    pieces += [(both_input, value_grad, half, i, False, (2, 0, i)) for i in range(2)]
-    for i in range(len(pieces)):
+    count = 2 * len(gated) + 4
+    for i in range(count):
         for n in range(1, stages - 1):
             stage(i, n)
-        if i + 2 < len(pieces):
-            if i == 1:
+        if i + 2 < count:
+            if i == 0:
                 last.append(late_grads[0])
             stage(i + 2, 0)
+            if i == 2:
+                value_grad = late_grads[1], flip(after(late_grads[1], key_grad[1], last[0]), gather_bit)
+                pieces += [(both_input, value_grad, half, j, False, (2, 0, j)) for j in range(2)]
         if i >= 1:
             stage(i - 1, stages - 1)
     stage(len(pieces) - 1, stages - 1)

time: 348 us -> 337 us (0.968)
  the two profiles are of different devices: /device:TPU:28 before, /device:TPU:0 now
where the time goes in v11:
time: 337 us; the launch traced here: 335 us
  Pallas kernels  120 us (36%)
  waiting for transfers between devices  116 us (34%)
  starting transfers between devices  60.5 us (18%)
  local copies, waits for them, and re-layouts  20.6 us (6%)
  between operations  14.2 us (4%)
  other arithmetic  3.72 us (1%)
    ppermute x26, waiting for transfers between devices, flip(): return lax.ppermute(array, 'seq', [(i, i ^ 1 << bit) for i in range(size)])  112 us
    pallas_call x24, Pallas kernels, term(): pl.pallas_call(functools.partial(term_kernel, turned, len(received)), gri...  81.4 us
    ppermute x26, starting transfers between devices, flip(): return lax.ppermute(array, 'seq', [(i, i ^ 1 << bit) for i in range(size)])  49.9 us
    pallas_call x8, Pallas kernels, by_heads(): pl.pallas_call(without(kernel, len(args), len(waits)), grid=(count,), in_...  38.8 us
    unnamed x58, local copies, waits for them, and re-layouts  19.4 us
  transfers between devices with their start and end apart: 34, of which 12 were waited for; matrix products, arithmetic and copies ran while one was open for 1% of the time, Pallas kernels for 35%

profile of v11, /device:TPU:0, one launch (start us, length us, event | category | flops | bytes accessed | tf_op | source)
XLA Modules:
  0.0 335.4 jit_solution(3011162606979657648)
XLA Ops:
  16.7 5.7 %collective-permute-done = bf16[8,128,128]{2,1,0:T(8,128)(2,1)S(1)} collective-permute-done((bf16[8,128,128]{2,1,0:T(8,128)(2,1)S(1)}, bf16[8,128,128]{2,1,0:T(8,128)(2,1)S(1)}, u32[]{:S(2)}, u32[]{:S(2)}) %collective-permute-start) | collective-permute-done | bytes 262176 | tf_op jit(solution)/shard_map/ppermute | solution.py:25
  24.9 6.9 %collective-permute-done.1 = bf16[8,128,128]{2,1,0:T(8,128)(2,1)S(1)} collective-permute-done((bf16[8,128,128]{2,1,0:T(8,128)(2,1)S(1)}, bf16[8,128,128]{2,1,0:T(8,128)(2,1)S(1)}, u32[]{:S(2)}, u32[]{:S(2)}) %collective-permute-start.1) | collective-permute-done | bytes 262176 | tf_op jit(solution)/shard_map/ppermute | solution.py:25
  31.9 5.2 %collective-permute-start.3 = (bf16[8,128,128]{2,1,0:T(8,128)(2,1)S(1)}, bf16[8,128,128]{2,1,0:T(8,128)(2,1)S(1)}, u32[]{:S(2)}, u32[]{:S(2)}) collective-permute-start(bf16[8,128,128]{2,1,0:T(8,128)(2,1)S(1)} %fusion.3.refs_3_), channel_id=1, source_target_pairs={{0,16},{4,20},{8,24},{12,28},{1,17},{5,21},{9,25},{13,29},{2,18},{... | collective-permute-start | bytes 786440 | tf_op jit(solution)/shard_map/ppermute | solution.py:47
  48.3 4.8 %shard_map.88 = (f32[512,1024]{1,0:T(8,128)S(1)}, bf16[512,512]{1,0:T(8,128)(2,1)}, bf16[512,512]{1,0:T(8,128)(2,1)}) custom-call(f32[512,1024]{1,0:T(8,128)} %copy-done.25, bf16[512,1024]{1,0:T(8,128)(2,1)S(1)} %copy-done.3, bf16[8,128,128]{2,1,0:T(8,128)(2,1)S(1)} %fusion.2.refs_2_.refs_3_, f32[1,1024]{1,0:T(1,128)S(1)} %bitcast.6), custom_call_target="tpu_custom_call" | custom-call | flops 5000000000 | bytes 1 | tf_op jit(solution)/shard_map/pallas_call | solution.py:196
  56.0 8.9 %shard_map.89.refs_0_ = f32[512,1024]{1,0:T(8,128)S(1)} custom-call(bf16[512,4096]{1,0:T(8,128)(2,1)} %all-gather.4.cloned.1.call-done.refs_0_.mine, bf16[1024,4096]{1,0:T(8,128)(2,1)} %refs_1_.9, f32[512,1024]{1,0:T(8,128)S(1)} %copy-done.22), custom_call_target="tpu_custom_call" | custom-call | flops 5000000000 | bytes 1 | tf_op jit(solution)/shard_map/pallas_call | solution.py:196
  67.6 4.3 %collective-permute-start.6 = (bf16[512,512]{1,0:T(8,128)(2,1)}, bf16[512,512]{1,0:T(8,128)(2,1)S(1)}, u32[]{:S(2)}, u32[]{:S(2)}) collective-permute-start(bf16[512,512]{1,0:T(8,128)(2,1)} %get-tuple-element.33.grad), channel_id=1, source_target_pairs={{0,8},{4,12},{8,0},{12,4},{16,24},{20,28},{24,16},{28,20},{1,9},{5... | collective-permute-start | bytes 1572872 | tf_op jit(solution)/shard_map/ppermute | solution.py:25
  73.6 4.3 %shard_map.90 = (bf16[512,1024]{1,0:T(8,128)(2,1)S(1)}, f32[8,128,128]{2,1,0:T(8,128)S(1)}, bf16[8,128,128]{2,1,0:T(8,128)(2,1)S(1)}) custom-call(f32[512,1024]{1,0:T(8,128)S(1)} %copy-done.24, f32[512,1024]{1,0:T(8,128)} %copy-done.21, bf16[512,1024]{1,0:T(8,128)(2,1)S(1)} %copy-done.3, f32[1,1024]{1,0:T(1,128)S(1)} %bitcast.7), custom_call_target="tpu_custom_call" | custom-call | flops 5000000000 | bytes 1 | tf_op jit(solution)/shard_map/pallas_call | solution.py:196
  79.4 4.5 %shard_map.91 = (bf16[512,512]{1,0:T(8,128)(2,1)}, bf16[512,512]{1,0:T(8,128)(2,1)}) custom-call(bf16[512,1024]{1,0:T(8,128)(2,1)S(1)} %get-tuple-element.30.refs_0_, bf16[512,1024]{1,0:T(8,128)(2,1)S(1)} %copy-done.5, bf16[512,1024]{1,0:T(8,128)(2,1)S(1)} %copy-done.9, bf16[8,128,128]{2,1,0:T(8,128)(2,1)S(1)} %fusion.2.refs_2_.refs_3_), custom_call_target="tpu_custom_call" | custom-call | flops 5000000000 | bytes 1 | tf_op jit(solution)/shard_map/pallas_call | solution.py:196
  98.6 8.0 %shard_map.93 = (f32[512,1024]{1,0:T(8,128)}, f32[512,1024]{1,0:T(8,128)}) custom-call(bf16[512,1024]{1,0:T(8,128)(2,1)S(1)} %copy-done.27, bf16[512,1024]{1,0:T(8,128)(2,1)S(1)} %copy-done.3, bf16[512,1024]{1,0:T(8,128)(2,1)S(1)} %copy-done.5, bf16[512,1024]{1,0:T(8,128)(2,1)S(1)} %copy-done.10, bf16[512,1024]{1,0:T(8,128)(2,1)S(1)} %shard_map.92.refs_4_.rest_0_, ...), custom_call_target="tpu_custom_call" | custom-call | flops 5000000000 | bytes 1 | tf_op jit(solution)/shard_map/pallas_call | solution.py:196
  108.2 4.3 %shard_map.95.rest_1_ = bf16[512,1024]{1,0:T(8,128)(2,1)} custom-call(s32[8]{0:T(128)S(1)} %concatenate.9.index, bf16[512,4096]{1,0:T(8,128)(2,1)} %all-gather.4.cloned.1.call-done.refs_0_.mine, bf16[512,2048]{1,0:T(8,128)(2,1)S(1)} %copy-done.1, bf16[512,512]{1,0:T(8,128)(2,1)} %get-tuple-element.42.grad, bf16[512,512]{1,0:T(8,128)(2,1)} %collective-permute-done.13.other, ...), custom_call_target="tpu_custom_call" | custom-call | flops 5000000000 | bytes 1 | tf_op jit(solution)/shard_map/pallas_call | solution.py:250
  120.2 15.5 %collective-permute-start.10 = (bf16[512,1024]{1,0:T(8,128)(2,1)S(1)}, bf16[512,1024]{1,0:T(8,128)(2,1)S(1)}, u32[]{:S(2)}, u32[]{:S(2)}) collective-permute-start(bf16[512,1024]{1,0:T(8,128)(2,1)S(1)} %get-tuple-element.40.rest_1_.grad), channel_id=1, source_target_pairs={{0,8},{4,12},{8,0},{12,4},{16,24},{20,28},{24,16},{28,20},{1,9},{5... | collective-permute-start | bytes 3145736 | tf_op jit(solution)/shard_map/ppermute | solution.py:25
  139.0 3.7 %shard_map.97.rest_1_ = bf16[1024,512]{1,0:T(8,128)(2,1)S(1)} custom-call(s32[8]{0:T(128)S(1)} %concatenate.8.index, bf16[512,4096]{1,0:T(8,128)(2,1)} %all-gather.6.cloned.1.call-done.mine.theirs, bf16[512,4096]{1,0:T(8,128)(2,1)} %all-gather.6.cloned.1.call-done.mine.theirs, bf16[512,512]{1,0:T(8,128)(2,1)} %get-tuple-element.41.rest_0_.grad, ...), custom_call_target="tpu_custom_call" | custom-call | flops 5000000000 | bytes 1 | tf_op jit(solution)/shard_map/pallas_call | solution.py:250
  155.6 15.1 %collective-permute-done.15.rest_1_ = bf16[512,512]{1,0:T(8,128)(2,1)} collective-permute-done((bf16[512,512]{1,0:T(8,128)(2,1)}, bf16[512,512]{1,0:T(8,128)(2,1)}, u32[]{:S(2)}, u32[]{:S(2)}) %collective-permute-start.15) | collective-permute-done | bytes 524320 | tf_op jit(solution)/shard_map/ppermute | solution.py:25
  182.9 4.1 %shard_map.102.rest_2_ = bf16[1024,512]{1,0:T(8,128)(2,1)} custom-call(s32[8]{0:T(128)S(1)} %concatenate.8.index, bf16[512,4096]{1,0:T(8,128)(2,1)} %all-gather.6.cloned.1.call-done.mine.theirs, bf16[512,4096]{1,0:T(8,128)(2,1)} %all-gather.6.cloned.1.call-done.mine.theirs, bf16[512,1024]{1,0:T(8,128)(2,1)S(1)} %get-tuple-element.40.rest_1_.grad, ...), custom_call_target="tpu_custom_call" | custom-call | flops 5000000000 | bytes 1 | tf_op jit(solution)/shard_map/pallas_call | solution.py:250
  188.5 11.4 %collective-permute-done.20.rest_1_ = bf16[512,512]{1,0:T(8,128)(2,1)S(1)} collective-permute-done((bf16[512,512]{1,0:T(8,128)(2,1)}, bf16[512,512]{1,0:T(8,128)(2,1)S(1)}, u32[]{:S(2)}, u32[]{:S(2)}) %collective-permute-start.20) | collective-permute-done | bytes 524320 | tf_op jit(solution)/shard_map/ppermute | solution.py:25
  201.7 3.8 %shard_map.103.rest_1_ = f32[1024,512]{1,0:T(8,128)} custom-call(s32[8]{0:T(128)S(1)} %concatenate.9.index, bf16[512,4096]{1,0:T(8,128)(2,1)} %all-gather.4.cloned.1.call-done.refs_0_.mine, bf16[512,2048]{1,0:T(8,128)(2,1)S(1)} %copy-done.2, bf16[512,512]{1,0:T(8,128)(2,1)} %get-tuple-element.42.grad, ...), custom_call_target="tpu_custom_call", output_to_operand_aliasing={{}: (8, {})} | custom-call | flops 5000000000 | bytes 1 | tf_op jit(solution)/shard_map/pallas_call | solution.py:250
  214.9 3.9 %shard_map.106.rest_1_.rest_3_ = f32[3,512,1024]{2,1,0:T(8,128)} custom-call(s32[8]{0:T(128)S(1)} %concatenate.8.index, bf16[512,4096]{1,0:T(8,128)(2,1)} %all-gather.6.cloned.1.call-done.mine.theirs, bf16[512,4096]{1,0:T(8,128)(2,1)} %all-gather.6.cloned.1.call-done.mine.theirs, bf16[512,512]{1,0:T(8,128)(2,1)} %get-tuple-element.41.rest_0_.grad, ...), custom_call_target="tpu_custom_call" | custom-call | flops 5000000000 | bytes 1 | tf_op jit(solution)/shard_map/pallas_call | solution.py:250
  224.3 8.8 %collective-permute-done.18.other = bf16[512,1024]{1,0:T(8,128)(2,1)S(1)} collective-permute-done((bf16[512,1024]{1,0:T(8,128)(2,1)S(1)}, bf16[512,1024]{1,0:T(8,128)(2,1)S(1)}, u32[]{:S(2)}, u32[]{:S(2)}) %collective-permute-start.18) | collective-permute-done | bytes 1048608 | tf_op jit(solution)/shard_map/ppermute | solution.py:25
  237.1 22.3 %collective-permute-done.22.rest_1_ = bf16[512,512]{1,0:T(8,128)(2,1)S(1)} collective-permute-done((bf16[512,512]{1,0:T(8,128)(2,1)S(1)}, bf16[512,512]{1,0:T(8,128)(2,1)S(1)}, u32[]{:S(2)}, u32[]{:S(2)}) %collective-permute-start.22) | collective-permute-done | bytes 524320 | tf_op jit(solution)/shard_map/ppermute | solution.py:25
  259.4 3.8 %shard_map.109.rest_1_.rest_3_ = f32[3,512,1024]{2,1,0:T(8,128)} custom-call(s32[8]{0:T(128)S(1)} %concatenate.8.index, bf16[512,4096]{1,0:T(8,128)(2,1)} %all-gather.6.cloned.1.call-done.mine.theirs, bf16[512,4096]{1,0:T(8,128)(2,1)} %all-gather.6.cloned.1.call-done.mine.theirs, ...), custom_call_target="tpu_custom_call", output_to_operand_aliasing={{}: (8, {})} | custom-call | flops 5000000000 | bytes 1 | tf_op jit(solution)/shard_map/pallas_call | solution.py:250
  270.9 11.0 %collective-permute-done.28.rest_1_ = bf16[512,512]{1,0:T(8,128)(2,1)S(1)} collective-permute-done((bf16[512,512]{1,0:T(8,128)(2,1)S(1)}, bf16[512,512]{1,0:T(8,128)(2,1)S(1)}, u32[]{:S(2)}, u32[]{:S(2)}) %collective-permute-start.28) | collective-permute-done | bytes 524320 | tf_op jit(solution)/shard_map/ppermute | solution.py:25
  287.9 16.4 %collective-permute-done.26.rest_1_ = bf16[512,512]{1,0:T(8,128)(2,1)S(1)} collective-permute-done((bf16[512,512]{1,0:T(8,128)(2,1)S(1)}, bf16[512,512]{1,0:T(8,128)(2,1)S(1)}, u32[]{:S(2)}, u32[]{:S(2)}) %collective-permute-start.26) | collective-permute-done | bytes 524320 | tf_op jit(solution)/shard_map/ppermute | solution.py:25
  310.4 5.2 %collective-permute-done.30.rest_1_ = bf16[512,512]{1,0:T(8,128)(2,1)S(1)} collective-permute-done((bf16[512,512]{1,0:T(8,128)(2,1)S(1)}, bf16[512,512]{1,0:T(8,128)(2,1)S(1)}, u32[]{:S(2)}, u32[]{:S(2)}) %collective-permute-start.30) | collective-permute-done | bytes 524320 | tf_op jit(solution)/shard_map/ppermute | solution.py:25
  319.1 6.4 %collective-permute-done.29.rest_1_ = bf16[512,512]{1,0:T(8,128)(2,1)S(1)} collective-permute-done((bf16[512,512]{1,0:T(8,128)(2,1)S(1)}, bf16[512,512]{1,0:T(8,128)(2,1)S(1)}, u32[]{:S(2)}, u32[]{:S(2)}) %collective-permute-start.29) | collective-permute-done | bytes 524320 | tf_op jit(solution)/shard_map/ppermute | solution.py:25
  (150 shorter events, 133.2 us)
Async XLA Ops:
  7.2 47.2 %all-gather.4.cloned.1.call-start = ((), (), s32[]{:S(2)}) async-start(), calls=%async_computation | async-start | bytes 5242880 | tf_op jit(solution)/shard_map/all_gather | solution.py:307
  7.9 83.0 %all-gather.8.cloned.1.call-start = ((), (), s32[]{:S(2)}) async-start(), calls=%async_computation.2 | async-start | bytes 2621440 | tf_op jit(solution)/shard_map/all_gather | solution.py:324
  8.0 29.1 %collective-permute-start.4 = (bf16[512,1024]{1,0:T(8,128)(2,1)}, bf16[512,1024]{1,0:T(8,128)(2,1)}, u32[]{:S(2)}, u32[]{:S(2)}) collective-permute-start(bf16[512,1024]{1,0:T(8,128)(2,1)} %param.13), channel_id=1, source_target_pairs={{1,8},{3,10},{5,12},{7,14},{8,1},{10,3},{12,5},{14,7},{17,24},{19,... | collective-permute-start | bytes 3145736 | tf_op jit(solution)/shard_map/ppermute | solution.py:293
  47.5 91.5 %all-gather.6.cloned.1.call-start = ((), (), s32[]{:S(2)}) async-start(), calls=%async_computation.1 | async-start | bytes 5242880 | tf_op jit(solution)/shard_map/all_gather | solution.py:337
  71.8 36.3 %collective-permute-start.13 = (bf16[512,512]{1,0:T(8,128)(2,1)}, bf16[512,512]{1,0:T(8,128)(2,1)}, u32[]{:S(2)}, u32[]{:S(2)}) collective-permute-start(bf16[512,512]{1,0:T(8,128)(2,1)} %get-tuple-element.42.grad), channel_id=1, source_target_pairs={{0,8},{4,12},{8,0},{12,4},{16,24},{20,28},{24,16},{28,20},{1,9},{5... | collective-permute-start | bytes 1572872 | tf_op jit(solution)/shard_map/ppermute | solution.py:25
  88.1 50.9 %collective-permute-start.11 = (bf16[512,512]{1,0:T(8,128)(2,1)}, bf16[512,512]{1,0:T(8,128)(2,1)}, u32[]{:S(2)}, u32[]{:S(2)}) collective-permute-start(bf16[512,512]{1,0:T(8,128)(2,1)} %get-tuple-element.41.rest_0_.grad), channel_id=1, source_target_pairs={{0,8},{4,12},{8,0},{12,4},{16,24},{20,28},{24,16},{28,20},{1,9},{5... | collective-permute-start | bytes 1572872 | tf_op jit(solution)/shard_map/ppermute | solution.py:25
  89.0 61.8 %collective-permute-start.16 = (bf16[512,512]{1,0:T(8,128)(2,1)}, bf16[512,512]{1,0:T(8,128)(2,1)}, u32[]{:S(2)}, u32[]{:S(2)}) collective-permute-start(bf16[512,512]{1,0:T(8,128)(2,1)} %get-tuple-element.44.grad), channel_id=1, source_target_pairs={{0,8},{4,12},{8,0},{12,4},{16,24},{20,28},{24,16},{28,20},{1,9},{5... | collective-permute-start | bytes 1572872 | tf_op jit(solution)/shard_map/ppermute | solution.py:25
  97.0 38.7 %collective-permute-start.12 = (bf16[512,1024]{1,0:T(8,128)(2,1)S(1)}, bf16[512,1024]{1,0:T(8,128)(2,1)S(1)}, u32[]{:S(2)}, u32[]{:S(2)}) collective-permute-start(bf16[512,1024]{1,0:T(8,128)(2,1)S(1)} %shard_map.92.refs_4_.rest_0_), channel_id=1, source_target_pairs={{0,4},{4,0},{8,12},{12,8},{16,20},{20,16},{24,28},{28,24},{1,5},{5... | collective-permute-start | bytes 3145736 | tf_op jit(solution)/shard_map/ppermute | solution.py:25
  112.5 31.8 %collective-permute-start.17 = (bf16[512,1024]{1,0:T(8,128)(2,1)}, bf16[512,1024]{1,0:T(8,128)(2,1)}, u32[]{:S(2)}, u32[]{:S(2)}) collective-permute-start(bf16[512,1024]{1,0:T(8,128)(2,1)} %shard_map.95.rest_1_), channel_id=1, source_target_pairs={{0,4},{4,0},{8,12},{12,8},{16,20},{20,16},{24,28},{28,24},{1,5},{5... | collective-permute-start | bytes 3145736 | tf_op jit(solution)/shard_map/ppermute | solution.py:25
  120.2 62.8 %collective-permute-start.10 = (bf16[512,1024]{1,0:T(8,128)(2,1)S(1)}, bf16[512,1024]{1,0:T(8,128)(2,1)S(1)}, u32[]{:S(2)}, u32[]{:S(2)}) collective-permute-start(bf16[512,1024]{1,0:T(8,128)(2,1)S(1)} %get-tuple-element.40.rest_1_.grad), channel_id=1, source_target_pairs={{0,8},{4,12},{8,0},{12,4},{16,24},{20,28},{24,16},{28,20},{1,9},{5... | collective-permute-start | bytes 3145736 | tf_op jit(solution)/shard_map/ppermute | solution.py:25
  139.0 31.6 %collective-permute-start.15 = (bf16[512,512]{1,0:T(8,128)(2,1)}, bf16[512,512]{1,0:T(8,128)(2,1)}, u32[]{:S(2)}, u32[]{:S(2)}) collective-permute-start(bf16[512,512]{1,0:T(8,128)(2,1)} %shard_map.96.rest_0_), channel_id=1, source_target_pairs={{0,16},{4,20},{8,24},{12,28},{16,0},{20,4},{24,8},{28,12},{1,17},{... | collective-permute-start | bytes 1572872 | tf_op jit(solution)/shard_map/ppermute | solution.py:25
  142.7 31.6 %collective-permute-start.14 = (bf16[1024,512]{1,0:T(8,128)(2,1)S(1)}, bf16[1024,512]{1,0:T(8,128)(2,1)S(1)}, u32[]{:S(2)}, u32[]{:S(2)}) collective-permute-start(bf16[1024,512]{1,0:T(8,128)(2,1)S(1)} %shard_map.97.rest_1_), channel_id=1, source_target_pairs={{0,4},{4,0},{8,12},{12,8},{16,20},{20,16},{24,28},{28,24},{1,5},{5... | collective-permute-start | bytes 3145736 | tf_op jit(solution)/shard_map/ppermute | solution.py:25
  147.9 52.0 %collective-permute-start.20 = (bf16[512,512]{1,0:T(8,128)(2,1)}, bf16[512,512]{1,0:T(8,128)(2,1)S(1)}, u32[]{:S(2)}, u32[]{:S(2)}) collective-permute-start(bf16[512,512]{1,0:T(8,128)(2,1)} %shard_map.98.rest_0_), channel_id=1, source_target_pairs={{0,16},{4,20},{8,24},{12,28},{16,0},{20,4},{24,8},{28,12},{1,17},{... | collective-permute-start | bytes 1572872 | tf_op jit(solution)/shard_map/ppermute | solution.py:25
  154.5 51.1 %collective-permute-start.19 = (bf16[1024,512]{1,0:T(8,128)(2,1)S(1)}, bf16[1024,512]{1,0:T(8,128)(2,1)S(1)}, u32[]{:S(2)}, u32[]{:S(2)}) collective-permute-start(bf16[1024,512]{1,0:T(8,128)(2,1)S(1)} %shard_map.99.rest_2_), channel_id=1, source_target_pairs={{0,4},{4,0},{8,12},{12,8},{16,20},{20,16},{24,28},{28,24},{1,5},{5... | collective-permute-start | bytes 3145736 | tf_op jit(solution)/shard_map/ppermute | solution.py:25
  179.5 35.4 %collective-permute-start.24 = (bf16[512,512]{1,0:T(8,128)(2,1)}, bf16[512,512]{1,0:T(8,128)(2,1)}, u32[]{:S(2)}, u32[]{:S(2)}) collective-permute-start(bf16[512,512]{1,0:T(8,128)(2,1)} %shard_map.101.rest_0_), channel_id=1, source_target_pairs={{0,16},{4,20},{8,24},{12,28},{16,0},{20,4},{24,8},{28,12},{1,17},{... | collective-permute-start | bytes 1572872 | tf_op jit(solution)/shard_map/ppermute | solution.py:25
  187.0 31.8 %collective-permute-start.23 = (bf16[1024,512]{1,0:T(8,128)(2,1)}, bf16[1024,512]{1,0:T(8,128)(2,1)S(1)}, u32[]{:S(2)}, u32[]{:S(2)}) collective-permute-start(bf16[1024,512]{1,0:T(8,128)(2,1)} %shard_map.102.rest_2_), channel_id=1, source_target_pairs={{0,4},{4,0},{8,12},{12,8},{16,20},{20,16},{24,28},{28,24},{1,5},{5... | collective-permute-start | bytes 3145736 | tf_op jit(solution)/shard_map/ppermute | solution.py:25
  188.5 44.6 %collective-permute-start.18 = (bf16[512,1024]{1,0:T(8,128)(2,1)S(1)}, bf16[512,1024]{1,0:T(8,128)(2,1)S(1)}, u32[]{:S(2)}, u32[]{:S(2)}) collective-permute-start(bf16[512,1024]{1,0:T(8,128)(2,1)S(1)} %get-tuple-element.45.grad), channel_id=1, source_target_pairs={{0,8},{4,12},{8,0},{12,4},{16,24},{20,28},{24,16},{28,20},{1,9},{5... | collective-permute-start | bytes 3145736 | tf_op jit(solution)/shard_map/ppermute | solution.py:25
  209.9 49.5 %collective-permute-start.22 = (bf16[512,512]{1,0:T(8,128)(2,1)S(1)}, bf16[512,512]{1,0:T(8,128)(2,1)S(1)}, u32[]{:S(2)}, u32[]{:S(2)}) collective-permute-start(bf16[512,512]{1,0:T(8,128)(2,1)S(1)} %shard_map.104.rest_0_), channel_id=1, source_target_pairs={{0,16},{4,20},{8,24},{12,28},{16,0},{20,4},{24,8},{28,12},{1,17},{... | collective-permute-start | bytes 1572872 | tf_op jit(solution)/shard_map/ppermute | solution.py:25
  213.3 49.9 %collective-permute-start.21 = (bf16[1024,512]{1,0:T(8,128)(2,1)S(1)}, bf16[1024,512]{1,0:T(8,128)(2,1)S(1)}, u32[]{:S(2)}, u32[]{:S(2)}) collective-permute-start(bf16[1024,512]{1,0:T(8,128)(2,1)S(1)} %shard_map.105.rest_2_), channel_id=1, source_target_pairs={{0,4},{4,0},{8,12},{12,8},{16,20},{20,16},{24,28},{28,24},{1,5},{5... | collective-permute-start | bytes 3145736 | tf_op jit(solution)/shard_map/ppermute | solution.py:25
  221.3 60.6 %collective-permute-start.28 = (bf16[512,512]{1,0:T(8,128)(2,1)S(1)}, bf16[512,512]{1,0:T(8,128)(2,1)S(1)}, u32[]{:S(2)}, u32[]{:S(2)}) collective-permute-start(bf16[512,512]{1,0:T(8,128)(2,1)S(1)} %shard_map.107.rest_0_), channel_id=1, source_target_pairs={{0,16},{4,20},{8,24},{12,28},{16,0},{20,4},{24,8},{28,12},{1,17},{... | collective-permute-start | bytes 1572872 | tf_op jit(solution)/shard_map/ppermute | solution.py:25
  236.4 48.9 %collective-permute-start.27 = (bf16[1024,512]{1,0:T(8,128)(2,1)S(1)}, bf16[1024,512]{1,0:T(8,128)(2,1)S(1)}, u32[]{:S(2)}, u32[]{:S(2)}) collective-permute-start(bf16[1024,512]{1,0:T(8,128)(2,1)S(1)} %shard_map.108.rest_2_), channel_id=1, source_target_pairs={{0,4},{4,0},{8,12},{12,8},{16,20},{20,16},{24,28},{28,24},{1,5},{5... | collective-permute-start | bytes 3145736 | tf_op jit(solution)/shard_map/ppermute | solution.py:25
  265.7 38.7 %collective-permute-start.26 = (bf16[512,512]{1,0:T(8,128)(2,1)S(1)}, bf16[512,512]{1,0:T(8,128)(2,1)S(1)}, u32[]{:S(2)}, u32[]{:S(2)}) collective-permute-start(bf16[512,512]{1,0:T(8,128)(2,1)S(1)} %shard_map.110.rest_0_), channel_id=1, source_target_pairs={{0,16},{4,20},{8,24},{12,28},{16,0},{20,4},{24,8},{28,12},{1,17},{... | collective-permute-start | bytes 1572872 | tf_op jit(solution)/shard_map/ppermute | solution.py:25
  269.3 38.5 %collective-permute-start.25 = (bf16[1024,512]{1,0:T(8,128)(2,1)S(1)}, bf16[1024,512]{1,0:T(8,128)(2,1)S(1)}, u32[]{:S(2)}, u32[]{:S(2)}) collective-permute-start(bf16[1024,512]{1,0:T(8,128)(2,1)S(1)} %shard_map.111.rest_2_), channel_id=1, source_target_pairs={{0,4},{4,0},{8,12},{12,8},{16,20},{20,16},{24,28},{28,24},{1,5},{5... | collective-permute-start | bytes 3145736 | tf_op jit(solution)/shard_map/ppermute | solution.py:25
  287.9 27.7 %collective-permute-start.30 = (bf16[512,512]{1,0:T(8,128)(2,1)S(1)}, bf16[512,512]{1,0:T(8,128)(2,1)S(1)}, u32[]{:S(2)}, u32[]{:S(2)}) collective-permute-start(bf16[512,512]{1,0:T(8,128)(2,1)S(1)} %shard_map.113.rest_2_), channel_id=1, source_target_pairs={{0,16},{4,20},{8,24},{12,28},{16,0},{20,4},{24,8},{28,12},{1,17},{... | collective-permute-start | bytes 1572872 | tf_op jit(solution)/shard_map/ppermute | solution.py:25
  (39 other events, 331.6 us)
Sparse Core Ops, SparseCore 0:
  9.6 37.1 all-gather.3
  48.3 25.3 all-gather.7
  75.3 34.4 all-gather.5

commit v12 on v11

--- a/solution.py
+++ b/solution.py
@@ -331,19 +331,19 @@
     (gated_grad,) = by_heads(
         gated_grad_kernel, [("whole", gathered_cot), ("weight", out_weight)], [("rows", F32)], [attention]
     )
+    pre, grad_block, grad_block_low = by_heads(
+        pre_kernel,
+        [("rows", gated_grad), ("rows", attention), q, ("gain", gain)],
+        [("rows", BF16), ("heads", F32), ("heads", BF16)],
+    )
+    grad_parts, sent, came = entering(grad_block, grad_block_low, True)
     if paired:
         swapped = across(after(layer_input, came_in[1]), 2, 1)
-        swapped = jnp.where(aligned, layer_input, after(swapped, gated_grad))
+        swapped = jnp.where(aligned, layer_input, after(swapped, pre))
         gathered_input = lax.all_gather(swapped, "head", axis=1, tiled=True)
         both_input = gathered_input, gathered_input, jnp.concatenate([there, there ^ 2])
     else:
         both_input = both(lax.all_gather(layer_input, "head", axis=1, tiled=True))
-    pre, grad_block, grad_block_low = by_heads(
-        pre_kernel,
-        [("rows", gated_grad), ("rows", attention), q, ("gain", gain)],
-        [("rows", BF16), ("heads", F32), ("heads", BF16)],
-    )
-    grad_parts, sent, came = entering(grad_block, grad_block_low, True)
     query_grad = by_heads(
         query_kernel,
         [("rows", pre), k, v, ("heads", state_low)],
@@ -382,23 +382,24 @@
     )
     last.append(key_local)
     stage(1, 0)
-    grad_low = (grad_parts[0] + grad_parts[1].astype(F32)).astype(BF16)
-    late_grads = by_heads(
-        key_value_kernel,
-        [("rows", key_local), ("rows", value_local), k, v, ("heads", grad_low)],
-        [("rows", BF16)] * 2,
-    )
     first = [(part, flip(after(part, sent[1]), gather_bit)) for part in query_grad]
-    key_grad = late_grads[0], flip(late_grads[0], gather_bit)
     pieces += [(both_input, first[i], half, 0, False, (0, 0, i)) for i in range(2)]
-    pieces += [(both_input, key_grad, half, i, False, (1, 0, i)) for i in range(2)]
     count = 2 * len(gated) + 4
     for i in range(count):
         for n in range(1, stages - 1):
             stage(i, n)
+        if i == 0:
+            grad_low = (grad_parts[0] + grad_parts[1].astype(F32)).astype(BF16)
+            late_grads = by_heads(
+                key_value_kernel,
+                [("rows", key_local), ("rows", value_local), k, v, ("heads", grad_low)],
+                [("rows", BF16)] * 2,
+                last,
+            )
+            key_grad = late_grads[0], flip(late_grads[0], gather_bit)
+            pieces += [(both_input, key_grad, half, i, False, (1, 0, i)) for i in range(2)]
+            last.append(late_grads[0])
         if i + 2 < count:
-            if i == 0:
-                last.append(late_grads[0])
             stage(i + 2, 0)
             if i == 2:
                 value_grad = late_grads[1], flip(after(late_grads[1], key_grad[1], last[0]), gather_bit)

time: 337 us -> 343 us (1.018)
  starting transfers between devices: 60.5 us -> 70.1 us
  waiting for transfers between devices: 116 us -> 108 us
  local copies, waits for them, and re-layouts: 20.6 us -> 27.4 us
  Pallas kernels: 120 us -> 116 us
    ppermute x26, waiting for transfers between devices: 112 us -> 102 us  [flip(): return lax.ppermute(array, 'seq', [(i, i ^ 1 << bit) for i in range(size)])]
    ppermute x26, starting transfers between devices: 49.9 us -> 58.7 us  [flip(): return lax.ppermute(array, 'seq', [(i, i ^ 1 << bit) for i in range(size)])]
    unnamed x58 -> x88, local copies, waits for them, and re-layouts: 19.4 us -> 26.1 us
  transfers between devices with their start and end apart: 34 -> 34, of which waited for: 12 -> 14; matrix products, arithmetic and copies ran while one was open for 1% -> 2% of each run, Pallas kernels for 35% -> 33%
where the time goes in v12:
time: 343 us; the launch traced here: 341 us
  Pallas kernels  116 us (34%)
  waiting for transfers between devices  108 us (31%)
  starting transfers between devices  70.1 us (20%)
  local copies, waits for them, and re-layouts  27.4 us (8%)
  between operations  14.3 us (4%)
  other arithmetic  5.66 us (2%)
    ppermute x26, waiting for transfers between devices, flip(): return lax.ppermute(array, 'seq', [(i, i ^ 1 << bit) for i in range(size)])  102 us
    pallas_call x24, Pallas kernels, term(): pl.pallas_call(functools.partial(term_kernel, turned, len(received)), gri...  78 us
    ppermute x26, starting transfers between devices, flip(): return lax.ppermute(array, 'seq', [(i, i ^ 1 << bit) for i in range(size)])  58.7 us
    pallas_call x8, Pallas kernels, by_heads(): pl.pallas_call(without(kernel, len(args), len(waits)), grid=(count,), in_...  38 us
    unnamed x88, local copies, waits for them, and re-layouts  26.1 us
  transfers between devices with their start and end apart: 34, of which 14 were waited for; matrix products, arithmetic and copies ran while one was open for 2% of the time, Pallas kernels for 33%

profile of v12, /device:TPU:0, one launch (start us, length us, event | category | flops | bytes accessed | tf_op | source)
XLA Modules:
  0.0 341.4 jit_solution(10934291017011126347)
XLA Ops:
  16.6 5.7 %collective-permute-done = bf16[8,128,128]{2,1,0:T(8,128)(2,1)S(1)} collective-permute-done((bf16[8,128,128]{2,1,0:T(8,128)(2,1)S(1)}, bf16[8,128,128]{2,1,0:T(8,128)(2,1)S(1)}, u32[]{:S(2)}, u32[]{:S(2)}) %collective-permute-start) | collective-permute-done | bytes 262176 | tf_op jit(solution)/shard_map/ppermute | solution.py:25
  24.9 6.9 %collective-permute-done.1 = bf16[8,128,128]{2,1,0:T(8,128)(2,1)S(1)} collective-permute-done((bf16[8,128,128]{2,1,0:T(8,128)(2,1)S(1)}, bf16[8,128,128]{2,1,0:T(8,128)(2,1)S(1)}, u32[]{:S(2)}, u32[]{:S(2)}) %collective-permute-start.1) | collective-permute-done | bytes 262176 | tf_op jit(solution)/shard_map/ppermute | solution.py:25
  31.9 5.1 %collective-permute-start.3 = (bf16[8,128,128]{2,1,0:T(8,128)(2,1)S(1)}, bf16[8,128,128]{2,1,0:T(8,128)(2,1)S(1)}, u32[]{:S(2)}, u32[]{:S(2)}) collective-permute-start(bf16[8,128,128]{2,1,0:T(8,128)(2,1)S(1)} %fusion.3.refs_3_), channel_id=1, source_target_pairs={{0,16},{4,20},{8,24},{12,28},{1,17},{5,21},{9,25},{13,29},{2,18},{... | collective-permute-start | bytes 786440 | tf_op jit(solution)/shard_map/ppermute | solution.py:47
  49.1 3.8 %shard_map.88 = (f32[512,1024]{1,0:T(8,128)S(1)}, bf16[512,512]{1,0:T(8,128)(2,1)S(1)}, bf16[512,512]{1,0:T(8,128)(2,1)S(1)}) custom-call(f32[512,1024]{1,0:T(8,128)} %copy-done.37, bf16[512,1024]{1,0:T(8,128)(2,1)S(1)} %copy-done.3, bf16[8,128,128]{2,1,0:T(8,128)(2,1)S(1)} %fusion.2.refs_2_.refs_3_, f32[1,1024]{1,0:T(1,128)S(1)} %bitcast.6), custom_call_target="tpu_custom_call" | custom-call | flops 5000000000 | bytes 1 | tf_op jit(solution)/shard_map/pallas_call | solution.py:196
  56.9 9.0 %shard_map.89.refs_0_ = f32[512,1024]{1,0:T(8,128)S(1)} custom-call(bf16[512,4096]{1,0:T(8,128)(2,1)} %all-gather.4.cloned.1.call-done.refs_0_.mine, bf16[1024,4096]{1,0:T(8,128)(2,1)} %refs_1_.9, f32[512,1024]{1,0:T(8,128)S(1)} %copy-done.36), custom_call_target="tpu_custom_call" | custom-call | flops 5000000000 | bytes 1 | tf_op jit(solution)/shard_map/pallas_call | solution.py:196
  65.9 4.4 %shard_map.90 = (bf16[512,1024]{1,0:T(8,128)(2,1)S(1)}, f32[8,128,128]{2,1,0:T(8,128)S(1)}, bf16[8,128,128]{2,1,0:T(8,128)(2,1)S(1)}) custom-call(f32[512,1024]{1,0:T(8,128)S(1)} %shard_map.89.refs_0_, f32[512,1024]{1,0:T(8,128)} %copy-done.35, bf16[512,1024]{1,0:T(8,128)(2,1)S(1)} %copy-done.3, f32[1,1024]{1,0:T(1,128)S(1)} %bitcast.7), custom_call_target="tpu_custom_call" | custom-call | flops 5000000000 | bytes 1 | tf_op jit(solution)/shard_map/pallas_call | solution.py:196
  73.4 4.4 %collective-permute-start.6 = (bf16[512,512]{1,0:T(8,128)(2,1)}, bf16[512,512]{1,0:T(8,128)(2,1)S(1)}, u32[]{:S(2)}, u32[]{:S(2)}) collective-permute-start(bf16[512,512]{1,0:T(8,128)(2,1)} %copy-done.15), channel_id=1, source_target_pairs={{0,8},{4,12},{8,0},{12,4},{16,24},{20,28},{24,16},{28,20},{1,9},{5... | collective-permute-start | bytes 1572872 | tf_op jit(solution)/shard_map/ppermute | solution.py:25
  81.8 4.4 %shard_map.91 = (bf16[512,512]{1,0:T(8,128)(2,1)S(1)}, bf16[512,512]{1,0:T(8,128)(2,1)}) custom-call(bf16[512,1024]{1,0:T(8,128)(2,1)S(1)} %copy-done.39, bf16[512,1024]{1,0:T(8,128)(2,1)S(1)} %copy-done.5, bf16[512,1024]{1,0:T(8,128)(2,1)S(1)} %copy-done.9, bf16[8,128,128]{2,1,0:T(8,128)(2,1)S(1)} %fusion.2.refs_2_.refs_3_), custom_call_target="tpu_custom_call" | custom-call | flops 5000000000 | bytes 1 | tf_op jit(solution)/shard_map/pallas_call | solution.py:196
  100.7 8.0 %shard_map.93 = (f32[512,1024]{1,0:T(8,128)}, f32[512,1024]{1,0:T(8,128)}) custom-call(bf16[512,1024]{1,0:T(8,128)(2,1)S(1)} %copy-done.40, bf16[512,1024]{1,0:T(8,128)(2,1)S(1)} %copy-done.3, bf16[512,1024]{1,0:T(8,128)(2,1)S(1)} %copy-done.5, bf16[512,1024]{1,0:T(8,128)(2,1)S(1)} %copy-done.10, bf16[512,1024]{1,0:T(8,128)(2,1)S(1)} %shard_map.92.refs_4_.rest_0_, ...), custom_call_target="tpu_custom_call" | custom-call | flops 5000000000 | bytes 1 | tf_op jit(solution)/shard_map/pallas_call | solution.py:196
  113.7 4.1 %shard_map.94.rest_1_ = bf16[512,1024]{1,0:T(8,128)(2,1)} custom-call(s32[8]{0:T(128)S(1)} %concatenate.9.index, bf16[512,4096]{1,0:T(8,128)(2,1)} %all-gather.4.cloned.1.call-done.refs_0_.mine, bf16[512,2048]{1,0:T(8,128)(2,1)S(1)} %copy-done.1, bf16[512,512]{1,0:T(8,128)(2,1)S(1)} %get-tuple-element.39.grad, ...), custom_call_target="tpu_custom_call" | custom-call | flops 5000000000 | bytes 1 | tf_op jit(solution)/shard_map/pallas_call | solution.py:250
  118.5 5.5 %collective-permute-done.9 = bf16[8,128,128]{2,1,0:T(8,128)(2,1)S(1)} collective-permute-done((bf16[8,128,128]{2,1,0:T(8,128)(2,1)S(1)}, bf16[8,128,128]{2,1,0:T(8,128)(2,1)S(1)}, u32[]{:S(2)}, u32[]{:S(2)}) %collective-permute-start.9) | collective-permute-done | bytes 262176 | tf_op jit(solution)/shard_map/ppermute | solution.py:47
  131.2 3.6 %shard_map.96 = (bf16[512,1024]{1,0:T(8,128)(2,1)S(1)}, bf16[512,1024]{1,0:T(8,128)(2,1)S(1)}) custom-call(f32[512,1024]{1,0:T(8,128)} %get-tuple-element.37.rest_1_.refs_0_, f32[512,1024]{1,0:T(8,128)} %get-tuple-element.38.refs_1_, bf16[512,1024]{1,0:T(8,128)(2,1)S(1)} %copy-done.6, bf16[512,1024]{1,0:T(8,128)(2,1)S(1)} %copy-done.10, ...), custom_call_target="tpu_custom_call" | custom-call | flops 5000000000 | bytes 1 | tf_op jit(solution)/shard_map/pallas_call | solution.py:196
  134.9 17.4 %collective-permute-start.12 = (bf16[512,1024]{1,0:T(8,128)(2,1)S(1)}, bf16[512,1024]{1,0:T(8,128)(2,1)S(1)}, u32[]{:S(2)}, u32[]{:S(2)}) collective-permute-start(bf16[512,1024]{1,0:T(8,128)(2,1)S(1)} %get-tuple-element.41.rest_1_.grad), channel_id=1, source_target_pairs={{0,8},{4,12},{8,0},{12,4},{16,24},{20,28},{24,16},{28,20},{1,9},{5... | collective-permute-start | bytes 3145736 | tf_op jit(solution)/shard_map/ppermute | solution.py:25
  173.6 11.1 %collective-permute-done.14.rest_0_ = bf16[1024,512]{1,0:T(8,128)(2,1)S(1)} collective-permute-done((bf16[1024,512]{1,0:T(8,128)(2,1)S(1)}, bf16[1024,512]{1,0:T(8,128)(2,1)S(1)}, u32[]{:S(2)}, u32[]{:S(2)}) %collective-permute-start.14) | collective-permute-done | bytes 1048608 | tf_op jit(solution)/shard_map/ppermute | solution.py:25
  191.9 4.1 %shard_map.102.rest_2_ = bf16[1024,512]{1,0:T(8,128)(2,1)} custom-call(s32[8]{0:T(128)S(1)} %concatenate.8.index, bf16[512,4096]{1,0:T(8,128)(2,1)} %all-gather.6.cloned.1.call-done.mine.theirs, bf16[512,4096]{1,0:T(8,128)(2,1)} %all-gather.6.cloned.1.call-done.mine.theirs, bf16[512,1024]{1,0:T(8,128)(2,1)S(1)} %get-tuple-element.41.rest_1_.grad, ...), custom_call_target="tpu_custom_call" | custom-call | flops 5000000000 | bytes 1 | tf_op jit(solution)/shard_map/pallas_call | solution.py:250
  196.6 3.6 %shard_map.103.rest_1_ = f32[1024,512]{1,0:T(8,128)} custom-call(s32[8]{0:T(128)S(1)} %concatenate.9.index, bf16[512,4096]{1,0:T(8,128)(2,1)} %all-gather.4.cloned.1.call-done.refs_0_.mine, bf16[512,2048]{1,0:T(8,128)(2,1)S(1)} %copy-done.2, bf16[512,512]{1,0:T(8,128)(2,1)S(1)} %copy-done.14, ...), custom_call_target="tpu_custom_call", output_to_operand_aliasing={{}: (8, {})} | custom-call | flops 5000000000 | bytes 1 | tf_op jit(solution)/shard_map/pallas_call | solution.py:250
  200.2 7.1 %collective-permute-done.19.rest_0_ = bf16[1024,512]{1,0:T(8,128)(2,1)S(1)} collective-permute-done((bf16[1024,512]{1,0:T(8,128)(2,1)S(1)}, bf16[1024,512]{1,0:T(8,128)(2,1)S(1)}, u32[]{:S(2)}, u32[]{:S(2)}) %collective-permute-start.19) | collective-permute-done | bytes 1048608 | tf_op jit(solution)/shard_map/ppermute | solution.py:25
  222.7 7.0 %collective-permute-done.23.rest_0_ = bf16[1024,512]{1,0:T(8,128)(2,1)S(1)} collective-permute-done((bf16[1024,512]{1,0:T(8,128)(2,1)}, bf16[1024,512]{1,0:T(8,128)(2,1)S(1)}, u32[]{:S(2)}, u32[]{:S(2)}) %collective-permute-start.23) | collective-permute-done | bytes 1048608 | tf_op jit(solution)/shard_map/ppermute | solution.py:25
  235.2 5.3 %collective-permute-done.18.other = bf16[512,1024]{1,0:T(8,128)(2,1)S(1)} collective-permute-done((bf16[512,1024]{1,0:T(8,128)(2,1)S(1)}, bf16[512,1024]{1,0:T(8,128)(2,1)S(1)}, u32[]{:S(2)}, u32[]{:S(2)}) %collective-permute-start.18) | collective-permute-done | bytes 1048608 | tf_op jit(solution)/shard_map/ppermute | solution.py:25
  245.3 3.8 %shard_map.109.rest_1_.rest_3_ = f32[3,512,1024]{2,1,0:T(8,128)} custom-call(s32[8]{0:T(128)S(1)} %concatenate.8.index, bf16[512,4096]{1,0:T(8,128)(2,1)} %all-gather.6.cloned.1.call-done.mine.theirs, bf16[512,4096]{1,0:T(8,128)(2,1)} %all-gather.6.cloned.1.call-done.mine.theirs, ...), custom_call_target="tpu_custom_call", output_to_operand_aliasing={{}: (8, {})} | custom-call | flops 5000000000 | bytes 1 | tf_op jit(solution)/shard_map/pallas_call | solution.py:250
  261.8 13.5 %collective-permute-done.28.rest_1_ = bf16[512,512]{1,0:T(8,128)(2,1)S(1)} collective-permute-done((bf16[512,512]{1,0:T(8,128)(2,1)S(1)}, bf16[512,512]{1,0:T(8,128)(2,1)S(1)}, u32[]{:S(2)}, u32[]{:S(2)}) %collective-permute-start.28) | collective-permute-done | bytes 524320 | tf_op jit(solution)/shard_map/ppermute | solution.py:25
  281.4 16.4 %collective-permute-done.26.rest_1_ = bf16[512,512]{1,0:T(8,128)(2,1)S(1)} collective-permute-done((bf16[512,512]{1,0:T(8,128)(2,1)S(1)}, bf16[512,512]{1,0:T(8,128)(2,1)S(1)}, u32[]{:S(2)}, u32[]{:S(2)}) %collective-permute-start.26) | collective-permute-done | bytes 524320 | tf_op jit(solution)/shard_map/ppermute | solution.py:25
  303.9 16.4 %collective-permute-done.30.rest_1_ = bf16[512,512]{1,0:T(8,128)(2,1)S(1)} collective-permute-done((bf16[512,512]{1,0:T(8,128)(2,1)S(1)}, bf16[512,512]{1,0:T(8,128)(2,1)S(1)}, u32[]{:S(2)}, u32[]{:S(2)}) %collective-permute-start.30) | collective-permute-done | bytes 524320 | tf_op jit(solution)/shard_map/ppermute | solution.py:25
  323.8 7.7 %collective-permute-done.29.rest_1_ = bf16[512,512]{1,0:T(8,128)(2,1)S(1)} collective-permute-done((bf16[512,512]{1,0:T(8,128)(2,1)S(1)}, bf16[512,512]{1,0:T(8,128)(2,1)S(1)}, u32[]{:S(2)}, u32[]{:S(2)}) %collective-permute-start.29) | collective-permute-done | bytes 524320 | tf_op jit(solution)/shard_map/ppermute | solution.py:25
  (180 shorter events, 148.7 us)
Async XLA Ops:
  7.2 47.9 %all-gather.4.cloned.1.call-start = ((), (), s32[]{:S(2)}) async-start(), calls=%async_computation | async-start | bytes 5242880 | tf_op jit(solution)/shard_map/all_gather | solution.py:307
  7.9 83.3 %all-gather.8.cloned.1.call-start = ((), (), s32[]{:S(2)}) async-start(), calls=%async_computation.2 | async-start | bytes 2621440 | tf_op jit(solution)/shard_map/all_gather | solution.py:324
  8.0 29.1 %collective-permute-start.4 = (bf16[512,1024]{1,0:T(8,128)(2,1)}, bf16[512,1024]{1,0:T(8,128)(2,1)}, u32[]{:S(2)}, u32[]{:S(2)}) collective-permute-start(bf16[512,1024]{1,0:T(8,128)(2,1)} %param.13), channel_id=1, source_target_pairs={{1,8},{3,10},{5,12},{7,14},{8,1},{10,3},{12,5},{14,7},{17,24},{19,... | collective-permute-start | bytes 3145736 | tf_op jit(solution)/shard_map/ppermute | solution.py:293
  47.4 105.6 %all-gather.6.cloned.1.call-start = ((), (), s32[]{:S(2)}) async-start(), calls=%async_computation.1 | async-start | bytes 5242880 | tf_op jit(solution)/shard_map/all_gather | solution.py:343
  77.8 35.9 %collective-permute-start.11 = (bf16[512,512]{1,0:T(8,128)(2,1)S(1)}, bf16[512,512]{1,0:T(8,128)(2,1)}, u32[]{:S(2)}, u32[]{:S(2)}) collective-permute-start(bf16[512,512]{1,0:T(8,128)(2,1)S(1)} %get-tuple-element.39.grad), channel_id=1, source_target_pairs={{0,8},{4,12},{8,0},{12,4},{16,24},{20,28},{24,16},{28,20},{1,9},{5... | collective-permute-start | bytes 1572872 | tf_op jit(solution)/shard_map/ppermute | solution.py:25
  108.7 43.5 %collective-permute-start.13 = (bf16[512,512]{1,0:T(8,128)(2,1)S(1)}, bf16[512,512]{1,0:T(8,128)(2,1)S(1)}, u32[]{:S(2)}, u32[]{:S(2)}) collective-permute-start(bf16[512,512]{1,0:T(8,128)(2,1)S(1)} %copy-done.21), channel_id=1, source_target_pairs={{0,8},{4,12},{8,0},{12,4},{16,24},{20,28},{24,16},{28,20},{1,9},{5... | collective-permute-start | bytes 1572872 | tf_op jit(solution)/shard_map/ppermute | solution.py:25
  111.1 53.9 %collective-permute-start.16 = (bf16[512,512]{1,0:T(8,128)(2,1)}, bf16[512,512]{1,0:T(8,128)(2,1)}, u32[]{:S(2)}, u32[]{:S(2)}) collective-permute-start(bf16[512,512]{1,0:T(8,128)(2,1)} %get-tuple-element.44.grad), channel_id=1, source_target_pairs={{0,8},{4,12},{8,0},{12,4},{16,24},{20,28},{24,16},{28,20},{1,9},{5... | collective-permute-start | bytes 1572872 | tf_op jit(solution)/shard_map/ppermute | solution.py:25
  117.9 41.4 %collective-permute-start.17 = (bf16[512,1024]{1,0:T(8,128)(2,1)}, bf16[512,1024]{1,0:T(8,128)(2,1)}, u32[]{:S(2)}, u32[]{:S(2)}) collective-permute-start(bf16[512,1024]{1,0:T(8,128)(2,1)} %shard_map.94.rest_1_), channel_id=1, source_target_pairs={{0,4},{4,0},{8,12},{12,8},{16,20},{20,16},{24,28},{28,24},{1,5},{5... | collective-permute-start | bytes 3145736 | tf_op jit(solution)/shard_map/ppermute | solution.py:25
  128.3 41.8 %collective-permute-start.15 = (bf16[512,512]{1,0:T(8,128)(2,1)}, bf16[512,512]{1,0:T(8,128)(2,1)}, u32[]{:S(2)}, u32[]{:S(2)}) collective-permute-start(bf16[512,512]{1,0:T(8,128)(2,1)} %shard_map.95.refs_5_.rest_0_), channel_id=1, source_target_pairs={{0,16},{4,20},{8,24},{12,28},{16,0},{20,4},{24,8},{28,12},{1,17},{... | collective-permute-start | bytes 1572872 | tf_op jit(solution)/shard_map/ppermute | solution.py:25
  134.9 57.0 %collective-permute-start.12 = (bf16[512,1024]{1,0:T(8,128)(2,1)S(1)}, bf16[512,1024]{1,0:T(8,128)(2,1)S(1)}, u32[]{:S(2)}, u32[]{:S(2)}) collective-permute-start(bf16[512,1024]{1,0:T(8,128)(2,1)S(1)} %get-tuple-element.41.rest_1_.grad), channel_id=1, source_target_pairs={{0,8},{4,12},{8,0},{12,4},{16,24},{20,28},{24,16},{28,20},{1,9},{5... | collective-permute-start | bytes 3145736 | tf_op jit(solution)/shard_map/ppermute | solution.py:25
  158.7 26.1 %collective-permute-start.14 = (bf16[1024,512]{1,0:T(8,128)(2,1)S(1)}, bf16[1024,512]{1,0:T(8,128)(2,1)S(1)}, u32[]{:S(2)}, u32[]{:S(2)}) collective-permute-start(bf16[1024,512]{1,0:T(8,128)(2,1)S(1)} %shard_map.97.rest_1_), channel_id=1, source_target_pairs={{0,4},{4,0},{8,12},{12,8},{16,20},{20,16},{24,28},{28,24},{1,5},{5... | collective-permute-start | bytes 3145736 | tf_op jit(solution)/shard_map/ppermute | solution.py:25
  162.0 34.6 %collective-permute-start.20 = (bf16[512,512]{1,0:T(8,128)(2,1)S(1)}, bf16[512,512]{1,0:T(8,128)(2,1)S(1)}, u32[]{:S(2)}, u32[]{:S(2)}) collective-permute-start(bf16[512,512]{1,0:T(8,128)(2,1)S(1)} %shard_map.98.rest_0_), channel_id=1, source_target_pairs={{0,16},{4,20},{8,24},{12,28},{16,0},{20,4},{24,8},{28,12},{1,17},{... | collective-permute-start | bytes 1572872 | tf_op jit(solution)/shard_map/ppermute | solution.py:25
  168.6 38.6 %collective-permute-start.19 = (bf16[1024,512]{1,0:T(8,128)(2,1)S(1)}, bf16[1024,512]{1,0:T(8,128)(2,1)S(1)}, u32[]{:S(2)}, u32[]{:S(2)}) collective-permute-start(bf16[1024,512]{1,0:T(8,128)(2,1)S(1)} %shard_map.99.rest_2_), channel_id=1, source_target_pairs={{0,4},{4,0},{8,12},{12,8},{16,20},{20,16},{24,28},{28,24},{1,5},{5... | collective-permute-start | bytes 3145736 | tf_op jit(solution)/shard_map/ppermute | solution.py:25
  188.9 30.4 %collective-permute-start.24 = (bf16[512,512]{1,0:T(8,128)(2,1)S(1)}, bf16[512,512]{1,0:T(8,128)(2,1)S(1)}, u32[]{:S(2)}, u32[]{:S(2)}) collective-permute-start(bf16[512,512]{1,0:T(8,128)(2,1)S(1)} %shard_map.101.rest_0_), channel_id=1, source_target_pairs={{0,16},{4,20},{8,24},{12,28},{16,0},{20,4},{24,8},{28,12},{1,17},{... | collective-permute-start | bytes 1572872 | tf_op jit(solution)/shard_map/ppermute | solution.py:25
  196.0 33.7 %collective-permute-start.23 = (bf16[1024,512]{1,0:T(8,128)(2,1)}, bf16[1024,512]{1,0:T(8,128)(2,1)S(1)}, u32[]{:S(2)}, u32[]{:S(2)}) collective-permute-start(bf16[1024,512]{1,0:T(8,128)(2,1)} %shard_map.102.rest_2_), channel_id=1, source_target_pairs={{0,4},{4,0},{8,12},{12,8},{16,20},{20,16},{24,28},{28,24},{1,5},{5... | collective-permute-start | bytes 3145736 | tf_op jit(solution)/shard_map/ppermute | solution.py:25
  196.6 44.0 %collective-permute-start.18 = (bf16[512,1024]{1,0:T(8,128)(2,1)S(1)}, bf16[512,1024]{1,0:T(8,128)(2,1)S(1)}, u32[]{:S(2)}, u32[]{:S(2)}) collective-permute-start(bf16[512,1024]{1,0:T(8,128)(2,1)S(1)} %get-tuple-element.45.grad), channel_id=1, source_target_pairs={{0,8},{4,12},{8,0},{12,4},{16,24},{20,28},{24,16},{28,20},{1,9},{5... | collective-permute-start | bytes 3145736 | tf_op jit(solution)/shard_map/ppermute | solution.py:25
  211.7 33.6 %collective-permute-start.22 = (bf16[512,512]{1,0:T(8,128)(2,1)S(1)}, bf16[512,512]{1,0:T(8,128)(2,1)S(1)}, u32[]{:S(2)}, u32[]{:S(2)}) collective-permute-start(bf16[512,512]{1,0:T(8,128)(2,1)S(1)} %shard_map.104.rest_0_), channel_id=1, source_target_pairs={{0,16},{4,20},{8,24},{12,28},{16,0},{20,4},{24,8},{28,12},{1,17},{... | collective-permute-start | bytes 1572872 | tf_op jit(solution)/shard_map/ppermute | solution.py:25
  218.0 34.2 %collective-permute-start.21 = (bf16[1024,512]{1,0:T(8,128)(2,1)S(1)}, bf16[1024,512]{1,0:T(8,128)(2,1)S(1)}, u32[]{:S(2)}, u32[]{:S(2)}) collective-permute-start(bf16[1024,512]{1,0:T(8,128)(2,1)S(1)} %shard_map.105.rest_2_), channel_id=1, source_target_pairs={{0,4},{4,0},{8,12},{12,8},{16,20},{20,16},{24,28},{28,24},{1,5},{5... | collective-permute-start | bytes 3145736 | tf_op jit(solution)/shard_map/ppermute | solution.py:25
  232.2 43.1 %collective-permute-start.28 = (bf16[512,512]{1,0:T(8,128)(2,1)S(1)}, bf16[512,512]{1,0:T(8,128)(2,1)S(1)}, u32[]{:S(2)}, u32[]{:S(2)}) collective-permute-start(bf16[512,512]{1,0:T(8,128)(2,1)S(1)} %shard_map.107.rest_0_), channel_id=1, source_target_pairs={{0,16},{4,20},{8,24},{12,28},{16,0},{20,4},{24,8},{28,12},{1,17},{... | collective-permute-start | bytes 1572872 | tf_op jit(solution)/shard_map/ppermute | solution.py:25
  243.8 35.0 %collective-permute-start.27 = (bf16[1024,512]{1,0:T(8,128)(2,1)S(1)}, bf16[1024,512]{1,0:T(8,128)(2,1)S(1)}, u32[]{:S(2)}, u32[]{:S(2)}) collective-permute-start(bf16[1024,512]{1,0:T(8,128)(2,1)S(1)} %shard_map.108.rest_2_), channel_id=1, source_target_pairs={{0,4},{4,0},{8,12},{12,8},{16,20},{20,16},{24,28},{28,24},{1,5},{5... | collective-permute-start | bytes 3145736 | tf_op jit(solution)/shard_map/ppermute | solution.py:25
  254.7 43.2 %collective-permute-start.26 = (bf16[512,512]{1,0:T(8,128)(2,1)S(1)}, bf16[512,512]{1,0:T(8,128)(2,1)S(1)}, u32[]{:S(2)}, u32[]{:S(2)}) collective-permute-start(bf16[512,512]{1,0:T(8,128)(2,1)S(1)} %shard_map.110.rest_0_), channel_id=1, source_target_pairs={{0,16},{4,20},{8,24},{12,28},{16,0},{20,4},{24,8},{28,12},{1,17},{... | collective-permute-start | bytes 1572872 | tf_op jit(solution)/shard_map/ppermute | solution.py:25
  261.2 40.1 %collective-permute-start.25 = (bf16[1024,512]{1,0:T(8,128)(2,1)S(1)}, bf16[1024,512]{1,0:T(8,128)(2,1)S(1)}, u32[]{:S(2)}, u32[]{:S(2)}) collective-permute-start(bf16[1024,512]{1,0:T(8,128)(2,1)S(1)} %shard_map.111.rest_2_), channel_id=1, source_target_pairs={{0,4},{4,0},{8,12},{12,8},{16,20},{20,16},{24,28},{28,24},{1,5},{5... | collective-permute-start | bytes 3145736 | tf_op jit(solution)/shard_map/ppermute | solution.py:25
  281.3 39.0 %collective-permute-start.30 = (bf16[512,512]{1,0:T(8,128)(2,1)S(1)}, bf16[512,512]{1,0:T(8,128)(2,1)S(1)}, u32[]{:S(2)}, u32[]{:S(2)}) collective-permute-start(bf16[512,512]{1,0:T(8,128)(2,1)S(1)} %shard_map.113.rest_2_), channel_id=1, source_target_pairs={{0,16},{4,20},{8,24},{12,28},{16,0},{20,4},{24,8},{28,12},{1,17},{... | collective-permute-start | bytes 1572872 | tf_op jit(solution)/shard_map/ppermute | solution.py:25
  303.8 27.7 %collective-permute-start.29 = (bf16[512,512]{1,0:T(8,128)(2,1)S(1)}, bf16[512,512]{1,0:T(8,128)(2,1)S(1)}, u32[]{:S(2)}, u32[]{:S(2)}) collective-permute-start(bf16[512,512]{1,0:T(8,128)(2,1)S(1)} %shard_map.115.rest_2_), channel_id=1, source_target_pairs={{0,16},{4,20},{8,24},{12,28},{16,0},{20,4},{24,8},{28,12},{1,17},{... | collective-permute-start | bytes 1572872 | tf_op jit(solution)/shard_map/ppermute | solution.py:25
  (54 other events, 456.5 us)
Sparse Core Ops, SparseCore 0:
  9.6 37.1 all-gather.3
  48.9 24.7 all-gather.7
  75.3 37.3 all-gather.5

commit v13 on v11

--- a/solution.py
+++ b/solution.py
@@ -389,9 +389,7 @@
         [("rows", BF16)] * 2,
     )
     first = [(part, flip(after(part, sent[1]), gather_bit)) for part in query_grad]
-    key_grad = late_grads[0], flip(late_grads[0], gather_bit)
     pieces += [(both_input, first[i], half, 0, False, (0, 0, i)) for i in range(2)]
-    pieces += [(both_input, key_grad, half, i, False, (1, 0, i)) for i in range(2)]
     count = 2 * len(gated) + 4
     for i in range(count):
         for n in range(1, stages - 1):
@@ -400,6 +398,9 @@
             if i == 0:
                 last.append(late_grads[0])
             stage(i + 2, 0)
+            if i == 0:
+                key_grad = late_grads[0], flip(after(late_grads[0], last[0]), gather_bit)
+                pieces += [(both_input, key_grad, half, j, False, (1, 0, j)) for j in range(2)]
             if i == 2:
                 value_grad = late_grads[1], flip(after(late_grads[1], key_grad[1], last[0]), gather_bit)
                 pieces += [(both_input, value_grad, half, j, False, (2, 0, j)) for j in range(2)]

time: 337 us -> 332 us (0.985)
  waiting for transfers between devices: 116 us -> 108 us
    ppermute x26, waiting for transfers between devices: 112 us -> 104 us  [flip(): return lax.ppermute(array, 'seq', [(i, i ^ 1 << bit) for i in range(size)])]
    unnamed x58 -> x60, local copies, waits for them, and re-layouts: 19.4 us -> 19.5 us
  transfers between devices with their start and end apart: 34 -> 34, of which waited for: 12 -> 14; matrix products, arithmetic and copies ran while one was open for 1% -> 2% of each run, Pallas kernels for 35% -> 36%
where the time goes in v13:
time: 332 us; the launch traced here: 330 us
  Pallas kernels  122 us (37%)
  waiting for transfers between devices  108 us (33%)
  starting transfers between devices  62 us (19%)
  local copies, waits for them, and re-layouts  20.7 us (6%)
  between operations  14.1 us (4%)
  other arithmetic  3.74 us (1%)
    ppermute x26, waiting for transfers between devices, flip(): return lax.ppermute(array, 'seq', [(i, i ^ 1 << bit) for i in range(size)])  104 us
    pallas_call x24, Pallas kernels, term(): pl.pallas_call(functools.partial(term_kernel, turned, len(received)), gri...  83.2 us
    ppermute x26, starting transfers between devices, flip(): return lax.ppermute(array, 'seq', [(i, i ^ 1 << bit) for i in range(size)])  51.4 us
    pallas_call x8, Pallas kernels, by_heads(): pl.pallas_call(without(kernel, len(args), len(waits)), grid=(count,), in_...  38.6 us
    unnamed x60, local copies, waits for them, and re-layouts  19.5 us
    ppermute x2, starting transfers between devices, entering(): came.append(lax.ppermute(low, 'seq', pairs))  6.68 us
  transfers between devices with their start and end apart: 34, of which 14 were waited for; matrix products, arithmetic and copies ran while one was open for 2% of the time, Pallas kernels for 36%

profile of v13, /device:TPU:0, one launch (start us, length us, event | category | flops | bytes accessed | tf_op | source)
XLA Modules:
  0.0 330.3 jit_solution(7061176517988376680)
XLA Ops:
  16.7 5.7 %collective-permute-done = bf16[8,128,128]{2,1,0:T(8,128)(2,1)S(1)} collective-permute-done((bf16[8,128,128]{2,1,0:T(8,128)(2,1)S(1)}, bf16[8,128,128]{2,1,0:T(8,128)(2,1)S(1)}, u32[]{:S(2)}, u32[]{:S(2)}) %collective-permute-start) | collective-permute-done | bytes 262176 | tf_op jit(solution)/shard_map/ppermute | solution.py:25
  24.9 6.9 %collective-permute-done.1 = bf16[8,128,128]{2,1,0:T(8,128)(2,1)S(1)} collective-permute-done((bf16[8,128,128]{2,1,0:T(8,128)(2,1)S(1)}, bf16[8,128,128]{2,1,0:T(8,128)(2,1)S(1)}, u32[]{:S(2)}, u32[]{:S(2)}) %collective-permute-start.1) | collective-permute-done | bytes 262176 | tf_op jit(solution)/shard_map/ppermute | solution.py:25
  31.9 5.2 %collective-permute-start.3 = (bf16[8,128,128]{2,1,0:T(8,128)(2,1)S(1)}, bf16[8,128,128]{2,1,0:T(8,128)(2,1)S(1)}, u32[]{:S(2)}, u32[]{:S(2)}) collective-permute-start(bf16[8,128,128]{2,1,0:T(8,128)(2,1)S(1)} %fusion.3.refs_3_), channel_id=1, source_target_pairs={{0,16},{4,20},{8,24},{12,28},{1,17},{5,21},{9,25},{13,29},{2,18},{... | collective-permute-start | bytes 786440 | tf_op jit(solution)/shard_map/ppermute | solution.py:47
  48.3 4.7 %shard_map.88 = (f32[512,1024]{1,0:T(8,128)S(1)}, bf16[512,512]{1,0:T(8,128)(2,1)}, bf16[512,512]{1,0:T(8,128)(2,1)}) custom-call(f32[512,1024]{1,0:T(8,128)} %copy-done.26, bf16[512,1024]{1,0:T(8,128)(2,1)S(1)} %copy-done.3, bf16[8,128,128]{2,1,0:T(8,128)(2,1)S(1)} %fusion.2.refs_2_.refs_3_, f32[1,1024]{1,0:T(1,128)S(1)} %bitcast.6), custom_call_target="tpu_custom_call" | custom-call | flops 5000000000 | bytes 1 | tf_op jit(solution)/shard_map/pallas_call | solution.py:196
  55.9 8.9 %shard_map.89.refs_0_ = f32[512,1024]{1,0:T(8,128)S(1)} custom-call(bf16[512,4096]{1,0:T(8,128)(2,1)} %all-gather.4.cloned.1.call-done.refs_0_.mine, bf16[1024,4096]{1,0:T(8,128)(2,1)} %refs_1_.9, f32[512,1024]{1,0:T(8,128)S(1)} %copy-done.23), custom_call_target="tpu_custom_call" | custom-call | flops 5000000000 | bytes 1 | tf_op jit(solution)/shard_map/pallas_call | solution.py:196
  67.5 4.3 %collective-permute-start.6 = (bf16[512,512]{1,0:T(8,128)(2,1)}, bf16[512,512]{1,0:T(8,128)(2,1)S(1)}, u32[]{:S(2)}, u32[]{:S(2)}) collective-permute-start(bf16[512,512]{1,0:T(8,128)(2,1)} %get-tuple-element.34.grad), channel_id=1, source_target_pairs={{0,8},{4,12},{8,0},{12,4},{16,24},{20,28},{24,16},{28,20},{1,9},{5... | collective-permute-start | bytes 1572872 | tf_op jit(solution)/shard_map/ppermute | solution.py:25
  73.7 4.3 %shard_map.90 = (bf16[512,1024]{1,0:T(8,128)(2,1)S(1)}, f32[8,128,128]{2,1,0:T(8,128)S(1)}, bf16[8,128,128]{2,1,0:T(8,128)(2,1)S(1)}) custom-call(f32[512,1024]{1,0:T(8,128)S(1)} %copy-done.25, f32[512,1024]{1,0:T(8,128)} %copy-done.22, bf16[512,1024]{1,0:T(8,128)(2,1)S(1)} %copy-done.3, f32[1,1024]{1,0:T(1,128)S(1)} %bitcast.7), custom_call_target="tpu_custom_call" | custom-call | flops 5000000000 | bytes 1 | tf_op jit(solution)/shard_map/pallas_call | solution.py:196
  79.6 4.4 %shard_map.91 = (bf16[512,512]{1,0:T(8,128)(2,1)}, bf16[512,512]{1,0:T(8,128)(2,1)S(1)}) custom-call(bf16[512,1024]{1,0:T(8,128)(2,1)S(1)} %get-tuple-element.31.refs_0_, bf16[512,1024]{1,0:T(8,128)(2,1)S(1)} %copy-done.6, bf16[512,1024]{1,0:T(8,128)(2,1)S(1)} %copy-done.10, bf16[8,128,128]{2,1,0:T(8,128)(2,1)S(1)} %fusion.2.refs_2_.refs_3_), custom_call_target="tpu_custom_call" | custom-call | flops 5000000000 | bytes 1 | tf_op jit(solution)/shard_map/pallas_call | solution.py:196
  99.0 8.0 %shard_map.93 = (f32[512,1024]{1,0:T(8,128)}, f32[512,1024]{1,0:T(8,128)}) custom-call(bf16[512,1024]{1,0:T(8,128)(2,1)S(1)} %copy-done.28, bf16[512,1024]{1,0:T(8,128)(2,1)S(1)} %copy-done.3, bf16[512,1024]{1,0:T(8,128)(2,1)S(1)} %copy-done.7, bf16[512,1024]{1,0:T(8,128)(2,1)S(1)} %copy-done.11, bf16[512,1024]{1,0:T(8,128)(2,1)S(1)} %shard_map.92.refs_4_.rest_0_, ...), custom_call_target="tpu_custom_call" | custom-call | flops 5000000000 | bytes 1 | tf_op jit(solution)/shard_map/pallas_call | solution.py:196
  108.6 4.3 %shard_map.95.rest_1_ = bf16[512,1024]{1,0:T(8,128)(2,1)} custom-call(s32[8]{0:T(128)S(1)} %concatenate.9.index, bf16[512,4096]{1,0:T(8,128)(2,1)} %all-gather.4.cloned.1.call-done.refs_0_.mine, bf16[512,2048]{1,0:T(8,128)(2,1)S(1)} %copy-done.1, bf16[512,512]{1,0:T(8,128)(2,1)} %get-tuple-element.43.grad, bf16[512,512]{1,0:T(8,128)(2,1)} %collective-permute-done.12.other, ...), custom_call_target="tpu_custom_call" | custom-call | flops 5000000000 | bytes 1 | tf_op jit(solution)/shard_map/pallas_call | solution.py:250
  135.2 9.1 %collective-permute-start.13 = (bf16[512,1024]{1,0:T(8,128)(2,1)S(1)}, bf16[512,1024]{1,0:T(8,128)(2,1)S(1)}, u32[]{:S(2)}, u32[]{:S(2)}) collective-permute-start(bf16[512,1024]{1,0:T(8,128)(2,1)S(1)} %get-tuple-element.44.rest_1_.grad), channel_id=1, source_target_pairs={{0,8},{4,12},{8,0},{12,4},{16,24},{20,28},{24,16},{28,20},{1,9},{5... | collective-permute-start | bytes 3145736 | tf_op jit(solution)/shard_map/ppermute | solution.py:25
  152.9 4.1 %shard_map.99.rest_2_ = bf16[1024,512]{1,0:T(8,128)(2,1)} custom-call(s32[8]{0:T(128)S(1)} %concatenate.8.index, bf16[512,4096]{1,0:T(8,128)(2,1)} %all-gather.6.cloned.1.call-done.mine.theirs, bf16[512,4096]{1,0:T(8,128)(2,1)} %all-gather.6.cloned.1.call-done.mine.theirs, bf16[512,512]{1,0:T(8,128)(2,1)S(1)} %get-tuple-element.46.grad, ...), custom_call_target="tpu_custom_call" | custom-call | flops 5000000000 | bytes 1 | tf_op jit(solution)/shard_map/pallas_call | solution.py:250
  162.0 6.5 %collective-permute-done.14.rest_0_ = bf16[1024,512]{1,0:T(8,128)(2,1)S(1)} collective-permute-done((bf16[1024,512]{1,0:T(8,128)(2,1)S(1)}, bf16[1024,512]{1,0:T(8,128)(2,1)S(1)}, u32[]{:S(2)}, u32[]{:S(2)}) %collective-permute-start.14) | collective-permute-done | bytes 1048608 | tf_op jit(solution)/shard_map/ppermute | solution.py:25
  176.8 5.7 %collective-permute-done.13.other = bf16[512,1024]{1,0:T(8,128)(2,1)S(1)} collective-permute-done((bf16[512,1024]{1,0:T(8,128)(2,1)S(1)}, bf16[512,1024]{1,0:T(8,128)(2,1)S(1)}, u32[]{:S(2)}, u32[]{:S(2)}) %collective-permute-start.13) | collective-permute-done | bytes 1048608 | tf_op jit(solution)/shard_map/ppermute | solution.py:25
  182.5 4.1 %shard_map.102.rest_2_ = bf16[1024,512]{1,0:T(8,128)(2,1)} custom-call(s32[8]{0:T(128)S(1)} %concatenate.8.index, bf16[512,4096]{1,0:T(8,128)(2,1)} %all-gather.6.cloned.1.call-done.mine.theirs, bf16[512,4096]{1,0:T(8,128)(2,1)} %all-gather.6.cloned.1.call-done.mine.theirs, bf16[512,1024]{1,0:T(8,128)(2,1)S(1)} %get-tuple-element.44.rest_1_.grad, ...), custom_call_target="tpu_custom_call" | custom-call | flops 5000000000 | bytes 1 | tf_op jit(solution)/shard_map/pallas_call | solution.py:250
  187.1 4.0 %shard_map.103.rest_1_ = f32[1024,512]{1,0:T(8,128)} custom-call(s32[8]{0:T(128)S(1)} %concatenate.9.index, bf16[512,4096]{1,0:T(8,128)(2,1)} %all-gather.4.cloned.1.call-done.refs_0_.mine, bf16[512,2048]{1,0:T(8,128)(2,1)S(1)} %copy-done.2, bf16[512,512]{1,0:T(8,128)(2,1)} %get-tuple-element.43.grad, ...), custom_call_target="tpu_custom_call", output_to_operand_aliasing={{}: (8, {})} | custom-call | flops 5000000000 | bytes 1 | tf_op jit(solution)/shard_map/pallas_call | solution.py:250
  195.9 7.2 %collective-permute-start.22 = (bf16[512,512]{1,0:T(8,128)(2,1)}, bf16[512,512]{1,0:T(8,128)(2,1)S(1)}, u32[]{:S(2)}, u32[]{:S(2)}) collective-permute-start(bf16[512,512]{1,0:T(8,128)(2,1)} %shard_map.104.rest_0_), channel_id=1, source_target_pairs={{0,16},{4,20},{8,24},{12,28},{16,0},{20,4},{24,8},{28,12},{1,17},{... | collective-permute-start | bytes 1572872 | tf_op jit(solution)/shard_map/ppermute | solution.py:25
  207.0 3.8 %collective-permute-done.24.rest_1_ = bf16[512,512]{1,0:T(8,128)(2,1)S(1)} collective-permute-done((bf16[512,512]{1,0:T(8,128)(2,1)}, bf16[512,512]{1,0:T(8,128)(2,1)S(1)}, u32[]{:S(2)}, u32[]{:S(2)}) %collective-permute-start.24) | collective-permute-done | bytes 524320 | tf_op jit(solution)/shard_map/ppermute | solution.py:25
  212.6 3.8 %shard_map.106.rest_1_.rest_3_ = f32[3,512,1024]{2,1,0:T(8,128)} custom-call(s32[8]{0:T(128)S(1)} %concatenate.8.index, bf16[512,4096]{1,0:T(8,128)(2,1)} %all-gather.6.cloned.1.call-done.mine.theirs, bf16[512,4096]{1,0:T(8,128)(2,1)} %all-gather.6.cloned.1.call-done.mine.theirs, bf16[512,512]{1,0:T(8,128)(2,1)} %get-tuple-element.42.rest_0_.grad, ...), custom_call_target="tpu_custom_call" | custom-call | flops 5000000000 | bytes 1 | tf_op jit(solution)/shard_map/pallas_call | solution.py:250
  219.9 14.2 %collective-permute-done.18.other = bf16[512,1024]{1,0:T(8,128)(2,1)S(1)} collective-permute-done((bf16[512,1024]{1,0:T(8,128)(2,1)S(1)}, bf16[512,1024]{1,0:T(8,128)(2,1)S(1)}, u32[]{:S(2)}, u32[]{:S(2)}) %collective-permute-start.18) | collective-permute-done | bytes 1048608 | tf_op jit(solution)/shard_map/ppermute | solution.py:25
  251.8 15.1 %collective-permute-done.28.rest_1_ = bf16[512,512]{1,0:T(8,128)(2,1)S(1)} collective-permute-done((bf16[512,512]{1,0:T(8,128)(2,1)}, bf16[512,512]{1,0:T(8,128)(2,1)S(1)}, u32[]{:S(2)}, u32[]{:S(2)}) %collective-permute-start.28) | collective-permute-done | bytes 524320 | tf_op jit(solution)/shard_map/ppermute | solution.py:25
  272.9 16.4 %collective-permute-done.26.rest_1_ = bf16[512,512]{1,0:T(8,128)(2,1)S(1)} collective-permute-done((bf16[512,512]{1,0:T(8,128)(2,1)S(1)}, bf16[512,512]{1,0:T(8,128)(2,1)S(1)}, u32[]{:S(2)}, u32[]{:S(2)}) %collective-permute-start.26) | collective-permute-done | bytes 524320 | tf_op jit(solution)/shard_map/ppermute | solution.py:25
  295.4 16.4 %collective-permute-done.30.rest_1_ = bf16[512,512]{1,0:T(8,128)(2,1)S(1)} collective-permute-done((bf16[512,512]{1,0:T(8,128)(2,1)S(1)}, bf16[512,512]{1,0:T(8,128)(2,1)S(1)}, u32[]{:S(2)}, u32[]{:S(2)}) %collective-permute-start.30) | collective-permute-done | bytes 524320 | tf_op jit(solution)/shard_map/ppermute | solution.py:25
  315.3 5.0 %collective-permute-done.29.rest_1_ = bf16[512,512]{1,0:T(8,128)(2,1)S(1)} collective-permute-done((bf16[512,512]{1,0:T(8,128)(2,1)S(1)}, bf16[512,512]{1,0:T(8,128)(2,1)S(1)}, u32[]{:S(2)}, u32[]{:S(2)}) %collective-permute-start.29) | collective-permute-done | bytes 524320 | tf_op jit(solution)/shard_map/ppermute | solution.py:25
  (152 shorter events, 144.3 us)
Async XLA Ops:
  7.2 47.1 %all-gather.4.cloned.1.call-start = ((), (), s32[]{:S(2)}) async-start(), calls=%async_computation | async-start | bytes 5242880 | tf_op jit(solution)/shard_map/all_gather | solution.py:307
  7.9 83.1 %all-gather.8.cloned.1.call-start = ((), (), s32[]{:S(2)}) async-start(), calls=%async_computation.2 | async-start | bytes 2621440 | tf_op jit(solution)/shard_map/all_gather | solution.py:324
  8.0 29.1 %collective-permute-start.4 = (bf16[512,1024]{1,0:T(8,128)(2,1)}, bf16[512,1024]{1,0:T(8,128)(2,1)}, u32[]{:S(2)}, u32[]{:S(2)}) collective-permute-start(bf16[512,1024]{1,0:T(8,128)(2,1)} %param.13), channel_id=1, source_target_pairs={{1,8},{3,10},{5,12},{7,14},{8,1},{10,3},{12,5},{14,7},{17,24},{19,... | collective-permute-start | bytes 3145736 | tf_op jit(solution)/shard_map/ppermute | solution.py:293
  47.5 82.5 %all-gather.6.cloned.1.call-start = ((), (), s32[]{:S(2)}) async-start(), calls=%async_computation.1 | async-start | bytes 5242880 | tf_op jit(solution)/shard_map/all_gather | solution.py:337
  71.8 36.7 %collective-permute-start.12 = (bf16[512,512]{1,0:T(8,128)(2,1)}, bf16[512,512]{1,0:T(8,128)(2,1)}, u32[]{:S(2)}, u32[]{:S(2)}) collective-permute-start(bf16[512,512]{1,0:T(8,128)(2,1)} %get-tuple-element.43.grad), channel_id=1, source_target_pairs={{0,8},{4,12},{8,0},{12,4},{16,24},{20,28},{24,16},{28,20},{1,9},{5... | collective-permute-start | bytes 1572872 | tf_op jit(solution)/shard_map/ppermute | solution.py:25
  88.2 41.7 %collective-permute-start.10 = (bf16[512,512]{1,0:T(8,128)(2,1)}, bf16[512,512]{1,0:T(8,128)(2,1)}, u32[]{:S(2)}, u32[]{:S(2)}) collective-permute-start(bf16[512,512]{1,0:T(8,128)(2,1)} %get-tuple-element.42.rest_0_.grad), channel_id=1, source_target_pairs={{0,8},{4,12},{8,0},{12,4},{16,24},{20,28},{24,16},{28,20},{1,9},{5... | collective-permute-start | bytes 1572872 | tf_op jit(solution)/shard_map/ppermute | solution.py:25
  89.1 63.7 %collective-permute-start.16 = (bf16[512,512]{1,0:T(8,128)(2,1)S(1)}, bf16[512,512]{1,0:T(8,128)(2,1)S(1)}, u32[]{:S(2)}, u32[]{:S(2)}) collective-permute-start(bf16[512,512]{1,0:T(8,128)(2,1)S(1)} %get-tuple-element.46.grad), channel_id=1, source_target_pairs={{0,8},{4,12},{8,0},{12,4},{16,24},{20,28},{24,16},{28,20},{1,9},{5... | collective-permute-start | bytes 1572872 | tf_op jit(solution)/shard_map/ppermute | solution.py:25
  97.5 26.2 %collective-permute-start.11 = (bf16[512,1024]{1,0:T(8,128)(2,1)S(1)}, bf16[512,1024]{1,0:T(8,128)(2,1)S(1)}, u32[]{:S(2)}, u32[]{:S(2)}) collective-permute-start(bf16[512,1024]{1,0:T(8,128)(2,1)S(1)} %shard_map.92.refs_4_.rest_0_), channel_id=1, source_target_pairs={{0,4},{4,0},{8,12},{12,8},{16,20},{20,16},{24,28},{28,24},{1,5},{5... | collective-permute-start | bytes 3145736 | tf_op jit(solution)/shard_map/ppermute | solution.py:25
  112.9 33.3 %collective-permute-start.17 = (bf16[512,1024]{1,0:T(8,128)(2,1)}, bf16[512,1024]{1,0:T(8,128)(2,1)}, u32[]{:S(2)}, u32[]{:S(2)}) collective-permute-start(bf16[512,1024]{1,0:T(8,128)(2,1)} %shard_map.95.rest_1_), channel_id=1, source_target_pairs={{0,4},{4,0},{8,12},{12,8},{16,20},{20,16},{24,28},{28,24},{1,5},{5... | collective-permute-start | bytes 3145736 | tf_op jit(solution)/shard_map/ppermute | solution.py:25
  126.9 31.5 %collective-permute-start.15 = (bf16[512,512]{1,0:T(8,128)(2,1)}, bf16[512,512]{1,0:T(8,128)(2,1)}, u32[]{:S(2)}, u32[]{:S(2)}) collective-permute-start(bf16[512,512]{1,0:T(8,128)(2,1)} %shard_map.96.rest_0_), channel_id=1, source_target_pairs={{0,16},{4,20},{8,24},{12,28},{16,0},{20,4},{24,8},{28,12},{1,17},{... | collective-permute-start | bytes 1572872 | tf_op jit(solution)/shard_map/ppermute | solution.py:25
  133.6 34.9 %collective-permute-start.14 = (bf16[1024,512]{1,0:T(8,128)(2,1)S(1)}, bf16[1024,512]{1,0:T(8,128)(2,1)S(1)}, u32[]{:S(2)}, u32[]{:S(2)}) collective-permute-start(bf16[1024,512]{1,0:T(8,128)(2,1)S(1)} %shard_map.97.rest_1_), channel_id=1, source_target_pairs={{0,4},{4,0},{8,12},{12,8},{16,20},{20,16},{24,28},{28,24},{1,5},{5... | collective-permute-start | bytes 3145736 | tf_op jit(solution)/shard_map/ppermute | solution.py:25
  135.2 47.3 %collective-permute-start.13 = (bf16[512,1024]{1,0:T(8,128)(2,1)S(1)}, bf16[512,1024]{1,0:T(8,128)(2,1)S(1)}, u32[]{:S(2)}, u32[]{:S(2)}) collective-permute-start(bf16[512,1024]{1,0:T(8,128)(2,1)S(1)} %get-tuple-element.44.rest_1_.grad), channel_id=1, source_target_pairs={{0,8},{4,12},{8,0},{12,4},{16,24},{20,28},{24,16},{28,20},{1,9},{5... | collective-permute-start | bytes 3145736 | tf_op jit(solution)/shard_map/ppermute | solution.py:25
  149.8 37.3 %collective-permute-start.20 = (bf16[512,512]{1,0:T(8,128)(2,1)}, bf16[512,512]{1,0:T(8,128)(2,1)}, u32[]{:S(2)}, u32[]{:S(2)}) collective-permute-start(bf16[512,512]{1,0:T(8,128)(2,1)} %shard_map.98.rest_0_), channel_id=1, source_target_pairs={{0,16},{4,20},{8,24},{12,28},{16,0},{20,4},{24,8},{28,12},{1,17},{... | collective-permute-start | bytes 1572872 | tf_op jit(solution)/shard_map/ppermute | solution.py:25
  156.9 34.2 %collective-permute-start.19 = (bf16[1024,512]{1,0:T(8,128)(2,1)}, bf16[1024,512]{1,0:T(8,128)(2,1)S(1)}, u32[]{:S(2)}, u32[]{:S(2)}) collective-permute-start(bf16[1024,512]{1,0:T(8,128)(2,1)} %shard_map.99.rest_2_), channel_id=1, source_target_pairs={{0,4},{4,0},{8,12},{12,8},{16,20},{20,16},{24,28},{28,24},{1,5},{5... | collective-permute-start | bytes 3145736 | tf_op jit(solution)/shard_map/ppermute | solution.py:25
  173.7 37.0 %collective-permute-start.24 = (bf16[512,512]{1,0:T(8,128)(2,1)}, bf16[512,512]{1,0:T(8,128)(2,1)S(1)}, u32[]{:S(2)}, u32[]{:S(2)}) collective-permute-start(bf16[512,512]{1,0:T(8,128)(2,1)} %shard_map.101.rest_0_), channel_id=1, source_target_pairs={{0,16},{4,20},{8,24},{12,28},{16,0},{20,4},{24,8},{28,12},{1,17},{... | collective-permute-start | bytes 1572872 | tf_op jit(solution)/shard_map/ppermute | solution.py:25
  186.6 29.8 %collective-permute-start.23 = (bf16[1024,512]{1,0:T(8,128)(2,1)}, bf16[1024,512]{1,0:T(8,128)(2,1)S(1)}, u32[]{:S(2)}, u32[]{:S(2)}) collective-permute-start(bf16[1024,512]{1,0:T(8,128)(2,1)} %shard_map.102.rest_2_), channel_id=1, source_target_pairs={{0,4},{4,0},{8,12},{12,8},{16,20},{20,16},{24,28},{28,24},{1,5},{5... | collective-permute-start | bytes 3145736 | tf_op jit(solution)/shard_map/ppermute | solution.py:25
  187.1 47.0 %collective-permute-start.18 = (bf16[512,1024]{1,0:T(8,128)(2,1)S(1)}, bf16[512,1024]{1,0:T(8,128)(2,1)S(1)}, u32[]{:S(2)}, u32[]{:S(2)}) collective-permute-start(bf16[512,1024]{1,0:T(8,128)(2,1)S(1)} %get-tuple-element.47.grad), channel_id=1, source_target_pairs={{0,8},{4,12},{8,0},{12,4},{16,24},{20,28},{24,16},{28,20},{1,9},{5... | collective-permute-start | bytes 3145736 | tf_op jit(solution)/shard_map/ppermute | solution.py:25
  195.9 43.0 %collective-permute-start.22 = (bf16[512,512]{1,0:T(8,128)(2,1)}, bf16[512,512]{1,0:T(8,128)(2,1)S(1)}, u32[]{:S(2)}, u32[]{:S(2)}) collective-permute-start(bf16[512,512]{1,0:T(8,128)(2,1)} %shard_map.104.rest_0_), channel_id=1, source_target_pairs={{0,16},{4,20},{8,24},{12,28},{16,0},{20,4},{24,8},{28,12},{1,17},{... | collective-permute-start | bytes 1572872 | tf_op jit(solution)/shard_map/ppermute | solution.py:25
  206.4 36.0 %collective-permute-start.21 = (bf16[1024,512]{1,0:T(8,128)(2,1)S(1)}, bf16[1024,512]{1,0:T(8,128)(2,1)S(1)}, u32[]{:S(2)}, u32[]{:S(2)}) collective-permute-start(bf16[1024,512]{1,0:T(8,128)(2,1)S(1)} %shard_map.105.rest_2_), channel_id=1, source_target_pairs={{0,4},{4,0},{8,12},{12,8},{16,20},{20,16},{24,28},{28,24},{1,5},{5... | collective-permute-start | bytes 3145736 | tf_op jit(solution)/shard_map/ppermute | solution.py:25
  219.7 47.2 %collective-permute-start.28 = (bf16[512,512]{1,0:T(8,128)(2,1)}, bf16[512,512]{1,0:T(8,128)(2,1)S(1)}, u32[]{:S(2)}, u32[]{:S(2)}) collective-permute-start(bf16[512,512]{1,0:T(8,128)(2,1)} %shard_map.107.rest_0_), channel_id=1, source_target_pairs={{0,16},{4,20},{8,24},{12,28},{16,0},{20,4},{24,8},{28,12},{1,17},{... | collective-permute-start | bytes 1572872 | tf_op jit(solution)/shard_map/ppermute | solution.py:25
  237.4 33.0 %collective-permute-start.27 = (bf16[1024,512]{1,0:T(8,128)(2,1)S(1)}, bf16[1024,512]{1,0:T(8,128)(2,1)S(1)}, u32[]{:S(2)}, u32[]{:S(2)}) collective-permute-start(bf16[1024,512]{1,0:T(8,128)(2,1)S(1)} %shard_map.108.rest_2_), channel_id=1, source_target_pairs={{0,4},{4,0},{8,12},{12,8},{16,20},{20,16},{24,28},{28,24},{1,5},{5... | collective-permute-start | bytes 3145736 | tf_op jit(solution)/shard_map/ppermute | solution.py:25
  244.9 44.4 %collective-permute-start.26 = (bf16[512,512]{1,0:T(8,128)(2,1)S(1)}, bf16[512,512]{1,0:T(8,128)(2,1)S(1)}, u32[]{:S(2)}, u32[]{:S(2)}) collective-permute-start(bf16[512,512]{1,0:T(8,128)(2,1)S(1)} %shard_map.110.rest_0_), channel_id=1, source_target_pairs={{0,16},{4,20},{8,24},{12,28},{16,0},{20,4},{24,8},{28,12},{1,17},{... | collective-permute-start | bytes 1572872 | tf_op jit(solution)/shard_map/ppermute | solution.py:25
  250.3 42.5 %collective-permute-start.25 = (bf16[1024,512]{1,0:T(8,128)(2,1)S(1)}, bf16[1024,512]{1,0:T(8,128)(2,1)S(1)}, u32[]{:S(2)}, u32[]{:S(2)}) collective-permute-start(bf16[1024,512]{1,0:T(8,128)(2,1)S(1)} %shard_map.111.rest_2_), channel_id=1, source_target_pairs={{0,4},{4,0},{8,12},{12,8},{16,20},{20,16},{24,28},{28,24},{1,5},{5... | collective-permute-start | bytes 3145736 | tf_op jit(solution)/shard_map/ppermute | solution.py:25
  272.8 39.0 %collective-permute-start.30 = (bf16[512,512]{1,0:T(8,128)(2,1)S(1)}, bf16[512,512]{1,0:T(8,128)(2,1)S(1)}, u32[]{:S(2)}, u32[]{:S(2)}) collective-permute-start(bf16[512,512]{1,0:T(8,128)(2,1)S(1)} %shard_map.113.rest_2_), channel_id=1, source_target_pairs={{0,16},{4,20},{8,24},{12,28},{16,0},{20,4},{24,8},{28,12},{1,17},{... | collective-permute-start | bytes 1572872 | tf_op jit(solution)/shard_map/ppermute | solution.py:25
  (40 other events, 330.2 us)
Sparse Core Ops, SparseCore 0:
  9.6 37.1 all-gather.3
  48.3 25.3 all-gather.7
  75.3 34.4 all-gather.5
